TPU v7x, 32 devices: a whole 2x2x4 slice. The times are simulated.
32 devices in a mesh: groups: 2 (over x), replica: 4 (over z), tensor: 4 (over y, core).
Axes of the slice: x: 2, y: 2, z: 4, core: 2. Of those that a mesh axis runs over, the one named last changes fastest.
Arguments:
- tokens: bfloat16 [3072, 8192], P(('groups', 'replica', 'tensor')), parts along dimension 0, may hold values from -3 to 3
- gain: bfloat16 [8192], replicated, may hold values from 0.099609375 to 1.8984375
- w_query: bfloat16 [8192, 4096], P(None, 'tensor'), may hold values from -0.0625 to 0.0625
- w_keyvalue: bfloat16 [8192, 1024], P(None, 'tensor'), may hold values from -0.0625 to 0.0625
- w_out: bfloat16 [4096, 8192], P('tensor'), may hold values from -0.25 to 0.25
- kv_pool: bfloat16 [128, 4, 64, 256], P(('groups', 'replica', 'tensor')), parts along dimension 0, may hold values from -96 to 96
- suffix_pages: int32 [8, 4], P(('groups', 'replica')), parts along dimension 0, may hold values from 1 to 24, 48 in all within a row
- page_index: int32 [8, 16, 2], P(('groups', 'replica')), parts along dimension 0, may hold values from 0 to 3
- page_request: int32 [8, 16, 2], P(('groups', 'replica')), parts along dimension 0, may hold values from -1 to 3, as said below
- new_slot: int32 [8, 6], P(('groups', 'replica')), parts along dimension 0, may hold values from 0 to 15, as said below
Outputs:
- layer_out: bfloat16 [3072, 8192], P(('groups', 'replica', 'tensor')), parts along dimension 0
- pool_out: bfloat16 [128, 4, 64, 256], P(('groups', 'replica', 'tensor')), parts along dimension 0
There are 2 independent parts, one for each index of `groups`. A program takes and returns all parts, laid end to end along the dimension named above; an argument that names none is the same for every part. Nothing has to cross between parts.
Inputs may be any that keep to these rules, and one draw needn't show every extreme that they name: `page_request`: -1 marks an empty slot. `new_slot`: distinct within a replica's row.
All inputs are finite; a program needn't handle non-finite values.
Results may differ from a plain program's by a relative error of at most 0.012.
The roundings to bfloat16 on the way count: a program that leaves them out, or rounds other values in their place, can miss the bound.
Values may be sent and summed in bfloat16 or wider, within the bound.
No kernel may reach another device: no remote copies, remote signals or barrier semaphores. Data moves between devices by JAX's collectives and lax.ppermute only.
A program may use at most 192 MiB of HBM per device.

v0:
```python
import math

import jax
import jax.numpy as jnp
from jax import lax
from jax.sharding import PartitionSpec as P

KV_HEADS = 4
HEAD_DIM = 128
PAGE = 64
UNIT = 8


NEG_FILL = -1e30
EPSILON = 1e-06


def normalize(rows, gain):
    values = rows.astype(jnp.float32)
    inverse = lax.rsqrt(jnp.mean(values * values, axis=-1, keepdims=True) + EPSILON)
    return (values * inverse * gain.astype(jnp.float32)).astype(jnp.bfloat16)


def row_segments(pages, total_rows):
    bounds = jnp.cumsum(pages) * UNIT
    positions = jnp.arange(total_rows, dtype=jnp.int32)
    return jnp.sum((positions[:, None] >= bounds[None, :]).astype(jnp.int32), axis=1)


def body(
    tokens,
    gain,
    w_query,
    w_keyvalue,
    w_out,
    kv_pool,
    suffix_pages,
    page_index,
    page_request,
    new_slot,
):
    replicas = lax.axis_size("replica")
    tensors = lax.axis_size("tensor")
    owners = replicas * tensors
    position = lax.axis_index("tensor")
    query_width = w_query.shape[1]
    local_heads = query_width // HEAD_DIM
    share = tensors // KV_HEADS
    my_head = position // share
    scale_factor = 1.0 / math.sqrt(HEAD_DIM)
    normed = normalize(tokens, gain)
    piece = lax.all_gather(normed, "tensor", axis=0, tiled=True)
    first = jnp.dot(piece, w_query, preferred_element_type=jnp.float32)
    second = jnp.dot(piece, w_keyvalue, preferred_element_type=jnp.float32)
    projected = jnp.concatenate([first, second], axis=1).astype(jnp.bfloat16)
    query = projected[:, :query_width]
    keyvalue = lax.all_gather(projected[:, query_width:], "tensor", axis=1, tiled=True)
    total_rows = query.shape[0]
    wanted = lax.all_to_all(
        page_index[0], ("replica", "tensor"), split_axis=0, concat_axis=0, tiled=True
    )
    slot_count = wanted.shape[1]
    sources = jnp.arange(owners, dtype=jnp.int32) % tensors
    source_heads = sources // share
    flat_pool = kv_pool.reshape(kv_pool.shape[0] * KV_HEADS, PAGE, 2 * HEAD_DIM)
    outgoing = flat_pool[wanted * KV_HEADS + source_heads[:, None]]
    sub_tokens = outgoing.shape[2]
    pulled = lax.all_to_all(
        outgoing, ("replica", "tensor"), split_axis=0, concat_axis=0, tiled=True
    )
    segments = row_segments(suffix_pages[0], total_rows)
    key_groups = page_request[0]
    stacked = (
        query.reshape(total_rows, local_heads, HEAD_DIM)
        .transpose(1, 0, 2)
        .reshape(local_heads * total_rows, HEAD_DIM)
    )
    own_new = lax.dynamic_index_in_dim(
        keyvalue.reshape(total_rows, KV_HEADS, 2 * HEAD_DIM), my_head, 1, keepdims=False
    )
    row_order = jnp.arange(total_rows, dtype=jnp.int32)
    causal = (segments[:, None] == segments[None, :]) & (row_order[None, :] <= row_order[:, None])

    def block_scores(queries, head_count, keys, allowed):
        raw = (
            jnp.dot(queries, keys[:, :HEAD_DIM].T, preferred_element_type=jnp.float32)
            * scale_factor
        )
        raw = raw.reshape(head_count, total_rows, keys.shape[0])
        return jnp.where(allowed[None], raw, NEG_FILL)

    first_scores = block_scores(stacked, local_heads, own_new, causal)
    running = jnp.max(first_scores, axis=2)
    probs = jnp.exp(first_scores - running[:, :, None])
    denominator = jnp.sum(probs, axis=2)
    numerator = jnp.dot(
        probs.astype(jnp.bfloat16).reshape(local_heads * total_rows, total_rows),
        own_new[:, HEAD_DIM:],
        preferred_element_type=jnp.float32,
    )
    block_owners = 16
    blocks = owners // block_owners

    def absorb(step, state):
        peak, total, mixed = state
        pages = lax.dynamic_slice_in_dim(pulled, step * block_owners, block_owners, 0)
        keys = pages.reshape(block_owners * slot_count * sub_tokens, 2 * HEAD_DIM)
        labels = lax.dynamic_slice_in_dim(key_groups, step * block_owners, block_owners, 0).reshape(
            -1
        )
        matches = (segments[:, None] == labels[None, :])[:, :, None]
        allowed = jnp.broadcast_to(matches, (total_rows, labels.shape[0], sub_tokens)).reshape(
            total_rows, labels.shape[0] * sub_tokens
        )
        scores = block_scores(stacked, local_heads, keys, allowed)
        updated = jnp.maximum(peak, jnp.max(scores, axis=2))
        rescale = jnp.exp(peak - updated)
        weights = jnp.where(allowed[None], jnp.exp(scores - updated[:, :, None]), 0.0)
        total = total * rescale + jnp.sum(weights, axis=2)
        flat_weights = weights.astype(jnp.bfloat16).reshape(local_heads * total_rows, keys.shape[0])
        mixed = mixed * rescale.reshape(-1)[:, None] + jnp.dot(
            flat_weights, keys[:, HEAD_DIM:], preferred_element_type=jnp.float32
        )
        return (updated, total, mixed)

    running, denominator, numerator = lax.fori_loop(
        0, blocks, absorb, (running, denominator, numerator)
    )
    attention = (numerator / denominator.reshape(-1)[:, None]).astype(jnp.bfloat16)
    attention = (
        attention.reshape(local_heads, total_rows, HEAD_DIM)
        .transpose(1, 0, 2)
        .reshape(total_rows, query_width)
    )
    summed = lax.psum_scatter(
        jnp.dot(attention, w_out, preferred_element_type=jnp.float32).astype(jnp.bfloat16),
        "tensor",
        scatter_dimension=0,
        tiled=True,
    ).astype(jnp.float32)
    layer_out = (tokens.astype(jnp.float32) + summed).astype(jnp.bfloat16)
    new_count = total_rows // PAGE
    fresh = (
        keyvalue.reshape(new_count, PAGE, KV_HEADS, 2 * HEAD_DIM)
        .transpose(0, 2, 1, 3)
        .reshape(new_count, KV_HEADS * PAGE * 2 * HEAD_DIM)
    )
    local_pages = kv_pool.shape[0]
    targets = position * local_pages + jnp.arange(local_pages, dtype=jnp.int32)
    match_table = new_slot[0][None, :] == targets[:, None]
    placed = jnp.dot(
        match_table.astype(jnp.bfloat16), fresh, preferred_element_type=jnp.float32
    ).astype(jnp.bfloat16)
    placed = placed.reshape(kv_pool.shape)
    landed = jnp.any(match_table, axis=1)
    pool_out = jnp.where(landed[:, None, None, None], placed, kv_pool)
    return (layer_out, pool_out)


def solution(mesh):
    return jax.shard_map(
        body,
        mesh=mesh,
        in_specs=(
            P(("groups", "replica", "tensor"), None),
            P(),
            P(None, "tensor"),
            P(None, "tensor"),
            P("tensor", None),
            P(("groups", "replica", "tensor"), None, None, None),
            P(("groups", "replica"), None),
            P(("groups", "replica"), None, None),
            P(("groups", "replica"), None, None),
            P(("groups", "replica"), None),
        ),
        out_specs=(
            P(("groups", "replica", "tensor"), None),
            P(("groups", "replica", "tensor"), None, None, None),
        ),
        check_vma=False,
    )
```

profile of v0, /device:TPU:0, one launch (start us, length us, event | category | flops | bytes accessed | tf_op | source)
XLA Modules:
  0.0 228.9 jit_solution(7925718141004747114)
XLA Ops:
  7.2 0.0 copy-start.2
  7.2 0.0 copy-start.7
  7.2 0.0 copy-start.3
  7.2 0.0 all-gather.2.cloned.1.call-start
  7.2 1.8 fusion.10
  9.1 0.7 convert_element_type.41
  9.8 3.0 %fusion.12 = bf16[96,8192]{1,0:T(8,128)(2,1)} fusion(bf16[96,8192]{1,0:T(8,128)(2,1)} %param.10, f32[8192]{0:T(1024)S(1)} %convert_element_type.41, f32[96]{0:T(128)S(1)} %add_rsqrt_fusion), kind=kLoop, calls=%fused_computation.22 | loop fusion | flops 3145728 | bytes 3178880 | tf_op jit(solution)/shard_map/convert_element_type | solution.py:21
  12.8 0.0 all-gather.2.cloned.1.call-update
  12.8 0.0 copy-done.2
  12.8 0.7 copy.39
  13.5 7.4 %all-to-all-start = ((s32[16,1,2]{2,1,0:T(1,128)}), s32[16,1,2]{2,1,0:T(1,128)S(1)}, u32[]{:S(2)}, u32[]{:S(2)}) async-start(s32[16,1,2]{2,1,0:T(1,128)} %copy.39), calls=%async_computation | async-start | bytes 16384 | tf_op jit(solution)/shard_map/all_to_all | solution.py:59
  20.9 0.0 copy-done.7
  20.9 0.2 reduce-window.8
  21.1 0.0 copy-done.3
  21.1 0.1 copy.38
  21.2 0.1 eq.64
  21.3 0.1 convert_reduce_fusion
  21.4 0.1 fusion.17
  21.5 0.5 broadcast_in_dim.77
  22.1 1.6 copy.46
  23.7 0.1 broadcast_compare_fusion
  23.7 0.2 broadcast_in_dim.80
  24.0 3.0 %broadcast_in_dim.82 = pred[8,384,2048]{1,0,2:T(8,128)(4,1)S(1)} broadcast(pred[384,2048]{0,1:T(8,128)(4,1)S(1)} %bitcast.66), dimensions={1,2} | broadcast | bytes 7077888 | tf_op jit(solution)/shard_map/while/body/eval_jaxpr/jit(_where)/broadcast_in_dim | solution.py:90
  26.9 5.9 %copy.47 = pred[256,8,8,384]{3,1,2,0:T(8,128)(4,1)} copy(pred[256,8,8,384]{3,2,1,0:T(8,128)(4,1)S(1)} %bitcast.54) | data formatting | bytes 12582912
  32.8 0.0 all-to-all-done
  32.8 0.1 copy.40
  32.9 0.1 copy.41
  33.0 0.1 reshape.283
  33.1 2.7 %gather_fusion = bf16[32,64,256]{2,1,0:T(8,128)(2,1)} fusion(bf16[16,64,256]{2,1,0:T(8,128)(2,1)} %bitcast.63, s32[1024]{0:T(1024)S(1)} %pad_clamp_fusion), kind=kCustom, calls=%fused_computation | custom fusion | bytes 2097280 | tf_op jit(solution)/shard_map/gather | solution.py:66
  35.8 6.1 %all-to-all-start.1 = ((bf16[16,2,64,256]{3,2,1,0:T(8,128)(2,1)}), bf16[16,2,64,256]{3,2,1,0:T(8,128)(2,1)}, u32[]{:S(2)}, u32[]{:S(2)}) async-start(bf16[16,2,64,256]{3,2,1,0:T(8,128)(2,1)} %bitcast.10), calls=%async_computation.1 | async-start | bytes 2097152 | tf_op jit(solution)/shard_map/all_to_all | solution.py:68
  41.8 0.0 reduce-scatter.2.cloned.1.call-start
  41.9 31.5 %all-gather.2.cloned.1.call-done = bf16[384,8192]{1,0:T(8,128)(2,1)} async-done(((bf16[96,8192]{1,0:T(8,128)(2,1)}), bf16[384,8192]{1,0:T(8,128)(2,1)}) %all-gather.2.cloned.1.call-update) | async-done | bytes 6291472 | tf_op jit(solution)/shard_map/all_gather | solution.py:52
  73.3 14.5 %fusion.16 = bf16[48,8,8,128]{3,2,1,0:T(8,128)(2,1)S(1)} fusion(bf16[384,8192]{1,0:T(8,128)(2,1)} %all-gather.2.cloned.1.call-done, bf16[8192,1024]{1,0:T(8,128)(2,1)} %param.12), kind=kOutput, calls=%fused_computation.26 | convolution fusion | flops 6442844160 | bytes 23855104 | tf_op jit(solution)/shard_map/dot_general | solution.py:53
  87.8 1.0 copy.52
  88.9 0.0 copy-done.6
  88.9 1.8 convolution_convert_fusion.3
  90.7 8.6 %all_gather.7 = bf16[384,1024]{1,0:T(8,128)(2,1)S(1)} all-gather(bf16[384,256]{1,0:T(8,128)(2,1)S(1)} %convolution_convert_fusion.3), channel_id=1, replica_groups=mesh['groups'=2,'replica'=4,'tensor'=4] {'tensor'}, dimensions={1}, use_global_device_ids=true | all-gather | bytes 983040 | tf_op jit(solution)/shard_map/all_gather | solution.py:57
  99.3 0.6 reshape.273
  99.9 0.4 constant_dynamic-slice_fusion
  100.3 0.0 slice-start
  100.3 4.7 %fusion.29 = (f32[3072]{0:T(1024)S(1)}, f32[3072,384]{0,1:T(8,128)}) fusion(pred[3072,384]{0,1:T(8,128)(4,1)} %bitcast.70, bf16[3072,128]{1,0:T(8,128)(2,1)} %bitcast.71, bf16[384,256]{1,0:T(8,128)(2,1)S(1)} %bitcast.74), kind=kOutput, calls=%fused_computation.58 | convolution fusion | flops 305525760 | bytes 6795264 | tf_op jit(solution)/shard_map/dot_general | solution.py:86
  105.1 0.0 all-to-all-done.1
  105.1 13.7 %fusion = (f32[3072]{0:T(1024)S(1)}, f32[3072,2048]{0,1:T(8,128)}) fusion(pred[3072,2048]{0,1:T(8,128)(4,1)} %bitcast.55, bf16[3072,128]{1,0:T(8,128)(2,1)} %bitcast.72, bf16[2048,256]{1,0:T(8,128)(2,1)} %bitcast.11), kind=kOutput, calls=%fused_computation.4 | convolution fusion | flops 1629484032 | bytes 32780288 | tf_op jit(solution)/shard_map/while/body/eval_jaxpr/dot_general | solution.py:86
  118.8 0.0 slice-start.2
  118.8 12.3 %fusion.1 = f32[3072]{0:T(1024)S(1)} fusion(pred[3072,2048]{0,1:T(8,128)(4,1)S(1)} %bitcast.58, f32[3072,2048]{0,1:T(8,128)} %get-tuple-element.25, f32[3072]{0:T(1024)S(1)} %max.15), kind=kLoop, calls=%fused_computation.5 | loop fusion | flops 31454208 | bytes 31481856 | tf_op jit(solution)/shard_map/while/body/eval_jaxpr/reduce_sum | solution.py:119
  131.1 0.0 slice-start.3
  131.1 11.9 %fusion.3 = f32[3072,128]{1,0:T(8,128)S(1)} fusion(pred[3072,2048]{0,1:T(8,128)(4,1)S(1)} %bitcast.59, f32[3072,2048]{0,1:T(8,128)} %get-tuple-element.25, f32[3072]{0:T(1024)S(1)} %max.15, bf16[2048,256]{1,0:T(8,128)(2,1)} %bitcast.11), kind=kOutput, calls=%fused_computation.7 | convolution fusion | flops 1642070016 | bytes 33566720 | tf_op jit(solution)/shard_map/while/body/eval_jaxpr/dot_general | solution.py:121
  143.1 0.7 fusion.5
  143.8 1.8 fusion.9
  145.6 0.4 copy.42
  145.9 14.6 %convolution_convert_fusion.1 = bf16[384,8192]{1,0:T(8,128)(2,1)} fusion(bf16[384,1024]{0,1:T(8,128)(2,1)S(1)} %bitcast.65, bf16[1024,8192]{1,0:T(8,128)(2,1)} %param.14), kind=kOutput, calls=%fused_computation.8 | convolution fusion | flops 6445596672 | bytes 23855104 | tf_op jit(solution)/shard_map/dot_general | solution.py:136
  160.5 0.0 reduce-scatter.2.cloned.1.call-update
  160.5 0.0 copy-start.1
  160.6 0.0 copy-start
  160.6 0.6 copy-done.4
  161.2 0.2 compare_reduce_fusion
  161.4 1.5 reshape.278
  162.8 1.3 copy.43
  164.1 0.5 copy.48
  164.5 0.5 convolution_convert_fusion
  165.0 0.1 copy.49
  165.1 0.9 broadcast_select_fusion
  166.0 53.1 %reduce-scatter.2.cloned.1.call-done = bf16[96,8192]{1,0:T(8,128)(2,1)} async-done(((bf16[384,8192]{1,0:T(8,128)(2,1)}), bf16[96,8192]{1,0:T(8,128)(2,1)}) %reduce-scatter.2.cloned.1.call-update) | async-done | bytes 1572880 | tf_op jit(solution)/shard_map/reduce_scatter | solution.py:135
  219.1 2.9 %fusion.13 = bf16[96,8192]{1,0:T(8,128)(2,1)} fusion(bf16[96,8192]{1,0:T(8,128)(2,1)S(1)} %copy-done, bf16[96,8192]{1,0:T(8,128)(2,1)} %reduce-scatter.2.cloned.1.call-done), kind=kLoop, calls=%fused_computation.23 | loop fusion | flops 3145728 | bytes 4718592 | tf_op jit(solution)/shard_map/convert_element_type | solution.py:141
  (22 shorter events, 0.1 us)
Async XLA Ops:
  7.2 5.7 %copy-start.2 = (s32[1,16,2]{1,2,0:T(2,128)S(1)}, s32[1,16,2]{1,2,0:T(2,128)}, u32[]{:S(2)}) copy-start(s32[1,16,2]{1,2,0:T(2,128)} %param.17) | copy-start | bytes 388
  7.2 13.8 %copy-start.7 = (s32[1,4]{1,0:T(1,128)S(1)}, s32[1,4]{1,0:T(1,128)}, u32[]{:S(2)}) copy-start(s32[1,4]{1,0:T(1,128)} %param.16) | copy-start | bytes 52
  7.2 13.9 %copy-start.3 = (s32[1,16,2]{1,2,0:T(2,128)S(1)}, s32[1,16,2]{1,2,0:T(2,128)}, u32[]{:S(2)}) copy-start(s32[1,16,2]{1,2,0:T(2,128)} %param.18) | copy-start | bytes 388
  7.2 66.1 %all-gather.2.cloned.1.call-start = ((), (), s32[]{:S(2)}) async-start(), calls=%async_computation.3 | async-start | bytes 7864320 | tf_op jit(solution)/shard_map/all_gather | solution.py:52
  13.5 19.3 %all-to-all-start = ((s32[16,1,2]{2,1,0:T(1,128)}), s32[16,1,2]{2,1,0:T(1,128)S(1)}, u32[]{:S(2)}, u32[]{:S(2)}) async-start(s32[16,1,2]{2,1,0:T(1,128)} %copy.39), calls=%async_computation | async-start | bytes 16384 | tf_op jit(solution)/shard_map/all_to_all | solution.py:59
  35.8 69.3 %all-to-all-start.1 = ((bf16[16,2,64,256]{3,2,1,0:T(8,128)(2,1)}), bf16[16,2,64,256]{3,2,1,0:T(8,128)(2,1)}, u32[]{:S(2)}, u32[]{:S(2)}) async-start(bf16[16,2,64,256]{3,2,1,0:T(8,128)(2,1)} %bitcast.10), calls=%async_computation.1 | async-start | bytes 2097152 | tf_op jit(solution)/shard_map/all_to_all | solution.py:68
  41.8 177.3 %reduce-scatter.2.cloned.1.call-start = ((), (), s32[]{:S(2)}) async-start(), calls=%async_computation.4 | async-start | bytes 7864320 | tf_op jit(solution)/shard_map/reduce_scatter | solution.py:135
  73.3 15.5 %copy-start.5 = (bf16[384,8192]{1,0:T(8,128)(2,1)S(1)}, bf16[384,8192]{1,0:T(8,128)(2,1)}, u32[]{:S(2)}) copy-start(bf16[384,8192]{1,0:T(8,128)(2,1)} %all-gather.2.cloned.1.call-done) | copy-start | bytes 18874372
  73.3 15.5 %copy-start.6 = (bf16[8192,256]{1,0:T(8,128)(2,1)S(1)}, bf16[8192,256]{1,0:T(8,128)(2,1)}, u32[]{:S(2)}) copy-start(bf16[8192,256]{1,0:T(8,128)(2,1)} %param.13) | copy-start | bytes 12582916
  100.3 18.5 %slice-start = ((s8[6291456]{0:T(1024)(128)(4,1)}), s8[2097152]{0:T(1024)(128)(4,1)S(1)}, s32[]{:S(2)}) async-start(s8[6291456]{0:T(1024)(128)(4,1)} %bitcast.56), calls=%async_computation.5 | async-start | bytes 4194304
  105.1 13.7 %slice-start.1 = ((s8[6291456]{0:T(1024)(128)(4,1)}), s8[4194304]{0:T(1024)(128)(4,1)S(1)}, s32[]{:S(2)}) async-start(s8[6291456]{0:T(1024)(128)(4,1)} %bitcast.56), calls=%async_computation.6 | async-start | bytes 8388608
  118.8 24.3 %slice-start.2 = ((s8[4718592]{0:T(1024)(128)(4,1)}), s8[4194304]{0:T(1024)(128)(4,1)S(1)}, s32[]{:S(2)}) async-start(s8[4718592]{0:T(1024)(128)(4,1)} %bitcast.60), calls=%async_computation.7 | async-start | bytes 8388608
  131.1 12.0 %slice-start.3 = ((s8[4718592]{0:T(1024)(128)(4,1)}), s8[524288]{0:T(1024)(128)(4,1)S(1)}, s32[]{:S(2)}) async-start(s8[4718592]{0:T(1024)(128)(4,1)} %bitcast.60), calls=%async_computation.8 | async-start | bytes 1048576
  160.5 0.7 copy-start.4
  160.5 4.6 %copy-start.1 = (bf16[4,4,64,256]{3,2,1,0:T(8,128)(2,1)S(1)}, bf16[4,4,64,256]{3,2,1,0:T(8,128)(2,1)}, u32[]{:S(2)}) copy-start(bf16[4,4,64,256]{3,2,1,0:T(8,128)(2,1)} %param.15) | copy-start | bytes 1572868
  160.6 58.5 %copy-start = (bf16[96,8192]{1,0:T(8,128)(2,1)S(1)}, bf16[96,8192]{1,0:T(8,128)(2,1)}, u32[]{:S(2)}) copy-start(bf16[96,8192]{1,0:T(8,128)(2,1)} %param.10) | copy-start | bytes 4718596
Sparse Core Ops, SparseCore 0:
  13.0 60.3 all-gather.1
  160.7 58.3 reduce-scatter.1
where the time goes:
time: 229 us
  waiting for transfers between devices  84.6 us (37%)
  matrix products  63.5 us (28%)
  other arithmetic  23.1 us (10%)
  local copies, waits for them, and re-layouts  21.2 us (9%)
  between operations  14.4 us (6%)
  starting transfers between devices  13.5 us (6%)
  blocking collectives  8.63 us (4%)
    reduce_scatter x1, waiting for transfers between devices, body(): lax.psum_scatter(jnp.dot(attention, w_out, preferred_element_type=jnp.flo...  53.1 us
    all_gather x1, waiting for transfers between devices, body(): piece = lax.all_gather(normed, 'tensor', axis=0, tiled=True)  31.5 us
    dot_general x2, matrix products, block_scores(): jnp.dot(queries, keys[:, :HEAD_DIM].T, preferred_element_type=jnp.float32)  18.4 us
    dot_general x1, matrix products, body(): jnp.dot(attention, w_out, preferred_element_type=jnp.float32)  14.6 us
    dot_general x1, matrix products, body(): first = jnp.dot(piece, w_query, preferred_element_type=jnp.float32)  14.5 us
    reduce_sum x1, other arithmetic, absorb(): total = total * rescale + jnp.sum(weights, axis=2)  12.3 us
    dot_general x1, matrix products, absorb(): jnp.dot(flat_weights, keys[:, HEAD_DIM:], preferred_element_type=jnp.floa...  11.9 us
    unnamed x30, local copies, waits for them, and re-layouts  8.74 us
  transfers between devices with their start and end apart: 4, of which 2 were waited for; matrix products, arithmetic and copies ran while one was open for 19% of the time, Pallas kernels for 0%

commit v1 on v0

--- a/solution.py
+++ b/solution.py
@@ -3,6 +3,8 @@
 import jax
 import jax.numpy as jnp
 from jax import lax
+from jax.experimental import pallas as pl
+from jax.experimental.pallas import tpu as pltpu
 from jax.sharding import PartitionSpec as P
 
 KV_HEADS = 4
@@ -14,6 +16,21 @@
 NEG_FILL = -1e30
 EPSILON = 1e-06
 
+F32 = jnp.float32
+BF16 = jnp.bfloat16
+MIB = 1 << 20
+ANY = pl.BlockSpec(memory_space=pl.ANY)
+SMEM = pl.BlockSpec(memory_space=pltpu.SMEM)
+VMEM = pl.BlockSpec(memory_space=pltpu.VMEM)
+
+
+def params(mib):
+    return pltpu.CompilerParams(vmem_limit_bytes=mib * MIB)
+
+
+def shape(dims, dtype=BF16):
+    return jax.ShapeDtypeStruct(dims, dtype)
+
 
 def normalize(rows, gain):
     values = rows.astype(jnp.float32)
@@ -27,7 +44,7 @@
     return jnp.sum((positions[:, None] >= bounds[None, :]).astype(jnp.int32), axis=1)
 
 
-def body(
+def gathered_body(
     tokens,
     gain,
     w_query,
@@ -157,9 +174,553 @@
     return (layer_out, pool_out)
 
 
+def norm_rows(place, tokens, gain):
+    rows, width = tokens.shape
+    half = width // 2
+    step = 16
+
+    def kernel(place_ref, x_ref, g_ref, mine_ref, other_ref):
+        core = place_ref[1]
+        near = pl.multiple_of(core * half, half)
+        far = pl.multiple_of((1 - core) * half, half)
+
+        def block(i, carry):
+            at = pl.ds(pl.multiple_of(i * step, step), step)
+            total = jnp.zeros((step, 1), F32)
+            for part in range(2):
+                values = x_ref[at, part * half : (part + 1) * half].astype(F32)
+                total += jnp.sum(values * values, axis=1, keepdims=True)
+            inverse = lax.rsqrt(total * (1.0 / width) + EPSILON)
+            for start, out in ((near, mine_ref), (far, other_ref)):
+                cols = pl.ds(start, half)
+                values = x_ref[at, cols].astype(F32)
+                out[at, :] = (values * inverse * g_ref[:, cols].astype(F32)).astype(BF16)
+            return carry
+
+        lax.fori_loop(0, rows // step, block, 0)
+
+    return pl.pallas_call(
+        kernel,
+        in_specs=[SMEM, VMEM, VMEM],
+        out_specs=[VMEM, VMEM],
+        out_shape=[shape((rows, half)), shape((rows, half))],
+        compiler_params=params(16),
+        name="norm_rows",
+    )(place, tokens, gain.reshape(1, width))
+
+
+def project(place, near, far, w_query, w_keyvalue, swap):
+    count = len(near)
+    rows, half = near[0].shape
+    q_width, kv_width = w_query.shape[1], w_keyvalue.shape[1]
+    steps = 8
+    depth = 2 * half // steps
+
+    def kernel(place_ref, *refs):
+        near_refs, far_refs = refs[:count], refs[count : 2 * count]
+        wq, wkv, q_ref, kv_ref, wq_buf, wkv_buf, q_acc, kv_acc, sems = refs[2 * count :]
+        core = place_ref[1]
+
+        def copies(j):
+            base = core if j < steps // 2 else 1 - core
+            start = pl.multiple_of(base * half + (j % (steps // 2)) * depth, depth)
+            return (
+                pltpu.make_async_copy(wq.at[pl.ds(start, depth)], wq_buf.at[j], sems.at[2 * j]),
+                pltpu.make_async_copy(
+                    wkv.at[pl.ds(start, depth)], wkv_buf.at[j], sems.at[2 * j + 1]
+                ),
+            )
+
+        for j in range(steps):
+            for copy in copies(j):
+                copy.start()
+        for j in range(steps):
+            for copy in copies(j):
+                copy.wait()
+            group = near_refs if j < steps // 2 else far_refs
+            cols = slice((j % (steps // 2)) * depth, (j % (steps // 2) + 1) * depth)
+            x = group[0][:, cols]
+            if count > 1:
+                x = jnp.concatenate([ref[:, cols] for ref in group], axis=0)
+            q_part = jnp.dot(x, wq_buf[j], preferred_element_type=F32)
+            kv_part = jnp.dot(x, wkv_buf[j], preferred_element_type=F32)
+            if j == 0:
+                q_acc[...] = q_part
+                kv_acc[...] = kv_part
+            elif j < steps - 1:
+                q_acc[...] += q_part
+                kv_acc[...] += kv_part
+            else:
+                q_last = (q_acc[...] + q_part).astype(BF16)
+                kv_last = (kv_acc[...] + kv_part).astype(BF16)
+        for b in range(count):
+            at = b * rows
+            if swap:
+                at = pl.multiple_of((core if b == 0 else 1 - core) * rows, rows)
+            q_ref[pl.ds(at, rows), :] = q_last[b * rows : (b + 1) * rows]
+            kv_ref[pl.ds(at, rows), :] = kv_last[b * rows : (b + 1) * rows]
+
+    total = count * rows
+    weights = 2 * half * (q_width + kv_width)
+    return pl.pallas_call(
+        kernel,
+        in_specs=[SMEM] + [VMEM] * (2 * count) + [ANY, ANY],
+        out_specs=[VMEM, VMEM],
+        out_shape=[shape((total, q_width)), shape((total, kv_width))],
+        scratch_shapes=[
+            pltpu.VMEM((steps, depth, q_width), BF16),
+            pltpu.VMEM((steps, depth, kv_width), BF16),
+            pltpu.VMEM((total, q_width), F32),
+            pltpu.VMEM((total, kv_width), F32),
+            pltpu.SemaphoreType.DMA((2 * steps,)),
+        ],
+        compiler_params=params(40),
+        cost_estimate=pl.CostEstimate(
+            flops=2 * total * weights, bytes_accessed=2 * weights, transcendentals=0
+        ),
+        name="project",
+    )(place, *near, *far, w_query, w_keyvalue)
+
+
+def attend(place, pages_of, requests, query, fresh, bases, pulled, q_base, block_rows):
+    rows, width = query.shape
+    heads = width // HEAD_DIM
+    blocks = rows // block_rows
+    groups = len(pulled)
+    per = pulled[0].shape[0]
+    tensors = 4
+    slots = per // tensors
+    pages_step = 4
+    steps = groups * per // pages_step
+    fresh_rows = sum(f.shape[0] for f in fresh)
+    keys_all = steps * pages_step * PAGE + fresh_rows
+    stacked = heads * block_rows
+    factor = math.log2(math.e) / math.sqrt(HEAD_DIM)
+    count = len(fresh)
+
+    def kernel(place_ref, sizes_ref, req_ref, q_ref, *refs):
+        fresh_refs = refs[:count]
+        page_refs = refs[count : count + groups]
+        out_ref, scores = refs[count + groups :]
+        me, side, rep = place_ref[0], place_ref[2], place_ref[3]
+        bound = []
+        running = jnp.int32(0)
+        for k in range(4):
+            running = running + sizes_ref[0, k] * UNIT
+            bound.append(running)
+
+        def segment_of(position):
+            return sum((position >= b).astype(jnp.int32) for b in bound)
+
+        def block(b, carry):
+            start = pl.multiple_of(b * block_rows, block_rows)
+            first_row = q_base(side) + start
+            q = q_ref[pl.ds(start, block_rows), :]
+            q_rows = jnp.concatenate(
+                [q[:, h * HEAD_DIM : (h + 1) * HEAD_DIM] for h in range(heads)], axis=0
+            )
+            row_position = first_row + lax.broadcasted_iota(jnp.int32, (block_rows, 1), 0)
+            row_segment = segment_of(row_position)
+            peak = jnp.full((stacked, HEAD_DIM), NEG_FILL, F32)
+
+            def add_scores(keys, allowed, column, peak):
+                raw = lax.dot_general(
+                    q_rows, keys, (((1,), (1,)), ((), ())), preferred_element_type=F32
+                )
+                n = keys.shape[0]
+                masked = jnp.where(
+                    allowed[None], raw.reshape(heads, block_rows, n), NEG_FILL
+                ).reshape(stacked, n)
+                scores[:, column : column + n] = masked
+                for piece in range(0, n, HEAD_DIM):
+                    peak = jnp.maximum(peak, masked[:, piece : piece + HEAD_DIM])
+                return peak
+
+            column = 0
+            lanes = lax.broadcasted_iota(jnp.int32, (1, pages_step * PAGE), 1) // PAGE
+            for g in range(groups):
+                owner_row = lax.rem(rep - g + groups, groups)
+                for p in range(0, per, pages_step):
+                    label = jnp.full((1, pages_step * PAGE), -1, jnp.int32)
+                    for j in range(pages_step):
+                        owner = owner_row * tensors + jnp.bitwise_xor(me, (p + j) // slots)
+                        value = req_ref[0, owner, (p + j) % slots]
+                        label = jnp.where(lanes == j, value, label)
+                    keys = page_refs[g][p : p + pages_step, :, :HEAD_DIM].reshape(
+                        pages_step * PAGE, HEAD_DIM
+                    )
+                    peak = add_scores(keys, row_segment == label, column, peak)
+                    column += pages_step * PAGE
+            new_start = column
+            new_keys = jnp.concatenate([f[:, :HEAD_DIM] for f in fresh_refs], axis=0)
+            key_position = jnp.concatenate(
+                [
+                    base(side) + lax.broadcasted_iota(jnp.int32, (1, f.shape[0]), 1)
+                    for base, f in zip(bases, fresh_refs)
+                ],
+                axis=1,
+            )
+            allowed = (row_segment == segment_of(key_position)) & (key_position <= row_position)
+            raw = lax.dot_general(
+                q_rows, new_keys, (((1,), (1,)), ((), ())), preferred_element_type=F32
+            )
+            masked = jnp.where(
+                allowed[None], raw.reshape(heads, block_rows, fresh_rows), NEG_FILL
+            ).reshape(stacked, fresh_rows)
+            scores[:, new_start:keys_all] = masked
+            top = jnp.maximum(
+                jnp.max(peak, axis=1, keepdims=True), jnp.max(masked, axis=1, keepdims=True)
+            )
+            top = top * factor
+            total = jnp.zeros((stacked, HEAD_DIM), F32)
+            mixed = jnp.zeros((stacked, HEAD_DIM), F32)
+            for g in range(groups):
+                for p in range(0, per, pages_step):
+                    column = (g * per + p) * PAGE
+                    probs = jnp.exp2(scores[:, column : column + pages_step * PAGE] * factor - top)
+                    for piece in range(0, pages_step * PAGE, HEAD_DIM):
+                        total += probs[:, piece : piece + HEAD_DIM]
+                    values = page_refs[g][p : p + pages_step, :, HEAD_DIM:].reshape(
+                        pages_step * PAGE, HEAD_DIM
+                    )
+                    mixed += jnp.dot(probs.astype(BF16), values, preferred_element_type=F32)
+            probs = jnp.exp2(scores[:, new_start:keys_all] * factor - top)
+            denominator = jnp.sum(total, axis=1, keepdims=True) + jnp.sum(
+                probs, axis=1, keepdims=True
+            )
+            new_values = jnp.concatenate([f[:, HEAD_DIM:] for f in fresh_refs], axis=0)
+            mixed += jnp.dot(probs.astype(BF16), new_values, preferred_element_type=F32)
+            result = (mixed / denominator).astype(BF16)
+            for h in range(heads):
+                out_ref[pl.ds(start, block_rows), h * HEAD_DIM : (h + 1) * HEAD_DIM] = result[
+                    h * block_rows : (h + 1) * block_rows
+                ]
+            return carry
+
+        if blocks == 1:
+            block(0, 0)
+        else:
+            lax.fori_loop(0, blocks, block, 0)
+
+    return pl.pallas_call(
+        kernel,
+        in_specs=[SMEM, SMEM, SMEM] + [VMEM] * (1 + count + groups),
+        out_specs=VMEM,
+        out_shape=shape((rows, width)),
+        scratch_shapes=[pltpu.VMEM((stacked, keys_all), F32)],
+        compiler_params=params(32),
+        cost_estimate=pl.CostEstimate(
+            flops=4 * rows * heads * keys_all * HEAD_DIM,
+            bytes_accessed=4 * MIB,
+            transcendentals=rows * heads * keys_all,
+        ),
+        name="attend",
+    )(place, pages_of, requests, query, *fresh, *pulled)
+
+
+def out_half(place, attention, w_out, near):
+    rows, depth = attention.shape
+    half = w_out.shape[1] // 2
+    steps = 4
+    wide = half // steps
+
+    def kernel(place_ref, a_ref, w, out_ref, buf, sems):
+        core = place_ref[1]
+        base = (core if near else 1 - core) * half
+
+        def copy(j):
+            start = pl.multiple_of(base + j * wide, wide)
+            return pltpu.make_async_copy(w.at[:, pl.ds(start, wide)], buf.at[j], sems.at[j])
+
+        for j in range(steps):
+            copy(j).start()
+        for j in range(steps):
+            copy(j).wait()
+            out_ref[:, j * wide : (j + 1) * wide] = jnp.dot(
+                a_ref[...], buf[j], preferred_element_type=F32
+            ).astype(BF16)
+
+    return pl.pallas_call(
+        kernel,
+        in_specs=[SMEM, VMEM, ANY],
+        out_specs=VMEM,
+        out_shape=shape((rows, half)),
+        scratch_shapes=[
+            pltpu.VMEM((steps, depth, wide), BF16),
+            pltpu.SemaphoreType.DMA((steps,)),
+        ],
+        compiler_params=params(24),
+        cost_estimate=pl.CostEstimate(
+            flops=2 * rows * depth * half, bytes_accessed=2 * depth * half, transcendentals=0
+        ),
+        name="out_half",
+    )(place, attention, w_out)
+
+
+def out_local(place, attention, w_out):
+    both, depth = attention.shape
+    rows = both // 2
+    width = w_out.shape[1]
+    steps = 8
+    wide = width // steps
+
+    def kernel(place_ref, a_ref, w, own_ref, peer_ref, buf, sems):
+        core = place_ref[1]
+        own_at = pl.ds(pl.multiple_of(core * rows, rows), rows)
+        peer_at = pl.ds(pl.multiple_of((1 - core) * rows, rows), rows)
+
+        def copy(j):
+            return pltpu.make_async_copy(
+                w.at[:, j * wide : (j + 1) * wide], buf.at[j], sems.at[j]
+            )
+
+        for j in range(steps):
+            copy(j).start()
+        a = jnp.concatenate([a_ref[own_at, :], a_ref[peer_at, :]], axis=0)
+        for j in range(steps):
+            copy(j).wait()
+            part = jnp.dot(a, buf[j], preferred_element_type=F32).astype(BF16)
+            own_ref[:, j * wide : (j + 1) * wide] = part[:rows]
+            peer_ref[:, j * wide : (j + 1) * wide] = part[rows:]
+
+    return pl.pallas_call(
+        kernel,
+        in_specs=[SMEM, VMEM, ANY],
+        out_specs=[VMEM, VMEM],
+        out_shape=[shape((rows, width)), shape((rows, width))],
+        scratch_shapes=[
+            pltpu.VMEM((steps, depth, wide), BF16),
+            pltpu.SemaphoreType.DMA((steps,)),
+        ],
+        compiler_params=params(36),
+        cost_estimate=pl.CostEstimate(
+            flops=2 * both * depth * width, bytes_accessed=2 * depth * width, transcendentals=0
+        ),
+        name="out_local",
+    )(place, attention, w_out)
+
+
+def finish(place, tokens, own, peer, near, far):
+    rows, width = tokens.shape
+    half = width // 2
+    step = 16
+
+    def kernel(place_ref, x_ref, own_ref, peer_ref, near_ref, far_ref, out_ref):
+        core = place_ref[1]
+
+        def block(i, carry):
+            at = pl.ds(pl.multiple_of(i * step, step), step)
+            for start, part in ((core, near_ref), (1 - core, far_ref)):
+                cols = pl.ds(pl.multiple_of(start * half, half), half)
+                local = own_ref[at, cols].astype(F32) + peer_ref[at, cols].astype(F32)
+                total = local + part[at, :].astype(F32)
+                out_ref[at, cols] = (x_ref[at, cols].astype(F32) + total).astype(BF16)
+            return carry
+
+        lax.fori_loop(0, rows // step, block, 0)
+
+    return pl.pallas_call(
+        kernel,
+        in_specs=[SMEM] + [VMEM] * 5,
+        out_specs=VMEM,
+        out_shape=shape((rows, width)),
+        compiler_params=params(16),
+        name="finish",
+    )(place, tokens, own, peer, near, far)
+
+
+def pick_pages(place, wanted, own, core_pages, y_pages):
+    replicas, _, slots = wanted.shape
+    count, page, width = own.shape
+    tensors = 4
+
+    def kernel(place_ref, want_ref, own_ref, core_ref, y_ref, *refs):
+        outs, sems = refs[:replicas], refs[replicas]
+        me, rep = place_ref[0], place_ref[3]
+        sources = (own_ref, core_ref.at[0], y_ref.at[0], core_ref.at[1])
+
+        def copies():
+            for k in range(replicas):
+                asker = lax.rem(rep + k, replicas)
+                for i in range(tensors):
+                    owner = rep * tensors + jnp.bitwise_xor(me, i)
+                    for s in range(slots):
+                        at = i * slots + s
+                        yield pltpu.make_async_copy(
+                            sources[i].at[want_ref[asker, owner, s]],
+                            outs[k].at[at],
+                            sems.at[k * tensors * slots + at],
+                        )
+
+        for copy in copies():
+            copy.start()
+        for copy in copies():
+            copy.wait()
+
+    total = tensors * slots
+    return pl.pallas_call(
+        kernel,
+        in_specs=[SMEM, SMEM] + [ANY] * 3,
+        out_specs=[ANY] * replicas,
+        out_shape=[shape((total, page, width))] * replicas,
+        scratch_shapes=[pltpu.SemaphoreType.DMA((replicas * total,))],
+        compiler_params=params(8),
+        name="pick_pages",
+    )(place, wanted, own, core_pages, y_pages)
+
+
+def write_pool(place, slots, kv_pool, own, core_new, y_new):
+    pages, heads = kv_pool.shape[:2]
+    new_count = slots.shape[1]
+    side_pages = new_count // 2
+
+    def kernel(place_ref, slot_ref, pool_ref, own_ref, core_ref, y_ref, out_ref, sems):
+        me, side = place_ref[0], place_ref[2]
+        sources = (own_ref, core_ref.at[0], y_ref, core_ref.at[1])
+        for p in range(pages):
+            found = jnp.int32(-1)
+            for j in range(new_count):
+                found = jnp.where(slot_ref[0, j] == me * pages + p, j, found)
+            far = (found >= side_pages).astype(jnp.int32)
+            inner = jnp.maximum(found - far * side_pages, 0)
+
+            @pl.when(found >= 0)
+            def _():
+                for i in range(heads):
+                    origin = side if i < 2 else 1 - side
+                    start = (jnp.bitwise_xor(far, origin) * side_pages + inner) * PAGE
+                    pltpu.make_async_copy(
+                        sources[i].at[pl.ds(pl.multiple_of(start, PAGE), PAGE)],
+                        out_ref.at[p, jnp.bitwise_xor(me, i)],
+                        sems.at[p * heads + i],
+                    ).start()
+
+            @pl.when(found < 0)
+            def _():
+                for i in range(heads):
+                    at = jnp.bitwise_xor(me, i)
+                    pltpu.make_async_copy(
+                        pool_ref.at[p, at], out_ref.at[p, at], sems.at[p * heads + i]
+                    ).start()
+
+        for p in range(pages):
+            for i in range(heads):
+                at = jnp.bitwise_xor(me, i)
+                pltpu.make_async_copy(
+                    pool_ref.at[p, at], out_ref.at[p, at], sems.at[p * heads + i]
+                ).wait()
+
+    return pl.pallas_call(
+        kernel,
+        in_specs=[SMEM, SMEM] + [ANY] * 4,
+        out_specs=ANY,
+        out_shape=shape(kv_pool.shape),
+        scratch_shapes=[pltpu.SemaphoreType.DMA((pages * heads,))],
+        compiler_params=params(8),
+        name="write_pool",
+    )(place, slots, kv_pool, own, core_new, y_new)
+
+
+def chip_pair_body(
+    tokens,
+    gain,
+    w_query,
+    w_keyvalue,
+    w_out,
+    kv_pool,
+    suffix_pages,
+    page_index,
+    page_request,
+    new_slot,
+):
+    replicas = lax.axis_size("replica")
+    me = lax.axis_index("tensor")
+    rep = lax.axis_index("replica")
+    core = me % 2
+    side = me // 2
+    rows = tokens.shape[0]
+    place = jnp.stack([me, core, side, rep]).astype(jnp.int32)
+
+    def over_core(x):
+        return lax.ppermute(x, "tensor", [(0, 1), (1, 0), (2, 3), (3, 2)])
+
+    def over_y(x):
+        return lax.ppermute(x, "tensor", [(0, 2), (2, 0), (1, 3), (3, 1)])
+
+    def head_of(i):
+        return lax.dynamic_index_in_dim(kv_pool, jnp.bitwise_xor(me, i), 1, keepdims=False)
+
+    wanted = lax.all_gather(page_index[0], "replica", axis=0)
+    y_pages = over_y(jnp.stack([head_of(2), head_of(3)]))
+    core_pages = over_core(jnp.stack([head_of(1), y_pages[1]]))
+
+    mine, other = norm_rows(place, tokens, gain)
+    peer_near = over_core(other)
+    peer_far = over_core(mine)
+    is_first = core == 0
+    first = over_y(jnp.where(is_first, mine, peer_near))
+    second = over_y(jnp.where(is_first, peer_near, mine))
+
+    picked = pick_pages(place, wanted, head_of(0), core_pages, y_pages)
+    pulled = [picked[0]]
+    for k in range(1, replicas):
+        pulled.append(
+            lax.ppermute(picked[k], "replica", [(i, (i + k) % replicas) for i in range(replicas)])
+        )
+
+    q_local, kv_local = project(
+        place, [mine, peer_near], [other, peer_far], w_query, w_keyvalue, True
+    )
+
+    def local_base(s):
+        return s * (2 * rows)
+
+    def first_base(s):
+        return (1 - s) * (2 * rows)
+
+    def second_base(s):
+        return (1 - s) * (2 * rows) + rows
+
+    q_first, kv_first = project(place, [first], [over_core(first)], w_query, w_keyvalue, False)
+    attended = attend(
+        place, suffix_pages, page_request, q_first, [kv_local, kv_first],
+        [local_base, first_base], pulled, first_base, rows,
+    )
+    away = over_core(out_half(place, attended, w_out, False))
+    stay = out_half(place, attended, w_out, True)
+    first_sum = over_y((stay.astype(F32) + away.astype(F32)).astype(BF16))
+
+    q_second, kv_second = project(place, [second], [over_core(second)], w_query, w_keyvalue, False)
+    fresh = [kv_local, kv_first, kv_second]
+    bases = [local_base, first_base, second_base]
+    attended = attend(
+        place, suffix_pages, page_request, q_second, fresh, bases, pulled, second_base, rows
+    )
+    away = over_core(out_half(place, attended, w_out, False))
+    stay = out_half(place, attended, w_out, True)
+    second_sum = over_y((stay.astype(F32) + away.astype(F32)).astype(BF16))
+
+    new_own = jnp.concatenate(fresh, axis=0)
+    y_new = over_y(new_own)
+    core_new = over_core(jnp.stack([new_own, y_new]))
+    pool_out = write_pool(place, new_slot, kv_pool, new_own, core_new, y_new)
+
+    attended = attend(
+        place, suffix_pages, page_request, q_local, fresh, bases, pulled, local_base, rows
+    )
+    own_part, peer_part = out_local(place, attended, w_out)
+    peer_part = over_core(peer_part)
+
+    near = jnp.where(is_first, first_sum, second_sum)
+    far = over_core(jnp.where(is_first, second_sum, first_sum))
+    layer_out = finish(place, tokens, own_part, peer_part, near, far)
+    return (layer_out, pool_out)
+
+
 def solution(mesh):
+    pair = mesh.shape["tensor"] == KV_HEADS
     return jax.shard_map(
-        body,
+        chip_pair_body if pair else gathered_body,
         mesh=mesh,
         in_specs=(
             P(("groups", "replica", "tensor"), None),

time: 229 us -> 181 us (0.79)
  Pallas kernels: 0 us -> 77.4 us
  matrix products: 63.5 us -> 0 us
  waiting for transfers between devices: 84.6 us -> 63.8 us
  other arithmetic: 23.1 us -> 2.62 us
  between operations: 14.4 us -> 1.1 us
  local copies, waits for them, and re-layouts: 21.2 us -> 9.39 us
  blocking collectives: 8.63 us -> 11.6 us
    pallas_call x0 -> x15, Pallas kernels: none -> 77.4 us  [the longest x3 26.9 us: project(): pl.pallas_call(kernel, in_specs=[SMEM] + [VMEM] * (2 * count) + [ANY, ANY...]
    ppermute x0 -> x19, waiting for transfers between devices: none -> 63.8 us  [the longest x6 61 us: over_y(): return lax.ppermute(x, 'tensor', [(0, 2), (2, 0), (1, 3), (3, 1)])]
    dot_general x8 -> x0, matrix products: 63.5 us -> none  [the longest x2 18.4 us: block_scores(): jnp.dot(queries, keys[:, :HEAD_DIM].T, preferred_element_type=jnp.float32)]
    reduce_scatter x1 -> x0, waiting for transfers between devices: 53.1 us -> none  [body(): lax.psum_scatter(jnp.dot(attention, w_out, preferred_element_type=jnp.flo...]
    all_gather x1 -> x0, waiting for transfers between devices: 31.5 us -> none  [body(): piece = lax.all_gather(normed, 'tensor', axis=0, tiled=True)]
    reduce_sum x4 -> x0, other arithmetic: 14.9 us -> none  [the longest x1 12.3 us: absorb(): total = total * rescale + jnp.sum(weights, axis=2)]
    ppermute x0 -> x19, starting transfers between devices: none -> 14.4 us  [the longest x6 8.73 us: over_y(): return lax.ppermute(x, 'tensor', [(0, 2), (2, 0), (1, 3), (3, 1)])]
    all_to_all x2 -> x0, starting transfers between devices: 13.4 us -> none  [the longest x1 7.39 us: body(): lax.all_to_all(page_index[0], ('replica', 'tensor'), split_axis=0, concat...]
  transfers between devices with their start and end apart: 4 -> 19, of which waited for: 2 -> 7; matrix products, arithmetic and copies ran while one was open for 19% -> 1% of each run, Pallas kernels for 0% -> 36%
where the time goes in v1:
time: 181 us; the launch traced here: 180 us
  Pallas kernels  77.4 us (43%)
  waiting for transfers between devices  63.8 us (35%)
  starting transfers between devices  14.4 us (8%)
  blocking collectives  11.6 us (6%)
  local copies, waits for them, and re-layouts  9.39 us (5%)
  other arithmetic  2.62 us (1%)
    ppermute x6, waiting for transfers between devices, over_y(): return lax.ppermute(x, 'tensor', [(0, 2), (2, 0), (1, 3), (3, 1)])  61 us
    pallas_call x3, Pallas kernels, project(): pl.pallas_call(kernel, in_specs=[SMEM] + [VMEM] * (2 * count) + [ANY, ANY...  26.9 us
    pallas_call x3, Pallas kernels, attend(): pl.pallas_call(kernel, in_specs=[SMEM, SMEM, SMEM] + [VMEM] * (1 + count...  20.6 us
    pallas_call x4, Pallas kernels, out_half(): pl.pallas_call(kernel, in_specs=[SMEM, VMEM, ANY], out_specs=VMEM, out_sh...  14.6 us
    all_gather x1, blocking collectives, chip_pair_body(): wanted = lax.all_gather(page_index[0], 'replica', axis=0)  11.6 us
    ppermute x6, starting transfers between devices, over_y(): return lax.ppermute(x, 'tensor', [(0, 2), (2, 0), (1, 3), (3, 1)])  8.73 us
    unnamed x43, local copies, waits for them, and re-layouts  7.9 us
    pallas_call x1, Pallas kernels, out_local(): pl.pallas_call(kernel, in_specs=[SMEM, VMEM, ANY], out_specs=[VMEM, VMEM]...  7.11 us
  transfers between devices with their start and end apart: 19, of which 7 were waited for; matrix products, arithmetic and copies ran while one was open for 1% of the time, Pallas kernels for 36%

profile of v1, /device:TPU:0, one launch (start us, length us, event | category | flops | bytes accessed | tf_op | source)
XLA Modules:
  0.0 180.4 jit_solution(11648715111135220796)
XLA Ops:
  0.6 0.7 reshape.10.g_ref
  1.4 0.1 pad_add_fusion.place_ref
  1.5 1.4 copy-done.3
  2.9 1.7 norm_rows.1
  4.6 0.5 collective-permute-start
  5.1 0.9 copy-done.6
  6.0 1.0 collective-permute-done.refs_1_
  7.0 1.3 broadcast_select_fusion.2
  8.3 2.9 %collective-permute-start.2 = (bf16[96,4096]{1,0:T(8,128)(2,1)}, bf16[96,4096]{1,0:T(8,128)(2,1)}, u32[]{:S(2)}, u32[]{:S(2)}) collective-permute-start(bf16[96,4096]{1,0:T(8,128)(2,1)} %get-tuple-element.33), channel_id=1, source_target_pairs={{0,2},{2,0},{1,3},{3,1},{4,6},{6,4},{5,7},{7,5},{8,10},{10,8},{9,1... | collective-permute-start | bytes 2359304 | tf_op jit(solution)/shard_map/ppermute | solution.py:648
  11.2 0.0 collective-permute-start.4
  11.2 0.0 collective-permute-start.1
  11.3 2.1 %collective-permute-start.6 = (bf16[2,4,64,256]{3,2,1,0:T(8,128)(2,1)S(1)}, bf16[2,4,64,256]{3,2,1,0:T(8,128)(2,1)S(1)}, u32[]{:S(2)}, u32[]{:S(2)}) collective-permute-start(bf16[2,4,64,256]{3,2,1,0:T(8,128)(2,1)S(1)} %pad_maximum_fusion.1), channel_id=1, source_target_pairs={{0,2},{2,0},{1,3},{3,1},{4,6},{6,4},{5,7},{7,5},{8,10},{10,8},{9,1... | collective-permute-start | bytes 786440 | tf_op jit(solution)/shard_map/ppermute | solution.py:648
  13.3 16.5 %collective-permute-done.2.refs_0_ = bf16[96,4096]{1,0:T(8,128)(2,1)} collective-permute-done((bf16[96,4096]{1,0:T(8,128)(2,1)}, bf16[96,4096]{1,0:T(8,128)(2,1)}, u32[]{:S(2)}, u32[]{:S(2)}) %collective-permute-start.2) | collective-permute-done | bytes 786464 | tf_op jit(solution)/shard_map/ppermute | solution.py:648
  29.8 0.0 collective-permute-start.3
  29.8 21.9 %collective-permute-done.6.y_ref = bf16[2,4,64,256]{3,2,1,0:T(8,128)(2,1)S(1)} collective-permute-done((bf16[2,4,64,256]{3,2,1,0:T(8,128)(2,1)S(1)}, bf16[2,4,64,256]{3,2,1,0:T(8,128)(2,1)S(1)}, u32[]{:S(2)}, u32[]{:S(2)}) %collective-permute-start.6) | collective-permute-done | bytes 262176 | tf_op jit(solution)/shard_map/ppermute | solution.py:648
  51.7 0.7 pad_maximum_fusion.2
  52.4 0.5 collective-permute-start.5
  52.9 0.1 copy.17.req_ref
  53.0 11.6 %all_gather.3 = s32[4,16,2]{1,2,0:T(2,128)S(1)} all-gather(s32[1,16,2]{1,2,0:T(2,128)} %param.17), channel_id=1, replica_groups=mesh['groups'=2,'replica'=4,'tensor'=4] {'replica'}, dimensions={0}, use_global_device_ids=true | all-gather | bytes 640 | tf_op jit(solution)/shard_map/all_gather | solution.py:653
  64.6 0.7 copy.16.want_ref
  65.3 0.8 copy-done.8
  66.1 2.6 %pick_pages.1 = (bf16[8,64,256]{2,1,0:T(8,128)(2,1)S(1)}, bf16[8,64,256]{2,1,0:T(8,128)(2,1)}, bf16[8,64,256]{2,1,0:T(8,128)(2,1)}, bf16[8,64,256]{2,1,0:T(8,128)(2,1)}) custom-call(s32[4]{0:T(128)S(1)} %pad_add_fusion.place_ref, s32[4,16,2]{2,1,0:T(8,128)S(1)} %copy-done.8, bf16[4,64,256]{2,1,0:T(8,128)(2,1)S(1)} %get-tuple-element.36.own_ref, ...), custom_call_target="tpu_custom_call" | custom-call | tf_op jit(solution)/shard_map/pick_pages/pallas_call | solution.py:561
  68.7 0.7 copy-done.10
  69.4 0.0 collective-permute-start.8
  69.4 0.3 collective-permute-start.9
  69.7 0.0 collective-permute-done.1.refs_3_
  69.7 3.5 %collective-permute-start.10 = (bf16[8,64,256]{2,1,0:T(8,128)(2,1)}, bf16[8,64,256]{2,1,0:T(8,128)(2,1)}, u32[]{:S(2)}, u32[]{:S(2)}) collective-permute-start(bf16[8,64,256]{2,1,0:T(8,128)(2,1)} %get-tuple-element.25), channel_id=1, source_target_pairs={{0,12},{4,0},{8,4},{12,8},{1,13},{5,1},{9,5},{13,9},{2,14},{6,2},{... | collective-permute-start | bytes 786440 | tf_op jit(solution)/shard_map/ppermute | solution.py:668
  73.2 2.2 %copy-done = bf16[8192,256]{1,0:T(8,128)(2,1)S(1)} copy-done((bf16[8192,256]{1,0:T(8,128)(2,1)S(1)}, bf16[8192,256]{1,0:T(8,128)(2,1)}, u32[]{:S(2)}) %copy-start) | copy-done | bytes 4194328
  75.4 1.1 copy-done.7
  76.6 9.1 %project.3 = (bf16[192,1024]{1,0:T(8,128)(2,1)S(1)}, bf16[192,256]{1,0:T(8,128)(2,1)S(1)}) custom-call(s32[4]{0:T(128)S(1)} %pad_add_fusion.place_ref, bf16[96,4096]{1,0:T(8,128)(2,1)S(1)} %get-tuple-element.16.refs_0_, bf16[96,4096]{1,0:T(8,128)(2,1)S(1)} %collective-permute-done.refs_1_, bf16[96,4096]{1,0:T(8,128)(2,1)S(1)} %copy-done.7, ...), custom_call_target="tpu_custom_call" | custom-call | flops 4026531840 | bytes 20971520 | tf_op jit(solution)/shard_map/project/pallas_call | solution.py:265
  85.7 0.0 copy-start.2
  85.7 0.0 slice-start
  85.8 8.9 %project.4 = (bf16[96,1024]{1,0:T(8,128)(2,1)S(1)}, bf16[96,256]{1,0:T(8,128)(2,1)S(1)}) custom-call(s32[4]{0:T(128)S(1)} %pad_add_fusion.place_ref, bf16[96,4096]{1,0:T(8,128)(2,1)} %collective-permute-done.2.refs_0_, bf16[96,4096]{1,0:T(8,128)(2,1)} %collective-permute-done.3.refs_1_, bf16[8192,1024]{1,0:T(8,128)(2,1)} %refs_2_.3, ...), custom_call_target="tpu_custom_call" | custom-call | flops 2013265920 | bytes 20971520 | tf_op jit(solution)/shard_map/project/pallas_call | solution.py:265
  94.6 0.0 copy-start.12
  94.6 0.7 copy-done.12
  95.3 8.9 %project.5 = (bf16[96,1024]{1,0:T(8,128)(2,1)S(1)}, bf16[96,256]{1,0:T(8,128)(2,1)S(1)}) custom-call(s32[4]{0:T(128)S(1)} %pad_add_fusion.place_ref, bf16[96,4096]{1,0:T(8,128)(2,1)S(1)} %collective-permute-done.4.refs_0_, bf16[96,4096]{1,0:T(8,128)(2,1)} %collective-permute-done.5.refs_1_, bf16[8192,1024]{1,0:T(8,128)(2,1)} %refs_2_.3, ...), custom_call_target="tpu_custom_call" | custom-call | flops 2013265920 | bytes 20971520 | tf_op jit(solution)/shard_map/project/pallas_call | solution.py:265
  104.3 5.3 %attend.5.a_ref = bf16[96,1024]{1,0:T(8,128)(2,1)S(1)} custom-call(s32[4]{0:T(128)S(1)} %pad_add_fusion.place_ref, s32[1,4]{1,0:T(1,128)S(1)} %copy-done.14, s32[1,16,2]{2,1,0:T(8,128)S(1)} %copy.17.req_ref, bf16[96,1024]{1,0:T(8,128)(2,1)S(1)} %get-tuple-element.29.q_ref, bf16[192,256]{1,0:T(8,128)(2,1)S(1)} %get-tuple-element.19.refs_0_, ...), custom_call_target="tpu_custom_call" | custom-call | flops 956301312 | bytes 4194304 | tf_op jit(solution)/shard_map/attend/pallas_call | solution.py:405
  109.7 0.0 copy-start.13
  109.7 3.8 %out_half.7 = bf16[96,4096]{1,0:T(8,128)(2,1)S(1)} custom-call(s32[4]{0:T(128)S(1)} %pad_add_fusion.place_ref, bf16[96,1024]{1,0:T(8,128)(2,1)S(1)} %attend.5.a_ref, bf16[1024,8192]{1,0:T(8,128)(2,1)S(1)} %bitcast.15), custom_call_target="tpu_custom_call" | custom-call | flops 805306368 | bytes 8388608 | tf_op jit(solution)/shard_map/out_half/pallas_call | solution.py:443
  113.5 0.1 collective-permute-start.14
  113.6 5.4 %attend.4.a_ref = bf16[96,1024]{1,0:T(8,128)(2,1)S(1)} custom-call(s32[4]{0:T(128)S(1)} %pad_add_fusion.place_ref, s32[1,4]{1,0:T(1,128)S(1)} %copy-done.14, s32[1,16,2]{2,1,0:T(8,128)S(1)} %copy.17.req_ref, bf16[96,1024]{1,0:T(8,128)(2,1)S(1)} %copy-done.13, bf16[192,256]{1,0:T(8,128)(2,1)S(1)} %get-tuple-element.19.refs_0_, ...), custom_call_target="tpu_custom_call" | custom-call | flops 918552576 | bytes 4194304 | tf_op jit(solution)/shard_map/attend/pallas_call | solution.py:405
  119.0 3.6 %out_half.5 = bf16[96,4096]{1,0:T(8,128)(2,1)S(1)} custom-call(s32[4]{0:T(128)S(1)} %pad_add_fusion.place_ref, bf16[96,1024]{1,0:T(8,128)(2,1)S(1)} %attend.4.a_ref, bf16[1024,8192]{1,0:T(8,128)(2,1)S(1)} %bitcast.15), custom_call_target="tpu_custom_call" | custom-call | flops 805306368 | bytes 8388608 | tf_op jit(solution)/shard_map/out_half/pallas_call | solution.py:443
  122.6 0.6 collective-permute-start.12
  123.2 3.6 %out_half.6 = bf16[96,4096]{1,0:T(8,128)(2,1)S(1)} custom-call(s32[4]{0:T(128)S(1)} %pad_add_fusion.place_ref, bf16[96,1024]{1,0:T(8,128)(2,1)S(1)} %attend.5.a_ref, bf16[1024,8192]{1,0:T(8,128)(2,1)S(1)} %bitcast.15), custom_call_target="tpu_custom_call" | custom-call | flops 805306368 | bytes 8388608 | tf_op jit(solution)/shard_map/out_half/pallas_call | solution.py:443
  126.8 3.6 %out_half.4 = bf16[96,4096]{1,0:T(8,128)(2,1)S(1)} custom-call(s32[4]{0:T(128)S(1)} %pad_add_fusion.place_ref, bf16[96,1024]{1,0:T(8,128)(2,1)S(1)} %attend.4.a_ref, bf16[1024,8192]{1,0:T(8,128)(2,1)S(1)} %bitcast.15), custom_call_target="tpu_custom_call" | custom-call | flops 805306368 | bytes 8388608 | tf_op jit(solution)/shard_map/out_half/pallas_call | solution.py:443
  130.4 0.2 add_convert_fusion
  130.6 1.6 collective-permute-start.15
  132.2 0.2 add_convert_fusion.1
  132.4 0.6 collective-permute-start.13
  133.0 9.8 %attend.3.a_ref = bf16[192,1024]{1,0:T(8,128)(2,1)S(1)} custom-call(s32[4]{0:T(128)S(1)} %pad_add_fusion.place_ref, s32[1,4]{1,0:T(1,128)S(1)} %copy-done.14, s32[1,16,2]{2,1,0:T(8,128)S(1)} %copy.17.req_ref, bf16[192,1024]{1,0:T(8,128)(2,1)S(1)} %get-tuple-element.18.q_ref, bf16[192,256]{1,0:T(8,128)(2,1)S(1)} %get-tuple-element.19.refs_0_, ...), custom_call_target="tpu_custom_call" | custom-call | flops 1912602624 | bytes 4194304 | tf_op jit(solution)/shard_map/attend/pallas_call | solution.py:405
  142.8 7.1 %out_local.1 = (bf16[96,8192]{1,0:T(8,128)(2,1)S(1)}, bf16[96,8192]{1,0:T(8,128)(2,1)S(1)}) custom-call(s32[4]{0:T(128)S(1)} %pad_add_fusion.place_ref, bf16[192,1024]{1,0:T(8,128)(2,1)S(1)} %attend.3.a_ref, bf16[1024,8192]{1,0:T(8,128)(2,1)} %w.9), custom_call_target="tpu_custom_call" | custom-call | flops 3221225472 | bytes 16777216 | tf_op jit(solution)/shard_map/out_local/pallas_call | solution.py:486
  149.9 0.1 collective-permute-start.11
  150.0 0.0 copy-start.9
  150.0 1.0 collective-permute-done.15
  151.1 15.9 %collective-permute-done.13 = bf16[96,4096]{1,0:T(8,128)(2,1)S(1)} collective-permute-done((bf16[96,4096]{1,0:T(8,128)(2,1)S(1)}, bf16[96,4096]{1,0:T(8,128)(2,1)S(1)}, u32[]{:S(2)}, u32[]{:S(2)}) %collective-permute-start.13) | collective-permute-done | bytes 786464 | tf_op jit(solution)/shard_map/ppermute | solution.py:648
  167.0 0.1 broadcast_select_fusion
  167.1 0.0 copy-start.4
  167.1 0.1 collective-permute-start.16
  167.2 1.6 collective-permute-start.17
  168.8 5.7 %collective-permute-done.17.y_ref = bf16[384,256]{1,0:T(8,128)(2,1)S(1)} collective-permute-done((bf16[384,256]{1,0:T(8,128)(2,1)S(1)}, bf16[384,256]{1,0:T(8,128)(2,1)S(1)}, u32[]{:S(2)}, u32[]{:S(2)}) %collective-permute-start.17) | collective-permute-done | bytes 196640 | tf_op jit(solution)/shard_map/ppermute | solution.py:648
  174.6 0.1 collective-permute-start.18
  174.6 1.7 collective-permute-done.18.core_ref
  176.3 1.5 write_pool.1
  177.9 2.5 %finish.1 = bf16[96,8192]{1,0:T(8,128)(2,1)} custom-call(s32[4]{0:T(128)S(1)} %pad_add_fusion.place_ref, bf16[96,8192]{1,0:T(8,128)(2,1)S(1)} %copy-done.4, bf16[96,8192]{1,0:T(8,128)(2,1)S(1)} %get-tuple-element.26.own_ref, bf16[96,8192]{1,0:T(8,128)(2,1)S(1)} %collective-permute-done.11.peer_ref, bf16[96,4096]{1,0:T(8,128)(2,1)S(1)} %get-tuple-element.31.near_ref, ...), custom_call_target="tpu_custom_call" | custom-call | tf_op jit(solution)/shard_map/finish/pallas_call | solution.py:522
  (47 shorter events, 0.2 us)
Async XLA Ops:
  1.5 1.4 copy-start.3
  4.6 2.4 %collective-permute-start = (bf16[96,4096]{1,0:T(8,128)(2,1)S(1)}, bf16[96,4096]{1,0:T(8,128)(2,1)S(1)}, u32[]{:S(2)}, u32[]{:S(2)}) collective-permute-start(bf16[96,4096]{1,0:T(8,128)(2,1)S(1)} %get-tuple-element.17.refs_2_), channel_id=1, source_target_pairs={{0,1},{1,0},{2,3},{3,2},{4,5},{5,4},{6,7},{7,6},{8,9},{9,8},{10,11... | collective-permute-start | bytes 2359304 | tf_op jit(solution)/shard_map/ppermute | solution.py:645
  5.1 0.9 copy-start.6
  7.0 4.2 %copy-start.5 = (bf16[4,4,64,256]{3,2,1,0:T(8,128)(2,1)S(1)}, bf16[4,4,64,256]{3,2,1,0:T(8,128)(2,1)}, u32[]{:S(2)}) copy-start(bf16[4,4,64,256]{3,2,1,0:T(8,128)(2,1)} %pool_ref.1) | copy-start | bytes 1572868
  8.3 44.7 %copy-start.15 = (s32[1,16,2]{1,2,0:T(2,128)S(1)}, s32[1,16,2]{1,2,0:T(2,128)}, u32[]{:S(2)}) copy-start(s32[1,16,2]{1,2,0:T(2,128)} %param.18) | copy-start | bytes 388
  8.3 21.5 %collective-permute-start.2 = (bf16[96,4096]{1,0:T(8,128)(2,1)}, bf16[96,4096]{1,0:T(8,128)(2,1)}, u32[]{:S(2)}, u32[]{:S(2)}) collective-permute-start(bf16[96,4096]{1,0:T(8,128)(2,1)} %get-tuple-element.33), channel_id=1, source_target_pairs={{0,2},{2,0},{1,3},{3,1},{4,6},{6,4},{5,7},{7,5},{8,10},{10,8},{9,1... | collective-permute-start | bytes 2359304 | tf_op jit(solution)/shard_map/ppermute | solution.py:648
  11.2 41.3 %collective-permute-start.4 = (bf16[96,4096]{1,0:T(8,128)(2,1)}, bf16[96,4096]{1,0:T(8,128)(2,1)S(1)}, u32[]{:S(2)}, u32[]{:S(2)}) collective-permute-start(bf16[96,4096]{1,0:T(8,128)(2,1)} %get-tuple-element.32), channel_id=1, source_target_pairs={{0,2},{2,0},{1,3},{3,1},{4,6},{6,4},{5,7},{7,5},{8,10},{10,8},{9,1... | collective-permute-start | bytes 2359304 | tf_op jit(solution)/shard_map/ppermute | solution.py:648
  11.2 58.5 %collective-permute-start.1 = (bf16[96,4096]{1,0:T(8,128)(2,1)S(1)}, bf16[96,4096]{1,0:T(8,128)(2,1)}, u32[]{:S(2)}, u32[]{:S(2)}) collective-permute-start(bf16[96,4096]{1,0:T(8,128)(2,1)S(1)} %get-tuple-element.16.refs_0_), channel_id=1, source_target_pairs={{0,1},{1,0},{2,3},{3,2},{4,5},{5,4},{6,7},{7,6},{8,9},{9,8},{10,11... | collective-permute-start | bytes 2359304 | tf_op jit(solution)/shard_map/ppermute | solution.py:645
  11.3 40.4 %collective-permute-start.6 = (bf16[2,4,64,256]{3,2,1,0:T(8,128)(2,1)S(1)}, bf16[2,4,64,256]{3,2,1,0:T(8,128)(2,1)S(1)}, u32[]{:S(2)}, u32[]{:S(2)}) collective-permute-start(bf16[2,4,64,256]{3,2,1,0:T(8,128)(2,1)S(1)} %pad_maximum_fusion.1), channel_id=1, source_target_pairs={{0,2},{2,0},{1,3},{3,1},{4,6},{6,4},{5,7},{7,5},{8,10},{10,8},{9,1... | collective-permute-start | bytes 786440 | tf_op jit(solution)/shard_map/ppermute | solution.py:648
  29.8 55.9 %collective-permute-start.3 = (bf16[96,4096]{1,0:T(8,128)(2,1)}, bf16[96,4096]{1,0:T(8,128)(2,1)}, u32[]{:S(2)}, u32[]{:S(2)}) collective-permute-start(bf16[96,4096]{1,0:T(8,128)(2,1)} %collective-permute-done.2.refs_0_), channel_id=1, source_target_pairs={{0,1},{1,0},{2,3},{3,2},{4,5},{5,4},{6,7},{7,6},{8,9},{9,8},{10,11... | collective-permute-start | bytes 2359304 | tf_op jit(solution)/shard_map/ppermute | solution.py:645
  52.4 12.9 %collective-permute-start.7 = (bf16[2,4,64,256]{3,2,1,0:T(8,128)(2,1)}, bf16[2,4,64,256]{3,2,1,0:T(8,128)(2,1)S(1)}, u32[]{:S(2)}, u32[]{:S(2)}) collective-permute-start(bf16[2,4,64,256]{3,2,1,0:T(8,128)(2,1)} %pad_maximum_fusion.2), channel_id=1, source_target_pairs={{0,1},{1,0},{2,3},{3,2},{4,5},{5,4},{6,7},{7,6},{8,9},{9,8},{10,11... | collective-permute-start | bytes 786440 | tf_op jit(solution)/shard_map/ppermute | solution.py:645
  52.4 42.9 %collective-permute-start.5 = (bf16[96,4096]{1,0:T(8,128)(2,1)S(1)}, bf16[96,4096]{1,0:T(8,128)(2,1)}, u32[]{:S(2)}, u32[]{:S(2)}) collective-permute-start(bf16[96,4096]{1,0:T(8,128)(2,1)S(1)} %collective-permute-done.4.refs_0_), channel_id=1, source_target_pairs={{0,1},{1,0},{2,3},{3,2},{4,5},{5,4},{6,7},{7,6},{8,9},{9,8},{10,11... | collective-permute-start | bytes 2359304 | tf_op jit(solution)/shard_map/ppermute | solution.py:645
  65.3 0.8 copy-start.8
  68.7 0.7 copy-start.10
  69.4 34.8 %collective-permute-start.8 = (bf16[8,64,256]{2,1,0:T(8,128)(2,1)}, bf16[8,64,256]{2,1,0:T(8,128)(2,1)}, u32[]{:S(2)}, u32[]{:S(2)}) collective-permute-start(bf16[8,64,256]{2,1,0:T(8,128)(2,1)} %get-tuple-element.23), channel_id=1, source_target_pairs={{0,4},{4,8},{8,12},{12,0},{1,5},{5,9},{9,13},{13,1},{2,6},{6,10},{... | collective-permute-start | bytes 786440 | tf_op jit(solution)/shard_map/ppermute | solution.py:668
  69.4 34.8 %collective-permute-start.9 = (bf16[8,64,256]{2,1,0:T(8,128)(2,1)}, bf16[8,64,256]{2,1,0:T(8,128)(2,1)}, u32[]{:S(2)}, u32[]{:S(2)}) collective-permute-start(bf16[8,64,256]{2,1,0:T(8,128)(2,1)} %get-tuple-element.24), channel_id=1, source_target_pairs={{0,8},{4,12},{8,0},{12,4},{1,9},{5,13},{9,1},{13,5},{2,10},{6,14},... | collective-permute-start | bytes 786440 | tf_op jit(solution)/shard_map/ppermute | solution.py:668
  69.7 34.5 %collective-permute-start.10 = (bf16[8,64,256]{2,1,0:T(8,128)(2,1)}, bf16[8,64,256]{2,1,0:T(8,128)(2,1)}, u32[]{:S(2)}, u32[]{:S(2)}) collective-permute-start(bf16[8,64,256]{2,1,0:T(8,128)(2,1)} %get-tuple-element.25), channel_id=1, source_target_pairs={{0,12},{4,0},{8,4},{12,8},{1,13},{5,1},{9,5},{13,9},{2,14},{6,2},{... | collective-permute-start | bytes 786440 | tf_op jit(solution)/shard_map/ppermute | solution.py:668
  73.2 2.2 %copy-start = (bf16[8192,256]{1,0:T(8,128)(2,1)S(1)}, bf16[8192,256]{1,0:T(8,128)(2,1)}, u32[]{:S(2)}) copy-start(bf16[8192,256]{1,0:T(8,128)(2,1)} %refs_3_.3) | copy-start | bytes 12582916
  75.4 1.1 copy-start.7
  76.6 9.2 %copy-start.1 = (bf16[8192,256]{1,0:T(8,128)(2,1)S(1)}, bf16[8192,256]{1,0:T(8,128)(2,1)}, u32[]{:S(2)}) copy-start(bf16[8192,256]{1,0:T(8,128)(2,1)} %refs_3_.3) | copy-start | bytes 12582916
  85.7 9.6 %copy-start.2 = (bf16[8192,256]{1,0:T(8,128)(2,1)S(1)}, bf16[8192,256]{1,0:T(8,128)(2,1)}, u32[]{:S(2)}) copy-start(bf16[8192,256]{1,0:T(8,128)(2,1)} %refs_3_.3) | copy-start | bytes 12582916
  85.7 23.9 %slice-start = ((s8[16777216]{0:T(1024)(128)(4,1)}), s8[4194304]{0:T(1024)(128)(4,1)S(1)}, s32[]{:S(2)}) async-start(s8[16777216]{0:T(1024)(128)(4,1)} %bitcast.14), calls=%async_computation | async-start | bytes 8388608
  85.7 23.9 %slice-start.1 = ((s8[16777216]{0:T(1024)(128)(4,1)}), s8[4194304]{0:T(1024)(128)(4,1)S(1)}, s32[]{:S(2)}) async-start(s8[16777216]{0:T(1024)(128)(4,1)} %bitcast.14), calls=%async_computation.1 | async-start | bytes 8388608
  94.6 0.7 copy-start.12
  95.3 9.0 %copy-start.11 = (bf16[8,64,256]{2,1,0:T(8,128)(2,1)S(1)}, bf16[8,64,256]{2,1,0:T(8,128)(2,1)}, u32[]{:S(2)}) copy-start(bf16[8,64,256]{2,1,0:T(8,128)(2,1)} %copy-done.10) | copy-start | bytes 786436
  95.3 9.0 %copy-start.14 = (s32[1,4]{1,0:T(1,128)S(1)}, s32[1,4]{1,0:T(1,128)}, u32[]{:S(2)}) copy-start(s32[1,4]{1,0:T(1,128)} %sizes_ref.5) | copy-start | bytes 52
  95.3 14.3 %slice-start.2 = ((s8[16777216]{0:T(1024)(128)(4,1)}), s8[4194304]{0:T(1024)(128)(4,1)S(1)}, s32[]{:S(2)}) async-start(s8[16777216]{0:T(1024)(128)(4,1)} %bitcast.14), calls=%async_computation.2 | async-start | bytes 8388608
  95.3 14.4 %slice-start.3 = ((s8[16777216]{0:T(1024)(128)(4,1)}), s8[4194304]{0:T(1024)(128)(4,1)S(1)}, s32[]{:S(2)}) async-start(s8[16777216]{0:T(1024)(128)(4,1)} %bitcast.14), calls=%async_computation.3 | async-start | bytes 8388608
  109.7 3.9 %copy-start.13 = (bf16[96,1024]{1,0:T(8,128)(2,1)S(1)}, bf16[96,1024]{1,0:T(8,128)(2,1)}, u32[]{:S(2)}) copy-start(bf16[96,1024]{1,0:T(8,128)(2,1)} %copy-done.12) | copy-start | bytes 589828
  113.5 16.9 %collective-permute-start.14 = (bf16[96,4096]{1,0:T(8,128)(2,1)S(1)}, bf16[96,4096]{1,0:T(8,128)(2,1)S(1)}, u32[]{:S(2)}, u32[]{:S(2)}) collective-permute-start(bf16[96,4096]{1,0:T(8,128)(2,1)S(1)} %out_half.7), channel_id=1, source_target_pairs={{0,1},{1,0},{2,3},{3,2},{4,5},{5,4},{6,7},{7,6},{8,9},{9,8},{10,11... | collective-permute-start | bytes 2359304 | tf_op jit(solution)/shard_map/ppermute | solution.py:645
  122.6 9.6 %collective-permute-start.12 = (bf16[96,4096]{1,0:T(8,128)(2,1)S(1)}, bf16[96,4096]{1,0:T(8,128)(2,1)S(1)}, u32[]{:S(2)}, u32[]{:S(2)}) collective-permute-start(bf16[96,4096]{1,0:T(8,128)(2,1)S(1)} %out_half.5), channel_id=1, source_target_pairs={{0,1},{1,0},{2,3},{3,2},{4,5},{5,4},{6,7},{7,6},{8,9},{9,8},{10,11... | collective-permute-start | bytes 2359304 | tf_op jit(solution)/shard_map/ppermute | solution.py:645
  130.6 20.5 %collective-permute-start.15 = (bf16[96,4096]{1,0:T(8,128)(2,1)S(1)}, bf16[96,4096]{1,0:T(8,128)(2,1)S(1)}, u32[]{:S(2)}, u32[]{:S(2)}) collective-permute-start(bf16[96,4096]{1,0:T(8,128)(2,1)S(1)} %add_convert_fusion), channel_id=1, source_target_pairs={{0,2},{2,0},{1,3},{3,1},{4,6},{6,4},{5,7},{7,5},{8,10},{10,8},{9,1... | collective-permute-start | bytes 2359304 | tf_op jit(solution)/shard_map/ppermute | solution.py:648
  132.4 34.6 %collective-permute-start.13 = (bf16[96,4096]{1,0:T(8,128)(2,1)S(1)}, bf16[96,4096]{1,0:T(8,128)(2,1)S(1)}, u32[]{:S(2)}, u32[]{:S(2)}) collective-permute-start(bf16[96,4096]{1,0:T(8,128)(2,1)S(1)} %add_convert_fusion.1), channel_id=1, source_target_pairs={{0,2},{2,0},{1,3},{3,1},{4,6},{6,4},{5,7},{7,5},{8,10},{10,8},{9,1... | collective-permute-start | bytes 2359304 | tf_op jit(solution)/shard_map/ppermute | solution.py:648
  149.9 27.9 %collective-permute-start.11 = (bf16[96,8192]{1,0:T(8,128)(2,1)S(1)}, bf16[96,8192]{1,0:T(8,128)(2,1)S(1)}, u32[]{:S(2)}, u32[]{:S(2)}) collective-permute-start(bf16[96,8192]{1,0:T(8,128)(2,1)S(1)} %get-tuple-element.27), channel_id=1, source_target_pairs={{0,1},{1,0},{2,3},{3,2},{4,5},{5,4},{6,7},{7,6},{8,9},{9,8},{10,11... | collective-permute-start | bytes 4718600 | tf_op jit(solution)/shard_map/ppermute | solution.py:645
  150.0 26.3 %copy-start.9 = (s32[1,6]{1,0:T(1,128)S(1)}, s32[1,6]{1,0:T(1,128)}, u32[]{:S(2)}) copy-start(s32[1,6]{1,0:T(1,128)} %slot_ref.1) | copy-start | bytes 76
  167.1 10.8 %copy-start.4 = (bf16[96,8192]{1,0:T(8,128)(2,1)S(1)}, bf16[96,8192]{1,0:T(8,128)(2,1)}, u32[]{:S(2)}) copy-start(bf16[96,8192]{1,0:T(8,128)(2,1)} %x_ref.3) | copy-start | bytes 4718596
  167.1 10.7 %collective-permute-start.16 = (bf16[96,4096]{1,0:T(8,128)(2,1)S(1)}, bf16[96,4096]{1,0:T(8,128)(2,1)S(1)}, u32[]{:S(2)}, u32[]{:S(2)}) collective-permute-start(bf16[96,4096]{1,0:T(8,128)(2,1)S(1)} %get-tuple-element.30), channel_id=1, source_target_pairs={{0,1},{1,0},{2,3},{3,2},{4,5},{5,4},{6,7},{7,6},{8,9},{9,8},{10,11... | collective-permute-start | bytes 2359304 | tf_op jit(solution)/shard_map/ppermute | solution.py:645
  167.2 7.3 %collective-permute-start.17 = (bf16[384,256]{1,0:T(8,128)(2,1)S(1)}, bf16[384,256]{1,0:T(8,128)(2,1)S(1)}, u32[]{:S(2)}, u32[]{:S(2)}) collective-permute-start(bf16[384,256]{1,0:T(8,128)(2,1)S(1)} %constant_dynamic-update-slice_fusion.own_ref), channel_id=1, source_target_pairs={{0,2},{2,0},{1,3},{3,1},{4,6},{6,4},{5,7},{7,5},{8,10},{10,8},{9,1... | collective-permute-start | bytes 589832 | tf_op jit(solution)/shard_map/ppermute | solution.py:648
  174.6 1.8 collective-permute-start.18

commit v2 on v0

--- a/solution.py
+++ b/solution.py
@@ -3,6 +3,8 @@
 import jax
 import jax.numpy as jnp
 from jax import lax
+from jax.experimental import pallas as pl
+from jax.experimental.pallas import tpu as pltpu
 from jax.sharding import PartitionSpec as P
 
 KV_HEADS = 4
@@ -14,6 +16,22 @@
 NEG_FILL = -1e30
 EPSILON = 1e-06
 
+F32 = jnp.float32
+BF16 = jnp.bfloat16
+MIB = 1 << 20
+ANY = pl.BlockSpec(memory_space=pl.ANY)
+SMEM = pl.BlockSpec(memory_space=pltpu.SMEM)
+VMEM = pl.BlockSpec(memory_space=pltpu.VMEM)
+SMALL = pl.CostEstimate(flops=1024, bytes_accessed=1024, transcendentals=0)
+
+
+def params(mib):
+    return pltpu.CompilerParams(vmem_limit_bytes=mib * MIB)
+
+
+def shape(dims, dtype=BF16):
+    return jax.ShapeDtypeStruct(dims, dtype)
+
 
 def normalize(rows, gain):
     values = rows.astype(jnp.float32)
@@ -27,7 +45,7 @@
     return jnp.sum((positions[:, None] >= bounds[None, :]).astype(jnp.int32), axis=1)
 
 
-def body(
+def gathered_body(
     tokens,
     gain,
     w_query,
@@ -157,9 +175,653 @@
     return (layer_out, pool_out)
 
 
+def norm_rows(place, tokens, gain):
+    rows, width = tokens.shape
+    half = width // 2
+    step = 16
+
+    def kernel(place_ref, x_ref, g_ref, mine_ref, other_ref):
+        core = place_ref[1]
+        near = pl.multiple_of(core * half, half)
+        far = pl.multiple_of((1 - core) * half, half)
+
+        def block(i, carry):
+            at = pl.ds(pl.multiple_of(i * step, step), step)
+            total = jnp.zeros((step, 1), F32)
+            for part in range(2):
+                values = x_ref[at, part * half : (part + 1) * half].astype(F32)
+                total += jnp.sum(values * values, axis=1, keepdims=True)
+            inverse = lax.rsqrt(total * (1.0 / width) + EPSILON)
+            for start, out in ((near, mine_ref), (far, other_ref)):
+                cols = pl.ds(start, half)
+                values = x_ref[at, cols].astype(F32)
+                out[at, :] = (values * inverse * g_ref[:, cols].astype(F32)).astype(BF16)
+            return carry
+
+        lax.fori_loop(0, rows // step, block, 0)
+
+    return pl.pallas_call(
+        kernel,
+        in_specs=[SMEM, VMEM, VMEM],
+        out_specs=[VMEM, VMEM],
+        out_shape=[shape((rows, half)), shape((rows, half))],
+        compiler_params=params(16),
+        cost_estimate=SMALL,
+        name="norm_rows",
+    )(place, tokens, gain.reshape(1, width))
+
+
+def project_local(place, near, far, w_query, w_keyvalue, after):
+    rows, half = near[0].shape
+    q_width, kv_width = w_query.shape[1], w_keyvalue.shape[1]
+    steps = 8
+    depth = 2 * half // steps
+    waits = len(after)
+
+    def kernel(place_ref, near_own, near_peer, far_own, far_peer, wq, wkv, *refs):
+        q_ref, kv_ref, wq_buf, wkv_buf, q_acc, kv_acc, sems = refs[waits:]
+        core = place_ref[1]
+        stream = weight_stream(core, half, steps, (wq, wkv), (wq_buf, wkv_buf), sems)
+        for j in range(steps):
+            for copy in stream(j):
+                copy.start()
+        for j in range(steps):
+            for copy in stream(j):
+                copy.wait()
+            group = (near_own, near_peer) if j < steps // 2 else (far_own, far_peer)
+            cols = slice((j % (steps // 2)) * depth, (j % (steps // 2) + 1) * depth)
+            x = jnp.concatenate([ref[:, cols] for ref in group], axis=0)
+            q_part = jnp.dot(x, wq_buf[j], preferred_element_type=F32)
+            kv_part = jnp.dot(x, wkv_buf[j], preferred_element_type=F32)
+            if j == 0:
+                q_acc[...] = q_part
+                kv_acc[...] = kv_part
+            elif j < steps - 1:
+                q_acc[...] += q_part
+                kv_acc[...] += kv_part
+            else:
+                q_last = (q_acc[...] + q_part).astype(BF16)
+                kv_last = (kv_acc[...] + kv_part).astype(BF16)
+        for b in range(2):
+            at = pl.ds(pl.multiple_of((core if b == 0 else 1 - core) * rows, rows), rows)
+            q_ref[at, :] = q_last[b * rows : (b + 1) * rows]
+            kv_ref[at, :] = kv_last[b * rows : (b + 1) * rows]
+
+    total = 2 * rows
+    return pl.pallas_call(
+        kernel,
+        in_specs=[SMEM] + [VMEM] * 4 + [ANY] * (2 + waits),
+        out_specs=[VMEM, VMEM],
+        out_shape=[shape((total, q_width)), shape((total, kv_width))],
+        scratch_shapes=[
+            pltpu.VMEM((steps, depth, q_width), BF16),
+            pltpu.VMEM((steps, depth, kv_width), BF16),
+            pltpu.VMEM((total, q_width), F32),
+            pltpu.VMEM((total, kv_width), F32),
+            pltpu.SemaphoreType.DMA((2 * steps,)),
+        ],
+        compiler_params=params(36),
+        cost_estimate=SMALL,
+        name="project_local",
+    )(place, *near, *far, w_query, w_keyvalue, *after)
+
+
+def weight_stream(core, half, steps, sources, buffers, sems):
+    depth = 2 * half // steps
+
+    def copies(j):
+        base = core if j < steps // 2 else 1 - core
+        start = pl.multiple_of(base * half + (j % (steps // 2)) * depth, depth)
+        count = len(sources)
+        return [
+            pltpu.make_async_copy(w.at[pl.ds(start, depth)], buf.at[j], sems.at[count * j + i])
+            for i, (w, buf) in enumerate(zip(sources, buffers))
+        ]
+
+    return copies
+
+
+PAGES_STEP = 4
+
+
+def attention_scratch(block_rows, heads, fresh_rows, slots):
+    stacked = heads * block_rows
+    return [
+        pltpu.VMEM((stacked, fresh_rows + slots * PAGE), F32),
+        pltpu.VMEM((stacked, HEAD_DIM), F32),
+        pltpu.VMEM((stacked, HEAD_DIM), F32),
+        pltpu.VMEM((slots * PAGE, 2 * HEAD_DIM), BF16),
+        pltpu.SMEM((slots,), jnp.int32),
+    ]
+
+
+def attend_block(place_ref, sizes_ref, req_ref, q, first_row, fresh, pulled, scratch):
+    scores, total_ref, mixed_ref, cache, labels = scratch
+    me = place_ref[0]
+    block_rows, width = q.shape
+    heads = width // HEAD_DIM
+    stacked = heads * block_rows
+    groups, per = pulled.shape[:2]
+    tensors = 4
+    slots = per // tensors
+    wide = PAGES_STEP * PAGE
+    factor = math.log2(math.e) / math.sqrt(HEAD_DIM)
+    bound = []
+    running = jnp.int32(0)
+    for k in range(sizes_ref.shape[1]):
+        running = running + sizes_ref[0, k] * UNIT
+        bound.append(running)
+
+    def segment_of(position):
+        return sum((position >= b).astype(jnp.int32) for b in bound)
+
+    lowest = segment_of(first_row)
+    highest = segment_of(first_row + block_rows - 1)
+    count = jnp.int32(0)
+    for g in range(groups):
+        for p in range(per):
+            owner = g * tensors + jnp.bitwise_xor(me, p // slots)
+            label = req_ref[0, owner, p % slots]
+            wanted = (label >= lowest) & (label <= highest)
+
+            @pl.when(wanted)
+            def _():
+                cache[pl.ds(pl.multiple_of(count * PAGE, PAGE), PAGE), :] = pulled[g, p]
+                labels[count] = label
+
+            count = count + wanted.astype(jnp.int32)
+    steps = (count + PAGES_STEP - 1) // PAGES_STEP
+    for k in range(PAGES_STEP - 1):
+
+        @pl.when(count + k < steps * PAGES_STEP)
+        def _():
+            cache[pl.ds(pl.multiple_of((count + k) * PAGE, PAGE), PAGE), :] = jnp.zeros(
+                (PAGE, 2 * HEAD_DIM), BF16
+            )
+            labels[count + k] = jnp.int32(-1)
+
+    q_rows = jnp.concatenate([q[:, h * HEAD_DIM : (h + 1) * HEAD_DIM] for h in range(heads)], axis=0)
+    row_position = first_row + lax.broadcasted_iota(jnp.int32, (block_rows, 1), 0)
+    row_segment = segment_of(row_position)
+
+    def masked_scores(keys, allowed):
+        raw = lax.dot_general(q_rows, keys, (((1,), (1,)), ((), ())), preferred_element_type=F32)
+        n = keys.shape[0]
+        return jnp.where(allowed[None], raw.reshape(heads, block_rows, n), NEG_FILL).reshape(
+            stacked, n
+        )
+
+    def fold(values, combine):
+        pieces = [values[:, i : i + HEAD_DIM] for i in range(0, values.shape[1], HEAD_DIM)]
+        result = pieces[0]
+        for piece in pieces[1:]:
+            result = combine(result, piece)
+        return result
+
+    new = jnp.concatenate([rows for rows, _ in fresh], axis=0)
+    fresh_rows = new.shape[0]
+    key_position = jnp.concatenate(
+        [
+            base + lax.broadcasted_iota(jnp.int32, (1, rows.shape[0]), 1)
+            for rows, base in fresh
+        ],
+        axis=1,
+    )
+    allowed = (row_segment == segment_of(key_position)) & (key_position <= row_position)
+    masked = masked_scores(new[:, :HEAD_DIM], allowed)
+    scores[:, :fresh_rows] = masked
+    total_ref[...] = fold(masked, jnp.maximum)
+    lanes = lax.broadcasted_iota(jnp.int32, (1, wide), 1) // PAGE
+
+    def add_scores(g, carry):
+        label = jnp.full((1, wide), -1, jnp.int32)
+        for j in range(PAGES_STEP):
+            label = jnp.where(lanes == j, labels[g * PAGES_STEP + j], label)
+        keys = cache[pl.ds(pl.multiple_of(g * wide, wide), wide), :HEAD_DIM]
+        masked = masked_scores(keys, row_segment == label)
+        scores[:, pl.ds(pl.multiple_of(fresh_rows + g * wide, PAGE), wide)] = masked
+        total_ref[...] = jnp.maximum(total_ref[...], fold(masked, jnp.maximum))
+        return carry
+
+    lax.fori_loop(0, steps, add_scores, 0)
+    top = jnp.max(total_ref[...], axis=1, keepdims=True) * factor
+    probs = jnp.exp2(scores[:, :fresh_rows] * factor - top)
+    total_ref[...] = fold(probs, jnp.add)
+    mixed_ref[...] = jnp.dot(probs.astype(BF16), new[:, HEAD_DIM:], preferred_element_type=F32)
+
+    def add_values(g, carry):
+        part = scores[:, pl.ds(pl.multiple_of(fresh_rows + g * wide, PAGE), wide)]
+        probs = jnp.exp2(part * factor - top)
+        values = cache[pl.ds(pl.multiple_of(g * wide, wide), wide), HEAD_DIM:]
+        total_ref[...] += fold(probs, jnp.add)
+        mixed_ref[...] += jnp.dot(probs.astype(BF16), values, preferred_element_type=F32)
+        return carry
+
+    lax.fori_loop(0, steps, add_values, 0)
+    denominator = jnp.sum(total_ref[...], axis=1, keepdims=True)
+    result = (mixed_ref[...] / denominator).astype(BF16)
+    return jnp.concatenate(
+        [result[h * block_rows : (h + 1) * block_rows] for h in range(heads)], axis=1
+    )
+
+
+def project_far(place, near, far, w_query, w_keyvalue, after):
+    rows, half = near.shape
+    q_width, kv_width = w_query.shape[1], w_keyvalue.shape[1]
+    steps = 8
+    depth = 2 * half // steps
+
+    def kernel(place_ref, near_ref, far_ref, wq, wkv, *refs):
+        q_ref, kv_ref, wq_buf, wkv_buf, sems = refs[len(after) :]
+        stream = weight_stream(place_ref[1], half, steps, (wq, wkv), (wq_buf, wkv_buf), sems)
+        for j in range(steps):
+            for copy in stream(j):
+                copy.start()
+        q_sum = kv_sum = None
+        for j in range(steps):
+            for copy in stream(j):
+                copy.wait()
+            x_ref = near_ref if j < steps // 2 else far_ref
+            x = x_ref[:, (j % (steps // 2)) * depth : (j % (steps // 2) + 1) * depth]
+            q_part = jnp.dot(x, wq_buf[j], preferred_element_type=F32)
+            kv_part = jnp.dot(x, wkv_buf[j], preferred_element_type=F32)
+            q_sum = q_part if j == 0 else q_sum + q_part
+            kv_sum = kv_part if j == 0 else kv_sum + kv_part
+        q_ref[...] = q_sum.astype(BF16)
+        kv_ref[...] = kv_sum.astype(BF16)
+
+    return pl.pallas_call(
+        kernel,
+        in_specs=[SMEM] + [VMEM] * 2 + [ANY] * (2 + len(after)),
+        out_specs=[VMEM] * 2,
+        out_shape=[shape((rows, q_width)), shape((rows, kv_width))],
+        scratch_shapes=[
+            pltpu.VMEM((steps, depth, q_width), BF16),
+            pltpu.VMEM((steps, depth, kv_width), BF16),
+            pltpu.SemaphoreType.DMA((2 * steps,)),
+        ],
+        compiler_params=params(32),
+        cost_estimate=SMALL,
+        name="project_far",
+    )(place, near, far, w_query, w_keyvalue, *after)
+
+
+def attend_out(place, sizes, requests, query, fresh, bases, base, pulled, w_out):
+    rows, depth = query.shape
+    width = w_out.shape[1]
+    half = width // 2
+    heads = depth // HEAD_DIM
+    out_steps = 4
+    wide = half // out_steps
+    known = len(fresh)
+    count = sum(f.shape[0] for f in fresh)
+    fresh_rows = -(-count // HEAD_DIM) * HEAD_DIM
+    pad = fresh_rows - count
+
+    def kernel(place_ref, sizes_ref, req_ref, q_ref, pulled_ref, *refs):
+        fresh_refs = refs[:known]
+        wo, there_ref, stay_ref, wo_buf, sems = refs[known : known + 5]
+        core, side = place_ref[1], place_ref[2]
+
+        def copy(j):
+            first = 1 - core if j < out_steps else core
+            start = pl.multiple_of(first * half + (j % out_steps) * wide, wide)
+            return pltpu.make_async_copy(wo.at[:, pl.ds(start, wide)], wo_buf.at[j], sems.at[j])
+
+        for j in range(2 * out_steps):
+            copy(j).start()
+        pairs = [(ref[...], at(side)) for ref, at in zip(fresh_refs, bases)]
+        if pad:
+            pairs.append((jnp.zeros((pad, 2 * HEAD_DIM), BF16), jnp.int32(1 << 20)))
+        mixed = attend_block(
+            place_ref, sizes_ref, req_ref, q_ref[...], base(side), pairs, pulled_ref,
+            refs[known + 5 :],
+        )
+        for j in range(2 * out_steps):
+            copy(j).wait()
+            out_ref = there_ref if j < out_steps else stay_ref
+            at = (j % out_steps) * wide
+            out_ref[:, at : at + wide] = jnp.dot(
+                mixed, wo_buf[j], preferred_element_type=F32
+            ).astype(BF16)
+
+    return pl.pallas_call(
+        kernel,
+        in_specs=[SMEM] * 3 + [VMEM] * (2 + known) + [ANY],
+        out_specs=[VMEM] * 2,
+        out_shape=[shape((rows, half)), shape((rows, half))],
+        scratch_shapes=[
+            pltpu.VMEM((2 * out_steps, depth, wide), BF16),
+            pltpu.SemaphoreType.DMA((2 * out_steps,)),
+        ]
+        + attention_scratch(rows, heads, fresh_rows, pulled.shape[0] * pulled.shape[1]),
+        compiler_params=params(36),
+        cost_estimate=SMALL,
+        name="attend_out",
+    )(place, sizes, requests, query, pulled, *fresh, w_out)
+
+
+def local_rows(place, sizes, requests, query, fresh, bases, base, pulled, w_out, after):
+    both, depth = query.shape
+    rows = both // 2
+    width = w_out.shape[1]
+    heads = depth // HEAD_DIM
+    steps = 8
+    wide = width // steps
+    known = len(fresh)
+    fresh_rows = sum(f.shape[0] for f in fresh)
+
+    def kernel(place_ref, sizes_ref, req_ref, q_ref, pulled_ref, *refs):
+        fresh_refs = refs[:known]
+        wo = refs[known]
+        rest = refs[known + 1 + len(after) :]
+        own_ref, peer_ref, wo_buf, a_buf, sems = rest[:5]
+        core, side = place_ref[1], place_ref[2]
+
+        def out_copy(j):
+            return pltpu.make_async_copy(
+                wo.at[:, j * wide : (j + 1) * wide], wo_buf.at[j], sems.at[j]
+            )
+
+        for j in range(steps):
+            out_copy(j).start()
+
+        def block(b, carry):
+            at = pl.ds(pl.multiple_of(b * rows, rows), rows)
+            a_buf[at, :] = attend_block(
+                place_ref,
+                sizes_ref,
+                req_ref,
+                q_ref[at, :],
+                base(side) + b * rows,
+                [(ref[...], first(side)) for ref, first in zip(fresh_refs, bases)],
+                pulled_ref,
+                rest[5:],
+            )
+            return carry
+
+        lax.fori_loop(0, 2, block, 0)
+        own_at = pl.ds(pl.multiple_of(core * rows, rows), rows)
+        peer_at = pl.ds(pl.multiple_of((1 - core) * rows, rows), rows)
+        a = jnp.concatenate([a_buf[own_at, :], a_buf[peer_at, :]], axis=0)
+        for j in range(steps):
+            out_copy(j).wait()
+            part = jnp.dot(a, wo_buf[j], preferred_element_type=F32).astype(BF16)
+            own_ref[:, j * wide : (j + 1) * wide] = part[:rows]
+            peer_ref[:, j * wide : (j + 1) * wide] = part[rows:]
+
+    return pl.pallas_call(
+        kernel,
+        in_specs=[SMEM] * 3 + [VMEM] * (2 + known) + [ANY] * (1 + len(after)),
+        out_specs=[VMEM, VMEM],
+        out_shape=[shape((rows, width)), shape((rows, width))],
+        scratch_shapes=[
+            pltpu.VMEM((steps, depth, wide), BF16),
+            pltpu.VMEM((both, depth), BF16),
+            pltpu.SemaphoreType.DMA((steps,)),
+        ]
+        + attention_scratch(rows, heads, fresh_rows, pulled.shape[0] * pulled.shape[1]),
+        compiler_params=params(40),
+        cost_estimate=SMALL,
+        name="local_rows",
+    )(place, sizes, requests, query, pulled, *fresh, w_out, *after)
+
+
+def add_pair(left, right):
+    rows, width = left.shape
+    step = 16
+
+    def kernel(left_ref, right_ref, out_ref):
+        def block(i, carry):
+            at = pl.ds(pl.multiple_of(i * step, step), step)
+            out_ref[at, :] = (left_ref[at, :].astype(F32) + right_ref[at, :].astype(F32)).astype(
+                BF16
+            )
+            return carry
+
+        lax.fori_loop(0, rows // step, block, 0)
+
+    return pl.pallas_call(
+        kernel,
+        in_specs=[VMEM, VMEM],
+        out_specs=VMEM,
+        out_shape=shape((rows, width)),
+        compiler_params=params(8),
+        cost_estimate=SMALL,
+        name="add_pair",
+    )(left, right)
+
+
+def finish(place, tokens, own, peer, near, far):
+    rows, width = tokens.shape
+    half = width // 2
+    step = 16
+
+    def kernel(place_ref, x_ref, own_ref, peer_ref, near_ref, far_ref, out_ref):
+        core = place_ref[1]
+
+        def block(i, carry):
+            at = pl.ds(pl.multiple_of(i * step, step), step)
+            for start, part in ((core, near_ref), (1 - core, far_ref)):
+                cols = pl.ds(pl.multiple_of(start * half, half), half)
+                local = own_ref[at, cols].astype(F32) + peer_ref[at, cols].astype(F32)
+                total = local + part[at, :].astype(F32)
+                out_ref[at, cols] = (x_ref[at, cols].astype(F32) + total).astype(BF16)
+            return carry
+
+        lax.fori_loop(0, rows // step, block, 0)
+
+    return pl.pallas_call(
+        kernel,
+        in_specs=[SMEM] + [VMEM] * 5,
+        out_specs=VMEM,
+        out_shape=shape((rows, width)),
+        compiler_params=params(16),
+        cost_estimate=SMALL,
+        name="finish",
+    )(place, tokens, own, peer, near, far)
+
+
+def pick_pages(place, wanted, own, core_pages, y_pages, after):
+    replicas, tensors, slots = wanted.shape
+    _, page, width = own.shape
+    total = tensors * slots
+
+    def kernel(place_ref, want_ref, own_ref, core_ref, y_ref, *refs):
+        out_ref, sems = refs[len(after) :]
+        me = place_ref[0]
+        sources = (own_ref, core_ref.at[0], y_ref.at[0], core_ref.at[1])
+
+        def copies():
+            for r in range(replicas):
+                for i in range(tensors):
+                    for s in range(slots):
+                        at = i * slots + s
+                        yield pltpu.make_async_copy(
+                            sources[i].at[want_ref[r, jnp.bitwise_xor(me, i), s]],
+                            out_ref.at[r, at],
+                            sems.at[r * total + at],
+                        )
+
+        for copy in copies():
+            copy.start()
+        for copy in copies():
+            copy.wait()
+
+    return pl.pallas_call(
+        kernel,
+        in_specs=[SMEM, SMEM] + [ANY] * (3 + len(after)),
+        out_specs=ANY,
+        out_shape=shape((replicas, total, page, width)),
+        scratch_shapes=[pltpu.SemaphoreType.DMA((replicas * total,))],
+        compiler_params=params(8),
+        cost_estimate=SMALL,
+        name="pick_pages",
+    )(place, wanted, own, core_pages, y_pages, *after)
+
+
+def write_pool(place, slots, kv_pool, own, core_new, y_new):
+    pages, heads = kv_pool.shape[:2]
+    new_count = slots.shape[1]
+    side_pages = new_count // 2
+
+    def kernel(place_ref, slot_ref, pool_ref, own_ref, core_ref, y_ref, out_ref, sems):
+        me, side = place_ref[0], place_ref[2]
+        sources = (own_ref, core_ref.at[0], y_ref, core_ref.at[1])
+        for p in range(pages):
+            found = jnp.int32(-1)
+            for j in range(new_count):
+                found = jnp.where(slot_ref[0, j] == me * pages + p, j, found)
+            far = (found >= side_pages).astype(jnp.int32)
+            inner = jnp.maximum(found - far * side_pages, 0)
+
+            @pl.when(found >= 0)
+            def _():
+                for i in range(heads):
+                    origin = side if i < 2 else 1 - side
+                    start = (jnp.bitwise_xor(far, origin) * side_pages + inner) * PAGE
+                    pltpu.make_async_copy(
+                        sources[i].at[pl.ds(pl.multiple_of(start, PAGE), PAGE)],
+                        out_ref.at[p, jnp.bitwise_xor(me, i)],
+                        sems.at[p * heads + i],
+                    ).start()
+
+            @pl.when(found < 0)
+            def _():
+                for i in range(heads):
+                    at = jnp.bitwise_xor(me, i)
+                    pltpu.make_async_copy(
+                        pool_ref.at[p, at], out_ref.at[p, at], sems.at[p * heads + i]
+                    ).start()
+
+        for p in range(pages):
+            for i in range(heads):
+                at = jnp.bitwise_xor(me, i)
+                pltpu.make_async_copy(
+                    pool_ref.at[p, at], out_ref.at[p, at], sems.at[p * heads + i]
+                ).wait()
+
+    return pl.pallas_call(
+        kernel,
+        in_specs=[SMEM, SMEM] + [ANY] * 4,
+        out_specs=ANY,
+        out_shape=shape(kv_pool.shape),
+        scratch_shapes=[pltpu.SemaphoreType.DMA((pages * heads,))],
+        compiler_params=params(8),
+        cost_estimate=SMALL,
+        name="write_pool",
+    )(place, slots, kv_pool, own, core_new, y_new)
+
+
+def chip_pair_body(
+    tokens,
+    gain,
+    w_query,
+    w_keyvalue,
+    w_out,
+    kv_pool,
+    suffix_pages,
+    page_index,
+    page_request,
+    new_slot,
+):
+    replicas = lax.axis_size("replica")
+    me = lax.axis_index("tensor")
+    core = me % 2
+    side = me // 2
+    rows = tokens.shape[0]
+    place = jnp.stack([me, core, side]).astype(jnp.int32)
+
+    def over_core(x):
+        return lax.ppermute(x, "tensor", [(0, 1), (1, 0), (2, 3), (3, 2)])
+
+    def over_y(x):
+        return lax.ppermute(x, "tensor", [(0, 2), (2, 0), (1, 3), (3, 1)])
+
+    def head_of(i):
+        return lax.dynamic_index_in_dim(kv_pool, jnp.bitwise_xor(me, i), 1, keepdims=False)
+
+    def to_replicas(x):
+        return lax.all_to_all(x, "replica", split_axis=0, concat_axis=0, tiled=True)
+
+    def tie(x, *others):
+        return lax.optimization_barrier((x, *others))[0]
+
+    wanted = to_replicas(page_index.reshape(replicas, -1, page_index.shape[2]))
+    y_pages = over_y(jnp.stack([head_of(2), head_of(3)]))
+    core_pages = over_core(jnp.stack([head_of(1), y_pages[1]]))
+
+    mine, other = norm_rows(place, tokens, gain)
+    peer_near = over_core(other)
+    peer_far = over_core(mine)
+    is_first = core == 0
+    near_tied = tie(peer_near, y_pages)
+    first_half = jnp.where(is_first, mine, near_tied)
+    second_half = jnp.where(is_first, near_tied, mine)
+    first = over_y(first_half)
+    second = over_y(second_half)
+
+    picked = pick_pages(
+        place, wanted, head_of(0), core_pages, y_pages, [first_half, second_half]
+    )
+    pulled = to_replicas(picked)
+
+    q_local, kv_local = project_local(
+        place, [mine, peer_near], [other, peer_far], w_query, w_keyvalue, [picked]
+    )
+
+    def local_base(s):
+        return s * (2 * rows)
+
+    def first_base(s):
+        return (1 - s) * (2 * rows)
+
+    def second_base(s):
+        return (1 - s) * (2 * rows) + rows
+
+    first = tie(first, q_local)
+    q_first, kv_first = project_far(place, first, over_core(first), w_query, w_keyvalue, [])
+    there, stay = attend_out(
+        place, suffix_pages, page_request, q_first, [kv_local, kv_first],
+        [local_base, first_base], first_base, pulled, w_out,
+    )
+    there = tie(there, second)
+    first_mix = add_pair(stay, over_core(there))
+    first_sum = over_y(first_mix)
+
+    second = tie(second, first_mix)
+    q_second, kv_second = project_far(place, second, over_core(second), w_query, w_keyvalue, [])
+    fresh = [kv_local, kv_first, kv_second]
+    bases = [local_base, first_base, second_base]
+    there, stay = attend_out(
+        place, suffix_pages, page_request, q_second, fresh, bases, second_base, pulled, w_out
+    )
+    there = tie(there, first_sum)
+    second_mix = add_pair(stay, over_core(there))
+
+
+    new_own = jnp.concatenate(fresh, axis=0)
+    y_new = over_y(new_own)
+    core_new = over_core(jnp.stack([new_own, y_new]))
+    second_sum = over_y(tie(second_mix, y_new))
+
+    own_part, peer_part = local_rows(
+        place, suffix_pages, page_request, q_local, fresh, bases, local_base, pulled, w_out,
+        [second_mix],
+    )
+    peer_part = over_core(peer_part)
+    pool_out = write_pool(place, new_slot, kv_pool, new_own, core_new, y_new)
+
+    near = jnp.where(is_first, first_sum, second_sum)
+    far = over_core(jnp.where(is_first, second_sum, first_sum))
+    layer_out = finish(place, tokens, own_part, peer_part, near, far)
+    return (layer_out, pool_out)
+
+
 def solution(mesh):
+    pair = mesh.shape["tensor"] == KV_HEADS
     return jax.shard_map(
-        body,
+        chip_pair_body if pair else gathered_body,
         mesh=mesh,
         in_specs=(
             P(("groups", "replica", "tensor"), None),

time: 229 us -> 126 us (0.55)
  matrix products: 63.5 us -> 0 us
  waiting for transfers between devices: 84.6 us -> 25.8 us
  Pallas kernels: 0 us -> 55.4 us
  other arithmetic: 23.1 us -> 1.26 us
  between operations: 14.4 us -> 1.04 us
  blocking collectives: 8.63 us -> 0 us
  local copies, waits for them, and re-layouts: 21.2 us -> 25.8 us
  starting transfers between devices: 13.5 us -> 16.3 us
    dot_general x8 -> x0, matrix products: 63.5 us -> none  [the longest x2 18.4 us: block_scores(): jnp.dot(queries, keys[:, :HEAD_DIM].T, preferred_element_type=jnp.float32)]
    pallas_call x0 -> x12, Pallas kernels: none -> 55.4 us  [the longest x2 15.2 us: attend_out(): pl.pallas_call(kernel, in_specs=[SMEM] * 3 + [VMEM] * (2 + known) + [ANY]...]
    reduce_scatter x1 -> x0, waiting for transfers between devices: 53.1 us -> none  [body(): lax.psum_scatter(jnp.dot(attention, w_out, preferred_element_type=jnp.flo...]
    all_gather x1 -> x0, waiting for transfers between devices: 31.5 us -> none  [body(): piece = lax.all_gather(normed, 'tensor', axis=0, tiled=True)]
    ppermute x0 -> x16, waiting for transfers between devices: none -> 24.3 us  [the longest x6 14.9 us: over_y(): return lax.ppermute(x, 'tensor', [(0, 2), (2, 0), (1, 3), (3, 1)])]
    unnamed x30 -> x55, local copies, waits for them, and re-layouts: 8.74 us -> 24.2 us
    reduce_sum x4 -> x0, other arithmetic: 14.9 us -> none  [the longest x1 12.3 us: absorb(): total = total * rescale + jnp.sum(weights, axis=2)]
    all_gather x1 -> x0, blocking collectives: 8.63 us -> none  [body(): lax.all_gather(projected[:, query_width:], 'tensor', axis=1, tiled=True)]
  transfers between devices with their start and end apart: 4 -> 18, of which waited for: 2 -> 9; matrix products, arithmetic and copies ran while one was open for 19% -> 2% of each run, Pallas kernels for 0% -> 41%
where the time goes in v2:
time: 126 us
  Pallas kernels  55.4 us (44%)
  local copies, waits for them, and re-layouts  25.8 us (20%)
  waiting for transfers between devices  25.8 us (20%)
  starting transfers between devices  16.3 us (13%)
  other arithmetic  1.26 us (1%)
    unnamed x55, local copies, waits for them, and re-layouts  24.2 us
    pallas_call x2, Pallas kernels, attend_out(): pl.pallas_call(kernel, in_specs=[SMEM] * 3 + [VMEM] * (2 + known) + [ANY]...  15.2 us
    ppermute x6, waiting for transfers between devices, over_y(): return lax.ppermute(x, 'tensor', [(0, 2), (2, 0), (1, 3), (3, 1)])  14.9 us
    pallas_call x2, Pallas kernels, project_far(): pl.pallas_call(kernel, in_specs=[SMEM] + [VMEM] * 2 + [ANY] * (2 + len(af...  13.7 us
    pallas_call x1, Pallas kernels, local_rows(): pl.pallas_call(kernel, in_specs=[SMEM] * 3 + [VMEM] * (2 + known) + [ANY]...  9.76 us
    ppermute x10, waiting for transfers between devices, over_core(): return lax.ppermute(x, 'tensor', [(0, 1), (1, 0), (2, 3), (3, 2)])  9.31 us
    pallas_call x1, Pallas kernels, project_local(): pl.pallas_call(kernel, in_specs=[SMEM] + [VMEM] * 4 + [ANY] * (2 + waits)...  8.74 us
    all_to_all x2, starting transfers between devices, to_replicas(): return lax.all_to_all(x, 'replica', split_axis=0, concat_axis=0, tiled=True)  8.4 us
  transfers between devices with their start and end apart: 18, of which 9 were waited for; matrix products, arithmetic and copies ran while one was open for 2% of the time, Pallas kernels for 41%

profile of v2, /device:TPU:0, one launch (start us, length us, event | category | flops | bytes accessed | tf_op | source)
XLA Modules:
  0.0 125.5 jit_solution(3040984151318638161)
XLA Ops:
  0.6 0.7 reshape.13.g_ref
  1.4 0.1 pad_add_fusion.place_ref
  1.5 1.4 %copy-done.5 = bf16[96,8192]{1,0:T(8,128)(2,1)S(1)} copy-done((bf16[96,8192]{1,0:T(8,128)(2,1)S(1)}, bf16[96,8192]{1,0:T(8,128)(2,1)}, u32[]{:S(2)}) %copy-start.5) | copy-done | bytes 1572888
  2.9 1.7 %norm_rows.1 = (bf16[96,4096]{1,0:T(8,128)(2,1)S(1)}, bf16[96,4096]{1,0:T(8,128)(2,1)S(1)}) custom-call(s32[3]{0:T(128)S(1)} %pad_add_fusion.place_ref, bf16[96,8192]{1,0:T(8,128)(2,1)S(1)} %copy-done.5, bf16[1,8192]{1,0:T(2,128)(2,1)S(1)} %reshape.13.g_ref), custom_call_target="tpu_custom_call" | custom-call | flops 1024 | bytes 1024 | tf_op jit(solution)/shard_map/norm_rows/pallas_call | solution.py:203
  4.6 0.5 collective-permute-start
  5.2 2.6 %collective-permute-start.2 = (bf16[2,4,64,256]{3,2,1,0:T(8,128)(2,1)S(1)}, bf16[2,4,64,256]{3,2,1,0:T(8,128)(2,1)S(1)}, u32[]{:S(2)}, u32[]{:S(2)}) collective-permute-start(bf16[2,4,64,256]{3,2,1,0:T(8,128)(2,1)S(1)} %pad_maximum_fusion.1), channel_id=1, source_target_pairs={{0,2},{2,0},{1,3},{3,1},{4,6},{6,4},{5,7},{7,5},{8,10},{10,8},{9,1... | collective-permute-start | bytes 786440 | tf_op jit(solution)/shard_map/ppermute | solution.py:739
  7.8 0.2 collective-permute-start.1
  8.0 0.1 reshape.14
  8.1 0.6 copy.16
  8.7 4.9 %all-to-all-start = ((s32[4,4,2]{1,2,0:T(2,128)}), s32[4,4,2]{1,2,0:T(2,128)S(1)}, u32[]{:S(2)}, u32[]{:S(2)}) async-start(s32[4,4,2]{1,2,0:T(2,128)} %copy.16), calls=%async_computation | async-start | bytes 8192 | tf_op jit(solution)/shard_map/all_to_all | solution.py:745
  13.6 1.2 collective-permute-done.2.y_ref
  14.8 0.1 collective-permute-start.3
  14.9 1.0 broadcast_select_fusion.2
  15.9 1.7 %collective-permute-start.4 = (bf16[96,4096]{1,0:T(8,128)(2,1)}, bf16[96,4096]{1,0:T(8,128)(2,1)}, u32[]{:S(2)}, u32[]{:S(2)}) collective-permute-start(bf16[96,4096]{1,0:T(8,128)(2,1)} %get-tuple-element.45.refs_0_), channel_id=1, source_target_pairs={{0,2},{2,0},{1,3},{3,1},{4,6},{6,4},{5,7},{7,5},{8,10},{10,8},{9,1... | collective-permute-start | bytes 2359304 | tf_op jit(solution)/shard_map/ppermute | solution.py:739
  17.6 1.5 %all-to-all-done = s32[4,4,2]{1,2,0:T(2,128)S(1)} async-done(((s32[4,4,2]{1,2,0:T(2,128)}), s32[4,4,2]{1,2,0:T(2,128)S(1)}, u32[]{:S(2)}, u32[]{:S(2)}) %all-to-all-start) | async-done | bytes 160 | tf_op jit(solution)/shard_map/all_to_all | solution.py:745
  19.1 0.1 copy.17.want_ref
  19.2 1.9 %pick_pages.1.refs_0_ = bf16[4,8,64,256]{3,2,1,0:T(8,128)(2,1)} custom-call(s32[3]{0:T(128)S(1)} %pad_add_fusion.place_ref, s32[4,4,2]{2,1,0:T(4,128)S(1)} %copy.17.want_ref, bf16[4,64,256]{2,1,0:T(8,128)(2,1)S(1)} %get-tuple-element.48.own_ref, bf16[2,4,64,256]{3,2,1,0:T(8,128)(2,1)S(1)} %collective-permute-done.3.core_ref, ...), custom_call_target="tpu_custom_call" | custom-call | flops 1024 | bytes 1024 | tf_op jit(solution)/shard_map/pick_pages/pallas_call | solution.py:651
  21.2 3.5 %all-to-all-start.1 = ((bf16[4,8,64,256]{3,2,1,0:T(8,128)(2,1)}), bf16[4,8,64,256]{3,2,1,0:T(8,128)(2,1)S(1)}, u32[]{:S(2)}, u32[]{:S(2)}) async-start(bf16[4,8,64,256]{3,2,1,0:T(8,128)(2,1)} %pick_pages.1.refs_0_), calls=%async_computation.1 | async-start | bytes 2097152 | tf_op jit(solution)/shard_map/all_to_all | solution.py:745
  24.7 0.0 copy-start.2
  24.7 2.2 %copy-done.2 = bf16[8192,256]{1,0:T(8,128)(2,1)S(1)} copy-done((bf16[8192,256]{1,0:T(8,128)(2,1)S(1)}, bf16[8192,256]{1,0:T(8,128)(2,1)}, u32[]{:S(2)}) %copy-start.2) | copy-done | bytes 4194328
  26.9 1.1 copy-done.10
  28.0 8.7 %project_local.1 = (bf16[192,1024]{1,0:T(8,128)(2,1)S(1)}, bf16[192,256]{1,0:T(8,128)(2,1)S(1)}) custom-call(s32[3]{0:T(128)S(1)} %pad_add_fusion.place_ref, bf16[96,4096]{1,0:T(8,128)(2,1)S(1)} %get-tuple-element.22.near_own, bf16[96,4096]{1,0:T(8,128)(2,1)S(1)} %collective-permute-done.near_peer, bf16[96,4096]{1,0:T(8,128)(2,1)S(1)} %copy-done.10, ...), custom_call_target="tpu_custom_call" | custom-call | flops 1024 | bytes 1024 | tf_op jit(solution)/shard_map/project_local/pallas_call | solution.py:251
  36.8 0.7 copy-done.11
  37.5 0.5 collective-permute-start.6
  38.1 0.7 copy.20.req_ref
  38.7 1.3 %collective-permute-done.5.far_ref = bf16[96,4096]{1,0:T(8,128)(2,1)S(1)} collective-permute-done((bf16[96,4096]{1,0:T(8,128)(2,1)}, bf16[96,4096]{1,0:T(8,128)(2,1)S(1)}, u32[]{:S(2)}, u32[]{:S(2)}) %collective-permute-start.5) | collective-permute-done | bytes 786464 | tf_op jit(solution)/shard_map/ppermute | solution.py:736
  40.0 5.8 %copy-done = bf16[8192,1024]{1,0:T(8,128)(2,1)S(1)} copy-done((bf16[8192,1024]{1,0:T(8,128)(2,1)S(1)}, bf16[8192,1024]{1,0:T(8,128)(2,1)}, u32[]{:S(2)}) %copy-start) | copy-done | bytes 16777240
  45.8 2.2 %copy-done.3 = bf16[8192,256]{1,0:T(8,128)(2,1)S(1)} copy-done((bf16[8192,256]{1,0:T(8,128)(2,1)S(1)}, bf16[8192,256]{1,0:T(8,128)(2,1)}, u32[]{:S(2)}) %copy-start.3) | copy-done | bytes 4194328
  48.0 0.7 copy-done.18
  48.7 7.1 %project_far.2 = (bf16[96,1024]{1,0:T(8,128)(2,1)S(1)}, bf16[96,256]{1,0:T(8,128)(2,1)S(1)}) custom-call(s32[3]{0:T(128)S(1)} %copy-done.18, bf16[96,4096]{1,0:T(8,128)(2,1)} %collective-permute-done.4.near_ref, bf16[96,4096]{1,0:T(8,128)(2,1)S(1)} %collective-permute-done.5.far_ref, bf16[8192,1024]{1,0:T(8,128)(2,1)S(1)} %copy-done, ...), custom_call_target="tpu_custom_call" | custom-call | flops 1024 | bytes 1024 | tf_op jit(solution)/shard_map/project_far/pallas_call | solution.py:433
  55.8 0.7 copy-done.13
  56.5 0.9 copy-done.14
  57.4 0.7 copy-done.15
  58.1 0.7 copy-done.19
  58.8 0.7 copy-done.21
  59.4 7.5 %attend_out.2 = (bf16[96,4096]{1,0:T(8,128)(2,1)S(1)}, bf16[96,4096]{1,0:T(8,128)(2,1)S(1)}) custom-call(s32[3]{0:T(128)S(1)} %copy-done.19, s32[1,4]{1,0:T(1,128)S(1)} %copy-done.21, s32[1,16,2]{2,1,0:T(8,128)S(1)} %copy-done.15, bf16[96,1024]{1,0:T(8,128)(2,1)S(1)} %copy-done.14, bf16[4,8,64,256]{3,2,1,0:T(8,128)(2,1)S(1)} %all-to-all-done.1.pulled_ref, ...), custom_call_target="tpu_custom_call" | custom-call | flops 1024 | bytes 1024 | tf_op jit(solution)/shard_map/attend_out/pallas_call | solution.py:488
  66.9 0.2 collective-permute-start.7
  67.1 2.1 %collective-permute-done.7.right_ref = bf16[96,4096]{1,0:T(8,128)(2,1)S(1)} collective-permute-done((bf16[96,4096]{1,0:T(8,128)(2,1)S(1)}, bf16[96,4096]{1,0:T(8,128)(2,1)S(1)}, u32[]{:S(2)}, u32[]{:S(2)}) %collective-permute-start.7) | collective-permute-done | bytes 786464 | tf_op jit(solution)/shard_map/ppermute | solution.py:736
  69.3 0.2 add_pair.2
  69.5 0.2 collective-permute-start.8
  69.7 0.5 collective-permute-start.9
  70.2 1.6 %collective-permute-done.8.far_ref = bf16[96,4096]{1,0:T(8,128)(2,1)S(1)} collective-permute-done((bf16[96,4096]{1,0:T(8,128)(2,1)S(1)}, bf16[96,4096]{1,0:T(8,128)(2,1)S(1)}, u32[]{:S(2)}, u32[]{:S(2)}) %collective-permute-start.8) | collective-permute-done | bytes 786464 | tf_op jit(solution)/shard_map/ppermute | solution.py:736
  71.9 5.8 %copy-done.1 = bf16[8192,1024]{1,0:T(8,128)(2,1)S(1)} copy-done((bf16[8192,1024]{1,0:T(8,128)(2,1)S(1)}, bf16[8192,1024]{1,0:T(8,128)(2,1)}, u32[]{:S(2)}) %copy-start.1) | copy-done | bytes 16777240
  77.6 6.5 %project_far.3 = (bf16[96,1024]{1,0:T(8,128)(2,1)S(1)}, bf16[96,256]{1,0:T(8,128)(2,1)S(1)}) custom-call(s32[3]{0:T(128)S(1)} %copy-done.20, bf16[96,4096]{1,0:T(8,128)(2,1)S(1)} %collective-permute-done.6.near_ref, bf16[96,4096]{1,0:T(8,128)(2,1)S(1)} %collective-permute-done.8.far_ref, bf16[8192,1024]{1,0:T(8,128)(2,1)S(1)} %copy-done.1, ...), custom_call_target="tpu_custom_call" | custom-call | flops 1024 | bytes 1024 | tf_op jit(solution)/shard_map/project_far/pallas_call | solution.py:433
  84.2 7.8 %attend_out.3 = (bf16[96,4096]{1,0:T(8,128)(2,1)S(1)}, bf16[96,4096]{1,0:T(8,128)(2,1)S(1)}) custom-call(s32[3]{0:T(128)S(1)} %copy-done.20, s32[1,4]{1,0:T(1,128)S(1)} %copy-done.21, s32[1,16,2]{2,1,0:T(8,128)S(1)} %copy-done.16, bf16[96,1024]{1,0:T(8,128)(2,1)S(1)} %get-tuple-element.35.q_ref, bf16[4,8,64,256]{3,2,1,0:T(8,128)(2,1)S(1)} %all-to-all-done.1.pulled_ref, ...), custom_call_target="tpu_custom_call" | custom-call | flops 1024 | bytes 1024 | tf_op jit(solution)/shard_map/attend_out/pallas_call | solution.py:488
  92.0 0.0 copy-start.12
  92.0 0.0 copy-start.22
  92.0 0.2 collective-permute-start.10
  92.2 0.1 collective-permute-start.12
  92.3 2.0 %collective-permute-done.10.right_ref = bf16[96,4096]{1,0:T(8,128)(2,1)S(1)} collective-permute-done((bf16[96,4096]{1,0:T(8,128)(2,1)S(1)}, bf16[96,4096]{1,0:T(8,128)(2,1)S(1)}, u32[]{:S(2)}, u32[]{:S(2)}) %collective-permute-start.10) | collective-permute-done | bytes 786464 | tf_op jit(solution)/shard_map/ppermute | solution.py:736
  94.3 0.2 add_pair.3.refs_4_
  94.5 4.9 %collective-permute-done.12.y_ref = bf16[384,256]{1,0:T(8,128)(2,1)S(1)} collective-permute-done((bf16[384,256]{1,0:T(8,128)(2,1)S(1)}, bf16[384,256]{1,0:T(8,128)(2,1)S(1)}, u32[]{:S(2)}, u32[]{:S(2)}) %collective-permute-start.12) | collective-permute-done | bytes 196640 | tf_op jit(solution)/shard_map/ppermute | solution.py:739
  99.5 0.3 collective-permute-start.13
  99.8 9.8 %local_rows.1 = (bf16[96,8192]{1,0:T(8,128)(2,1)S(1)}, bf16[96,8192]{1,0:T(8,128)(2,1)S(1)}) custom-call(s32[3]{0:T(128)S(1)} %copy-done.20, s32[1,4]{1,0:T(1,128)S(1)} %copy-done.22, s32[1,16,2]{2,1,0:T(8,128)S(1)} %copy-done.16, bf16[192,1024]{1,0:T(8,128)(2,1)S(1)} %copy-done.12, bf16[4,8,64,256]{3,2,1,0:T(8,128)(2,1)S(1)} %all-to-all-done.1.pulled_ref, ...), custom_call_target="tpu_custom_call" | custom-call | flops 1024 | bytes 1024 | tf_op jit(solution)/shard_map/local_rows/pallas_call | solution.py:553
  109.5 0.0 copy-start.8
  109.5 0.0 copy-start.23
  109.5 0.1 collective-permute-start.11
  109.6 8.8 %collective-permute-done.13 = bf16[96,4096]{1,0:T(8,128)(2,1)S(1)} collective-permute-done((bf16[96,4096]{1,0:T(8,128)(2,1)S(1)}, bf16[96,4096]{1,0:T(8,128)(2,1)S(1)}, u32[]{:S(2)}, u32[]{:S(2)}) %collective-permute-start.13) | collective-permute-done | bytes 786464 | tf_op jit(solution)/shard_map/ppermute | solution.py:739
  118.5 0.1 broadcast_select_fusion
  118.6 0.1 collective-permute-start.14
  118.7 0.6 collective-permute-start.15
  119.3 2.2 %collective-permute-done.15.core_ref = bf16[2,384,256]{2,1,0:T(8,128)(2,1)S(1)} collective-permute-done((bf16[2,384,256]{2,1,0:T(8,128)(2,1)S(1)}, bf16[2,384,256]{2,1,0:T(8,128)(2,1)S(1)}, u32[]{:S(2)}, u32[]{:S(2)}) %collective-permute-start.15) | collective-permute-done | bytes 393248 | tf_op jit(solution)/shard_map/ppermute | solution.py:736
  121.5 1.5 %write_pool.1 = bf16[4,4,64,256]{3,2,1,0:T(8,128)(2,1)} custom-call(s32[3]{0:T(128)S(1)} %copy-done.20, s32[1,6]{1,0:T(1,128)S(1)} %copy-done.23, bf16[4,4,64,256]{3,2,1,0:T(8,128)(2,1)S(1)} %copy-done.8, bf16[384,256]{1,0:T(8,128)(2,1)S(1)} %constant_dynamic-update-slice_fusion.own_ref, bf16[2,384,256]{2,1,0:T(8,128)(2,1)S(1)} %collective-permute-done.15.core_ref, ...), custom_call_target="tpu_custom_call" | custom-call | flops 1024 | bytes 1024 | tf_op jit(solution)/shard_map/write_pool/pallas_call | solution.py:704
  123.0 2.5 %finish.1 = bf16[96,8192]{1,0:T(8,128)(2,1)} custom-call(s32[3]{0:T(128)S(1)} %copy-done.20, bf16[96,8192]{1,0:T(8,128)(2,1)S(1)} %copy-done.6, bf16[96,8192]{1,0:T(8,128)(2,1)S(1)} %get-tuple-element.39.own_ref, bf16[96,8192]{1,0:T(8,128)(2,1)S(1)} %collective-permute-done.11.peer_ref, bf16[96,4096]{1,0:T(8,128)(2,1)S(1)} %get-tuple-element.43.near_ref, ...), custom_call_target="tpu_custom_call" | custom-call | flops 1024 | bytes 1024 | tf_op jit(solution)/shard_map/finish/pallas_call | solution.py:614
  (52 shorter events, 0.3 us)
Async XLA Ops:
  1.5 1.4 %copy-start.5 = (bf16[96,8192]{1,0:T(8,128)(2,1)S(1)}, bf16[96,8192]{1,0:T(8,128)(2,1)}, u32[]{:S(2)}) copy-start(bf16[96,8192]{1,0:T(8,128)(2,1)} %x_ref.3) | copy-start | bytes 4718596
  2.9 21.8 %copy-start.17 = (s32[3]{0:T(128)}, s32[3]{0:T(128)S(1)}, u32[]{:S(2)}) copy-start(s32[3]{0:T(128)S(1)} %pad_add_fusion.place_ref) | copy-start | bytes 40
  2.9 2.2 %copy-start.7 = (bf16[4,4,64,256]{3,2,1,0:T(8,128)(2,1)S(1)}, bf16[4,4,64,256]{3,2,1,0:T(8,128)(2,1)}, u32[]{:S(2)}) copy-start(bf16[4,4,64,256]{3,2,1,0:T(8,128)(2,1)} %pool_ref.1) | copy-start | bytes 1572868
  2.9 5.1 %copy-start.24 = (s32[1,16,2]{1,2,0:T(2,128)S(1)}, s32[1,16,2]{1,2,0:T(2,128)}, u32[]{:S(2)}) copy-start(s32[1,16,2]{1,2,0:T(2,128)} %param.17) | copy-start | bytes 388
  4.6 10.3 %copy-start.9 = (bf16[96,4096]{1,0:T(8,128)(2,1)}, bf16[96,4096]{1,0:T(8,128)(2,1)S(1)}, u32[]{:S(2)}) copy-start(bf16[96,4096]{1,0:T(8,128)(2,1)S(1)} %get-tuple-element.23.far_own) | copy-start | bytes 2359300
  4.6 10.3 %collective-permute-start = (bf16[96,4096]{1,0:T(8,128)(2,1)S(1)}, bf16[96,4096]{1,0:T(8,128)(2,1)S(1)}, u32[]{:S(2)}, u32[]{:S(2)}) collective-permute-start(bf16[96,4096]{1,0:T(8,128)(2,1)S(1)} %get-tuple-element.23.far_own), channel_id=1, source_target_pairs={{0,1},{1,0},{2,3},{3,2},{4,5},{5,4},{6,7},{7,6},{8,9},{9,8},{10,11... | collective-permute-start | bytes 2359304 | tf_op jit(solution)/shard_map/ppermute | solution.py:736
  5.2 9.6 %collective-permute-start.2 = (bf16[2,4,64,256]{3,2,1,0:T(8,128)(2,1)S(1)}, bf16[2,4,64,256]{3,2,1,0:T(8,128)(2,1)S(1)}, u32[]{:S(2)}, u32[]{:S(2)}) collective-permute-start(bf16[2,4,64,256]{3,2,1,0:T(8,128)(2,1)S(1)} %pad_maximum_fusion.1), channel_id=1, source_target_pairs={{0,2},{2,0},{1,3},{3,1},{4,6},{6,4},{5,7},{7,5},{8,10},{10,8},{9,1... | collective-permute-start | bytes 786440 | tf_op jit(solution)/shard_map/ppermute | solution.py:739
  7.8 16.9 %collective-permute-start.1 = (bf16[96,4096]{1,0:T(8,128)(2,1)S(1)}, bf16[96,4096]{1,0:T(8,128)(2,1)}, u32[]{:S(2)}, u32[]{:S(2)}) collective-permute-start(bf16[96,4096]{1,0:T(8,128)(2,1)S(1)} %get-tuple-element.22.near_own), channel_id=1, source_target_pairs={{0,1},{1,0},{2,3},{3,2},{4,5},{5,4},{6,7},{7,6},{8,9},{9,8},{10,11... | collective-permute-start | bytes 2359304 | tf_op jit(solution)/shard_map/ppermute | solution.py:736
  8.7 10.4 %all-to-all-start = ((s32[4,4,2]{1,2,0:T(2,128)}), s32[4,4,2]{1,2,0:T(2,128)S(1)}, u32[]{:S(2)}, u32[]{:S(2)}) async-start(s32[4,4,2]{1,2,0:T(2,128)} %copy.16), calls=%async_computation | async-start | bytes 8192 | tf_op jit(solution)/shard_map/all_to_all | solution.py:745
  14.8 4.4 %collective-permute-start.3 = (bf16[2,4,64,256]{3,2,1,0:T(8,128)(2,1)S(1)}, bf16[2,4,64,256]{3,2,1,0:T(8,128)(2,1)S(1)}, u32[]{:S(2)}, u32[]{:S(2)}) collective-permute-start(bf16[2,4,64,256]{3,2,1,0:T(8,128)(2,1)S(1)} %pad_maximum_fusion.2), channel_id=1, source_target_pairs={{0,1},{1,0},{2,3},{3,2},{4,5},{5,4},{6,7},{7,6},{8,9},{9,8},{10,11... | collective-permute-start | bytes 786440 | tf_op jit(solution)/shard_map/ppermute | solution.py:736
  15.9 21.7 %collective-permute-start.4 = (bf16[96,4096]{1,0:T(8,128)(2,1)}, bf16[96,4096]{1,0:T(8,128)(2,1)}, u32[]{:S(2)}, u32[]{:S(2)}) collective-permute-start(bf16[96,4096]{1,0:T(8,128)(2,1)} %get-tuple-element.45.refs_0_), channel_id=1, source_target_pairs={{0,2},{2,0},{1,3},{3,1},{4,6},{6,4},{5,7},{7,5},{8,10},{10,8},{9,1... | collective-permute-start | bytes 2359304 | tf_op jit(solution)/shard_map/ppermute | solution.py:739
  21.2 35.3 %all-to-all-start.1 = ((bf16[4,8,64,256]{3,2,1,0:T(8,128)(2,1)}), bf16[4,8,64,256]{3,2,1,0:T(8,128)(2,1)S(1)}, u32[]{:S(2)}, u32[]{:S(2)}) async-start(bf16[4,8,64,256]{3,2,1,0:T(8,128)(2,1)} %pick_pages.1.refs_0_), calls=%async_computation.1 | async-start | bytes 2097152 | tf_op jit(solution)/shard_map/all_to_all | solution.py:745
  24.7 2.2 %copy-start.2 = (bf16[8192,256]{1,0:T(8,128)(2,1)S(1)}, bf16[8192,256]{1,0:T(8,128)(2,1)}, u32[]{:S(2)}) copy-start(bf16[8192,256]{1,0:T(8,128)(2,1)} %wkv.5) | copy-start | bytes 12582916
  26.9 1.1 copy-start.10
  28.0 10.0 %copy-start.25 = (s32[1,16,2]{1,2,0:T(2,128)S(1)}, s32[1,16,2]{1,2,0:T(2,128)}, u32[]{:S(2)}) copy-start(s32[1,16,2]{1,2,0:T(2,128)} %param.18) | copy-start | bytes 388
  36.8 0.7 copy-start.11
  37.5 2.5 %collective-permute-start.5 = (bf16[96,4096]{1,0:T(8,128)(2,1)}, bf16[96,4096]{1,0:T(8,128)(2,1)S(1)}, u32[]{:S(2)}, u32[]{:S(2)}) collective-permute-start(bf16[96,4096]{1,0:T(8,128)(2,1)} %collective-permute-done.4.near_ref), channel_id=1, source_target_pairs={{0,1},{1,0},{2,3},{3,2},{4,5},{5,4},{6,7},{7,6},{8,9},{9,8},{10,11... | collective-permute-start | bytes 2359304 | tf_op jit(solution)/shard_map/ppermute | solution.py:736
  37.5 29.4 %collective-permute-start.6 = (bf16[96,4096]{1,0:T(8,128)(2,1)S(1)}, bf16[96,4096]{1,0:T(8,128)(2,1)S(1)}, u32[]{:S(2)}, u32[]{:S(2)}) collective-permute-start(bf16[96,4096]{1,0:T(8,128)(2,1)S(1)} %get-tuple-element.44.refs_1_), channel_id=1, source_target_pairs={{0,2},{2,0},{1,3},{3,1},{4,6},{6,4},{5,7},{7,5},{8,10},{10,8},{9,1... | collective-permute-start | bytes 2359304 | tf_op jit(solution)/shard_map/ppermute | solution.py:739
  40.0 5.8 %copy-start = (bf16[8192,1024]{1,0:T(8,128)(2,1)S(1)}, bf16[8192,1024]{1,0:T(8,128)(2,1)}, u32[]{:S(2)}) copy-start(bf16[8192,1024]{1,0:T(8,128)(2,1)} %wq.5) | copy-start | bytes 50331652
  45.8 2.2 %copy-start.3 = (bf16[8192,256]{1,0:T(8,128)(2,1)S(1)}, bf16[8192,256]{1,0:T(8,128)(2,1)}, u32[]{:S(2)}) copy-start(bf16[8192,256]{1,0:T(8,128)(2,1)} %wkv.5) | copy-start | bytes 12582916
  48.0 0.7 copy-start.18
  55.8 0.7 copy-start.13
  56.5 0.9 copy-start.14
  57.4 0.7 copy-start.15
  58.1 0.7 copy-start.19
  58.8 0.7 copy-start.21
  59.4 12.4 %copy-start.4 = (bf16[8192,256]{1,0:T(8,128)(2,1)S(1)}, bf16[8192,256]{1,0:T(8,128)(2,1)}, u32[]{:S(2)}) copy-start(bf16[8192,256]{1,0:T(8,128)(2,1)} %wkv.5) | copy-start | bytes 12582916
  66.9 4.9 %copy-start.20 = (s32[3]{0:T(128)S(1)}, s32[3]{0:T(128)}, u32[]{:S(2)}) copy-start(s32[3]{0:T(128)} %copy-done.17) | copy-start | bytes 40
  66.9 2.4 %collective-permute-start.7 = (bf16[96,4096]{1,0:T(8,128)(2,1)S(1)}, bf16[96,4096]{1,0:T(8,128)(2,1)S(1)}, u32[]{:S(2)}, u32[]{:S(2)}) collective-permute-start(bf16[96,4096]{1,0:T(8,128)(2,1)S(1)} %get-tuple-element.32), channel_id=1, source_target_pairs={{0,1},{1,0},{2,3},{3,2},{4,5},{5,4},{6,7},{7,6},{8,9},{9,8},{10,11... | collective-permute-start | bytes 2359304 | tf_op jit(solution)/shard_map/ppermute | solution.py:736
  69.3 14.9 %copy-start.16 = (s32[1,16,2]{2,1,0:T(8,128)S(1)}, s32[1,16,2]{2,1,0:T(8,128)}, u32[]{:S(2)}) copy-start(s32[1,16,2]{2,1,0:T(8,128)} %copy.20.req_ref) | copy-start | bytes 388
  69.5 2.4 %collective-permute-start.8 = (bf16[96,4096]{1,0:T(8,128)(2,1)S(1)}, bf16[96,4096]{1,0:T(8,128)(2,1)S(1)}, u32[]{:S(2)}, u32[]{:S(2)}) collective-permute-start(bf16[96,4096]{1,0:T(8,128)(2,1)S(1)} %collective-permute-done.6.near_ref), channel_id=1, source_target_pairs={{0,1},{1,0},{2,3},{3,2},{4,5},{5,4},{6,7},{7,6},{8,9},{9,8},{10,11... | collective-permute-start | bytes 2359304 | tf_op jit(solution)/shard_map/ppermute | solution.py:736
  69.7 22.3 %collective-permute-start.9 = (bf16[96,4096]{1,0:T(8,128)(2,1)S(1)}, bf16[96,4096]{1,0:T(8,128)(2,1)S(1)}, u32[]{:S(2)}, u32[]{:S(2)}) collective-permute-start(bf16[96,4096]{1,0:T(8,128)(2,1)S(1)} %add_pair.2), channel_id=1, source_target_pairs={{0,2},{2,0},{1,3},{3,1},{4,6},{6,4},{5,7},{7,5},{8,10},{10,8},{9,1... | collective-permute-start | bytes 2359304 | tf_op jit(solution)/shard_map/ppermute | solution.py:739
  71.8 5.8 %copy-start.1 = (bf16[8192,1024]{1,0:T(8,128)(2,1)S(1)}, bf16[8192,1024]{1,0:T(8,128)(2,1)}, u32[]{:S(2)}) copy-start(bf16[8192,1024]{1,0:T(8,128)(2,1)} %wq.5) | copy-start | bytes 50331652
  92.0 7.8 %copy-start.12 = (bf16[192,1024]{1,0:T(8,128)(2,1)S(1)}, bf16[192,1024]{1,0:T(8,128)(2,1)}, u32[]{:S(2)}) copy-start(bf16[192,1024]{1,0:T(8,128)(2,1)} %copy-done.11) | copy-start | bytes 1179652
  92.0 7.8 %copy-start.22 = (s32[1,4]{1,0:T(1,128)S(1)}, s32[1,4]{1,0:T(1,128)}, u32[]{:S(2)}) copy-start(s32[1,4]{1,0:T(1,128)} %sizes_ref.5) | copy-start | bytes 52
  92.0 2.4 %collective-permute-start.10 = (bf16[96,4096]{1,0:T(8,128)(2,1)S(1)}, bf16[96,4096]{1,0:T(8,128)(2,1)S(1)}, u32[]{:S(2)}, u32[]{:S(2)}) collective-permute-start(bf16[96,4096]{1,0:T(8,128)(2,1)S(1)} %get-tuple-element.38), channel_id=1, source_target_pairs={{0,1},{1,0},{2,3},{3,2},{4,5},{5,4},{6,7},{7,6},{8,9},{9,8},{10,11... | collective-permute-start | bytes 2359304 | tf_op jit(solution)/shard_map/ppermute | solution.py:736
  92.2 7.2 %collective-permute-start.12 = (bf16[384,256]{1,0:T(8,128)(2,1)S(1)}, bf16[384,256]{1,0:T(8,128)(2,1)S(1)}, u32[]{:S(2)}, u32[]{:S(2)}) collective-permute-start(bf16[384,256]{1,0:T(8,128)(2,1)S(1)} %constant_dynamic-update-slice_fusion.own_ref), channel_id=1, source_target_pairs={{0,2},{2,0},{1,3},{3,1},{4,6},{6,4},{5,7},{7,5},{8,10},{10,8},{9,1... | collective-permute-start | bytes 589832 | tf_op jit(solution)/shard_map/ppermute | solution.py:739
  99.5 19.0 %collective-permute-start.13 = (bf16[96,4096]{1,0:T(8,128)(2,1)S(1)}, bf16[96,4096]{1,0:T(8,128)(2,1)S(1)}, u32[]{:S(2)}, u32[]{:S(2)}) collective-permute-start(bf16[96,4096]{1,0:T(8,128)(2,1)S(1)} %add_pair.3.refs_4_), channel_id=1, source_target_pairs={{0,2},{2,0},{1,3},{3,1},{4,6},{6,4},{5,7},{7,5},{8,10},{10,8},{9,1... | collective-permute-start | bytes 2359304 | tf_op jit(solution)/shard_map/ppermute | solution.py:739
  109.5 12.0 %copy-start.8 = (bf16[4,4,64,256]{3,2,1,0:T(8,128)(2,1)S(1)}, bf16[4,4,64,256]{3,2,1,0:T(8,128)(2,1)}, u32[]{:S(2)}) copy-start(bf16[4,4,64,256]{3,2,1,0:T(8,128)(2,1)} %pool_ref.1) | copy-start | bytes 1572868
  109.5 12.0 %copy-start.23 = (s32[1,6]{1,0:T(1,128)S(1)}, s32[1,6]{1,0:T(1,128)}, u32[]{:S(2)}) copy-start(s32[1,6]{1,0:T(1,128)} %slot_ref.1) | copy-start | bytes 76
  109.5 13.4 %collective-permute-start.11 = (bf16[96,8192]{1,0:T(8,128)(2,1)S(1)}, bf16[96,8192]{1,0:T(8,128)(2,1)S(1)}, u32[]{:S(2)}, u32[]{:S(2)}) collective-permute-start(bf16[96,8192]{1,0:T(8,128)(2,1)S(1)} %get-tuple-element.40), channel_id=1, source_target_pairs={{0,1},{1,0},{2,3},{3,2},{4,5},{5,4},{6,7},{7,6},{8,9},{9,8},{10,11... | collective-permute-start | bytes 4718600 | tf_op jit(solution)/shard_map/ppermute | solution.py:736
  118.6 4.4 %copy-start.6 = (bf16[96,8192]{1,0:T(8,128)(2,1)S(1)}, bf16[96,8192]{1,0:T(8,128)(2,1)}, u32[]{:S(2)}) copy-start(bf16[96,8192]{1,0:T(8,128)(2,1)} %x_ref.3) | copy-start | bytes 4718596
  118.6 4.4 %collective-permute-start.14 = (bf16[96,4096]{1,0:T(8,128)(2,1)S(1)}, bf16[96,4096]{1,0:T(8,128)(2,1)S(1)}, u32[]{:S(2)}, u32[]{:S(2)}) collective-permute-start(bf16[96,4096]{1,0:T(8,128)(2,1)S(1)} %get-tuple-element.42), channel_id=1, source_target_pairs={{0,1},{1,0},{2,3},{3,2},{4,5},{5,4},{6,7},{7,6},{8,9},{9,8},{10,11... | collective-permute-start | bytes 2359304 | tf_op jit(solution)/shard_map/ppermute | solution.py:736
  118.7 2.8 %collective-permute-start.15 = (bf16[2,384,256]{2,1,0:T(8,128)(2,1)S(1)}, bf16[2,384,256]{2,1,0:T(8,128)(2,1)S(1)}, u32[]{:S(2)}, u32[]{:S(2)}) collective-permute-start(bf16[2,384,256]{2,1,0:T(8,128)(2,1)S(1)} %pad_maximum_fusion), channel_id=1, source_target_pairs={{0,1},{1,0},{2,3},{3,2},{4,5},{5,4},{6,7},{7,6},{8,9},{9,8},{10,11... | collective-permute-start | bytes 1179656 | tf_op jit(solution)/shard_map/ppermute | solution.py:736

commit v3 on v2

--- a/solution.py
+++ b/solution.py
@@ -20,6 +20,7 @@
 BF16 = jnp.bfloat16
 MIB = 1 << 20
 ANY = pl.BlockSpec(memory_space=pl.ANY)
+HBM = pl.BlockSpec(memory_space=pltpu.HBM)
 SMEM = pl.BlockSpec(memory_space=pltpu.SMEM)
 VMEM = pl.BlockSpec(memory_space=pltpu.VMEM)
 SMALL = pl.CostEstimate(flops=1024, bytes_accessed=1024, transcendentals=0)
@@ -195,7 +196,7 @@
             for start, out in ((near, mine_ref), (far, other_ref)):
                 cols = pl.ds(start, half)
                 values = x_ref[at, cols].astype(F32)
-                out[at, :] = (values * inverse * g_ref[:, cols].astype(F32)).astype(BF16)
+                out[at, :] = (values * inverse * g_ref[cols].astype(F32)[None, :]).astype(BF16)
             return carry
 
         lax.fori_loop(0, rows // step, block, 0)
@@ -208,7 +209,7 @@
         compiler_params=params(16),
         cost_estimate=SMALL,
         name="norm_rows",
-    )(place, tokens, gain.reshape(1, width))
+    )(place, tokens, gain)
 
 
 def project_local(place, near, far, w_query, w_keyvalue, after):
@@ -250,7 +251,7 @@
     total = 2 * rows
     return pl.pallas_call(
         kernel,
-        in_specs=[SMEM] + [VMEM] * 4 + [ANY] * (2 + waits),
+        in_specs=[SMEM] + [VMEM] * 4 + [HBM] * 2 + [ANY] * waits,
         out_specs=[VMEM, VMEM],
         out_shape=[shape((total, q_width)), shape((total, kv_width))],
         scratch_shapes=[
@@ -321,7 +322,7 @@
     for g in range(groups):
         for p in range(per):
             owner = g * tensors + jnp.bitwise_xor(me, p // slots)
-            label = req_ref[0, owner, p % slots]
+            label = req_ref[0, p % slots, owner]
             wanted = (label >= lowest) & (label <= highest)
 
             @pl.when(wanted)
@@ -432,7 +433,7 @@
 
     return pl.pallas_call(
         kernel,
-        in_specs=[SMEM] + [VMEM] * 2 + [ANY] * (2 + len(after)),
+        in_specs=[SMEM] + [VMEM] * 2 + [HBM] * 2 + [ANY] * len(after),
         out_specs=[VMEM] * 2,
         out_shape=[shape((rows, q_width)), shape((rows, kv_width))],
         scratch_shapes=[
@@ -487,7 +488,7 @@
 
     return pl.pallas_call(
         kernel,
-        in_specs=[SMEM] * 3 + [VMEM] * (2 + known) + [ANY],
+        in_specs=[SMEM] * 3 + [VMEM] * (2 + known) + [HBM],
         out_specs=[VMEM] * 2,
         out_shape=[shape((rows, half)), shape((rows, half))],
         scratch_shapes=[
@@ -552,7 +553,7 @@
 
     return pl.pallas_call(
         kernel,
-        in_specs=[SMEM] * 3 + [VMEM] * (2 + known) + [ANY] * (1 + len(after)),
+        in_specs=[SMEM] * 3 + [VMEM] * (2 + known) + [HBM] + [ANY] * len(after),
         out_specs=[VMEM, VMEM],
         out_shape=[shape((rows, width)), shape((rows, width))],
         scratch_shapes=[
@@ -622,15 +623,15 @@
     )(place, tokens, own, peer, near, far)
 
 
-def pick_pages(place, wanted, own, core_pages, y_pages, after):
+def pick_pages(place, wanted, held, after):
     replicas, tensors, slots = wanted.shape
-    _, page, width = own.shape
+    _, page, width = held[0].shape
     total = tensors * slots
 
-    def kernel(place_ref, want_ref, own_ref, core_ref, y_ref, *refs):
-        out_ref, sems = refs[len(after) :]
+    def kernel(place_ref, want_ref, *refs):
+        sources = refs[:tensors]
+        out_ref, sems = refs[tensors + len(after) :]
         me = place_ref[0]
-        sources = (own_ref, core_ref.at[0], y_ref.at[0], core_ref.at[1])
 
         def copies():
             for r in range(replicas):
@@ -650,14 +651,14 @@
 
     return pl.pallas_call(
         kernel,
-        in_specs=[SMEM, SMEM] + [ANY] * (3 + len(after)),
+        in_specs=[SMEM, SMEM] + [ANY] * (tensors + len(after)),
         out_specs=ANY,
         out_shape=shape((replicas, total, page, width)),
         scratch_shapes=[pltpu.SemaphoreType.DMA((replicas * total,))],
         compiler_params=params(8),
         cost_estimate=SMALL,
         name="pick_pages",
-    )(place, wanted, own, core_pages, y_pages, *after)
+    )(place, wanted, *held, *after)
 
 
 def write_pool(place, slots, kv_pool, own, core_new, y_new):
@@ -741,29 +742,34 @@
     def head_of(i):
         return lax.dynamic_index_in_dim(kv_pool, jnp.bitwise_xor(me, i), 1, keepdims=False)
 
+    requests = jnp.swapaxes(page_request, 1, 2)
+
     def to_replicas(x):
         return lax.all_to_all(x, "replica", split_axis=0, concat_axis=0, tiled=True)
 
     def tie(x, *others):
         return lax.optimization_barrier((x, *others))[0]
 
-    wanted = to_replicas(page_index.reshape(replicas, -1, page_index.shape[2]))
-    y_pages = over_y(jnp.stack([head_of(2), head_of(3)]))
-    core_pages = over_core(jnp.stack([head_of(1), y_pages[1]]))
+    w_query = pltpu.with_memory_space_constraint(w_query, pltpu.HBM)
+    w_keyvalue = pltpu.with_memory_space_constraint(w_keyvalue, pltpu.HBM)
+    w_out = pltpu.with_memory_space_constraint(w_out, pltpu.HBM)
+    held = [head_of(0)]
+    for i in range(1, 4):
+        held.append(lax.ppermute(head_of(i), "tensor", [(t, t ^ i) for t in range(4)]))
 
     mine, other = norm_rows(place, tokens, gain)
     peer_near = over_core(other)
     peer_far = over_core(mine)
     is_first = core == 0
-    near_tied = tie(peer_near, y_pages)
+    near_tied = tie(peer_near, held[2], held[3])
     first_half = jnp.where(is_first, mine, near_tied)
     second_half = jnp.where(is_first, near_tied, mine)
     first = over_y(first_half)
     second = over_y(second_half)
 
-    picked = pick_pages(
-        place, wanted, head_of(0), core_pages, y_pages, [first_half, second_half]
-    )
+    numbers = page_index.reshape(replicas, -1, page_index.shape[2])
+    wanted = to_replicas(tie(numbers, first_half))
+    picked = pick_pages(place, wanted, held, [first_half, second_half])
     pulled = to_replicas(picked)
 
     q_local, kv_local = project_local(
@@ -782,7 +788,7 @@
     first = tie(first, q_local)
     q_first, kv_first = project_far(place, first, over_core(first), w_query, w_keyvalue, [])
     there, stay = attend_out(
-        place, suffix_pages, page_request, q_first, [kv_local, kv_first],
+        place, suffix_pages, requests, q_first, [kv_local, kv_first],
         [local_base, first_base], first_base, pulled, w_out,
     )
     there = tie(there, second)
@@ -794,7 +800,7 @@
     fresh = [kv_local, kv_first, kv_second]
     bases = [local_base, first_base, second_base]
     there, stay = attend_out(
-        place, suffix_pages, page_request, q_second, fresh, bases, second_base, pulled, w_out
+        place, suffix_pages, requests, q_second, fresh, bases, second_base, pulled, w_out
     )
     there = tie(there, first_sum)
     second_mix = add_pair(stay, over_core(there))
@@ -805,12 +811,13 @@
     core_new = over_core(jnp.stack([new_own, y_new]))
     second_sum = over_y(tie(second_mix, y_new))
 
+    pool_out = write_pool(place, new_slot, kv_pool, new_own, core_new, y_new)
+
     own_part, peer_part = local_rows(
-        place, suffix_pages, page_request, q_local, fresh, bases, local_base, pulled, w_out,
-        [second_mix],
+        place, suffix_pages, requests, q_local, fresh, bases, local_base, pulled, w_out,
+        [second_mix, pool_out],
     )
     peer_part = over_core(peer_part)
-    pool_out = write_pool(place, new_slot, kv_pool, new_own, core_new, y_new)
 
     near = jnp.where(is_first, first_sum, second_sum)
     far = over_core(jnp.where(is_first, second_sum, first_sum))

time: 126 us -> 123 us (0.976)
  local copies, waits for them, and re-layouts: 25.8 us -> 10.9 us
  starting transfers between devices: 16.3 us -> 20.2 us
  waiting for transfers between devices: 25.8 us -> 29.7 us
  Pallas kernels: 55.4 us -> 59.1 us
    unnamed x55 -> x46, local copies, waits for them, and re-layouts: 24.2 us -> 9.35 us
    ppermute x0 -> x3, waiting for transfers between devices: none -> 6.08 us  [chip_pair_body(): lax.ppermute(head_of(i), 'tensor', [(t, t ^ i) for t in range(4)])]
    ppermute x6 -> x5, waiting for transfers between devices: 14.9 us -> 9.46 us  [over_y(): return lax.ppermute(x, 'tensor', [(0, 2), (2, 0), (1, 3), (3, 1)])]
    all_to_all x2, waiting for transfers between devices: 1.51 us -> 5.5 us  [to_replicas(): return lax.all_to_all(x, 'replica', split_axis=0, concat_axis=0, tiled=True)]
    pallas_call x7, Pallas kernels: 49.3 us -> 53 us  [the longest x2 17.1 us: project_far(): pl.pallas_call(kernel, in_specs=[SMEM] + [VMEM] * 2 + [HBM] * 2 + [ANY] *...]
    ppermute x0 -> x3, starting transfers between devices: none -> 3.07 us  [chip_pair_body(): lax.ppermute(head_of(i), 'tensor', [(t, t ^ i) for t in range(4)])]
    ppermute x6 -> x5, starting transfers between devices: 5.76 us -> 7.45 us  [over_y(): return lax.ppermute(x, 'tensor', [(0, 2), (2, 0), (1, 3), (3, 1)])]
    reshape x3 -> x1, local copies, waits for them, and re-layouts: 1.42 us -> 0.08 us  [chip_pair_body(): numbers = page_index.reshape(replicas, -1, page_index.shape[2])]
  transfers between devices with their start and end apart: 18 -> 19, of which waited for: 9 -> 13; matrix products, arithmetic and copies ran while one was open for 2% -> 2% of each run, Pallas kernels for 41% -> 45%
where the time goes in v3:
time: 123 us; the launch traced here: 122 us
  Pallas kernels  59.1 us (48%)
  waiting for transfers between devices  29.7 us (24%)
  starting transfers between devices  20.2 us (16%)
  local copies, waits for them, and re-layouts  10.9 us (9%)
    pallas_call x2, Pallas kernels, project_far(): pl.pallas_call(kernel, in_specs=[SMEM] + [VMEM] * 2 + [HBM] * 2 + [ANY] *...  17.1 us
    pallas_call x2, Pallas kernels, attend_out(): pl.pallas_call(kernel, in_specs=[SMEM] * 3 + [VMEM] * (2 + known) + [HBM]...  15.3 us
    pallas_call x1, Pallas kernels, local_rows(): pl.pallas_call(kernel, in_specs=[SMEM] * 3 + [VMEM] * (2 + known) + [HBM]...  9.7 us
    ppermute x5, waiting for transfers between devices, over_y(): return lax.ppermute(x, 'tensor', [(0, 2), (2, 0), (1, 3), (3, 1)])  9.46 us
    unnamed x46, local copies, waits for them, and re-layouts  9.35 us
    pallas_call x1, Pallas kernels, project_local(): pl.pallas_call(kernel, in_specs=[SMEM] + [VMEM] * 4 + [HBM] * 2 + [ANY] *...  9.02 us
    ppermute x9, waiting for transfers between devices, over_core(): return lax.ppermute(x, 'tensor', [(0, 1), (1, 0), (2, 3), (3, 2)])  8.65 us
    all_to_all x2, starting transfers between devices, to_replicas(): return lax.all_to_all(x, 'replica', split_axis=0, concat_axis=0, tiled=True)  8.42 us
  transfers between devices with their start and end apart: 19, of which 13 were waited for; matrix products, arithmetic and copies ran while one was open for 2% of the time, Pallas kernels for 45%

profile of v3, /device:TPU:0, one launch (start us, length us, event | category | flops | bytes accessed | tf_op | source)
XLA Modules:
  0.0 122.1 jit_solution(16915200252066808698)
XLA Ops:
  0.7 0.1 pad_add_fusion.place_ref
  0.7 1.4 %copy-done = bf16[96,8192]{1,0:T(8,128)(2,1)S(1)} copy-done((bf16[96,8192]{1,0:T(8,128)(2,1)S(1)}, bf16[96,8192]{1,0:T(8,128)(2,1)}, u32[]{:S(2)}) %copy-start) | copy-done | bytes 1572888
  2.1 0.7 copy-done.15
  2.9 1.7 %norm_rows.1 = (bf16[96,4096]{1,0:T(8,128)(2,1)S(1)}, bf16[96,4096]{1,0:T(8,128)(2,1)S(1)}) custom-call(s32[3]{0:T(128)S(1)} %pad_add_fusion.place_ref, bf16[96,8192]{1,0:T(8,128)(2,1)S(1)} %copy-done, bf16[8192]{0:T(1024)(128)(2,1)S(1)} %copy-done.15), custom_call_target="tpu_custom_call" | custom-call | flops 1024 | bytes 1024 | tf_op jit(solution)/shard_map/norm_rows/pallas_call | solution.py:204
  4.6 0.5 collective-permute-start
  5.1 0.8 dynamic-slice_bitcast_fusion
  5.8 2.7 %collective-permute-start.2 = (bf16[4,64,256]{2,1,0:T(8,128)(2,1)}, bf16[4,64,256]{2,1,0:T(8,128)(2,1)S(1)}, u32[]{:S(2)}, u32[]{:S(2)}) collective-permute-start(bf16[4,64,256]{2,1,0:T(8,128)(2,1)} %get-tuple-element.51), channel_id=1, source_target_pairs={{0,2},{1,3},{2,0},{3,1},{4,6},{5,7},{6,4},{7,5},{8,10},{9,11},{10,... | collective-permute-start | bytes 393224 | tf_op jit(solution)/shard_map/ppermute | solution.py:758
  8.5 0.1 collective-permute-start.1
  8.7 0.4 collective-permute-start.4
  9.0 0.1 reshape.7
  9.1 3.9 %collective-permute-done.2.refs_2_ = bf16[4,64,256]{2,1,0:T(8,128)(2,1)S(1)} collective-permute-done((bf16[4,64,256]{2,1,0:T(8,128)(2,1)}, bf16[4,64,256]{2,1,0:T(8,128)(2,1)S(1)}, u32[]{:S(2)}, u32[]{:S(2)}) %collective-permute-start.2) | collective-permute-done | bytes 131104 | tf_op jit(solution)/shard_map/ppermute | solution.py:758
  13.1 2.1 %collective-permute-done.3.refs_3_ = bf16[4,64,256]{2,1,0:T(8,128)(2,1)S(1)} collective-permute-done((bf16[4,64,256]{2,1,0:T(8,128)(2,1)}, bf16[4,64,256]{2,1,0:T(8,128)(2,1)S(1)}, u32[]{:S(2)}, u32[]{:S(2)}) %collective-permute-start.3) | collective-permute-done | bytes 131104 | tf_op jit(solution)/shard_map/ppermute | solution.py:758
  15.2 1.0 broadcast_select_fusion.2
  16.2 0.6 copy.13
  16.8 4.9 %all-to-all-start = ((s32[4,4,2]{1,2,0:T(2,128)}), s32[4,4,2]{1,2,0:T(2,128)S(1)}, u32[]{:S(2)}, u32[]{:S(2)}) async-start(s32[4,4,2]{1,2,0:T(2,128)} %copy.13), calls=%async_computation | async-start | bytes 8192 | tf_op jit(solution)/shard_map/all_to_all | solution.py:748
  21.7 1.5 %collective-permute-start.5 = (bf16[96,4096]{1,0:T(8,128)(2,1)}, bf16[96,4096]{1,0:T(8,128)(2,1)}, u32[]{:S(2)}, u32[]{:S(2)}) collective-permute-start(bf16[96,4096]{1,0:T(8,128)(2,1)} %get-tuple-element.47.refs_4_), channel_id=1, source_target_pairs={{0,2},{2,0},{1,3},{3,1},{4,6},{6,4},{5,7},{7,5},{8,10},{10,8},{9,1... | collective-permute-start | bytes 2359304 | tf_op jit(solution)/shard_map/ppermute | solution.py:740
  23.2 4.1 %all-to-all-done = s32[4,4,2]{1,2,0:T(2,128)S(1)} async-done(((s32[4,4,2]{1,2,0:T(2,128)}), s32[4,4,2]{1,2,0:T(2,128)S(1)}, u32[]{:S(2)}, u32[]{:S(2)}) %all-to-all-start) | async-done | bytes 160 | tf_op jit(solution)/shard_map/all_to_all | solution.py:748
  27.3 0.1 copy.14.want_ref
  27.4 1.9 %pick_pages.1.refs_0_ = bf16[4,8,64,256]{3,2,1,0:T(8,128)(2,1)} custom-call(s32[3]{0:T(128)S(1)} %pad_add_fusion.place_ref, s32[4,4,2]{2,1,0:T(4,128)S(1)} %copy.14.want_ref, bf16[4,64,256]{2,1,0:T(8,128)(2,1)S(1)} %get-tuple-element.49.refs_0_, bf16[4,64,256]{2,1,0:T(8,128)(2,1)S(1)} %collective-permute-done.4.refs_1_, ...), custom_call_target="tpu_custom_call" | custom-call | flops 1024 | bytes 1024 | tf_op jit(solution)/shard_map/pick_pages/pallas_call | solution.py:652
  29.3 3.5 %all-to-all-start.1 = ((bf16[4,8,64,256]{3,2,1,0:T(8,128)(2,1)}), bf16[4,8,64,256]{3,2,1,0:T(8,128)(2,1)S(1)}, u32[]{:S(2)}, u32[]{:S(2)}) async-start(bf16[4,8,64,256]{3,2,1,0:T(8,128)(2,1)} %pick_pages.1.refs_0_), calls=%async_computation.1 | async-start | bytes 2097152 | tf_op jit(solution)/shard_map/all_to_all | solution.py:748
  32.9 1.1 copy-done.6
  34.0 9.0 %project_local.1 = (bf16[192,1024]{1,0:T(8,128)(2,1)S(1)}, bf16[192,256]{1,0:T(8,128)(2,1)S(1)}) custom-call(s32[3]{0:T(128)S(1)} %pad_add_fusion.place_ref, bf16[96,4096]{1,0:T(8,128)(2,1)S(1)} %get-tuple-element.23.near_own, bf16[96,4096]{1,0:T(8,128)(2,1)S(1)} %collective-permute-done.near_peer, bf16[96,4096]{1,0:T(8,128)(2,1)S(1)} %copy-done.6, ...), custom_call_target="tpu_custom_call" | custom-call | flops 1024 | bytes 1024 | tf_op jit(solution)/shard_map/project_local/pallas_call | solution.py:252
  43.0 0.7 copy-done.7
  43.8 1.5 %collective-permute-start.7 = (bf16[96,4096]{1,0:T(8,128)(2,1)S(1)}, bf16[96,4096]{1,0:T(8,128)(2,1)S(1)}, u32[]{:S(2)}, u32[]{:S(2)}) collective-permute-start(bf16[96,4096]{1,0:T(8,128)(2,1)S(1)} %get-tuple-element.46.refs_5_), channel_id=1, source_target_pairs={{0,2},{2,0},{1,3},{3,1},{4,6},{6,4},{5,7},{7,5},{8,10},{10,8},{9,1... | collective-permute-start | bytes 2359304 | tf_op jit(solution)/shard_map/ppermute | solution.py:740
  45.3 1.0 collective-permute-done.6.far_ref
  46.3 0.7 copy-done.12
  46.9 8.8 %project_far.2 = (bf16[96,1024]{1,0:T(8,128)(2,1)S(1)}, bf16[96,256]{1,0:T(8,128)(2,1)S(1)}) custom-call(s32[3]{0:T(128)S(1)} %copy-done.12, bf16[96,4096]{1,0:T(8,128)(2,1)} %collective-permute-done.5.near_ref, bf16[96,4096]{1,0:T(8,128)(2,1)S(1)} %collective-permute-done.6.far_ref, bf16[8192,1024]{1,0:T(8,128)(2,1)} %wq.5, bf16[8192,256]{1,0:T(8,128)(2,1)} %wkv.5), custom_call_target="tpu_custom_call" | custom-call | flops 1024 | bytes 1024 | tf_op jit(solution)/shard_map/project_far/pallas_call | solution.py:434
  55.8 0.0 copy-start.9
  55.8 0.7 copy-done.9
  56.5 1.4 %all-to-all-done.1.pulled_ref = bf16[4,8,64,256]{3,2,1,0:T(8,128)(2,1)S(1)} async-done(((bf16[4,8,64,256]{3,2,1,0:T(8,128)(2,1)}), bf16[4,8,64,256]{3,2,1,0:T(8,128)(2,1)S(1)}, u32[]{:S(2)}, u32[]{:S(2)}) %all-to-all-start.1) | async-done | bytes 1048608 | tf_op jit(solution)/shard_map/all_to_all | solution.py:748
  57.9 0.9 copy-done.10
  58.8 0.7 copy-done.13
  59.5 0.7 copy-done.16
  60.2 0.7 copy-done.18
  60.8 7.1 %attend_out.2 = (bf16[96,4096]{1,0:T(8,128)(2,1)S(1)}, bf16[96,4096]{1,0:T(8,128)(2,1)S(1)}) custom-call(s32[3]{0:T(128)S(1)} %copy-done.13, s32[1,4]{1,0:T(1,128)S(1)} %copy-done.18, s32[1,2,16]{2,1,0:T(2,128)S(1)} %bitcast.18, bf16[96,1024]{1,0:T(8,128)(2,1)S(1)} %copy-done.10, bf16[4,8,64,256]{3,2,1,0:T(8,128)(2,1)S(1)} %all-to-all-done.1.pulled_ref, ...), custom_call_target="tpu_custom_call" | custom-call | flops 1024 | bytes 1024 | tf_op jit(solution)/shard_map/attend_out/pallas_call | solution.py:489
  67.9 0.1 collective-permute-start.8
  68.0 2.3 %collective-permute-done.8.right_ref = bf16[96,4096]{1,0:T(8,128)(2,1)S(1)} collective-permute-done((bf16[96,4096]{1,0:T(8,128)(2,1)S(1)}, bf16[96,4096]{1,0:T(8,128)(2,1)S(1)}, u32[]{:S(2)}, u32[]{:S(2)}) %collective-permute-start.8) | collective-permute-done | bytes 786464 | tf_op jit(solution)/shard_map/ppermute | solution.py:737
  70.3 0.2 add_pair.2
  70.5 0.0 copy-start.19
  70.5 0.2 collective-permute-start.9
  70.7 1.5 %collective-permute-start.10 = (bf16[96,4096]{1,0:T(8,128)(2,1)S(1)}, bf16[96,4096]{1,0:T(8,128)(2,1)S(1)}, u32[]{:S(2)}, u32[]{:S(2)}) collective-permute-start(bf16[96,4096]{1,0:T(8,128)(2,1)S(1)} %add_pair.2), channel_id=1, source_target_pairs={{0,2},{2,0},{1,3},{3,1},{4,6},{6,4},{5,7},{7,5},{8,10},{10,8},{9,1... | collective-permute-start | bytes 2359304 | tf_op jit(solution)/shard_map/ppermute | solution.py:740
  72.2 0.7 collective-permute-done.9.far_ref
  72.9 8.2 %project_far.3 = (bf16[96,1024]{1,0:T(8,128)(2,1)S(1)}, bf16[96,256]{1,0:T(8,128)(2,1)S(1)}) custom-call(s32[3]{0:T(128)S(1)} %copy-done.14, bf16[96,4096]{1,0:T(8,128)(2,1)S(1)} %collective-permute-done.7.near_ref, bf16[96,4096]{1,0:T(8,128)(2,1)S(1)} %collective-permute-done.9.far_ref, bf16[8192,1024]{1,0:T(8,128)(2,1)} %wq.5, bf16[8192,256]{1,0:T(8,128)(2,1)} %wkv.5), custom_call_target="tpu_custom_call" | custom-call | flops 1024 | bytes 1024 | tf_op jit(solution)/shard_map/project_far/pallas_call | solution.py:434
  81.1 8.3 %attend_out.3 = (bf16[96,4096]{1,0:T(8,128)(2,1)S(1)}, bf16[96,4096]{1,0:T(8,128)(2,1)S(1)}) custom-call(s32[3]{0:T(128)S(1)} %copy-done.14, s32[1,4]{1,0:T(1,128)S(1)} %copy-done.19, s32[1,2,16]{2,1,0:T(2,128)S(1)} %bitcast.19, bf16[96,1024]{1,0:T(8,128)(2,1)S(1)} %get-tuple-element.37.q_ref, bf16[4,8,64,256]{3,2,1,0:T(8,128)(2,1)S(1)} %all-to-all-done.1.pulled_ref, ...), custom_call_target="tpu_custom_call" | custom-call | flops 1024 | bytes 1024 | tf_op jit(solution)/shard_map/attend_out/pallas_call | solution.py:489
  89.4 1.1 collective-permute-done.10
  90.6 1.5 %collective-permute-start.12 = (bf16[384,256]{1,0:T(8,128)(2,1)S(1)}, bf16[384,256]{1,0:T(8,128)(2,1)S(1)}, u32[]{:S(2)}, u32[]{:S(2)}) collective-permute-start(bf16[384,256]{1,0:T(8,128)(2,1)S(1)} %constant_dynamic-update-slice_fusion.own_ref), channel_id=1, source_target_pairs={{0,2},{2,0},{1,3},{3,1},{4,6},{6,4},{5,7},{7,5},{8,10},{10,8},{9,1... | collective-permute-start | bytes 589832 | tf_op jit(solution)/shard_map/ppermute | solution.py:740
  92.1 0.7 collective-permute-done.11.right_ref
  92.8 0.2 add_pair.3.refs_4_
  93.1 0.0 copy-start.17
  93.1 4.9 %collective-permute-done.12.y_ref = bf16[384,256]{1,0:T(8,128)(2,1)S(1)} collective-permute-done((bf16[384,256]{1,0:T(8,128)(2,1)S(1)}, bf16[384,256]{1,0:T(8,128)(2,1)S(1)}, u32[]{:S(2)}, u32[]{:S(2)}) %collective-permute-start.12) | collective-permute-done | bytes 196640 | tf_op jit(solution)/shard_map/ppermute | solution.py:740
  98.0 1.4 %collective-permute-start.15 = (bf16[96,4096]{1,0:T(8,128)(2,1)S(1)}, bf16[96,4096]{1,0:T(8,128)(2,1)S(1)}, u32[]{:S(2)}, u32[]{:S(2)}) collective-permute-start(bf16[96,4096]{1,0:T(8,128)(2,1)S(1)} %add_pair.3.refs_4_), channel_id=1, source_target_pairs={{0,2},{2,0},{1,3},{3,1},{4,6},{6,4},{5,7},{7,5},{8,10},{10,8},{9,1... | collective-permute-start | bytes 2359304 | tf_op jit(solution)/shard_map/ppermute | solution.py:740
  99.4 0.1 collective-permute-start.13
  99.5 1.7 %collective-permute-done.13.core_ref = bf16[2,384,256]{2,1,0:T(8,128)(2,1)S(1)} collective-permute-done((bf16[2,384,256]{2,1,0:T(8,128)(2,1)S(1)}, bf16[2,384,256]{2,1,0:T(8,128)(2,1)S(1)}, u32[]{:S(2)}, u32[]{:S(2)}) %collective-permute-start.13) | collective-permute-done | bytes 393248 | tf_op jit(solution)/shard_map/ppermute | solution.py:737
  101.2 1.5 %write_pool.1.refs_5_ = bf16[4,4,64,256]{3,2,1,0:T(8,128)(2,1)} custom-call(s32[3]{0:T(128)S(1)} %copy-done.14, s32[1,6]{1,0:T(1,128)S(1)} %copy-done.20, bf16[4,4,64,256]{3,2,1,0:T(8,128)(2,1)S(1)} %copy-done.4, bf16[384,256]{1,0:T(8,128)(2,1)S(1)} %constant_dynamic-update-slice_fusion.own_ref, bf16[2,384,256]{2,1,0:T(8,128)(2,1)S(1)} %collective-permute-done.13.core_ref, ...), custom_call_target="tpu_custom_call" | custom-call | flops 1024 | bytes 1024 | tf_op jit(solution)/shard_map/write_pool/pallas_call | solution.py:705
  102.7 0.0 copy-start.2
  102.8 1.0 copy-done.2
  103.8 9.7 %local_rows.1 = (bf16[96,8192]{1,0:T(8,128)(2,1)S(1)}, bf16[96,8192]{1,0:T(8,128)(2,1)S(1)}) custom-call(s32[3]{0:T(128)S(1)} %copy-done.14, s32[1,4]{1,0:T(1,128)S(1)} %copy-done.19, s32[1,2,16]{2,1,0:T(2,128)S(1)} %bitcast.20, bf16[192,1024]{1,0:T(8,128)(2,1)S(1)} %copy-done.8, bf16[4,8,64,256]{3,2,1,0:T(8,128)(2,1)S(1)} %all-to-all-done.1.pulled_ref, ...), custom_call_target="tpu_custom_call" | custom-call | flops 1024 | bytes 1024 | tf_op jit(solution)/shard_map/local_rows/pallas_call | solution.py:554
  113.5 0.0 copy-start.1
  113.5 0.2 collective-permute-start.14
  113.7 3.4 %collective-permute-done.15 = bf16[96,4096]{1,0:T(8,128)(2,1)S(1)} collective-permute-done((bf16[96,4096]{1,0:T(8,128)(2,1)S(1)}, bf16[96,4096]{1,0:T(8,128)(2,1)S(1)}, u32[]{:S(2)}, u32[]{:S(2)}) %collective-permute-start.15) | collective-permute-done | bytes 786464 | tf_op jit(solution)/shard_map/ppermute | solution.py:740
  117.1 0.1 broadcast_select_fusion
  117.2 0.1 collective-permute-start.16
  117.3 2.3 %collective-permute-done.16.far_ref = bf16[96,4096]{1,0:T(8,128)(2,1)S(1)} collective-permute-done((bf16[96,4096]{1,0:T(8,128)(2,1)S(1)}, bf16[96,4096]{1,0:T(8,128)(2,1)S(1)}, u32[]{:S(2)}, u32[]{:S(2)}) %collective-permute-start.16) | collective-permute-done | bytes 786464 | tf_op jit(solution)/shard_map/ppermute | solution.py:737
  119.6 2.5 %finish.1 = bf16[96,8192]{1,0:T(8,128)(2,1)} custom-call(s32[3]{0:T(128)S(1)} %copy-done.14, bf16[96,8192]{1,0:T(8,128)(2,1)S(1)} %copy-done.1, bf16[96,8192]{1,0:T(8,128)(2,1)S(1)} %get-tuple-element.41.own_ref, bf16[96,8192]{1,0:T(8,128)(2,1)S(1)} %collective-permute-done.14.peer_ref, bf16[96,4096]{1,0:T(8,128)(2,1)S(1)} %get-tuple-element.45.near_ref, ...), custom_call_target="tpu_custom_call" | custom-call | flops 1024 | bytes 1024 | tf_op jit(solution)/shard_map/finish/pallas_call | solution.py:615
  (41 shorter events, 0.1 us)
Async XLA Ops:
  0.6 8.4 %copy-start.21 = (s32[1,16,2]{1,2,0:T(2,128)S(1)}, s32[1,16,2]{1,2,0:T(2,128)}, u32[]{:S(2)}) copy-start(s32[1,16,2]{1,2,0:T(2,128)} %param.17) | copy-start | bytes 388
  0.7 1.4 %copy-start = (bf16[96,8192]{1,0:T(8,128)(2,1)S(1)}, bf16[96,8192]{1,0:T(8,128)(2,1)}, u32[]{:S(2)}) copy-start(bf16[96,8192]{1,0:T(8,128)(2,1)} %x_ref.3) | copy-start | bytes 4718596
  2.1 0.7 copy-start.15
  2.9 30.0 %copy-start.11 = (s32[3]{0:T(128)}, s32[3]{0:T(128)S(1)}, u32[]{:S(2)}) copy-start(s32[3]{0:T(128)S(1)} %pad_add_fusion.place_ref) | copy-start | bytes 40
  2.9 2.2 %copy-start.3 = (bf16[4,4,64,256]{3,2,1,0:T(8,128)(2,1)S(1)}, bf16[4,4,64,256]{3,2,1,0:T(8,128)(2,1)}, u32[]{:S(2)}) copy-start(bf16[4,4,64,256]{3,2,1,0:T(8,128)(2,1)} %pool_ref.1) | copy-start | bytes 1572868
  4.6 10.7 %copy-start.5 = (bf16[96,4096]{1,0:T(8,128)(2,1)}, bf16[96,4096]{1,0:T(8,128)(2,1)S(1)}, u32[]{:S(2)}) copy-start(bf16[96,4096]{1,0:T(8,128)(2,1)S(1)} %get-tuple-element.24.far_own) | copy-start | bytes 2359300
  4.6 10.6 %collective-permute-start = (bf16[96,4096]{1,0:T(8,128)(2,1)S(1)}, bf16[96,4096]{1,0:T(8,128)(2,1)S(1)}, u32[]{:S(2)}, u32[]{:S(2)}) collective-permute-start(bf16[96,4096]{1,0:T(8,128)(2,1)S(1)} %get-tuple-element.24.far_own), channel_id=1, source_target_pairs={{0,1},{1,0},{2,3},{3,2},{4,5},{5,4},{6,7},{7,6},{8,9},{9,8},{10,11... | collective-permute-start | bytes 2359304 | tf_op jit(solution)/shard_map/ppermute | solution.py:737
  5.8 7.2 %collective-permute-start.2 = (bf16[4,64,256]{2,1,0:T(8,128)(2,1)}, bf16[4,64,256]{2,1,0:T(8,128)(2,1)S(1)}, u32[]{:S(2)}, u32[]{:S(2)}) collective-permute-start(bf16[4,64,256]{2,1,0:T(8,128)(2,1)} %get-tuple-element.51), channel_id=1, source_target_pairs={{0,2},{1,3},{2,0},{3,1},{4,6},{5,7},{6,4},{7,5},{8,10},{9,11},{10,... | collective-permute-start | bytes 393224 | tf_op jit(solution)/shard_map/ppermute | solution.py:758
  8.5 6.7 %collective-permute-start.3 = (bf16[4,64,256]{2,1,0:T(8,128)(2,1)}, bf16[4,64,256]{2,1,0:T(8,128)(2,1)S(1)}, u32[]{:S(2)}, u32[]{:S(2)}) collective-permute-start(bf16[4,64,256]{2,1,0:T(8,128)(2,1)} %get-tuple-element.50), channel_id=1, source_target_pairs={{0,3},{1,2},{2,1},{3,0},{4,7},{5,6},{6,5},{7,4},{8,11},{9,10},{10,... | collective-permute-start | bytes 393224 | tf_op jit(solution)/shard_map/ppermute | solution.py:758
  8.5 24.3 %collective-permute-start.1 = (bf16[96,4096]{1,0:T(8,128)(2,1)S(1)}, bf16[96,4096]{1,0:T(8,128)(2,1)}, u32[]{:S(2)}, u32[]{:S(2)}) collective-permute-start(bf16[96,4096]{1,0:T(8,128)(2,1)S(1)} %get-tuple-element.23.near_own), channel_id=1, source_target_pairs={{0,1},{1,0},{2,3},{3,2},{4,5},{5,4},{6,7},{7,6},{8,9},{9,8},{10,11... | collective-permute-start | bytes 2359304 | tf_op jit(solution)/shard_map/ppermute | solution.py:737
  8.7 18.7 %collective-permute-start.4 = (bf16[4,64,256]{2,1,0:T(8,128)(2,1)}, bf16[4,64,256]{2,1,0:T(8,128)(2,1)S(1)}, u32[]{:S(2)}, u32[]{:S(2)}) collective-permute-start(bf16[4,64,256]{2,1,0:T(8,128)(2,1)} %get-tuple-element.48), channel_id=1, source_target_pairs={{0,1},{1,0},{2,3},{3,2},{4,5},{5,4},{6,7},{7,6},{8,9},{9,8},{10,11... | collective-permute-start | bytes 393224 | tf_op jit(solution)/shard_map/ppermute | solution.py:758
  16.8 10.5 %all-to-all-start = ((s32[4,4,2]{1,2,0:T(2,128)}), s32[4,4,2]{1,2,0:T(2,128)S(1)}, u32[]{:S(2)}, u32[]{:S(2)}) async-start(s32[4,4,2]{1,2,0:T(2,128)} %copy.13), calls=%async_computation | async-start | bytes 8192 | tf_op jit(solution)/shard_map/all_to_all | solution.py:748
  21.7 22.1 %collective-permute-start.5 = (bf16[96,4096]{1,0:T(8,128)(2,1)}, bf16[96,4096]{1,0:T(8,128)(2,1)}, u32[]{:S(2)}, u32[]{:S(2)}) collective-permute-start(bf16[96,4096]{1,0:T(8,128)(2,1)} %get-tuple-element.47.refs_4_), channel_id=1, source_target_pairs={{0,2},{2,0},{1,3},{3,1},{4,6},{6,4},{5,7},{7,5},{8,10},{10,8},{9,1... | collective-permute-start | bytes 2359304 | tf_op jit(solution)/shard_map/ppermute | solution.py:740
  29.3 28.6 %all-to-all-start.1 = ((bf16[4,8,64,256]{3,2,1,0:T(8,128)(2,1)}), bf16[4,8,64,256]{3,2,1,0:T(8,128)(2,1)S(1)}, u32[]{:S(2)}, u32[]{:S(2)}) async-start(bf16[4,8,64,256]{3,2,1,0:T(8,128)(2,1)} %pick_pages.1.refs_0_), calls=%async_computation.1 | async-start | bytes 2097152 | tf_op jit(solution)/shard_map/all_to_all | solution.py:748
  32.8 1.1 copy-start.6
  43.0 0.8 copy-start.7
  43.8 2.5 %collective-permute-start.6 = (bf16[96,4096]{1,0:T(8,128)(2,1)}, bf16[96,4096]{1,0:T(8,128)(2,1)S(1)}, u32[]{:S(2)}, u32[]{:S(2)}) collective-permute-start(bf16[96,4096]{1,0:T(8,128)(2,1)} %collective-permute-done.5.near_ref), channel_id=1, source_target_pairs={{0,1},{1,0},{2,3},{3,2},{4,5},{5,4},{6,7},{7,6},{8,9},{9,8},{10,11... | collective-permute-start | bytes 2359304 | tf_op jit(solution)/shard_map/ppermute | solution.py:737
  43.8 24.2 %collective-permute-start.7 = (bf16[96,4096]{1,0:T(8,128)(2,1)S(1)}, bf16[96,4096]{1,0:T(8,128)(2,1)S(1)}, u32[]{:S(2)}, u32[]{:S(2)}) collective-permute-start(bf16[96,4096]{1,0:T(8,128)(2,1)S(1)} %get-tuple-element.46.refs_5_), channel_id=1, source_target_pairs={{0,2},{2,0},{1,3},{3,1},{4,6},{6,4},{5,7},{7,5},{8,10},{10,8},{9,1... | collective-permute-start | bytes 2359304 | tf_op jit(solution)/shard_map/ppermute | solution.py:740
  46.3 0.7 copy-start.12
  55.8 0.7 copy-start.9
  57.9 0.9 copy-start.10
  58.8 0.7 copy-start.13
  59.5 0.7 copy-start.16
  60.2 0.7 copy-start.18
  67.9 5.0 %copy-start.14 = (s32[3]{0:T(128)S(1)}, s32[3]{0:T(128)}, u32[]{:S(2)}) copy-start(s32[3]{0:T(128)} %copy-done.11) | copy-start | bytes 40
  67.9 2.4 %collective-permute-start.8 = (bf16[96,4096]{1,0:T(8,128)(2,1)S(1)}, bf16[96,4096]{1,0:T(8,128)(2,1)S(1)}, u32[]{:S(2)}, u32[]{:S(2)}) collective-permute-start(bf16[96,4096]{1,0:T(8,128)(2,1)S(1)} %get-tuple-element.34), channel_id=1, source_target_pairs={{0,1},{1,0},{2,3},{3,2},{4,5},{5,4},{6,7},{7,6},{8,9},{9,8},{10,11... | collective-permute-start | bytes 2359304 | tf_op jit(solution)/shard_map/ppermute | solution.py:737
  70.5 10.6 %copy-start.19 = (s32[1,4]{1,0:T(1,128)S(1)}, s32[1,4]{1,0:T(1,128)}, u32[]{:S(2)}) copy-start(s32[1,4]{1,0:T(1,128)} %sizes_ref.5) | copy-start | bytes 52
  70.5 2.4 %collective-permute-start.9 = (bf16[96,4096]{1,0:T(8,128)(2,1)S(1)}, bf16[96,4096]{1,0:T(8,128)(2,1)S(1)}, u32[]{:S(2)}, u32[]{:S(2)}) collective-permute-start(bf16[96,4096]{1,0:T(8,128)(2,1)S(1)} %collective-permute-done.7.near_ref), channel_id=1, source_target_pairs={{0,1},{1,0},{2,3},{3,2},{4,5},{5,4},{6,7},{7,6},{8,9},{9,8},{10,11... | collective-permute-start | bytes 2359304 | tf_op jit(solution)/shard_map/ppermute | solution.py:737
  70.7 19.8 %collective-permute-start.10 = (bf16[96,4096]{1,0:T(8,128)(2,1)S(1)}, bf16[96,4096]{1,0:T(8,128)(2,1)S(1)}, u32[]{:S(2)}, u32[]{:S(2)}) collective-permute-start(bf16[96,4096]{1,0:T(8,128)(2,1)S(1)} %add_pair.2), channel_id=1, source_target_pairs={{0,2},{2,0},{1,3},{3,1},{4,6},{6,4},{5,7},{7,5},{8,10},{10,8},{9,1... | collective-permute-start | bytes 2359304 | tf_op jit(solution)/shard_map/ppermute | solution.py:740
  90.5 2.3 %collective-permute-start.11 = (bf16[96,4096]{1,0:T(8,128)(2,1)S(1)}, bf16[96,4096]{1,0:T(8,128)(2,1)S(1)}, u32[]{:S(2)}, u32[]{:S(2)}) collective-permute-start(bf16[96,4096]{1,0:T(8,128)(2,1)S(1)} %get-tuple-element.40), channel_id=1, source_target_pairs={{0,1},{1,0},{2,3},{3,2},{4,5},{5,4},{6,7},{7,6},{8,9},{9,8},{10,11... | collective-permute-start | bytes 2359304 | tf_op jit(solution)/shard_map/ppermute | solution.py:737
  90.6 7.4 %collective-permute-start.12 = (bf16[384,256]{1,0:T(8,128)(2,1)S(1)}, bf16[384,256]{1,0:T(8,128)(2,1)S(1)}, u32[]{:S(2)}, u32[]{:S(2)}) collective-permute-start(bf16[384,256]{1,0:T(8,128)(2,1)S(1)} %constant_dynamic-update-slice_fusion.own_ref), channel_id=1, source_target_pairs={{0,2},{2,0},{1,3},{3,1},{4,6},{6,4},{5,7},{7,5},{8,10},{10,8},{9,1... | collective-permute-start | bytes 589832 | tf_op jit(solution)/shard_map/ppermute | solution.py:740
  92.8 8.4 %copy-start.4 = (bf16[4,4,64,256]{3,2,1,0:T(8,128)(2,1)S(1)}, bf16[4,4,64,256]{3,2,1,0:T(8,128)(2,1)}, u32[]{:S(2)}) copy-start(bf16[4,4,64,256]{3,2,1,0:T(8,128)(2,1)} %pool_ref.1) | copy-start | bytes 1572868
  92.8 8.4 %copy-start.20 = (s32[1,6]{1,0:T(1,128)S(1)}, s32[1,6]{1,0:T(1,128)}, u32[]{:S(2)}) copy-start(s32[1,6]{1,0:T(1,128)} %slot_ref.1) | copy-start | bytes 76
  93.0 9.7 %copy-start.8 = (bf16[192,1024]{1,0:T(8,128)(2,1)S(1)}, bf16[192,1024]{1,0:T(8,128)(2,1)}, u32[]{:S(2)}) copy-start(bf16[192,1024]{1,0:T(8,128)(2,1)} %copy-done.7) | copy-start | bytes 1179652
  93.1 9.7 %copy-start.17 = (s32[1,16,2]{1,2,0:T(2,128)S(1)}, s32[1,16,2]{1,2,0:T(2,128)}, u32[]{:S(2)}) copy-start(s32[1,16,2]{1,2,0:T(2,128)} %param.18) | copy-start | bytes 388
  98.0 19.2 %collective-permute-start.15 = (bf16[96,4096]{1,0:T(8,128)(2,1)S(1)}, bf16[96,4096]{1,0:T(8,128)(2,1)S(1)}, u32[]{:S(2)}, u32[]{:S(2)}) collective-permute-start(bf16[96,4096]{1,0:T(8,128)(2,1)S(1)} %add_pair.3.refs_4_), channel_id=1, source_target_pairs={{0,2},{2,0},{1,3},{3,1},{4,6},{6,4},{5,7},{7,5},{8,10},{10,8},{9,1... | collective-permute-start | bytes 2359304 | tf_op jit(solution)/shard_map/ppermute | solution.py:740
  99.4 1.8 %collective-permute-start.13 = (bf16[2,384,256]{2,1,0:T(8,128)(2,1)S(1)}, bf16[2,384,256]{2,1,0:T(8,128)(2,1)S(1)}, u32[]{:S(2)}, u32[]{:S(2)}) collective-permute-start(bf16[2,384,256]{2,1,0:T(8,128)(2,1)S(1)} %pad_maximum_fusion), channel_id=1, source_target_pairs={{0,1},{1,0},{2,3},{3,2},{4,5},{5,4},{6,7},{7,6},{8,9},{9,8},{10,11... | collective-permute-start | bytes 1179656 | tf_op jit(solution)/shard_map/ppermute | solution.py:737
  102.7 1.0 copy-start.2
  113.5 6.1 %copy-start.1 = (bf16[96,8192]{1,0:T(8,128)(2,1)S(1)}, bf16[96,8192]{1,0:T(8,128)(2,1)}, u32[]{:S(2)}) copy-start(bf16[96,8192]{1,0:T(8,128)(2,1)} %x_ref.3) | copy-start | bytes 4718596
  113.5 3.8 %collective-permute-start.14 = (bf16[96,8192]{1,0:T(8,128)(2,1)S(1)}, bf16[96,8192]{1,0:T(8,128)(2,1)S(1)}, u32[]{:S(2)}, u32[]{:S(2)}) collective-permute-start(bf16[96,8192]{1,0:T(8,128)(2,1)S(1)} %get-tuple-element.42), channel_id=1, source_target_pairs={{0,1},{1,0},{2,3},{3,2},{4,5},{5,4},{6,7},{7,6},{8,9},{9,8},{10,11... | collective-permute-start | bytes 4718600 | tf_op jit(solution)/shard_map/ppermute | solution.py:737
  117.2 2.4 %collective-permute-start.16 = (bf16[96,4096]{1,0:T(8,128)(2,1)S(1)}, bf16[96,4096]{1,0:T(8,128)(2,1)S(1)}, u32[]{:S(2)}, u32[]{:S(2)}) collective-permute-start(bf16[96,4096]{1,0:T(8,128)(2,1)S(1)} %get-tuple-element.44), channel_id=1, source_target_pairs={{0,1},{1,0},{2,3},{3,2},{4,5},{5,4},{6,7},{7,6},{8,9},{9,8},{10,11... | collective-permute-start | bytes 2359304 | tf_op jit(solution)/shard_map/ppermute | solution.py:737

commit v4 on v3

--- a/solution.py
+++ b/solution.py
@@ -28,6 +28,10 @@
 
 def params(mib):
     return pltpu.CompilerParams(vmem_limit_bytes=mib * MIB)
+
+
+def in_hbm(x):
+    return pltpu.with_memory_space_constraint(x, pltpu.HBM)
 
 
 def shape(dims, dtype=BF16):
@@ -252,16 +256,19 @@
     return pl.pallas_call(
         kernel,
         in_specs=[SMEM] + [VMEM] * 4 + [HBM] * 2 + [ANY] * waits,
-        out_specs=[VMEM, VMEM],
-        out_shape=[shape((total, q_width)), shape((total, kv_width))],
-        scratch_shapes=[
+        out_specs=[VMEM] * 4,
+        out_shape=[
+            shape((total, q_width)),
+            shape((total, kv_width)),
             pltpu.VMEM((steps, depth, q_width), BF16),
             pltpu.VMEM((steps, depth, kv_width), BF16),
+        ],
+        scratch_shapes=[
             pltpu.VMEM((total, q_width), F32),
             pltpu.VMEM((total, kv_width), F32),
             pltpu.SemaphoreType.DMA((2 * steps,)),
         ],
-        compiler_params=params(36),
+        compiler_params=params(10),
         cost_estimate=SMALL,
         name="project_local",
     )(place, *near, *far, w_query, w_keyvalue, *after)
@@ -283,6 +290,9 @@
 
 
 PAGES_STEP = 4
+REQUESTS = 4
+SIZES_AT = 4
+REQUESTS_AT = 8
 
 
 def attention_scratch(block_rows, heads, fresh_rows, slots):
@@ -296,7 +306,7 @@
     ]
 
 
-def attend_block(place_ref, sizes_ref, req_ref, q, first_row, fresh, pulled, scratch):
+def attend_block(place_ref, q, first_row, fresh, pulled, scratch):
     scores, total_ref, mixed_ref, cache, labels = scratch
     me = place_ref[0]
     block_rows, width = q.shape
@@ -309,8 +319,8 @@
     factor = math.log2(math.e) / math.sqrt(HEAD_DIM)
     bound = []
     running = jnp.int32(0)
-    for k in range(sizes_ref.shape[1]):
-        running = running + sizes_ref[0, k] * UNIT
+    for k in range(REQUESTS):
+        running = running + place_ref[SIZES_AT + k] * UNIT
         bound.append(running)
 
     def segment_of(position):
@@ -322,7 +332,7 @@
     for g in range(groups):
         for p in range(per):
             owner = g * tensors + jnp.bitwise_xor(me, p // slots)
-            label = req_ref[0, p % slots, owner]
+            label = place_ref[REQUESTS_AT + p % slots * groups * tensors + owner]
             wanted = (label >= lowest) & (label <= highest)
 
             @pl.when(wanted)
@@ -404,6 +414,33 @@
     return jnp.concatenate(
         [result[h * block_rows : (h + 1) * block_rows] for h in range(heads)], axis=1
     )
+
+
+def project_held(near, far, w_query, w_keyvalue, after):
+    rows, half = near.shape
+    steps, depth, q_width = w_query.shape
+    kv_width = w_keyvalue.shape[2]
+
+    def kernel(near_ref, far_ref, wq, wkv, *refs):
+        q_ref, kv_ref = refs[len(after) :]
+        for w, out in ((wq, q_ref), (wkv, kv_ref)):
+            total = None
+            for j in range(steps):
+                x_ref = near_ref if j < steps // 2 else far_ref
+                x = x_ref[:, (j % (steps // 2)) * depth : (j % (steps // 2) + 1) * depth]
+                part = jnp.dot(x, w[j], preferred_element_type=F32)
+                total = part if j == 0 else total + part
+            out[...] = total.astype(BF16)
+
+    return pl.pallas_call(
+        kernel,
+        in_specs=[VMEM] * 4 + [ANY] * len(after),
+        out_specs=[VMEM] * 2,
+        out_shape=[shape((rows, q_width)), shape((rows, kv_width))],
+        compiler_params=params(6),
+        cost_estimate=SMALL,
+        name="project_held",
+    )(near, far, w_query, w_keyvalue, *after)
 
 
 def project_far(place, near, far, w_query, w_keyvalue, after):
@@ -447,7 +484,7 @@
     )(place, near, far, w_query, w_keyvalue, *after)
 
 
-def attend_out(place, sizes, requests, query, fresh, bases, base, pulled, w_out):
+def attend_out(place, query, fresh, bases, base, pulled, w_out):
     rows, depth = query.shape
     width = w_out.shape[1]
     half = width // 2
@@ -459,9 +496,9 @@
     fresh_rows = -(-count // HEAD_DIM) * HEAD_DIM
     pad = fresh_rows - count
 
-    def kernel(place_ref, sizes_ref, req_ref, q_ref, pulled_ref, *refs):
+    def kernel(place_ref, q_ref, pulled_ref, *refs):
         fresh_refs = refs[:known]
-        wo, there_ref, stay_ref, wo_buf, sems = refs[known : known + 5]
+        wo, there_ref, stay_ref, wo_buf, q_buf, sems = refs[known : known + 6]
         core, side = place_ref[1], place_ref[2]
 
         def copy(j):
@@ -469,14 +506,16 @@
             start = pl.multiple_of(first * half + (j % out_steps) * wide, wide)
             return pltpu.make_async_copy(wo.at[:, pl.ds(start, wide)], wo_buf.at[j], sems.at[j])
 
+        q_copy = pltpu.make_async_copy(q_ref, q_buf, sems.at[2 * out_steps])
+        q_copy.start()
         for j in range(2 * out_steps):
             copy(j).start()
+        q_copy.wait()
         pairs = [(ref[...], at(side)) for ref, at in zip(fresh_refs, bases)]
         if pad:
             pairs.append((jnp.zeros((pad, 2 * HEAD_DIM), BF16), jnp.int32(1 << 20)))
         mixed = attend_block(
-            place_ref, sizes_ref, req_ref, q_ref[...], base(side), pairs, pulled_ref,
-            refs[known + 5 :],
+            place_ref, q_buf[...], base(side), pairs, pulled_ref, refs[known + 6 :]
         )
         for j in range(2 * out_steps):
             copy(j).wait()
@@ -488,21 +527,22 @@
 
     return pl.pallas_call(
         kernel,
-        in_specs=[SMEM] * 3 + [VMEM] * (2 + known) + [HBM],
+        in_specs=[SMEM, HBM] + [VMEM] * (1 + known) + [HBM],
         out_specs=[VMEM] * 2,
         out_shape=[shape((rows, half)), shape((rows, half))],
         scratch_shapes=[
             pltpu.VMEM((2 * out_steps, depth, wide), BF16),
-            pltpu.SemaphoreType.DMA((2 * out_steps,)),
+            pltpu.VMEM((rows, depth), BF16),
+            pltpu.SemaphoreType.DMA((2 * out_steps + 1,)),
         ]
         + attention_scratch(rows, heads, fresh_rows, pulled.shape[0] * pulled.shape[1]),
-        compiler_params=params(36),
+        compiler_params=params(30),
         cost_estimate=SMALL,
         name="attend_out",
-    )(place, sizes, requests, query, pulled, *fresh, w_out)
-
-
-def local_rows(place, sizes, requests, query, fresh, bases, base, pulled, w_out, after):
+    )(place, query, pulled, *fresh, w_out)
+
+
+def local_rows(place, query, fresh, bases, base, pulled, w_out, after):
     both, depth = query.shape
     rows = both // 2
     width = w_out.shape[1]
@@ -512,7 +552,7 @@
     known = len(fresh)
     fresh_rows = sum(f.shape[0] for f in fresh)
 
-    def kernel(place_ref, sizes_ref, req_ref, q_ref, pulled_ref, *refs):
+    def kernel(place_ref, q_ref, pulled_ref, *refs):
         fresh_refs = refs[:known]
         wo = refs[known]
         rest = refs[known + 1 + len(after) :]
@@ -531,8 +571,6 @@
             at = pl.ds(pl.multiple_of(b * rows, rows), rows)
             a_buf[at, :] = attend_block(
                 place_ref,
-                sizes_ref,
-                req_ref,
                 q_ref[at, :],
                 base(side) + b * rows,
                 [(ref[...], first(side)) for ref, first in zip(fresh_refs, bases)],
@@ -553,7 +591,7 @@
 
     return pl.pallas_call(
         kernel,
-        in_specs=[SMEM] * 3 + [VMEM] * (2 + known) + [HBM] + [ANY] * len(after),
+        in_specs=[SMEM] + [VMEM] * (2 + known) + [HBM] + [ANY] * len(after),
         out_specs=[VMEM, VMEM],
         out_shape=[shape((rows, width)), shape((rows, width))],
         scratch_shapes=[
@@ -565,7 +603,7 @@
         compiler_params=params(40),
         cost_estimate=SMALL,
         name="local_rows",
-    )(place, sizes, requests, query, pulled, *fresh, w_out, *after)
+    )(place, query, pulled, *fresh, w_out, *after)
 
 
 def add_pair(left, right):
@@ -731,7 +769,9 @@
     core = me % 2
     side = me // 2
     rows = tokens.shape[0]
-    place = jnp.stack([me, core, side]).astype(jnp.int32)
+    requests = jnp.swapaxes(page_request, 1, 2).reshape(-1)
+    place = jnp.stack([me, core, side, 0 * me]).astype(jnp.int32)
+    place = in_hbm(jnp.concatenate([place, suffix_pages[0], requests]))
 
     def over_core(x):
         return lax.ppermute(x, "tensor", [(0, 1), (1, 0), (2, 3), (3, 2)])
@@ -742,39 +782,38 @@
     def head_of(i):
         return lax.dynamic_index_in_dim(kv_pool, jnp.bitwise_xor(me, i), 1, keepdims=False)
 
-    requests = jnp.swapaxes(page_request, 1, 2)
-
     def to_replicas(x):
         return lax.all_to_all(x, "replica", split_axis=0, concat_axis=0, tiled=True)
 
     def tie(x, *others):
         return lax.optimization_barrier((x, *others))[0]
 
-    w_query = pltpu.with_memory_space_constraint(w_query, pltpu.HBM)
-    w_keyvalue = pltpu.with_memory_space_constraint(w_keyvalue, pltpu.HBM)
-    w_out = pltpu.with_memory_space_constraint(w_out, pltpu.HBM)
+    w_query, w_keyvalue, w_out = in_hbm(w_query), in_hbm(w_keyvalue), in_hbm(w_out)
     held = [head_of(0)]
     for i in range(1, 4):
         held.append(lax.ppermute(head_of(i), "tensor", [(t, t ^ i) for t in range(4)]))
+
+    numbers = page_index.reshape(replicas, -1, page_index.shape[2])
+    wanted = to_replicas(numbers)
 
     mine, other = norm_rows(place, tokens, gain)
     peer_near = over_core(other)
     peer_far = over_core(mine)
     is_first = core == 0
-    near_tied = tie(peer_near, held[2], held[3])
+    near_tied = tie(peer_near, held[2], held[3], wanted)
     first_half = jnp.where(is_first, mine, near_tied)
     second_half = jnp.where(is_first, near_tied, mine)
     first = over_y(first_half)
     second = over_y(second_half)
 
-    numbers = page_index.reshape(replicas, -1, page_index.shape[2])
-    wanted = to_replicas(tie(numbers, first_half))
     picked = pick_pages(place, wanted, held, [first_half, second_half])
     pulled = to_replicas(picked)
 
-    q_local, kv_local = project_local(
+    q_local, kv_local, wq, wkv = project_local(
         place, [mine, peer_near], [other, peer_far], w_query, w_keyvalue, [picked]
     )
+
+    q_local = in_hbm(q_local)
 
     def local_base(s):
         return s * (2 * rows)
@@ -786,9 +825,10 @@
         return (1 - s) * (2 * rows) + rows
 
     first = tie(first, q_local)
-    q_first, kv_first = project_far(place, first, over_core(first), w_query, w_keyvalue, [])
+    q_first, kv_first = project_held(first, over_core(first), wq, wkv, [])
+    q_first = in_hbm(q_first)
     there, stay = attend_out(
-        place, suffix_pages, requests, q_first, [kv_local, kv_first],
+        place, q_first, [kv_local, kv_first],
         [local_base, first_base], first_base, pulled, w_out,
     )
     there = tie(there, second)
@@ -800,7 +840,7 @@
     fresh = [kv_local, kv_first, kv_second]
     bases = [local_base, first_base, second_base]
     there, stay = attend_out(
-        place, suffix_pages, requests, q_second, fresh, bases, second_base, pulled, w_out
+        place, q_second, fresh, bases, second_base, pulled, w_out
     )
     there = tie(there, first_sum)
     second_mix = add_pair(stay, over_core(there))
@@ -814,7 +854,7 @@
     pool_out = write_pool(place, new_slot, kv_pool, new_own, core_new, y_new)
 
     own_part, peer_part = local_rows(
-        place, suffix_pages, requests, q_local, fresh, bases, local_base, pulled, w_out,
+        place, q_local, fresh, bases, local_base, pulled, w_out,
         [second_mix, pool_out],
     )
     peer_part = over_core(peer_part)

time: 123 us -> 128 us (1.041)
  Pallas kernels: 59.1 us -> 65.3 us
  starting transfers between devices: 20.2 us -> 18.1 us
    pallas_call x2 -> x1, Pallas kernels: 17.1 us -> 8.36 us  [project_far(): pl.pallas_call(kernel, in_specs=[SMEM] + [VMEM] * 2 + [HBM] * 2 + [ANY] *...]
    pallas_call x1, Pallas kernels: 1.9 us -> 10 us  [pick_pages(): pl.pallas_call(kernel, in_specs=[SMEM, SMEM] + [ANY] * (tensors + len(aft...]
    pallas_call x3 -> x4, Pallas kernels: 25 us -> 31.5 us  [the longest x2 15.7 us: attend_out(): pl.pallas_call(kernel, in_specs=[SMEM, HBM] + [VMEM] * (1 + known) + [HBM...]
    ppermute x3, waiting for transfers between devices: 6.08 us -> 0.01 us  [chip_pair_body(): lax.ppermute(head_of(i), 'tensor', [(t, t ^ i) for t in range(4)])]
    all_to_all x2, waiting for transfers between devices: 5.5 us -> 11.3 us  [to_replicas(): return lax.all_to_all(x, 'replica', split_axis=0, concat_axis=0, tiled=True)]
    unnamed x46 -> x22, local copies, waits for them, and re-layouts: 9.35 us -> 5.74 us
    ppermute x5, starting transfers between devices: 7.45 us -> 5.22 us  [over_y(): return lax.ppermute(x, 'tensor', [(0, 2), (2, 0), (1, 3), (3, 1)])]
    ppermute x9, waiting for transfers between devices: 8.65 us -> 10.5 us  [over_core(): return lax.ppermute(x, 'tensor', [(0, 1), (1, 0), (2, 3), (3, 2)])]
  transfers between devices with their start and end apart: 19 -> 19, of which waited for: 13 -> 11; matrix products, arithmetic and copies ran while one was open for 2% -> 3% of each run, Pallas kernels for 45% -> 48%
where the time goes in v4:
time: 128 us; the launch traced here: 127 us
  Pallas kernels  65.3 us (51%)
  waiting for transfers between devices  30.6 us (24%)
  starting transfers between devices  18.1 us (14%)
  local copies, waits for them, and re-layouts  11 us (9%)
    pallas_call x2, Pallas kernels, attend_out(): pl.pallas_call(kernel, in_specs=[SMEM, HBM] + [VMEM] * (1 + known) + [HBM...  15.7 us
    all_to_all x2, waiting for transfers between devices, to_replicas(): return lax.all_to_all(x, 'replica', split_axis=0, concat_axis=0, tiled=True)  11.3 us
    pallas_call x1, Pallas kernels, local_rows(): pl.pallas_call(kernel, in_specs=[SMEM] + [VMEM] * (2 + known) + [HBM] + [...  11.2 us
    ppermute x9, waiting for transfers between devices, over_core(): return lax.ppermute(x, 'tensor', [(0, 1), (1, 0), (2, 3), (3, 2)])  10.5 us
    pallas_call x1, Pallas kernels, pick_pages(): pl.pallas_call(kernel, in_specs=[SMEM, SMEM] + [ANY] * (tensors + len(aft...  10 us
    pallas_call x1, Pallas kernels, project_local(): pl.pallas_call(kernel, in_specs=[SMEM] + [VMEM] * 4 + [HBM] * 2 + [ANY] *...  9.01 us
    ppermute x5, waiting for transfers between devices, over_y(): return lax.ppermute(x, 'tensor', [(0, 2), (2, 0), (1, 3), (3, 1)])  8.76 us
    all_to_all x2, starting transfers between devices, to_replicas(): return lax.all_to_all(x, 'replica', split_axis=0, concat_axis=0, tiled=True)  8.52 us
  transfers between devices with their start and end apart: 19, of which 11 were waited for; matrix products, arithmetic and copies ran while one was open for 3% of the time, Pallas kernels for 48%

profile of v4, /device:TPU:0, one launch (start us, length us, event | category | flops | bytes accessed | tf_op | source)
XLA Modules:
  0.0 127.0 jit_solution(8494363332215038508)
XLA Ops:
  0.6 0.8 reshape.10
  1.4 1.3 %concatenate.6.place_ref = s32[40]{0:T(128)} concatenate(s32[1]{0:T(128)} %bitcast, s32[1]{0:T(128)} %bitcast.1, s32[1]{0:T(128)} %bitcast.2, s32[1]{0:T(128)} %constant.42.clone.1, s32[4]{0:T(128)} %bitcast.19, s32[32]{0:T(128)S(1)} %reshape.10), dimensions={0} | concatenate | bytes 320 | tf_op jit(solution)/shard_map/concatenate | solution.py:774
  2.7 1.4 %copy-done = bf16[96,8192]{1,0:T(8,128)(2,1)S(1)} copy-done((bf16[96,8192]{1,0:T(8,128)(2,1)S(1)}, bf16[96,8192]{1,0:T(8,128)(2,1)}, u32[]{:S(2)}) %copy-start) | copy-done | bytes 1572888
  4.1 0.7 copy-done.8
  4.8 1.8 %norm_rows.1 = (bf16[96,4096]{1,0:T(8,128)(2,1)S(1)}, bf16[96,4096]{1,0:T(8,128)(2,1)S(1)}) custom-call(s32[40]{0:T(128)} %concatenate.6.place_ref, bf16[96,8192]{1,0:T(8,128)(2,1)S(1)} %copy-done, bf16[8192]{0:T(1024)(128)(2,1)S(1)} %copy-done.8), custom_call_target="tpu_custom_call" | custom-call | flops 1024 | bytes 1024 | tf_op jit(solution)/shard_map/norm_rows/pallas_call | solution.py:208
  6.6 0.5 collective-permute-start
  7.1 1.8 %dynamic-slice_bitcast_fusion = (bf16[4,64,256]{2,1,0:T(8,128)(2,1)S(1)}, bf16[4,64,256]{2,1,0:T(8,128)(2,1)S(1)}, bf16[4,64,256]{2,1,0:T(8,128)(2,1)}, bf16[4,64,256]{2,1,0:T(8,128)(2,1)S(1)}) fusion(bf16[4,4,64,256]{3,2,1,0:T(8,128)(2,1)} %pool_ref.1, s32[]{:T(128)S(6)} %select_n.49, s32[]{:T(128)S(6)} %select_n.48, s32[]{:T(128)S(6)} %select_n.47, ...), kind=kLoop, calls=%fused_computation.5 | loop fusion | bytes 1048592 | tf_op jit(solution)/shard_map/jit(dynamic_index_in_dim)/squeeze | solution.py:783
  8.9 2.7 %collective-permute-start.3 = (bf16[4,64,256]{2,1,0:T(8,128)(2,1)S(1)}, bf16[4,64,256]{2,1,0:T(8,128)(2,1)S(1)}, u32[]{:S(2)}, u32[]{:S(2)}) collective-permute-start(bf16[4,64,256]{2,1,0:T(8,128)(2,1)S(1)} %get-tuple-element.51), channel_id=1, source_target_pairs={{0,2},{1,3},{2,0},{3,1},{4,6},{5,7},{6,4},{7,5},{8,10},{9,11},{10,... | collective-permute-start | bytes 393224 | tf_op jit(solution)/shard_map/ppermute | solution.py:794
  11.7 0.0 collective-permute-start.4
  11.7 0.8 reshape.11
  12.4 0.6 copy.13
  13.0 5.0 %all-to-all-start = ((s32[4,4,2]{1,2,0:T(2,128)}), s32[4,4,2]{1,2,0:T(2,128)S(1)}, u32[]{:S(2)}, u32[]{:S(2)}) async-start(s32[4,4,2]{1,2,0:T(2,128)} %copy.13), calls=%async_computation | async-start | bytes 8192 | tf_op jit(solution)/shard_map/all_to_all | solution.py:786
  18.0 0.2 collective-permute-start.2
  18.2 0.3 collective-permute-start.1
  18.5 5.1 %all-to-all-done = s32[4,4,2]{1,2,0:T(2,128)S(1)} async-done(((s32[4,4,2]{1,2,0:T(2,128)}), s32[4,4,2]{1,2,0:T(2,128)S(1)}, u32[]{:S(2)}, u32[]{:S(2)}) %all-to-all-start) | async-done | bytes 160 | tf_op jit(solution)/shard_map/all_to_all | solution.py:786
  23.6 0.0 collective-permute-done.3.refs_2_
  23.6 0.0 collective-permute-done.4.refs_3_
  23.6 0.0 collective-permute-done.near_peer
  23.6 1.0 broadcast_select_fusion.2
  24.6 1.5 %collective-permute-start.5 = (bf16[96,4096]{1,0:T(8,128)(2,1)}, bf16[96,4096]{1,0:T(8,128)(2,1)}, u32[]{:S(2)}, u32[]{:S(2)}) collective-permute-start(bf16[96,4096]{1,0:T(8,128)(2,1)} %get-tuple-element.49.refs_4_), channel_id=1, source_target_pairs={{0,2},{2,0},{1,3},{3,1},{4,6},{6,4},{5,7},{7,5},{8,10},{10,8},{9,1... | collective-permute-start | bytes 2359304 | tf_op jit(solution)/shard_map/ppermute | solution.py:780
  26.1 0.1 copy.14.want_ref
  26.2 0.0 collective-permute-done.2.refs_1_
  26.2 10.0 %pick_pages.1.refs_0_ = bf16[4,8,64,256]{3,2,1,0:T(8,128)(2,1)} custom-call(s32[40]{0:T(128)} %concatenate.6.place_ref, s32[4,4,2]{2,1,0:T(4,128)S(1)} %copy.14.want_ref, bf16[4,64,256]{2,1,0:T(8,128)(2,1)S(1)} %get-tuple-element.53.refs_0_, bf16[4,64,256]{2,1,0:T(8,128)(2,1)} %collective-permute-done.2.refs_1_, ...), custom_call_target="tpu_custom_call" | custom-call | flops 1024 | bytes 1024 | tf_op jit(solution)/shard_map/pick_pages/pallas_call | solution.py:690
  36.3 3.5 %all-to-all-start.1 = ((bf16[4,8,64,256]{3,2,1,0:T(8,128)(2,1)}), bf16[4,8,64,256]{3,2,1,0:T(8,128)(2,1)S(1)}, u32[]{:S(2)}, u32[]{:S(2)}) async-start(bf16[4,8,64,256]{3,2,1,0:T(8,128)(2,1)} %pick_pages.1.refs_0_), calls=%async_computation.1 | async-start | bytes 2097152 | tf_op jit(solution)/shard_map/all_to_all | solution.py:786
  39.8 1.1 copy-done.5
  40.9 9.0 %project_local.1 = (bf16[192,1024]{1,0:T(8,128)(2,1)S(1)}, bf16[192,256]{1,0:T(8,128)(2,1)S(1)}, bf16[8,1024,1024]{2,1,0:T(8,128)(2,1)S(1)}, bf16[8,1024,256]{2,1,0:T(8,128)(2,1)S(1)}) custom-call(s32[40]{0:T(128)} %concatenate.6.place_ref, bf16[96,4096]{1,0:T(8,128)(2,1)S(1)} %get-tuple-element.24.near_own, ...), custom_call_target="tpu_custom_call" | custom-call | flops 1024 | bytes 1024 | tf_op jit(solution)/shard_map/project_local/pallas_call | solution.py:256
  50.0 0.7 copy-done.6
  50.7 0.0 collective-permute-done.5.near_ref
  50.7 0.5 collective-permute-start.7
  51.2 2.0 %collective-permute-done.6.far_ref = bf16[96,4096]{1,0:T(8,128)(2,1)S(1)} collective-permute-done((bf16[96,4096]{1,0:T(8,128)(2,1)}, bf16[96,4096]{1,0:T(8,128)(2,1)S(1)}, u32[]{:S(2)}, u32[]{:S(2)}) %collective-permute-start.6) | collective-permute-done | bytes 786464 | tf_op jit(solution)/shard_map/ppermute | solution.py:777
  53.2 4.6 %project_held.1 = (bf16[96,1024]{1,0:T(8,128)(2,1)S(1)}, bf16[96,256]{1,0:T(8,128)(2,1)S(1)}) custom-call(bf16[96,4096]{1,0:T(8,128)(2,1)} %collective-permute-done.5.near_ref, bf16[96,4096]{1,0:T(8,128)(2,1)S(1)} %collective-permute-done.6.far_ref, bf16[8,1024,1024]{2,1,0:T(8,128)(2,1)S(1)} %get-tuple-element.30.wq, ...), custom_call_target="tpu_custom_call" | custom-call | flops 1024 | bytes 1024 | tf_op jit(solution)/shard_map/project_held/pallas_call | solution.py:435
  57.8 0.0 copy-start.7
  57.8 0.7 copy-done.7
  58.5 6.2 %all-to-all-done.1.pulled_ref = bf16[4,8,64,256]{3,2,1,0:T(8,128)(2,1)S(1)} async-done(((bf16[4,8,64,256]{3,2,1,0:T(8,128)(2,1)}), bf16[4,8,64,256]{3,2,1,0:T(8,128)(2,1)S(1)}, u32[]{:S(2)}, u32[]{:S(2)}) %all-to-all-start.1) | async-done | bytes 1048608 | tf_op jit(solution)/shard_map/all_to_all | solution.py:786
  64.7 8.1 %attend_out.2 = (bf16[96,4096]{1,0:T(8,128)(2,1)S(1)}, bf16[96,4096]{1,0:T(8,128)(2,1)S(1)}) custom-call(s32[40]{0:T(128)} %concatenate.6.place_ref, bf16[96,1024]{1,0:T(8,128)(2,1)} %copy-done.7, bf16[4,8,64,256]{3,2,1,0:T(8,128)(2,1)S(1)} %all-to-all-done.1.pulled_ref, bf16[192,256]{1,0:T(8,128)(2,1)S(1)} %get-tuple-element.28.refs_0_, ...), custom_call_target="tpu_custom_call" | custom-call | flops 1024 | bytes 1024 | tf_op jit(solution)/shard_map/attend_out/pallas_call | solution.py:528
  72.8 0.1 collective-permute-start.8
  72.9 2.3 %collective-permute-done.8.right_ref = bf16[96,4096]{1,0:T(8,128)(2,1)S(1)} collective-permute-done((bf16[96,4096]{1,0:T(8,128)(2,1)S(1)}, bf16[96,4096]{1,0:T(8,128)(2,1)S(1)}, u32[]{:S(2)}, u32[]{:S(2)}) %collective-permute-start.8) | collective-permute-done | bytes 786464 | tf_op jit(solution)/shard_map/ppermute | solution.py:777
  75.1 0.2 add_pair.2
  75.4 0.2 collective-permute-start.9
  75.6 1.1 collective-permute-start.10
  76.6 1.1 collective-permute-done.9.far_ref
  77.7 8.4 %project_far.1 = (bf16[96,1024]{1,0:T(8,128)(2,1)S(1)}, bf16[96,256]{1,0:T(8,128)(2,1)S(1)}) custom-call(s32[40]{0:T(128)} %concatenate.6.place_ref, bf16[96,4096]{1,0:T(8,128)(2,1)S(1)} %collective-permute-done.7.near_ref, bf16[96,4096]{1,0:T(8,128)(2,1)S(1)} %collective-permute-done.9.far_ref, bf16[8192,1024]{1,0:T(8,128)(2,1)} %wq.3, bf16[8192,256]{1,0:T(8,128)(2,1)} %wkv.3), custom_call_target="tpu_custom_call" | custom-call | flops 1024 | bytes 1024 | tf_op jit(solution)/shard_map/project_far/pallas_call | solution.py:471
  86.1 0.0 copy-start.3
  86.1 0.0 copy-start.9
  86.1 7.6 %attend_out.3 = (bf16[96,4096]{1,0:T(8,128)(2,1)S(1)}, bf16[96,4096]{1,0:T(8,128)(2,1)S(1)}) custom-call(s32[40]{0:T(128)} %concatenate.6.place_ref, bf16[96,1024]{1,0:T(8,128)(2,1)S(1)} %get-tuple-element.39.q_ref, bf16[4,8,64,256]{3,2,1,0:T(8,128)(2,1)S(1)} %all-to-all-done.1.pulled_ref, bf16[192,256]{1,0:T(8,128)(2,1)S(1)} %get-tuple-element.28.refs_0_, ...), custom_call_target="tpu_custom_call" | custom-call | flops 1024 | bytes 1024 | tf_op jit(solution)/shard_map/attend_out/pallas_call | solution.py:528
  93.7 1.7 %collective-permute-done.10 = bf16[96,4096]{1,0:T(8,128)(2,1)S(1)} collective-permute-done((bf16[96,4096]{1,0:T(8,128)(2,1)S(1)}, bf16[96,4096]{1,0:T(8,128)(2,1)S(1)}, u32[]{:S(2)}, u32[]{:S(2)}) %collective-permute-start.10) | collective-permute-done | bytes 786464 | tf_op jit(solution)/shard_map/ppermute | solution.py:780
  95.4 1.1 collective-permute-start.12
  96.5 1.1 collective-permute-done.11.right_ref
  97.7 0.2 add_pair.3.refs_4_
  97.9 4.9 %collective-permute-done.12.y_ref = bf16[384,256]{1,0:T(8,128)(2,1)S(1)} collective-permute-done((bf16[384,256]{1,0:T(8,128)(2,1)S(1)}, bf16[384,256]{1,0:T(8,128)(2,1)S(1)}, u32[]{:S(2)}, u32[]{:S(2)}) %collective-permute-start.12) | collective-permute-done | bytes 196640 | tf_op jit(solution)/shard_map/ppermute | solution.py:780
  102.8 1.0 collective-permute-start.15
  103.9 0.1 collective-permute-start.13
  104.0 1.7 %collective-permute-done.13.core_ref = bf16[2,384,256]{2,1,0:T(8,128)(2,1)S(1)} collective-permute-done((bf16[2,384,256]{2,1,0:T(8,128)(2,1)S(1)}, bf16[2,384,256]{2,1,0:T(8,128)(2,1)S(1)}, u32[]{:S(2)}, u32[]{:S(2)}) %collective-permute-start.13) | collective-permute-done | bytes 393248 | tf_op jit(solution)/shard_map/ppermute | solution.py:777
  105.7 1.6 %write_pool.1.refs_5_ = bf16[4,4,64,256]{3,2,1,0:T(8,128)(2,1)} custom-call(s32[40]{0:T(128)} %concatenate.6.place_ref, s32[1,6]{1,0:T(1,128)S(1)} %copy-done.9, bf16[4,4,64,256]{3,2,1,0:T(8,128)(2,1)S(1)} %copy-done.3, bf16[384,256]{1,0:T(8,128)(2,1)S(1)} %constant_dynamic-update-slice_fusion.own_ref, ...), custom_call_target="tpu_custom_call" | custom-call | flops 1024 | bytes 1024 | tf_op jit(solution)/shard_map/write_pool/pallas_call | solution.py:743
  107.3 0.0 copy-start.2
  107.3 1.0 copy-done.2
  108.3 11.2 %local_rows.1 = (bf16[96,8192]{1,0:T(8,128)(2,1)S(1)}, bf16[96,8192]{1,0:T(8,128)(2,1)S(1)}) custom-call(s32[40]{0:T(128)} %concatenate.6.place_ref, bf16[192,1024]{1,0:T(8,128)(2,1)} %copy-done.6, bf16[4,8,64,256]{3,2,1,0:T(8,128)(2,1)S(1)} %all-to-all-done.1.pulled_ref, bf16[192,256]{1,0:T(8,128)(2,1)S(1)} %get-tuple-element.28.refs_0_, ...), custom_call_target="tpu_custom_call" | custom-call | flops 1024 | bytes 1024 | tf_op jit(solution)/shard_map/local_rows/pallas_call | solution.py:592
  119.6 0.0 copy-start.1
  119.6 0.2 collective-permute-start.14
  119.8 2.2 %collective-permute-done.15 = bf16[96,4096]{1,0:T(8,128)(2,1)S(1)} collective-permute-done((bf16[96,4096]{1,0:T(8,128)(2,1)S(1)}, bf16[96,4096]{1,0:T(8,128)(2,1)S(1)}, u32[]{:S(2)}, u32[]{:S(2)}) %collective-permute-start.15) | collective-permute-done | bytes 786464 | tf_op jit(solution)/shard_map/ppermute | solution.py:780
  122.0 0.1 broadcast_select_fusion
  122.1 0.1 collective-permute-start.16
  122.2 2.3 %collective-permute-done.16.far_ref = bf16[96,4096]{1,0:T(8,128)(2,1)S(1)} collective-permute-done((bf16[96,4096]{1,0:T(8,128)(2,1)S(1)}, bf16[96,4096]{1,0:T(8,128)(2,1)S(1)}, u32[]{:S(2)}, u32[]{:S(2)}) %collective-permute-start.16) | collective-permute-done | bytes 786464 | tf_op jit(solution)/shard_map/ppermute | solution.py:777
  124.4 2.6 %finish.1 = bf16[96,8192]{1,0:T(8,128)(2,1)} custom-call(s32[40]{0:T(128)} %concatenate.6.place_ref, bf16[96,8192]{1,0:T(8,128)(2,1)S(1)} %copy-done.1, bf16[96,8192]{1,0:T(8,128)(2,1)S(1)} %get-tuple-element.43.own_ref, bf16[96,8192]{1,0:T(8,128)(2,1)S(1)} %collective-permute-done.14.peer_ref, bf16[96,4096]{1,0:T(8,128)(2,1)S(1)} %get-tuple-element.47.near_ref, ...), custom_call_target="tpu_custom_call" | custom-call | flops 1024 | bytes 1024 | tf_op jit(solution)/shard_map/finish/pallas_call | solution.py:653
  (18 shorter events, 0.1 us)
Async XLA Ops:
  2.7 1.4 %copy-start = (bf16[96,8192]{1,0:T(8,128)(2,1)S(1)}, bf16[96,8192]{1,0:T(8,128)(2,1)}, u32[]{:S(2)}) copy-start(bf16[96,8192]{1,0:T(8,128)(2,1)} %x_ref.3) | copy-start | bytes 4718596
  4.1 0.7 copy-start.8
  6.6 29.6 %copy-start.4 = (bf16[96,4096]{1,0:T(8,128)(2,1)}, bf16[96,4096]{1,0:T(8,128)(2,1)S(1)}, u32[]{:S(2)}) copy-start(bf16[96,4096]{1,0:T(8,128)(2,1)S(1)} %get-tuple-element.25.far_own) | copy-start | bytes 2359300
  6.6 17.0 %collective-permute-start = (bf16[96,4096]{1,0:T(8,128)(2,1)S(1)}, bf16[96,4096]{1,0:T(8,128)(2,1)S(1)}, u32[]{:S(2)}, u32[]{:S(2)}) collective-permute-start(bf16[96,4096]{1,0:T(8,128)(2,1)S(1)} %get-tuple-element.25.far_own), channel_id=1, source_target_pairs={{0,1},{1,0},{2,3},{3,2},{4,5},{5,4},{6,7},{7,6},{8,9},{9,8},{10,11... | collective-permute-start | bytes 2359304 | tf_op jit(solution)/shard_map/ppermute | solution.py:777
  8.9 14.7 %collective-permute-start.3 = (bf16[4,64,256]{2,1,0:T(8,128)(2,1)S(1)}, bf16[4,64,256]{2,1,0:T(8,128)(2,1)S(1)}, u32[]{:S(2)}, u32[]{:S(2)}) collective-permute-start(bf16[4,64,256]{2,1,0:T(8,128)(2,1)S(1)} %get-tuple-element.51), channel_id=1, source_target_pairs={{0,2},{1,3},{2,0},{3,1},{4,6},{5,7},{6,4},{7,5},{8,10},{9,11},{10,... | collective-permute-start | bytes 393224 | tf_op jit(solution)/shard_map/ppermute | solution.py:794
  11.7 11.9 %collective-permute-start.4 = (bf16[4,64,256]{2,1,0:T(8,128)(2,1)S(1)}, bf16[4,64,256]{2,1,0:T(8,128)(2,1)S(1)}, u32[]{:S(2)}, u32[]{:S(2)}) collective-permute-start(bf16[4,64,256]{2,1,0:T(8,128)(2,1)S(1)} %get-tuple-element.50), channel_id=1, source_target_pairs={{0,3},{1,2},{2,1},{3,0},{4,7},{5,6},{6,5},{7,4},{8,11},{9,10},{10,... | collective-permute-start | bytes 393224 | tf_op jit(solution)/shard_map/ppermute | solution.py:794
  13.0 10.6 %all-to-all-start = ((s32[4,4,2]{1,2,0:T(2,128)}), s32[4,4,2]{1,2,0:T(2,128)S(1)}, u32[]{:S(2)}, u32[]{:S(2)}) async-start(s32[4,4,2]{1,2,0:T(2,128)} %copy.13), calls=%async_computation | async-start | bytes 8192 | tf_op jit(solution)/shard_map/all_to_all | solution.py:786
  18.0 8.2 %collective-permute-start.2 = (bf16[4,64,256]{2,1,0:T(8,128)(2,1)}, bf16[4,64,256]{2,1,0:T(8,128)(2,1)}, u32[]{:S(2)}, u32[]{:S(2)}) collective-permute-start(bf16[4,64,256]{2,1,0:T(8,128)(2,1)} %get-tuple-element.52), channel_id=1, source_target_pairs={{0,1},{1,0},{2,3},{3,2},{4,5},{5,4},{6,7},{7,6},{8,9},{9,8},{10,11... | collective-permute-start | bytes 393224 | tf_op jit(solution)/shard_map/ppermute | solution.py:794
  18.2 21.6 %collective-permute-start.1 = (bf16[96,4096]{1,0:T(8,128)(2,1)S(1)}, bf16[96,4096]{1,0:T(8,128)(2,1)}, u32[]{:S(2)}, u32[]{:S(2)}) collective-permute-start(bf16[96,4096]{1,0:T(8,128)(2,1)S(1)} %get-tuple-element.24.near_own), channel_id=1, source_target_pairs={{0,1},{1,0},{2,3},{3,2},{4,5},{5,4},{6,7},{7,6},{8,9},{9,8},{10,11... | collective-permute-start | bytes 2359304 | tf_op jit(solution)/shard_map/ppermute | solution.py:777
  24.6 26.1 %collective-permute-start.5 = (bf16[96,4096]{1,0:T(8,128)(2,1)}, bf16[96,4096]{1,0:T(8,128)(2,1)}, u32[]{:S(2)}, u32[]{:S(2)}) collective-permute-start(bf16[96,4096]{1,0:T(8,128)(2,1)} %get-tuple-element.49.refs_4_), channel_id=1, source_target_pairs={{0,2},{2,0},{1,3},{3,1},{4,6},{6,4},{5,7},{7,5},{8,10},{10,8},{9,1... | collective-permute-start | bytes 2359304 | tf_op jit(solution)/shard_map/ppermute | solution.py:780
  36.3 28.5 %all-to-all-start.1 = ((bf16[4,8,64,256]{3,2,1,0:T(8,128)(2,1)}), bf16[4,8,64,256]{3,2,1,0:T(8,128)(2,1)S(1)}, u32[]{:S(2)}, u32[]{:S(2)}) async-start(bf16[4,8,64,256]{3,2,1,0:T(8,128)(2,1)} %pick_pages.1.refs_0_), calls=%async_computation.1 | async-start | bytes 2097152 | tf_op jit(solution)/shard_map/all_to_all | solution.py:786
  39.8 1.1 copy-start.5
  50.0 0.8 copy-start.6
  50.7 2.5 %collective-permute-start.6 = (bf16[96,4096]{1,0:T(8,128)(2,1)}, bf16[96,4096]{1,0:T(8,128)(2,1)S(1)}, u32[]{:S(2)}, u32[]{:S(2)}) collective-permute-start(bf16[96,4096]{1,0:T(8,128)(2,1)} %collective-permute-done.5.near_ref), channel_id=1, source_target_pairs={{0,1},{1,0},{2,3},{3,2},{4,5},{5,4},{6,7},{7,6},{8,9},{9,8},{10,11... | collective-permute-start | bytes 2359304 | tf_op jit(solution)/shard_map/ppermute | solution.py:777
  50.7 22.1 %collective-permute-start.7 = (bf16[96,4096]{1,0:T(8,128)(2,1)S(1)}, bf16[96,4096]{1,0:T(8,128)(2,1)S(1)}, u32[]{:S(2)}, u32[]{:S(2)}) collective-permute-start(bf16[96,4096]{1,0:T(8,128)(2,1)S(1)} %get-tuple-element.48.refs_5_), channel_id=1, source_target_pairs={{0,2},{2,0},{1,3},{3,1},{4,6},{6,4},{5,7},{7,5},{8,10},{10,8},{9,1... | collective-permute-start | bytes 2359304 | tf_op jit(solution)/shard_map/ppermute | solution.py:780
  57.8 0.7 copy-start.7
  72.8 2.4 %collective-permute-start.8 = (bf16[96,4096]{1,0:T(8,128)(2,1)S(1)}, bf16[96,4096]{1,0:T(8,128)(2,1)S(1)}, u32[]{:S(2)}, u32[]{:S(2)}) collective-permute-start(bf16[96,4096]{1,0:T(8,128)(2,1)S(1)} %get-tuple-element.36), channel_id=1, source_target_pairs={{0,1},{1,0},{2,3},{3,2},{4,5},{5,4},{6,7},{7,6},{8,9},{9,8},{10,11... | collective-permute-start | bytes 2359304 | tf_op jit(solution)/shard_map/ppermute | solution.py:777
  75.4 2.4 %collective-permute-start.9 = (bf16[96,4096]{1,0:T(8,128)(2,1)S(1)}, bf16[96,4096]{1,0:T(8,128)(2,1)S(1)}, u32[]{:S(2)}, u32[]{:S(2)}) collective-permute-start(bf16[96,4096]{1,0:T(8,128)(2,1)S(1)} %collective-permute-done.7.near_ref), channel_id=1, source_target_pairs={{0,1},{1,0},{2,3},{3,2},{4,5},{5,4},{6,7},{7,6},{8,9},{9,8},{10,11... | collective-permute-start | bytes 2359304 | tf_op jit(solution)/shard_map/ppermute | solution.py:777
  75.6 19.8 %collective-permute-start.10 = (bf16[96,4096]{1,0:T(8,128)(2,1)S(1)}, bf16[96,4096]{1,0:T(8,128)(2,1)S(1)}, u32[]{:S(2)}, u32[]{:S(2)}) collective-permute-start(bf16[96,4096]{1,0:T(8,128)(2,1)S(1)} %add_pair.2), channel_id=1, source_target_pairs={{0,2},{2,0},{1,3},{3,1},{4,6},{6,4},{5,7},{7,5},{8,10},{10,8},{9,1... | collective-permute-start | bytes 2359304 | tf_op jit(solution)/shard_map/ppermute | solution.py:780
  86.1 19.6 %copy-start.3 = (bf16[4,4,64,256]{3,2,1,0:T(8,128)(2,1)S(1)}, bf16[4,4,64,256]{3,2,1,0:T(8,128)(2,1)}, u32[]{:S(2)}) copy-start(bf16[4,4,64,256]{3,2,1,0:T(8,128)(2,1)} %pool_ref.1) | copy-start | bytes 1572868
  86.1 19.6 %copy-start.9 = (s32[1,6]{1,0:T(1,128)S(1)}, s32[1,6]{1,0:T(1,128)}, u32[]{:S(2)}) copy-start(s32[1,6]{1,0:T(1,128)} %slot_ref.1) | copy-start | bytes 76
  95.4 2.3 %collective-permute-start.11 = (bf16[96,4096]{1,0:T(8,128)(2,1)S(1)}, bf16[96,4096]{1,0:T(8,128)(2,1)S(1)}, u32[]{:S(2)}, u32[]{:S(2)}) collective-permute-start(bf16[96,4096]{1,0:T(8,128)(2,1)S(1)} %get-tuple-element.42), channel_id=1, source_target_pairs={{0,1},{1,0},{2,3},{3,2},{4,5},{5,4},{6,7},{7,6},{8,9},{9,8},{10,11... | collective-permute-start | bytes 2359304 | tf_op jit(solution)/shard_map/ppermute | solution.py:777
  95.4 7.4 %collective-permute-start.12 = (bf16[384,256]{1,0:T(8,128)(2,1)S(1)}, bf16[384,256]{1,0:T(8,128)(2,1)S(1)}, u32[]{:S(2)}, u32[]{:S(2)}) collective-permute-start(bf16[384,256]{1,0:T(8,128)(2,1)S(1)} %constant_dynamic-update-slice_fusion.own_ref), channel_id=1, source_target_pairs={{0,2},{2,0},{1,3},{3,1},{4,6},{6,4},{5,7},{7,5},{8,10},{10,8},{9,1... | collective-permute-start | bytes 589832 | tf_op jit(solution)/shard_map/ppermute | solution.py:780
  102.8 19.2 %collective-permute-start.15 = (bf16[96,4096]{1,0:T(8,128)(2,1)S(1)}, bf16[96,4096]{1,0:T(8,128)(2,1)S(1)}, u32[]{:S(2)}, u32[]{:S(2)}) collective-permute-start(bf16[96,4096]{1,0:T(8,128)(2,1)S(1)} %add_pair.3.refs_4_), channel_id=1, source_target_pairs={{0,2},{2,0},{1,3},{3,1},{4,6},{6,4},{5,7},{7,5},{8,10},{10,8},{9,1... | collective-permute-start | bytes 2359304 | tf_op jit(solution)/shard_map/ppermute | solution.py:780
  103.9 1.8 %collective-permute-start.13 = (bf16[2,384,256]{2,1,0:T(8,128)(2,1)S(1)}, bf16[2,384,256]{2,1,0:T(8,128)(2,1)S(1)}, u32[]{:S(2)}, u32[]{:S(2)}) collective-permute-start(bf16[2,384,256]{2,1,0:T(8,128)(2,1)S(1)} %pad_maximum_fusion), channel_id=1, source_target_pairs={{0,1},{1,0},{2,3},{3,2},{4,5},{5,4},{6,7},{7,6},{8,9},{9,8},{10,11... | collective-permute-start | bytes 1179656 | tf_op jit(solution)/shard_map/ppermute | solution.py:777
  107.3 1.0 copy-start.2
  119.6 4.9 %copy-start.1 = (bf16[96,8192]{1,0:T(8,128)(2,1)S(1)}, bf16[96,8192]{1,0:T(8,128)(2,1)}, u32[]{:S(2)}) copy-start(bf16[96,8192]{1,0:T(8,128)(2,1)} %x_ref.3) | copy-start | bytes 4718596
  119.6 4.8 %collective-permute-start.14 = (bf16[96,8192]{1,0:T(8,128)(2,1)S(1)}, bf16[96,8192]{1,0:T(8,128)(2,1)S(1)}, u32[]{:S(2)}, u32[]{:S(2)}) collective-permute-start(bf16[96,8192]{1,0:T(8,128)(2,1)S(1)} %get-tuple-element.44), channel_id=1, source_target_pairs={{0,1},{1,0},{2,3},{3,2},{4,5},{5,4},{6,7},{7,6},{8,9},{9,8},{10,11... | collective-permute-start | bytes 4718600 | tf_op jit(solution)/shard_map/ppermute | solution.py:777
  122.1 2.4 %collective-permute-start.16 = (bf16[96,4096]{1,0:T(8,128)(2,1)S(1)}, bf16[96,4096]{1,0:T(8,128)(2,1)S(1)}, u32[]{:S(2)}, u32[]{:S(2)}) collective-permute-start(bf16[96,4096]{1,0:T(8,128)(2,1)S(1)} %get-tuple-element.46), channel_id=1, source_target_pairs={{0,1},{1,0},{2,3},{3,2},{4,5},{5,4},{6,7},{7,6},{8,9},{9,8},{10,11... | collective-permute-start | bytes 2359304 | tf_op jit(solution)/shard_map/ppermute | solution.py:777

commit v5 on v4

--- a/solution.py
+++ b/solution.py
@@ -180,40 +180,71 @@
     return (layer_out, pool_out)
 
 
-def norm_rows(place, tokens, gain):
+def prepare(place, tokens, gain, kv_pool):
     rows, width = tokens.shape
     half = width // 2
-    step = 16
-
-    def kernel(place_ref, x_ref, g_ref, mine_ref, other_ref):
-        core = place_ref[1]
+    step = 32
+    pages, heads = kv_pool.shape[:2]
+    blocks = rows // step
+
+    def kernel(place_ref, x, g, pool, mine_ref, other_ref, *refs):
+        held, (x_buf, g_buf, sems) = refs[:heads], refs[heads:]
+        me, core = place_ref[0], place_ref[1]
+
+        def head_copy(i):
+            return pltpu.make_async_copy(
+                pool.at[:, jnp.bitwise_xor(me, i)], held[i], sems.at[blocks + 1 + i]
+            )
+
+        def row_copy(b):
+            at = pl.ds(b * step, step)
+            return pltpu.make_async_copy(x.at[at], x_buf.at[at], sems.at[b])
+
+        gain_copy = pltpu.make_async_copy(g, g_buf, sems.at[blocks])
+        row_copy(0).start()
+        gain_copy.start()
+        for b in range(1, blocks):
+            row_copy(b).start()
+        for i in range(heads):
+            head_copy(i).start()
         near = pl.multiple_of(core * half, half)
         far = pl.multiple_of((1 - core) * half, half)
-
-        def block(i, carry):
-            at = pl.ds(pl.multiple_of(i * step, step), step)
-            total = jnp.zeros((step, 1), F32)
-            for part in range(2):
-                values = x_ref[at, part * half : (part + 1) * half].astype(F32)
-                total += jnp.sum(values * values, axis=1, keepdims=True)
-            inverse = lax.rsqrt(total * (1.0 / width) + EPSILON)
-            for start, out in ((near, mine_ref), (far, other_ref)):
-                cols = pl.ds(start, half)
-                values = x_ref[at, cols].astype(F32)
-                out[at, :] = (values * inverse * g_ref[cols].astype(F32)[None, :]).astype(BF16)
-            return carry
-
-        lax.fori_loop(0, rows // step, block, 0)
+        for b in range(blocks):
+            row_copy(b).wait()
+            if b == 0:
+                gain_copy.wait()
+
+            def block(i, carry):
+                at = pl.ds(pl.multiple_of(b * step + i * 16, 16), 16)
+                total = jnp.zeros((16, 1), F32)
+                for part in range(2):
+                    values = x_buf[at, part * half : (part + 1) * half].astype(F32)
+                    total += jnp.sum(values * values, axis=1, keepdims=True)
+                inverse = lax.rsqrt(total * (1.0 / width) + EPSILON)
+                for start, out in ((near, mine_ref), (far, other_ref)):
+                    cols = pl.ds(start, half)
+                    values = x_buf[at, cols].astype(F32)
+                    out[at, :] = (values * inverse * g_buf[cols].astype(F32)[None, :]).astype(BF16)
+                return carry
+
+            lax.fori_loop(0, step // 16, block, 0)
+        for i in range(heads):
+            head_copy(i).wait()
 
     return pl.pallas_call(
         kernel,
-        in_specs=[SMEM, VMEM, VMEM],
-        out_specs=[VMEM, VMEM],
-        out_shape=[shape((rows, half)), shape((rows, half))],
+        in_specs=[SMEM] + [HBM] * 3,
+        out_specs=[VMEM, VMEM] + [HBM] * heads,
+        out_shape=[shape((rows, half))] * 2 + [shape((pages,) + kv_pool.shape[2:])] * heads,
+        scratch_shapes=[
+            pltpu.VMEM((rows, width), BF16),
+            pltpu.VMEM((width,), BF16),
+            pltpu.SemaphoreType.DMA((blocks + 1 + heads,)),
+        ],
         compiler_params=params(16),
         cost_estimate=SMALL,
-        name="norm_rows",
-    )(place, tokens, gain)
+        name="prepare",
+    )(place, tokens, gain, kv_pool)
 
 
 def project_local(place, near, far, w_query, w_keyvalue, after):
@@ -662,24 +693,28 @@
 
 
 def pick_pages(place, wanted, held, after):
-    replicas, tensors, slots = wanted.shape
+    replicas = len(wanted)
+    slots = wanted[0].shape[2]
+    tensors = len(held)
     _, page, width = held[0].shape
     total = tensors * slots
 
-    def kernel(place_ref, want_ref, *refs):
-        sources = refs[:tensors]
-        out_ref, sems = refs[tensors + len(after) :]
-        me = place_ref[0]
+    def kernel(place_ref, *refs):
+        wants, sources = refs[:replicas], refs[replicas : replicas + tensors]
+        out_ref, sems = refs[replicas + tensors + len(after) :]
+        me, rep = place_ref[0], place_ref[3]
 
         def copies():
-            for r in range(replicas):
+            for k in range(replicas):
+                asker = lax.rem(rep + k, replicas)
                 for i in range(tensors):
+                    owner = rep * tensors + jnp.bitwise_xor(me, i)
                     for s in range(slots):
                         at = i * slots + s
                         yield pltpu.make_async_copy(
-                            sources[i].at[want_ref[r, jnp.bitwise_xor(me, i), s]],
-                            out_ref.at[r, at],
-                            sems.at[r * total + at],
+                            sources[i].at[wants[k][0, owner, s]],
+                            out_ref.at[asker, at],
+                            sems.at[k * total + at],
                         )
 
         for copy in copies():
@@ -689,14 +724,14 @@
 
     return pl.pallas_call(
         kernel,
-        in_specs=[SMEM, SMEM] + [ANY] * (tensors + len(after)),
+        in_specs=[SMEM] * (1 + replicas) + [ANY] * (tensors + len(after)),
         out_specs=ANY,
         out_shape=shape((replicas, total, page, width)),
         scratch_shapes=[pltpu.SemaphoreType.DMA((replicas * total,))],
         compiler_params=params(8),
         cost_estimate=SMALL,
         name="pick_pages",
-    )(place, wanted, *held, *after)
+    )(place, *wanted, *held, *after)
 
 
 def write_pool(place, slots, kv_pool, own, core_new, y_new):
@@ -769,9 +804,10 @@
     core = me % 2
     side = me // 2
     rows = tokens.shape[0]
+    rep = lax.axis_index("replica")
+    place = jnp.stack([me, core, side, rep]).astype(jnp.int32)
     requests = jnp.swapaxes(page_request, 1, 2).reshape(-1)
-    place = jnp.stack([me, core, side, 0 * me]).astype(jnp.int32)
-    place = in_hbm(jnp.concatenate([place, suffix_pages[0], requests]))
+    scalars = in_hbm(jnp.concatenate([place, suffix_pages[0], requests]))
 
     def over_core(x):
         return lax.ppermute(x, "tensor", [(0, 1), (1, 0), (2, 3), (3, 2)])
@@ -779,9 +815,6 @@
     def over_y(x):
         return lax.ppermute(x, "tensor", [(0, 2), (2, 0), (1, 3), (3, 1)])
 
-    def head_of(i):
-        return lax.dynamic_index_in_dim(kv_pool, jnp.bitwise_xor(me, i), 1, keepdims=False)
-
     def to_replicas(x):
         return lax.all_to_all(x, "replica", split_axis=0, concat_axis=0, tiled=True)
 
@@ -789,20 +822,21 @@
         return lax.optimization_barrier((x, *others))[0]
 
     w_query, w_keyvalue, w_out = in_hbm(w_query), in_hbm(w_keyvalue), in_hbm(w_out)
-    held = [head_of(0)]
+
+    wanted = [page_index]
+    for k in range(1, replicas):
+        back = [(i, (i - k) % replicas) for i in range(replicas)]
+        wanted.append(lax.ppermute(page_index, "replica", back))
+
+    mine, other, *held = prepare(place, in_hbm(tokens), in_hbm(gain), in_hbm(kv_pool))
     for i in range(1, 4):
-        held.append(lax.ppermute(head_of(i), "tensor", [(t, t ^ i) for t in range(4)]))
-
-    numbers = page_index.reshape(replicas, -1, page_index.shape[2])
-    wanted = to_replicas(numbers)
-
-    mine, other = norm_rows(place, tokens, gain)
+        held[i] = lax.ppermute(held[i], "tensor", [(t, t ^ i) for t in range(4)])
+
     peer_near = over_core(other)
     peer_far = over_core(mine)
     is_first = core == 0
-    near_tied = tie(peer_near, held[2], held[3], wanted)
-    first_half = jnp.where(is_first, mine, near_tied)
-    second_half = jnp.where(is_first, near_tied, mine)
+    first_half = jnp.where(is_first, mine, peer_near)
+    second_half = jnp.where(is_first, peer_near, mine)
     first = over_y(first_half)
     second = over_y(second_half)
 
@@ -810,7 +844,7 @@
     pulled = to_replicas(picked)
 
     q_local, kv_local, wq, wkv = project_local(
-        place, [mine, peer_near], [other, peer_far], w_query, w_keyvalue, [picked]
+        place, [mine, peer_near], [other, peer_far], w_query, w_keyvalue, [picked, scalars]
     )
 
     q_local = in_hbm(q_local)
@@ -828,7 +862,7 @@
     q_first, kv_first = project_held(first, over_core(first), wq, wkv, [])
     q_first = in_hbm(q_first)
     there, stay = attend_out(
-        place, q_first, [kv_local, kv_first],
+        scalars, q_first, [kv_local, kv_first],
         [local_base, first_base], first_base, pulled, w_out,
     )
     there = tie(there, second)
@@ -840,7 +874,7 @@
     fresh = [kv_local, kv_first, kv_second]
     bases = [local_base, first_base, second_base]
     there, stay = attend_out(
-        place, q_second, fresh, bases, second_base, pulled, w_out
+        scalars, q_second, fresh, bases, second_base, pulled, w_out
     )
     there = tie(there, first_sum)
     second_mix = add_pair(stay, over_core(there))
@@ -854,7 +888,7 @@
     pool_out = write_pool(place, new_slot, kv_pool, new_own, core_new, y_new)
 
     own_part, peer_part = local_rows(
-        place, q_local, fresh, bases, local_base, pulled, w_out,
+        scalars, q_local, fresh, bases, local_base, pulled, w_out,
         [second_mix, pool_out],
     )
     peer_part = over_core(peer_part)

time: 128 us -> 127 us (level)
  local copies, waits for them, and re-layouts: 11 us -> 5.09 us
  Pallas kernels: 65.3 us -> 68.2 us
  waiting for transfers between devices: 30.6 us -> 33.3 us
    all_to_all x2 -> x1, waiting for transfers between devices: 11.3 us -> 6.04 us  [to_replicas(): return lax.all_to_all(x, 'replica', split_axis=0, concat_axis=0, tiled=True)]
    ppermute x3 -> x6, waiting for transfers between devices: 0.01 us -> 4.78 us  [the longest x3 2.76 us: chip_pair_body(): held[i] = lax.ppermute(held[i], 'tensor', [(t, t ^ i) for t in range(4)])]
    ppermute x3 -> x6, starting transfers between devices: 2.96 us -> 7.34 us  [the longest x3 5.67 us: chip_pair_body(): wanted.append(lax.ppermute(page_index, 'replica', back))]
    pallas_call x2, Pallas kernels: 11.8 us -> 15.9 us  [the longest x1 13.6 us: prepare(): pl.pallas_call(kernel, in_specs=[SMEM] + [HBM] * 3, out_specs=[VMEM, VMEM...]
    all_to_all x2 -> x1, starting transfers between devices: 8.52 us -> 4.8 us  [to_replicas(): return lax.all_to_all(x, 'replica', split_axis=0, concat_axis=0, tiled=True)]
    ppermute x5, waiting for transfers between devices: 8.76 us -> 11.6 us  [over_y(): return lax.ppermute(x, 'tensor', [(0, 2), (2, 0), (1, 3), (3, 1)])]
    ppermute x5, starting transfers between devices: 5.22 us -> 3.06 us  [over_y(): return lax.ppermute(x, 'tensor', [(0, 2), (2, 0), (1, 3), (3, 1)])]
    squeeze x1 -> x0, local copies, waits for them, and re-layouts: 1.79 us -> none  [head_of(): lax.dynamic_index_in_dim(kv_pool, jnp.bitwise_xor(me, i), 1, keepdims=False)]
  transfers between devices with their start and end apart: 19 -> 21, of which waited for: 11 -> 13; matrix products, arithmetic and copies ran while one was open for 3% -> 2% of each run, Pallas kernels for 48% -> 41%
where the time goes in v5:
time: 127 us; the launch traced here: 126 us
  Pallas kernels  68.2 us (54%)
  waiting for transfers between devices  33.3 us (26%)
  starting transfers between devices  17.8 us (14%)
  local copies, waits for them, and re-layouts  5.09 us (4%)
    pallas_call x2, Pallas kernels, attend_out(): pl.pallas_call(kernel, in_specs=[SMEM, HBM] + [VMEM] * (1 + known) + [HBM...  16.3 us
    pallas_call x1, Pallas kernels, prepare(): pl.pallas_call(kernel, in_specs=[SMEM] + [HBM] * 3, out_specs=[VMEM, VMEM...  13.6 us
    ppermute x5, waiting for transfers between devices, over_y(): return lax.ppermute(x, 'tensor', [(0, 2), (2, 0), (1, 3), (3, 1)])  11.6 us
    ppermute x9, waiting for transfers between devices, over_core(): return lax.ppermute(x, 'tensor', [(0, 1), (1, 0), (2, 3), (3, 2)])  10.9 us
    pallas_call x1, Pallas kernels, local_rows(): pl.pallas_call(kernel, in_specs=[SMEM] + [VMEM] * (2 + known) + [HBM] + [...  9.51 us
    pallas_call x1, Pallas kernels, project_local(): pl.pallas_call(kernel, in_specs=[SMEM] + [VMEM] * 4 + [HBM] * 2 + [ANY] *...  9.03 us
    pallas_call x1, Pallas kernels, project_far(): pl.pallas_call(kernel, in_specs=[SMEM] + [VMEM] * 2 + [HBM] * 2 + [ANY] *...  8.24 us
    all_to_all x1, waiting for transfers between devices, to_replicas(): return lax.all_to_all(x, 'replica', split_axis=0, concat_axis=0, tiled=True)  6.04 us
  transfers between devices with their start and end apart: 21, of which 13 were waited for; matrix products, arithmetic and copies ran while one was open for 2% of the time, Pallas kernels for 41%

profile of v5, /device:TPU:0, one launch (start us, length us, event | category | flops | bytes accessed | tf_op | source)
XLA Modules:
  0.0 126.5 jit_solution(12774083408743993502)
XLA Ops:
  0.6 0.1 pad_add_fusion.place_ref
  0.7 13.6 %prepare.1 = (bf16[96,4096]{1,0:T(8,128)(2,1)S(1)}, bf16[96,4096]{1,0:T(8,128)(2,1)S(1)}, bf16[4,64,256]{2,1,0:T(8,128)(2,1)S(1)}, bf16[4,64,256]{2,1,0:T(8,128)...) custom-call(s32[4]{0:T(128)S(1)} %pad_add_fusion.place_ref, bf16[96,8192]{1,0:T(8,128)(2,1)} %x_ref.1, ...), custom_call_target="tpu_custom_call" | custom-call | flops 1024 | bytes 1024 | tf_op jit(solution)/shard_map/prepare/pallas_call | solution.py:234
  14.4 0.5 collective-permute-start
  14.9 0.8 copy.15.refs_0_
  15.7 4.7 %collective-permute-start.2 = (s32[1,16,2]{2,1,0:T(8,128)S(1)}, s32[1,16,2]{2,1,0:T(8,128)S(1)}, u32[]{:S(2)}, u32[]{:S(2)}) collective-permute-start(s32[1,16,2]{2,1,0:T(8,128)S(1)} %copy.15.refs_0_), channel_id=1, source_target_pairs={{0,12},{4,0},{8,4},{12,8},{1,13},{5,1},{9,5},{13,9},{2,14},{6,2},{... | collective-permute-start | bytes 392 | tf_op jit(solution)/shard_map/ppermute | solution.py:829
  20.3 1.0 collective-permute-start.4
  21.3 0.0 collective-permute-start.5
  21.3 0.3 collective-permute-done.2.refs_1_
  21.7 1.5 %collective-permute-start.6 = (bf16[4,64,256]{2,1,0:T(8,128)(2,1)}, bf16[4,64,256]{2,1,0:T(8,128)(2,1)S(1)}, u32[]{:S(2)}, u32[]{:S(2)}) collective-permute-start(bf16[4,64,256]{2,1,0:T(8,128)(2,1)} %get-tuple-element.31), channel_id=1, source_target_pairs={{0,2},{1,3},{2,0},{3,1},{4,6},{5,7},{6,4},{7,5},{8,10},{9,11},{10,... | collective-permute-start | bytes 393224 | tf_op jit(solution)/shard_map/ppermute | solution.py:833
  23.2 1.7 %collective-permute-done.3.refs_2_ = s32[1,16,2]{2,1,0:T(8,128)S(1)} collective-permute-done((s32[1,16,2]{2,1,0:T(8,128)S(1)}, s32[1,16,2]{2,1,0:T(8,128)S(1)}, u32[]{:S(2)}, u32[]{:S(2)}) %collective-permute-start.3) | collective-permute-done | bytes 160 | tf_op jit(solution)/shard_map/ppermute | solution.py:829
  24.9 0.1 collective-permute-start.7
  25.0 0.0 collective-permute-done.near_peer
  25.0 1.5 %collective-permute-start.1 = (bf16[96,4096]{1,0:T(8,128)(2,1)S(1)}, bf16[96,4096]{1,0:T(8,128)(2,1)}, u32[]{:S(2)}, u32[]{:S(2)}) collective-permute-start(bf16[96,4096]{1,0:T(8,128)(2,1)S(1)} %get-tuple-element.27.near_own), channel_id=1, source_target_pairs={{0,1},{1,0},{2,3},{3,2},{4,5},{5,4},{6,7},{7,6},{8,9},{9,8},{10,11... | collective-permute-start | bytes 2359304 | tf_op jit(solution)/shard_map/ppermute | solution.py:813
  26.5 1.0 broadcast_select_fusion.2
  27.5 0.0 collective-permute-done.4.refs_3_
  27.5 0.5 collective-permute-start.8
  28.0 0.0 collective-permute-done.5.refs_5_
  28.0 0.0 collective-permute-done.6.refs_6_
  28.0 2.8 %collective-permute-done.7.refs_7_ = bf16[4,64,256]{2,1,0:T(8,128)(2,1)S(1)} collective-permute-done((bf16[4,64,256]{2,1,0:T(8,128)(2,1)}, bf16[4,64,256]{2,1,0:T(8,128)(2,1)S(1)}, u32[]{:S(2)}, u32[]{:S(2)}) %collective-permute-start.7) | collective-permute-done | bytes 131104 | tf_op jit(solution)/shard_map/ppermute | solution.py:833
  30.8 2.3 %pick_pages.1.refs_0_ = bf16[4,8,64,256]{3,2,1,0:T(8,128)(2,1)} custom-call(s32[4]{0:T(128)S(1)} %pad_add_fusion.place_ref, s32[1,16,2]{2,1,0:T(8,128)S(1)} %copy.15.refs_0_, s32[1,16,2]{2,1,0:T(8,128)S(1)} %collective-permute-done.2.refs_1_, s32[1,16,2]{2,1,0:T(8,128)S(1)} %collective-permute-done.3.refs_2_, ...), custom_call_target="tpu_custom_call" | custom-call | flops 1024 | bytes 1024 | tf_op jit(solution)/shard_map/pick_pages/pallas_call | solution.py:725
  33.1 4.8 %all-to-all-start = ((bf16[4,8,64,256]{3,2,1,0:T(8,128)(2,1)}), bf16[4,8,64,256]{3,2,1,0:T(8,128)(2,1)S(1)}, u32[]{:S(2)}, u32[]{:S(2)}) async-start(bf16[4,8,64,256]{3,2,1,0:T(8,128)(2,1)} %pick_pages.1.refs_0_), calls=%async_computation | async-start | bytes 2097152 | tf_op jit(solution)/shard_map/all_to_all | solution.py:819
  37.9 0.1 reshape.7
  38.0 0.6 concatenate.7.refs_1_.place_ref
  38.6 0.0 collective-permute-done.1.far_peer
  38.6 1.1 copy-done.4
  39.8 9.0 %project_local.1 = (bf16[192,1024]{1,0:T(8,128)(2,1)S(1)}, bf16[192,256]{1,0:T(8,128)(2,1)S(1)}, bf16[8,1024,1024]{2,1,0:T(8,128)(2,1)S(1)}, bf16[8,1024,256]{2,1,0:T(8,128)(2,1)S(1)}) custom-call(s32[4]{0:T(128)S(1)} %pad_add_fusion.place_ref, bf16[96,4096]{1,0:T(8,128)(2,1)S(1)} %get-tuple-element.27.near_own, ...), custom_call_target="tpu_custom_call" | custom-call | flops 1024 | bytes 1024 | tf_op jit(solution)/shard_map/project_local/pallas_call | solution.py:287
  48.8 0.7 copy-done.5
  49.5 0.0 collective-permute-done.8.near_ref
  49.5 0.0 collective-permute-start.9
  49.6 1.9 %collective-permute-start.10 = (bf16[96,4096]{1,0:T(8,128)(2,1)S(1)}, bf16[96,4096]{1,0:T(8,128)(2,1)S(1)}, u32[]{:S(2)}, u32[]{:S(2)}) collective-permute-start(bf16[96,4096]{1,0:T(8,128)(2,1)S(1)} %get-tuple-element.54.refs_9_), channel_id=1, source_target_pairs={{0,2},{2,0},{1,3},{3,1},{4,6},{6,4},{5,7},{7,5},{8,10},{10,8},{9,1... | collective-permute-start | bytes 2359304 | tf_op jit(solution)/shard_map/ppermute | solution.py:816
  51.5 0.6 collective-permute-done.9.far_ref
  52.0 4.8 %project_held.1 = (bf16[96,1024]{1,0:T(8,128)(2,1)S(1)}, bf16[96,256]{1,0:T(8,128)(2,1)S(1)}) custom-call(bf16[96,4096]{1,0:T(8,128)(2,1)} %collective-permute-done.8.near_ref, bf16[96,4096]{1,0:T(8,128)(2,1)S(1)} %collective-permute-done.9.far_ref, bf16[8,1024,1024]{2,1,0:T(8,128)(2,1)S(1)} %get-tuple-element.36.wq, ...), custom_call_target="tpu_custom_call" | custom-call | flops 1024 | bytes 1024 | tf_op jit(solution)/shard_map/project_held/pallas_call | solution.py:466
  56.8 0.0 copy-start.6
  56.8 0.7 copy-done.6
  57.5 6.0 %all-to-all-done.pulled_ref = bf16[4,8,64,256]{3,2,1,0:T(8,128)(2,1)S(1)} async-done(((bf16[4,8,64,256]{3,2,1,0:T(8,128)(2,1)}), bf16[4,8,64,256]{3,2,1,0:T(8,128)(2,1)S(1)}, u32[]{:S(2)}, u32[]{:S(2)}) %all-to-all-start) | async-done | bytes 1048608 | tf_op jit(solution)/shard_map/all_to_all | solution.py:819
  63.6 8.8 %attend_out.2 = (bf16[96,4096]{1,0:T(8,128)(2,1)S(1)}, bf16[96,4096]{1,0:T(8,128)(2,1)S(1)}) custom-call(s32[40]{0:T(128)} %concatenate.7.refs_1_.place_ref, bf16[96,1024]{1,0:T(8,128)(2,1)} %copy-done.6, bf16[4,8,64,256]{3,2,1,0:T(8,128)(2,1)S(1)} %all-to-all-done.pulled_ref, bf16[192,256]{1,0:T(8,128)(2,1)S(1)} %get-tuple-element.34.refs_0_, ...), custom_call_target="tpu_custom_call" | custom-call | flops 1024 | bytes 1024 | tf_op jit(solution)/shard_map/attend_out/pallas_call | solution.py:559
  72.3 0.1 collective-permute-start.11
  72.4 2.3 %collective-permute-done.11.right_ref = bf16[96,4096]{1,0:T(8,128)(2,1)S(1)} collective-permute-done((bf16[96,4096]{1,0:T(8,128)(2,1)S(1)}, bf16[96,4096]{1,0:T(8,128)(2,1)S(1)}, u32[]{:S(2)}, u32[]{:S(2)}) %collective-permute-start.11) | collective-permute-done | bytes 786464 | tf_op jit(solution)/shard_map/ppermute | solution.py:813
  74.7 0.2 add_pair.2
  74.9 0.2 collective-permute-start.12
  75.1 2.1 %collective-permute-done.12.far_ref = bf16[96,4096]{1,0:T(8,128)(2,1)S(1)} collective-permute-done((bf16[96,4096]{1,0:T(8,128)(2,1)S(1)}, bf16[96,4096]{1,0:T(8,128)(2,1)S(1)}, u32[]{:S(2)}, u32[]{:S(2)}) %collective-permute-start.12) | collective-permute-done | bytes 786464 | tf_op jit(solution)/shard_map/ppermute | solution.py:813
  77.2 8.2 %project_far.1 = (bf16[96,1024]{1,0:T(8,128)(2,1)S(1)}, bf16[96,256]{1,0:T(8,128)(2,1)S(1)}) custom-call(s32[4]{0:T(128)S(1)} %copy-done.8, bf16[96,4096]{1,0:T(8,128)(2,1)S(1)} %collective-permute-done.10.near_ref, bf16[96,4096]{1,0:T(8,128)(2,1)S(1)} %collective-permute-done.12.far_ref, bf16[8192,1024]{1,0:T(8,128)(2,1)} %wq.3, bf16[8192,256]{1,0:T(8,128)(2,1)} %wkv.3), custom_call_target="tpu_custom_call" | custom-call | flops 1024 | bytes 1024 | tf_op jit(solution)/shard_map/project_far/pallas_call | solution.py:502
  85.5 0.0 copy-start.1
  85.5 0.0 copy-start.9
  85.5 7.5 %attend_out.3 = (bf16[96,4096]{1,0:T(8,128)(2,1)S(1)}, bf16[96,4096]{1,0:T(8,128)(2,1)S(1)}) custom-call(s32[40]{0:T(128)} %concatenate.7.refs_1_.place_ref, bf16[96,1024]{1,0:T(8,128)(2,1)S(1)} %get-tuple-element.45.q_ref, bf16[4,8,64,256]{3,2,1,0:T(8,128)(2,1)S(1)} %all-to-all-done.pulled_ref, bf16[192,256]{1,0:T(8,128)(2,1)S(1)} %get-tuple-element.34.refs_0_, ...), custom_call_target="tpu_custom_call" | custom-call | flops 1024 | bytes 1024 | tf_op jit(solution)/shard_map/attend_out/pallas_call | solution.py:559
  93.0 1.9 %collective-permute-done.13 = bf16[96,4096]{1,0:T(8,128)(2,1)S(1)} collective-permute-done((bf16[96,4096]{1,0:T(8,128)(2,1)S(1)}, bf16[96,4096]{1,0:T(8,128)(2,1)S(1)}, u32[]{:S(2)}, u32[]{:S(2)}) %collective-permute-start.13) | collective-permute-done | bytes 786464 | tf_op jit(solution)/shard_map/ppermute | solution.py:816
  95.0 0.3 collective-permute-start.15
  95.3 1.9 %collective-permute-done.14.right_ref = bf16[96,4096]{1,0:T(8,128)(2,1)S(1)} collective-permute-done((bf16[96,4096]{1,0:T(8,128)(2,1)S(1)}, bf16[96,4096]{1,0:T(8,128)(2,1)S(1)}, u32[]{:S(2)}, u32[]{:S(2)}) %collective-permute-start.14) | collective-permute-done | bytes 786464 | tf_op jit(solution)/shard_map/ppermute | solution.py:813
  97.2 0.2 add_pair.3.refs_4_
  97.4 4.9 %collective-permute-done.15.y_ref = bf16[384,256]{1,0:T(8,128)(2,1)S(1)} collective-permute-done((bf16[384,256]{1,0:T(8,128)(2,1)S(1)}, bf16[384,256]{1,0:T(8,128)(2,1)S(1)}, u32[]{:S(2)}, u32[]{:S(2)}) %collective-permute-start.15) | collective-permute-done | bytes 196640 | tf_op jit(solution)/shard_map/ppermute | solution.py:816
  102.3 0.3 collective-permute-start.18
  102.7 0.1 collective-permute-start.16
  102.7 1.7 %collective-permute-done.16.core_ref = bf16[2,384,256]{2,1,0:T(8,128)(2,1)S(1)} collective-permute-done((bf16[2,384,256]{2,1,0:T(8,128)(2,1)S(1)}, bf16[2,384,256]{2,1,0:T(8,128)(2,1)S(1)}, u32[]{:S(2)}, u32[]{:S(2)}) %collective-permute-start.16) | collective-permute-done | bytes 393248 | tf_op jit(solution)/shard_map/ppermute | solution.py:813
  104.5 1.5 %write_pool.1.refs_5_ = bf16[4,4,64,256]{3,2,1,0:T(8,128)(2,1)} custom-call(s32[4]{0:T(128)S(1)} %copy-done.8, s32[1,6]{1,0:T(1,128)S(1)} %copy-done.9, bf16[4,4,64,256]{3,2,1,0:T(8,128)(2,1)S(1)} %copy-done.1, bf16[384,256]{1,0:T(8,128)(2,1)S(1)} %constant_dynamic-update-slice_fusion.own_ref, bf16[2,384,256]{2,1,0:T(8,128)(2,1)S(1)} %collective-permute-done.16.core_ref, ...), custom_call_target="tpu_custom_call" | custom-call | flops 1024 | bytes 1024 | tf_op jit(solution)/shard_map/write_pool/pallas_call | solution.py:778
  105.9 0.0 copy-start.2
  106.0 1.0 copy-done.2
  107.0 9.5 %local_rows.1 = (bf16[96,8192]{1,0:T(8,128)(2,1)S(1)}, bf16[96,8192]{1,0:T(8,128)(2,1)S(1)}) custom-call(s32[40]{0:T(128)} %concatenate.7.refs_1_.place_ref, bf16[192,1024]{1,0:T(8,128)(2,1)} %copy-done.5, bf16[4,8,64,256]{3,2,1,0:T(8,128)(2,1)S(1)} %all-to-all-done.pulled_ref, bf16[192,256]{1,0:T(8,128)(2,1)S(1)} %get-tuple-element.34.refs_0_, ...), custom_call_target="tpu_custom_call" | custom-call | flops 1024 | bytes 1024 | tf_op jit(solution)/shard_map/local_rows/pallas_call | solution.py:623
  116.5 0.0 copy-start
  116.5 0.2 collective-permute-start.17
  116.7 4.8 %collective-permute-done.18 = bf16[96,4096]{1,0:T(8,128)(2,1)S(1)} collective-permute-done((bf16[96,4096]{1,0:T(8,128)(2,1)S(1)}, bf16[96,4096]{1,0:T(8,128)(2,1)S(1)}, u32[]{:S(2)}, u32[]{:S(2)}) %collective-permute-start.18) | collective-permute-done | bytes 786464 | tf_op jit(solution)/shard_map/ppermute | solution.py:816
  121.5 0.1 broadcast_select_fusion
  121.6 0.1 collective-permute-start.19
  121.7 2.3 %collective-permute-done.19.far_ref = bf16[96,4096]{1,0:T(8,128)(2,1)S(1)} collective-permute-done((bf16[96,4096]{1,0:T(8,128)(2,1)S(1)}, bf16[96,4096]{1,0:T(8,128)(2,1)S(1)}, u32[]{:S(2)}, u32[]{:S(2)}) %collective-permute-start.19) | collective-permute-done | bytes 786464 | tf_op jit(solution)/shard_map/ppermute | solution.py:813
  124.0 2.5 %finish.1 = bf16[96,8192]{1,0:T(8,128)(2,1)} custom-call(s32[4]{0:T(128)S(1)} %copy-done.8, bf16[96,8192]{1,0:T(8,128)(2,1)S(1)} %copy-done, bf16[96,8192]{1,0:T(8,128)(2,1)S(1)} %get-tuple-element.49.own_ref, bf16[96,8192]{1,0:T(8,128)(2,1)S(1)} %collective-permute-done.17.peer_ref, bf16[96,4096]{1,0:T(8,128)(2,1)S(1)} %get-tuple-element.53.near_ref, ...), custom_call_target="tpu_custom_call" | custom-call | flops 1024 | bytes 1024 | tf_op jit(solution)/shard_map/finish/pallas_call | solution.py:684
  (24 shorter events, 0.1 us)
Async XLA Ops:
  0.7 37.9 %copy-start.7 = (s32[4]{0:T(128)}, s32[4]{0:T(128)S(1)}, u32[]{:S(2)}) copy-start(s32[4]{0:T(128)S(1)} %pad_add_fusion.place_ref) | copy-start | bytes 52
  14.4 18.7 %copy-start.3 = (bf16[96,4096]{1,0:T(8,128)(2,1)}, bf16[96,4096]{1,0:T(8,128)(2,1)S(1)}, u32[]{:S(2)}) copy-start(bf16[96,4096]{1,0:T(8,128)(2,1)S(1)} %get-tuple-element.28.far_own) | copy-start | bytes 2359300
  14.4 10.6 %collective-permute-start = (bf16[96,4096]{1,0:T(8,128)(2,1)S(1)}, bf16[96,4096]{1,0:T(8,128)(2,1)S(1)}, u32[]{:S(2)}, u32[]{:S(2)}) collective-permute-start(bf16[96,4096]{1,0:T(8,128)(2,1)S(1)} %get-tuple-element.28.far_own), channel_id=1, source_target_pairs={{0,1},{1,0},{2,3},{3,2},{4,5},{5,4},{6,7},{7,6},{8,9},{9,8},{10,11... | collective-permute-start | bytes 2359304 | tf_op jit(solution)/shard_map/ppermute | solution.py:813
  15.7 6.0 %collective-permute-start.2 = (s32[1,16,2]{2,1,0:T(8,128)S(1)}, s32[1,16,2]{2,1,0:T(8,128)S(1)}, u32[]{:S(2)}, u32[]{:S(2)}) collective-permute-start(s32[1,16,2]{2,1,0:T(8,128)S(1)} %copy.15.refs_0_), channel_id=1, source_target_pairs={{0,12},{4,0},{8,4},{12,8},{1,13},{5,1},{9,5},{13,9},{2,14},{6,2},{... | collective-permute-start | bytes 392 | tf_op jit(solution)/shard_map/ppermute | solution.py:829
  20.3 4.5 %collective-permute-start.3 = (s32[1,16,2]{2,1,0:T(8,128)S(1)}, s32[1,16,2]{2,1,0:T(8,128)S(1)}, u32[]{:S(2)}, u32[]{:S(2)}) collective-permute-start(s32[1,16,2]{2,1,0:T(8,128)S(1)} %copy.15.refs_0_), channel_id=1, source_target_pairs={{0,8},{4,12},{8,0},{12,4},{1,9},{5,13},{9,1},{13,5},{2,10},{6,14},... | collective-permute-start | bytes 392 | tf_op jit(solution)/shard_map/ppermute | solution.py:829
  20.3 7.2 %collective-permute-start.4 = (s32[1,16,2]{2,1,0:T(8,128)S(1)}, s32[1,16,2]{2,1,0:T(8,128)S(1)}, u32[]{:S(2)}, u32[]{:S(2)}) collective-permute-start(s32[1,16,2]{2,1,0:T(8,128)S(1)} %copy.15.refs_0_), channel_id=1, source_target_pairs={{0,4},{4,8},{8,12},{12,0},{1,5},{5,9},{9,13},{13,1},{2,6},{6,10},{... | collective-permute-start | bytes 392 | tf_op jit(solution)/shard_map/ppermute | solution.py:829
  21.3 6.7 %collective-permute-start.5 = (bf16[4,64,256]{2,1,0:T(8,128)(2,1)}, bf16[4,64,256]{2,1,0:T(8,128)(2,1)S(1)}, u32[]{:S(2)}, u32[]{:S(2)}) collective-permute-start(bf16[4,64,256]{2,1,0:T(8,128)(2,1)} %get-tuple-element.30), channel_id=1, source_target_pairs={{0,1},{1,0},{2,3},{3,2},{4,5},{5,4},{6,7},{7,6},{8,9},{9,8},{10,11... | collective-permute-start | bytes 393224 | tf_op jit(solution)/shard_map/ppermute | solution.py:833
  21.7 6.4 %collective-permute-start.6 = (bf16[4,64,256]{2,1,0:T(8,128)(2,1)}, bf16[4,64,256]{2,1,0:T(8,128)(2,1)S(1)}, u32[]{:S(2)}, u32[]{:S(2)}) collective-permute-start(bf16[4,64,256]{2,1,0:T(8,128)(2,1)} %get-tuple-element.31), channel_id=1, source_target_pairs={{0,2},{1,3},{2,0},{3,1},{4,6},{5,7},{6,4},{7,5},{8,10},{9,11},{10,... | collective-permute-start | bytes 393224 | tf_op jit(solution)/shard_map/ppermute | solution.py:833
  24.9 5.9 %collective-permute-start.7 = (bf16[4,64,256]{2,1,0:T(8,128)(2,1)}, bf16[4,64,256]{2,1,0:T(8,128)(2,1)S(1)}, u32[]{:S(2)}, u32[]{:S(2)}) collective-permute-start(bf16[4,64,256]{2,1,0:T(8,128)(2,1)} %get-tuple-element.32), channel_id=1, source_target_pairs={{0,3},{1,2},{2,1},{3,0},{4,7},{5,6},{6,5},{7,4},{8,11},{9,10},{10,... | collective-permute-start | bytes 393224 | tf_op jit(solution)/shard_map/ppermute | solution.py:833
  25.0 12.9 %copy-start.11 = (s32[1,16,2]{1,2,0:T(2,128)S(1)}, s32[1,16,2]{1,2,0:T(2,128)}, u32[]{:S(2)}) copy-start(s32[1,16,2]{1,2,0:T(2,128)} %param.18) | copy-start | bytes 388
  25.0 13.0 %copy-start.10 = (s32[1,4]{1,0:T(1,128)S(1)}, s32[1,4]{1,0:T(1,128)}, u32[]{:S(2)}) copy-start(s32[1,4]{1,0:T(1,128)} %param.16) | copy-start | bytes 52
  25.0 13.6 %collective-permute-start.1 = (bf16[96,4096]{1,0:T(8,128)(2,1)S(1)}, bf16[96,4096]{1,0:T(8,128)(2,1)}, u32[]{:S(2)}, u32[]{:S(2)}) collective-permute-start(bf16[96,4096]{1,0:T(8,128)(2,1)S(1)} %get-tuple-element.27.near_own), channel_id=1, source_target_pairs={{0,1},{1,0},{2,3},{3,2},{4,5},{5,4},{6,7},{7,6},{8,9},{9,8},{10,11... | collective-permute-start | bytes 2359304 | tf_op jit(solution)/shard_map/ppermute | solution.py:813
  27.5 22.0 %collective-permute-start.8 = (bf16[96,4096]{1,0:T(8,128)(2,1)}, bf16[96,4096]{1,0:T(8,128)(2,1)}, u32[]{:S(2)}, u32[]{:S(2)}) collective-permute-start(bf16[96,4096]{1,0:T(8,128)(2,1)} %get-tuple-element.55.refs_8_), channel_id=1, source_target_pairs={{0,2},{2,0},{1,3},{3,1},{4,6},{6,4},{5,7},{7,5},{8,10},{10,8},{9,1... | collective-permute-start | bytes 2359304 | tf_op jit(solution)/shard_map/ppermute | solution.py:816
  33.1 30.4 %all-to-all-start = ((bf16[4,8,64,256]{3,2,1,0:T(8,128)(2,1)}), bf16[4,8,64,256]{3,2,1,0:T(8,128)(2,1)S(1)}, u32[]{:S(2)}, u32[]{:S(2)}) async-start(bf16[4,8,64,256]{3,2,1,0:T(8,128)(2,1)} %pick_pages.1.refs_0_), calls=%async_computation | async-start | bytes 2097152 | tf_op jit(solution)/shard_map/all_to_all | solution.py:819
  38.6 1.1 copy-start.4
  48.8 0.8 copy-start.5
  49.5 2.5 %collective-permute-start.9 = (bf16[96,4096]{1,0:T(8,128)(2,1)}, bf16[96,4096]{1,0:T(8,128)(2,1)S(1)}, u32[]{:S(2)}, u32[]{:S(2)}) collective-permute-start(bf16[96,4096]{1,0:T(8,128)(2,1)} %collective-permute-done.8.near_ref), channel_id=1, source_target_pairs={{0,1},{1,0},{2,3},{3,2},{4,5},{5,4},{6,7},{7,6},{8,9},{9,8},{10,11... | collective-permute-start | bytes 2359304 | tf_op jit(solution)/shard_map/ppermute | solution.py:813
  49.6 22.8 %collective-permute-start.10 = (bf16[96,4096]{1,0:T(8,128)(2,1)S(1)}, bf16[96,4096]{1,0:T(8,128)(2,1)S(1)}, u32[]{:S(2)}, u32[]{:S(2)}) collective-permute-start(bf16[96,4096]{1,0:T(8,128)(2,1)S(1)} %get-tuple-element.54.refs_9_), channel_id=1, source_target_pairs={{0,2},{2,0},{1,3},{3,1},{4,6},{6,4},{5,7},{7,5},{8,10},{10,8},{9,1... | collective-permute-start | bytes 2359304 | tf_op jit(solution)/shard_map/ppermute | solution.py:816
  56.8 0.7 copy-start.6
  63.6 13.7 %copy-start.8 = (s32[4]{0:T(128)S(1)}, s32[4]{0:T(128)}, u32[]{:S(2)}) copy-start(s32[4]{0:T(128)} %copy-done.7) | copy-start | bytes 52
  72.3 2.4 %collective-permute-start.11 = (bf16[96,4096]{1,0:T(8,128)(2,1)S(1)}, bf16[96,4096]{1,0:T(8,128)(2,1)S(1)}, u32[]{:S(2)}, u32[]{:S(2)}) collective-permute-start(bf16[96,4096]{1,0:T(8,128)(2,1)S(1)} %get-tuple-element.42), channel_id=1, source_target_pairs={{0,1},{1,0},{2,3},{3,2},{4,5},{5,4},{6,7},{7,6},{8,9},{9,8},{10,11... | collective-permute-start | bytes 2359304 | tf_op jit(solution)/shard_map/ppermute | solution.py:813
  74.9 2.4 %collective-permute-start.12 = (bf16[96,4096]{1,0:T(8,128)(2,1)S(1)}, bf16[96,4096]{1,0:T(8,128)(2,1)S(1)}, u32[]{:S(2)}, u32[]{:S(2)}) collective-permute-start(bf16[96,4096]{1,0:T(8,128)(2,1)S(1)} %collective-permute-done.10.near_ref), channel_id=1, source_target_pairs={{0,1},{1,0},{2,3},{3,2},{4,5},{5,4},{6,7},{7,6},{8,9},{9,8},{10,11... | collective-permute-start | bytes 2359304 | tf_op jit(solution)/shard_map/ppermute | solution.py:813
  75.1 19.8 %collective-permute-start.13 = (bf16[96,4096]{1,0:T(8,128)(2,1)S(1)}, bf16[96,4096]{1,0:T(8,128)(2,1)S(1)}, u32[]{:S(2)}, u32[]{:S(2)}) collective-permute-start(bf16[96,4096]{1,0:T(8,128)(2,1)S(1)} %add_pair.2), channel_id=1, source_target_pairs={{0,2},{2,0},{1,3},{3,1},{4,6},{6,4},{5,7},{7,5},{8,10},{10,8},{9,1... | collective-permute-start | bytes 2359304 | tf_op jit(solution)/shard_map/ppermute | solution.py:816
  85.5 19.0 %copy-start.1 = (bf16[4,4,64,256]{3,2,1,0:T(8,128)(2,1)S(1)}, bf16[4,4,64,256]{3,2,1,0:T(8,128)(2,1)}, u32[]{:S(2)}) copy-start(bf16[4,4,64,256]{3,2,1,0:T(8,128)(2,1)} %pool_ref.1) | copy-start | bytes 1572868
  85.5 18.9 %copy-start.9 = (s32[1,6]{1,0:T(1,128)S(1)}, s32[1,6]{1,0:T(1,128)}, u32[]{:S(2)}) copy-start(s32[1,6]{1,0:T(1,128)} %slot_ref.1) | copy-start | bytes 76
  94.9 2.3 %collective-permute-start.14 = (bf16[96,4096]{1,0:T(8,128)(2,1)S(1)}, bf16[96,4096]{1,0:T(8,128)(2,1)S(1)}, u32[]{:S(2)}, u32[]{:S(2)}) collective-permute-start(bf16[96,4096]{1,0:T(8,128)(2,1)S(1)} %get-tuple-element.48), channel_id=1, source_target_pairs={{0,1},{1,0},{2,3},{3,2},{4,5},{5,4},{6,7},{7,6},{8,9},{9,8},{10,11... | collective-permute-start | bytes 2359304 | tf_op jit(solution)/shard_map/ppermute | solution.py:813
  95.0 7.4 %collective-permute-start.15 = (bf16[384,256]{1,0:T(8,128)(2,1)S(1)}, bf16[384,256]{1,0:T(8,128)(2,1)S(1)}, u32[]{:S(2)}, u32[]{:S(2)}) collective-permute-start(bf16[384,256]{1,0:T(8,128)(2,1)S(1)} %constant_dynamic-update-slice_fusion.own_ref), channel_id=1, source_target_pairs={{0,2},{2,0},{1,3},{3,1},{4,6},{6,4},{5,7},{7,5},{8,10},{10,8},{9,1... | collective-permute-start | bytes 589832 | tf_op jit(solution)/shard_map/ppermute | solution.py:816
  102.3 19.2 %collective-permute-start.18 = (bf16[96,4096]{1,0:T(8,128)(2,1)S(1)}, bf16[96,4096]{1,0:T(8,128)(2,1)S(1)}, u32[]{:S(2)}, u32[]{:S(2)}) collective-permute-start(bf16[96,4096]{1,0:T(8,128)(2,1)S(1)} %add_pair.3.refs_4_), channel_id=1, source_target_pairs={{0,2},{2,0},{1,3},{3,1},{4,6},{6,4},{5,7},{7,5},{8,10},{10,8},{9,1... | collective-permute-start | bytes 2359304 | tf_op jit(solution)/shard_map/ppermute | solution.py:816
  102.7 1.8 %collective-permute-start.16 = (bf16[2,384,256]{2,1,0:T(8,128)(2,1)S(1)}, bf16[2,384,256]{2,1,0:T(8,128)(2,1)S(1)}, u32[]{:S(2)}, u32[]{:S(2)}) collective-permute-start(bf16[2,384,256]{2,1,0:T(8,128)(2,1)S(1)} %pad_maximum_fusion), channel_id=1, source_target_pairs={{0,1},{1,0},{2,3},{3,2},{4,5},{5,4},{6,7},{7,6},{8,9},{9,8},{10,11... | collective-permute-start | bytes 1179656 | tf_op jit(solution)/shard_map/ppermute | solution.py:813
  105.9 1.0 copy-start.2
  116.5 7.5 %copy-start = (bf16[96,8192]{1,0:T(8,128)(2,1)S(1)}, bf16[96,8192]{1,0:T(8,128)(2,1)}, u32[]{:S(2)}) copy-start(bf16[96,8192]{1,0:T(8,128)(2,1)} %x_ref.1) | copy-start | bytes 4718596
  116.5 7.5 %collective-permute-start.17 = (bf16[96,8192]{1,0:T(8,128)(2,1)S(1)}, bf16[96,8192]{1,0:T(8,128)(2,1)S(1)}, u32[]{:S(2)}, u32[]{:S(2)}) collective-permute-start(bf16[96,8192]{1,0:T(8,128)(2,1)S(1)} %get-tuple-element.50), channel_id=1, source_target_pairs={{0,1},{1,0},{2,3},{3,2},{4,5},{5,4},{6,7},{7,6},{8,9},{9,8},{10,11... | collective-permute-start | bytes 4718600 | tf_op jit(solution)/shard_map/ppermute | solution.py:813
  121.6 2.4 %collective-permute-start.19 = (bf16[96,4096]{1,0:T(8,128)(2,1)S(1)}, bf16[96,4096]{1,0:T(8,128)(2,1)S(1)}, u32[]{:S(2)}, u32[]{:S(2)}) collective-permute-start(bf16[96,4096]{1,0:T(8,128)(2,1)S(1)} %get-tuple-element.52), channel_id=1, source_target_pairs={{0,1},{1,0},{2,3},{3,2},{4,5},{5,4},{6,7},{7,6},{8,9},{9,8},{10,11... | collective-permute-start | bytes 2359304 | tf_op jit(solution)/shard_map/ppermute | solution.py:813

commit v6 on v5

--- a/solution.py
+++ b/solution.py
@@ -24,6 +24,7 @@
 SMEM = pl.BlockSpec(memory_space=pltpu.SMEM)
 VMEM = pl.BlockSpec(memory_space=pltpu.VMEM)
 SMALL = pl.CostEstimate(flops=1024, bytes_accessed=1024, transcendentals=0)
+LARGE = pl.CostEstimate(flops=20000000000, bytes_accessed=200000000, transcendentals=0)
 
 
 def params(mib):
@@ -188,13 +189,9 @@
     blocks = rows // step
 
     def kernel(place_ref, x, g, pool, mine_ref, other_ref, *refs):
-        held, (x_buf, g_buf, sems) = refs[:heads], refs[heads:]
+        held, (x_buf, g_buf, pool_buf, sems) = refs[:heads], refs[heads:]
         me, core = place_ref[0], place_ref[1]
-
-        def head_copy(i):
-            return pltpu.make_async_copy(
-                pool.at[:, jnp.bitwise_xor(me, i)], held[i], sems.at[blocks + 1 + i]
-            )
+        pool_copy = pltpu.make_async_copy(pool, pool_buf, sems.at[blocks + 1])
 
         def row_copy(b):
             at = pl.ds(b * step, step)
@@ -205,8 +202,7 @@
         gain_copy.start()
         for b in range(1, blocks):
             row_copy(b).start()
-        for i in range(heads):
-            head_copy(i).start()
+        pool_copy.start()
         near = pl.multiple_of(core * half, half)
         far = pl.multiple_of((1 - core) * half, half)
         for b in range(blocks):
@@ -228,18 +224,21 @@
                 return carry
 
             lax.fori_loop(0, step // 16, block, 0)
+        pool_copy.wait()
         for i in range(heads):
-            head_copy(i).wait()
+            for p in range(pages):
+                held[i][p] = pool_buf[p, jnp.bitwise_xor(me, i)]
 
     return pl.pallas_call(
         kernel,
         in_specs=[SMEM] + [HBM] * 3,
-        out_specs=[VMEM, VMEM] + [HBM] * heads,
+        out_specs=[VMEM] * (2 + heads),
         out_shape=[shape((rows, half))] * 2 + [shape((pages,) + kv_pool.shape[2:])] * heads,
         scratch_shapes=[
             pltpu.VMEM((rows, width), BF16),
             pltpu.VMEM((width,), BF16),
-            pltpu.SemaphoreType.DMA((blocks + 1 + heads,)),
+            pltpu.VMEM(kv_pool.shape, BF16),
+            pltpu.SemaphoreType.DMA((blocks + 2,)),
         ],
         compiler_params=params(16),
         cost_estimate=SMALL,
@@ -300,7 +299,7 @@
             pltpu.SemaphoreType.DMA((2 * steps,)),
         ],
         compiler_params=params(10),
-        cost_estimate=SMALL,
+        cost_estimate=LARGE,
         name="project_local",
     )(place, *near, *far, w_query, w_keyvalue, *after)
 
@@ -447,31 +446,37 @@
     )
 
 
-def project_held(near, far, w_query, w_keyvalue, after):
+def project_held(near, far, w_query, w_keyvalue):
     rows, half = near.shape
+    pieces = len(far)
     steps, depth, q_width = w_query.shape
     kv_width = w_keyvalue.shape[2]
 
-    def kernel(near_ref, far_ref, wq, wkv, *refs):
-        q_ref, kv_ref = refs[len(after) :]
+    def kernel(near_ref, *refs):
+        far_refs = refs[:pieces]
+        wq, wkv, q_ref, kv_ref = refs[pieces:]
         for w, out in ((wq, q_ref), (wkv, kv_ref)):
             total = None
             for j in range(steps):
-                x_ref = near_ref if j < steps // 2 else far_ref
-                x = x_ref[:, (j % (steps // 2)) * depth : (j % (steps // 2) + 1) * depth]
+                at = j * depth
+                if at < half:
+                    x = near_ref[:, at : at + depth]
+                else:
+                    wide = half // pieces
+                    x = far_refs[(at - half) // wide][:, at % wide : at % wide + depth]
                 part = jnp.dot(x, w[j], preferred_element_type=F32)
                 total = part if j == 0 else total + part
             out[...] = total.astype(BF16)
 
     return pl.pallas_call(
         kernel,
-        in_specs=[VMEM] * 4 + [ANY] * len(after),
+        in_specs=[VMEM] * (3 + pieces),
         out_specs=[VMEM] * 2,
         out_shape=[shape((rows, q_width)), shape((rows, kv_width))],
         compiler_params=params(6),
         cost_estimate=SMALL,
         name="project_held",
-    )(near, far, w_query, w_keyvalue, *after)
+    )(near, *far, w_query, w_keyvalue)
 
 
 def project_far(place, near, far, w_query, w_keyvalue, after):
@@ -529,7 +534,7 @@
 
     def kernel(place_ref, q_ref, pulled_ref, *refs):
         fresh_refs = refs[:known]
-        wo, there_ref, stay_ref, wo_buf, q_buf, sems = refs[known : known + 6]
+        wo, there_ref, stay_ref, wo_buf, sems = refs[known : known + 5]
         core, side = place_ref[1], place_ref[2]
 
         def copy(j):
@@ -537,16 +542,13 @@
             start = pl.multiple_of(first * half + (j % out_steps) * wide, wide)
             return pltpu.make_async_copy(wo.at[:, pl.ds(start, wide)], wo_buf.at[j], sems.at[j])
 
-        q_copy = pltpu.make_async_copy(q_ref, q_buf, sems.at[2 * out_steps])
-        q_copy.start()
         for j in range(2 * out_steps):
             copy(j).start()
-        q_copy.wait()
         pairs = [(ref[...], at(side)) for ref, at in zip(fresh_refs, bases)]
         if pad:
             pairs.append((jnp.zeros((pad, 2 * HEAD_DIM), BF16), jnp.int32(1 << 20)))
         mixed = attend_block(
-            place_ref, q_buf[...], base(side), pairs, pulled_ref, refs[known + 6 :]
+            place_ref, q_ref[...], base(side), pairs, pulled_ref, refs[known + 5 :]
         )
         for j in range(2 * out_steps):
             copy(j).wait()
@@ -558,13 +560,12 @@
 
     return pl.pallas_call(
         kernel,
-        in_specs=[SMEM, HBM] + [VMEM] * (1 + known) + [HBM],
+        in_specs=[SMEM] + [VMEM] * (2 + known) + [HBM],
         out_specs=[VMEM] * 2,
         out_shape=[shape((rows, half)), shape((rows, half))],
         scratch_shapes=[
             pltpu.VMEM((2 * out_steps, depth, wide), BF16),
-            pltpu.VMEM((rows, depth), BF16),
-            pltpu.SemaphoreType.DMA((2 * out_steps + 1,)),
+            pltpu.SemaphoreType.DMA((2 * out_steps,)),
         ]
         + attention_scratch(rows, heads, fresh_rows, pulled.shape[0] * pulled.shape[1]),
         compiler_params=params(30),
@@ -694,40 +695,27 @@
 
 def pick_pages(place, wanted, held, after):
     replicas = len(wanted)
-    slots = wanted[0].shape[2]
+    slots = wanted[0].shape[1]
     tensors = len(held)
     _, page, width = held[0].shape
     total = tensors * slots
 
     def kernel(place_ref, *refs):
         wants, sources = refs[:replicas], refs[replicas : replicas + tensors]
-        out_ref, sems = refs[replicas + tensors + len(after) :]
+        out_ref = refs[replicas + tensors + len(after)]
         me, rep = place_ref[0], place_ref[3]
-
-        def copies():
-            for k in range(replicas):
-                asker = lax.rem(rep + k, replicas)
-                for i in range(tensors):
-                    owner = rep * tensors + jnp.bitwise_xor(me, i)
-                    for s in range(slots):
-                        at = i * slots + s
-                        yield pltpu.make_async_copy(
-                            sources[i].at[wants[k][0, owner, s]],
-                            out_ref.at[asker, at],
-                            sems.at[k * total + at],
-                        )
-
-        for copy in copies():
-            copy.start()
-        for copy in copies():
-            copy.wait()
+        for k in range(replicas):
+            asker = lax.rem(rep + k, replicas)
+            for i in range(tensors):
+                owner = rep * tensors + jnp.bitwise_xor(me, i)
+                for s in range(slots):
+                    out_ref[asker, i * slots + s] = sources[i][wants[k][0, s, owner]]
 
     return pl.pallas_call(
         kernel,
-        in_specs=[SMEM] * (1 + replicas) + [ANY] * (tensors + len(after)),
-        out_specs=ANY,
+        in_specs=[SMEM] * (1 + replicas) + [VMEM] * tensors + [ANY] * len(after),
+        out_specs=VMEM,
         out_shape=shape((replicas, total, page, width)),
-        scratch_shapes=[pltpu.SemaphoreType.DMA((replicas * total,))],
         compiler_params=params(8),
         cost_estimate=SMALL,
         name="pick_pages",
@@ -807,7 +795,7 @@
     rep = lax.axis_index("replica")
     place = jnp.stack([me, core, side, rep]).astype(jnp.int32)
     requests = jnp.swapaxes(page_request, 1, 2).reshape(-1)
-    scalars = in_hbm(jnp.concatenate([place, suffix_pages[0], requests]))
+    scalars = jnp.concatenate([place, suffix_pages[0], requests])
 
     def over_core(x):
         return lax.ppermute(x, "tensor", [(0, 1), (1, 0), (2, 3), (3, 2)])
@@ -815,18 +803,15 @@
     def over_y(x):
         return lax.ppermute(x, "tensor", [(0, 2), (2, 0), (1, 3), (3, 1)])
 
-    def to_replicas(x):
-        return lax.all_to_all(x, "replica", split_axis=0, concat_axis=0, tiled=True)
-
     def tie(x, *others):
         return lax.optimization_barrier((x, *others))[0]
 
     w_query, w_keyvalue, w_out = in_hbm(w_query), in_hbm(w_keyvalue), in_hbm(w_out)
 
-    wanted = [page_index]
+    wanted = [jnp.swapaxes(page_index, 1, 2)]
     for k in range(1, replicas):
         back = [(i, (i - k) % replicas) for i in range(replicas)]
-        wanted.append(lax.ppermute(page_index, "replica", back))
+        wanted.append(lax.ppermute(wanted[0], "replica", back))
 
     mine, other, *held = prepare(place, in_hbm(tokens), in_hbm(gain), in_hbm(kv_pool))
     for i in range(1, 4):
@@ -835,19 +820,19 @@
     peer_near = over_core(other)
     peer_far = over_core(mine)
     is_first = core == 0
-    first_half = jnp.where(is_first, mine, peer_near)
-    second_half = jnp.where(is_first, peer_near, mine)
+    near_tied = tie(peer_near, held[2], held[3])
+    first_half = jnp.where(is_first, mine, near_tied)
+    second_half = jnp.where(is_first, near_tied, mine)
     first = over_y(first_half)
     second = over_y(second_half)
 
     picked = pick_pages(place, wanted, held, [first_half, second_half])
-    pulled = to_replicas(picked)
+    pulled = lax.all_to_all(picked, "replica", split_axis=0, concat_axis=0, tiled=True)
 
     q_local, kv_local, wq, wkv = project_local(
         place, [mine, peer_near], [other, peer_far], w_query, w_keyvalue, [picked, scalars]
     )
 
-    q_local = in_hbm(q_local)
 
     def local_base(s):
         return s * (2 * rows)
@@ -859,8 +844,9 @@
         return (1 - s) * (2 * rows) + rows
 
     first = tie(first, q_local)
-    q_first, kv_first = project_held(first, over_core(first), wq, wkv, [])
-    q_first = in_hbm(q_first)
+    wide = first.shape[1] // 4
+    pieces = [over_core(first[:, i * wide : (i + 1) * wide]) for i in range(4)]
+    q_first, kv_first = project_held(first, pieces, wq, wkv)
     there, stay = attend_out(
         scalars, q_first, [kv_local, kv_first],
         [local_base, first_base], first_base, pulled, w_out,

time: 127 us -> 113 us (0.89)
  Pallas kernels: 68.2 us -> 56.5 us
  waiting for transfers between devices: 33.3 us -> 31 us
    pallas_call x5, Pallas kernels: 37 us -> 24.4 us  [the longest x2 15.3 us: attend_out(): pl.pallas_call(kernel, in_specs=[SMEM] + [VMEM] * (2 + known) + [HBM], ou...]
    ppermute x3, waiting for transfers between devices: 2.76 us -> 0.23 us  [chip_pair_body(): held[i] = lax.ppermute(held[i], 'tensor', [(t, t ^ i) for t in range(4)])]
    all_to_all x1, waiting for transfers between devices: 6.04 us -> 7.94 us  [chip_pair_body(): lax.all_to_all(picked, 'replica', split_axis=0, concat_axis=0, tiled=True)]
    ppermute x3, waiting for transfers between devices: 2.01 us -> 0.47 us  [chip_pair_body(): wanted.append(lax.ppermute(wanted[0], 'replica', back))]
    unnamed x27 -> x24, local copies, waits for them, and re-layouts: 4.39 us -> 3.36 us
    ppermute x9 -> x12, waiting for transfers between devices: 10.9 us -> 11.4 us  [over_core(): return lax.ppermute(x, 'tensor', [(0, 1), (1, 0), (2, 3), (3, 2)])]
    ppermute x9 -> x12, starting transfers between devices: 2.63 us -> 2.6 us  [over_core(): return lax.ppermute(x, 'tensor', [(0, 1), (1, 0), (2, 3), (3, 2)])]
  transfers between devices with their start and end apart: 21 -> 24, of which waited for: 13 -> 15; matrix products, arithmetic and copies ran while one was open for 2% -> 3% of each run, Pallas kernels for 41% -> 44%
where the time goes in v6:
time: 113 us
  Pallas kernels  56.5 us (50%)
  waiting for transfers between devices  31 us (27%)
  starting transfers between devices  17.9 us (16%)
  local copies, waits for them, and re-layouts  4.91 us (4%)
  other arithmetic  1.46 us (1%)
    pallas_call x2, Pallas kernels, attend_out(): pl.pallas_call(kernel, in_specs=[SMEM] + [VMEM] * (2 + known) + [HBM], ou...  15.3 us
    ppermute x12, waiting for transfers between devices, over_core(): return lax.ppermute(x, 'tensor', [(0, 1), (1, 0), (2, 3), (3, 2)])  11.4 us
    ppermute x5, waiting for transfers between devices, over_y(): return lax.ppermute(x, 'tensor', [(0, 2), (2, 0), (1, 3), (3, 1)])  11 us
    pallas_call x1, Pallas kernels, local_rows(): pl.pallas_call(kernel, in_specs=[SMEM] + [VMEM] * (2 + known) + [HBM] + [...  9.63 us
    pallas_call x1, Pallas kernels, project_local(): pl.pallas_call(kernel, in_specs=[SMEM] + [VMEM] * 4 + [HBM] * 2 + [ANY] *...  9.27 us
    pallas_call x1, Pallas kernels, project_far(): pl.pallas_call(kernel, in_specs=[SMEM] + [VMEM] * 2 + [HBM] * 2 + [ANY] *...  8.84 us
    all_to_all x1, waiting for transfers between devices, chip_pair_body(): lax.all_to_all(picked, 'replica', split_axis=0, concat_axis=0, tiled=True)  7.94 us
    ppermute x3, starting transfers between devices, chip_pair_body(): wanted.append(lax.ppermute(wanted[0], 'replica', back))  4.84 us
  transfers between devices with their start and end apart: 24, of which 15 were waited for; matrix products, arithmetic and copies ran while one was open for 3% of the time, Pallas kernels for 44%

profile of v6, /device:TPU:0, one launch (start us, length us, event | category | flops | bytes accessed | tf_op | source)
XLA Modules:
  0.0 112.8 jit_solution(8027463713959234977)
XLA Ops:
  0.6 0.0 copy-start.7
  0.7 0.1 pad_add_fusion.place_ref
  0.7 3.7 %prepare.1 = (bf16[96,4096]{1,0:T(8,128)(2,1)}, bf16[96,4096]{1,0:T(8,128)(2,1)S(1)}, bf16[4,64,256]{2,1,0:T(8,128)(2,1)S(1)}, bf16[4,64,256]{2,1,0:T(8,128)(2,1...) custom-call(s32[4]{0:T(128)S(1)} %pad_add_fusion.place_ref, bf16[96,8192]{1,0:T(8,128)(2,1)} %x_ref.1, ...), custom_call_target="tpu_custom_call" | custom-call | flops 1024 | bytes 1024 | tf_op jit(solution)/shard_map/prepare/pallas_call | solution.py:232
  4.4 0.5 collective-permute-start
  4.9 2.6 %collective-permute-start.6 = (bf16[4,64,256]{2,1,0:T(8,128)(2,1)S(1)}, bf16[4,64,256]{2,1,0:T(8,128)(2,1)S(1)}, u32[]{:S(2)}, u32[]{:S(2)}) collective-permute-start(bf16[4,64,256]{2,1,0:T(8,128)(2,1)S(1)} %get-tuple-element.32), channel_id=1, source_target_pairs={{0,2},{1,3},{2,0},{3,1},{4,6},{5,7},{6,4},{7,5},{8,10},{9,11},{10,... | collective-permute-start | bytes 393224 | tf_op jit(solution)/shard_map/ppermute | solution.py:818
  7.5 0.1 collective-permute-start.7
  7.6 3.8 %collective-permute-start.2 = (s32[1,2,16]{2,1,0:T(2,128)}, s32[1,2,16]{2,1,0:T(2,128)S(1)}, u32[]{:S(2)}, u32[]{:S(2)}) collective-permute-start(s32[1,2,16]{2,1,0:T(2,128)} %bitcast.11), channel_id=1, source_target_pairs={{0,12},{4,0},{8,4},{12,8},{1,13},{5,1},{9,5},{13,9},{2,14},{6,2},{... | collective-permute-start | bytes 392 | tf_op jit(solution)/shard_map/ppermute | solution.py:814
  11.4 0.0 collective-permute-start.3
  11.4 0.8 reshape.7
  12.2 0.7 concatenate.7.refs_1_.place_ref
  12.9 1.0 collective-permute-start.4
  13.9 0.2 collective-permute-done.7.refs_7_
  14.2 0.1 collective-permute-start.5
  14.3 0.4 collective-permute-start.1
  14.7 1.2 %broadcast_select_fusion.2 = (bf16[96,4096]{1,0:T(8,128)(2,1)S(1)}, bf16[96,4096]{1,0:T(8,128)(2,1)S(1)}) fusion(bf16[96,4096]{1,0:T(8,128)(2,1)S(1)} %collective-permute-done.near_peer, bf16[96,4096]{1,0:T(8,128)(2,1)} %get-tuple-element.28.near_own, pred[]{:T(512)S(6)} %eq.5), kind=kLoop, calls=%fused_computation.2 | loop fusion | flops 786432 | bytes 3145729 | tf_op jit(solution)/shard_map/jit(_where)/select_n | solution.py:825
  15.9 1.7 %collective-permute-start.8 = (bf16[96,4096]{1,0:T(8,128)(2,1)S(1)}, bf16[96,4096]{1,0:T(8,128)(2,1)S(1)}, u32[]{:S(2)}, u32[]{:S(2)}) collective-permute-start(bf16[96,4096]{1,0:T(8,128)(2,1)S(1)} %get-tuple-element.57.refs_8_), channel_id=1, source_target_pairs={{0,2},{2,0},{1,3},{3,1},{4,6},{6,4},{5,7},{7,5},{8,10},{10,8},{9,1... | collective-permute-start | bytes 2359304 | tf_op jit(solution)/shard_map/ppermute | solution.py:804
  17.6 0.4 collective-permute-start.13
  18.0 0.5 collective-permute-done.4.refs_3_
  18.5 1.8 %pick_pages.1.refs_0_ = bf16[4,8,64,256]{3,2,1,0:T(8,128)(2,1)} custom-call(s32[4]{0:T(128)S(1)} %pad_add_fusion.place_ref, s32[1,2,16]{2,1,0:T(2,128)S(1)} %bitcast.14, s32[1,2,16]{2,1,0:T(2,128)S(1)} %collective-permute-done.2.refs_1_, s32[1,2,16]{2,1,0:T(2,128)} %collective-permute-done.3.refs_2_, s32[1,2,16]{2,1,0:T(2,128)S(1)} %collective-permute-done.4.refs_3_, ...), custom_call_target="tpu_custom_call" | custom-call | flops 1024 | bytes 1024 | tf_op jit(solution)/shard_map/pick_pages/pallas_call | solution.py:714
  20.3 4.5 %all-to-all-start = ((bf16[4,8,64,256]{3,2,1,0:T(8,128)(2,1)}), bf16[4,8,64,256]{3,2,1,0:T(8,128)(2,1)S(1)}, u32[]{:S(2)}, u32[]{:S(2)}) async-start(bf16[4,8,64,256]{3,2,1,0:T(8,128)(2,1)} %pick_pages.1.refs_0_), calls=%async_computation | async-start | bytes 2097152 | tf_op jit(solution)/shard_map/all_to_all | solution.py:830
  24.8 1.1 %copy-done.4 = bf16[96,4096]{1,0:T(8,128)(2,1)S(1)} copy-done((bf16[96,4096]{1,0:T(8,128)(2,1)S(1)}, bf16[96,4096]{1,0:T(8,128)(2,1)}, u32[]{:S(2)}) %copy-start.4) | copy-done | bytes 786456
  26.0 1.1 %copy-done.10 = bf16[96,4096]{1,0:T(8,128)(2,1)S(1)} copy-done((bf16[96,4096]{1,0:T(8,128)(2,1)S(1)}, bf16[96,4096]{1,0:T(8,128)(2,1)}, u32[]{:S(2)}) %copy-start.10) | copy-done | bytes 786456
  27.1 9.3 %project_local.1 = (bf16[192,1024]{1,0:T(8,128)(2,1)S(1)}, bf16[192,256]{1,0:T(8,128)(2,1)S(1)}, bf16[8,1024,1024]{2,1,0:T(8,128)(2,1)S(1)}, bf16[8,1024,256]{2,1,0:T(8,128)(2,1)S(1)}) custom-call(s32[4]{0:T(128)S(1)} %pad_add_fusion.place_ref, bf16[96,4096]{1,0:T(8,128)(2,1)} %get-tuple-element.28.near_own, bf16[96,4096]{1,0:T(8,128)(2,1)S(1)} %copy-done.4, ...), custom_call_target="tpu_custom_call" | custom-call | flops 20000000000 | bytes 200000000 | tf_op jit(solution)/shard_map/project_local/pallas_call | solution.py:286
  36.4 0.1 fusion
  36.4 0.1 collective-permute-start.10
  36.5 0.5 collective-permute-start.11
  37.0 0.1 collective-permute-start.12
  37.1 0.4 collective-permute-start.9
  37.5 0.4 collective-permute-done.10.refs_1_
  38.0 0.3 collective-permute-done.11.refs_2_
  38.2 0.3 collective-permute-done.12.refs_3_
  38.5 0.3 collective-permute-done.9.refs_0_
  38.8 3.6 %project_held.1 = (bf16[96,1024]{1,0:T(8,128)(2,1)S(1)}, bf16[96,256]{1,0:T(8,128)(2,1)S(1)}) custom-call(bf16[96,4096]{1,0:T(8,128)(2,1)S(1)} %collective-permute-done.8.near_ref, bf16[96,1024]{1,0:T(8,128)(2,1)S(1)} %collective-permute-done.9.refs_0_, bf16[96,1024]{1,0:T(8,128)(2,1)S(1)} %collective-permute-done.10.refs_1_, ...), custom_call_target="tpu_custom_call" | custom-call | flops 1024 | bytes 1024 | tf_op jit(solution)/shard_map/project_held/pallas_call | solution.py:471
  42.4 7.9 %all-to-all-done.pulled_ref = bf16[4,8,64,256]{3,2,1,0:T(8,128)(2,1)S(1)} async-done(((bf16[4,8,64,256]{3,2,1,0:T(8,128)(2,1)}), bf16[4,8,64,256]{3,2,1,0:T(8,128)(2,1)S(1)}, u32[]{:S(2)}, u32[]{:S(2)}) %all-to-all-start) | async-done | bytes 1048608 | tf_op jit(solution)/shard_map/all_to_all | solution.py:830
  50.4 8.2 %attend_out.2 = (bf16[96,4096]{1,0:T(8,128)(2,1)S(1)}, bf16[96,4096]{1,0:T(8,128)(2,1)S(1)}) custom-call(s32[40]{0:T(128)S(1)} %concatenate.7.refs_1_.place_ref, bf16[96,1024]{1,0:T(8,128)(2,1)S(1)} %get-tuple-element.41.q_ref, bf16[4,8,64,256]{3,2,1,0:T(8,128)(2,1)S(1)} %all-to-all-done.pulled_ref, bf16[192,256]{1,0:T(8,128)(2,1)S(1)} %get-tuple-element.36.refs_0_, ...), custom_call_target="tpu_custom_call" | custom-call | flops 1024 | bytes 1024 | tf_op jit(solution)/shard_map/attend_out/pallas_call | solution.py:561
  58.6 0.1 collective-permute-start.14
  58.7 2.3 %collective-permute-done.14.right_ref = bf16[96,4096]{1,0:T(8,128)(2,1)S(1)} collective-permute-done((bf16[96,4096]{1,0:T(8,128)(2,1)S(1)}, bf16[96,4096]{1,0:T(8,128)(2,1)S(1)}, u32[]{:S(2)}, u32[]{:S(2)}) %collective-permute-start.14) | collective-permute-done | bytes 786464 | tf_op jit(solution)/shard_map/ppermute | solution.py:801
  61.0 0.2 add_pair.2
  61.2 0.2 collective-permute-start.15
  61.4 0.4 collective-permute-start.16
  61.7 2.0 %collective-permute-done.15.far_ref = bf16[96,4096]{1,0:T(8,128)(2,1)S(1)} collective-permute-done((bf16[96,4096]{1,0:T(8,128)(2,1)}, bf16[96,4096]{1,0:T(8,128)(2,1)S(1)}, u32[]{:S(2)}, u32[]{:S(2)}) %collective-permute-start.15) | collective-permute-done | bytes 786464 | tf_op jit(solution)/shard_map/ppermute | solution.py:801
  63.7 8.8 %project_far.1 = (bf16[96,1024]{1,0:T(8,128)(2,1)S(1)}, bf16[96,256]{1,0:T(8,128)(2,1)S(1)}) custom-call(s32[4]{0:T(128)S(1)} %pad_add_fusion.place_ref, bf16[96,4096]{1,0:T(8,128)(2,1)} %collective-permute-done.13.near_ref, bf16[96,4096]{1,0:T(8,128)(2,1)S(1)} %collective-permute-done.15.far_ref, bf16[8192,1024]{1,0:T(8,128)(2,1)} %wq.3, bf16[8192,256]{1,0:T(8,128)(2,1)} %wkv.3), custom_call_target="tpu_custom_call" | custom-call | flops 1024 | bytes 1024 | tf_op jit(solution)/shard_map/project_far/pallas_call | solution.py:507
  72.6 0.0 copy-start.1
  72.6 0.0 copy-start.8
  72.6 7.1 %attend_out.3 = (bf16[96,4096]{1,0:T(8,128)(2,1)S(1)}, bf16[96,4096]{1,0:T(8,128)(2,1)S(1)}) custom-call(s32[40]{0:T(128)S(1)} %concatenate.7.refs_1_.place_ref, bf16[96,1024]{1,0:T(8,128)(2,1)S(1)} %get-tuple-element.47.q_ref, bf16[4,8,64,256]{3,2,1,0:T(8,128)(2,1)S(1)} %all-to-all-done.pulled_ref, bf16[192,256]{1,0:T(8,128)(2,1)S(1)} %get-tuple-element.36.refs_0_, ...), custom_call_target="tpu_custom_call" | custom-call | flops 1024 | bytes 1024 | tf_op jit(solution)/shard_map/attend_out/pallas_call | solution.py:561
  79.7 1.5 %collective-permute-done.16 = bf16[96,4096]{1,0:T(8,128)(2,1)S(1)} collective-permute-done((bf16[96,4096]{1,0:T(8,128)(2,1)S(1)}, bf16[96,4096]{1,0:T(8,128)(2,1)S(1)}, u32[]{:S(2)}, u32[]{:S(2)}) %collective-permute-start.16) | collective-permute-done | bytes 786464 | tf_op jit(solution)/shard_map/ppermute | solution.py:804
  81.2 0.4 collective-permute-start.18
  81.6 1.8 %collective-permute-done.17.right_ref = bf16[96,4096]{1,0:T(8,128)(2,1)S(1)} collective-permute-done((bf16[96,4096]{1,0:T(8,128)(2,1)S(1)}, bf16[96,4096]{1,0:T(8,128)(2,1)S(1)}, u32[]{:S(2)}, u32[]{:S(2)}) %collective-permute-start.17) | collective-permute-done | bytes 786464 | tf_op jit(solution)/shard_map/ppermute | solution.py:801
  83.5 0.2 add_pair.3.refs_4_
  83.7 4.9 %collective-permute-done.18.y_ref = bf16[384,256]{1,0:T(8,128)(2,1)S(1)} collective-permute-done((bf16[384,256]{1,0:T(8,128)(2,1)S(1)}, bf16[384,256]{1,0:T(8,128)(2,1)S(1)}, u32[]{:S(2)}, u32[]{:S(2)}) %collective-permute-start.18) | collective-permute-done | bytes 196640 | tf_op jit(solution)/shard_map/ppermute | solution.py:804
  88.6 0.3 collective-permute-start.21
  89.0 0.1 collective-permute-start.19
  89.1 1.7 %collective-permute-done.19.core_ref = bf16[2,384,256]{2,1,0:T(8,128)(2,1)S(1)} collective-permute-done((bf16[2,384,256]{2,1,0:T(8,128)(2,1)S(1)}, bf16[2,384,256]{2,1,0:T(8,128)(2,1)S(1)}, u32[]{:S(2)}, u32[]{:S(2)}) %collective-permute-start.19) | collective-permute-done | bytes 393248 | tf_op jit(solution)/shard_map/ppermute | solution.py:801
  90.8 1.5 %write_pool.1.refs_5_ = bf16[4,4,64,256]{3,2,1,0:T(8,128)(2,1)} custom-call(s32[4]{0:T(128)S(1)} %pad_add_fusion.place_ref, s32[1,6]{1,0:T(1,128)S(1)} %copy-done.8, bf16[4,4,64,256]{3,2,1,0:T(8,128)(2,1)S(1)} %copy-done.1, bf16[384,256]{1,0:T(8,128)(2,1)S(1)} %constant_dynamic-update-slice_fusion.own_ref, ...), custom_call_target="tpu_custom_call" | custom-call | flops 1024 | bytes 1024 | tf_op jit(solution)/shard_map/write_pool/pallas_call | solution.py:766
  92.3 0.0 copy-start.2
  92.3 1.0 copy-done.2
  93.3 9.6 %local_rows.1 = (bf16[96,8192]{1,0:T(8,128)(2,1)S(1)}, bf16[96,8192]{1,0:T(8,128)(2,1)S(1)}) custom-call(s32[40]{0:T(128)S(1)} %concatenate.7.refs_1_.place_ref, bf16[192,1024]{1,0:T(8,128)(2,1)S(1)} %copy-done.6, bf16[4,8,64,256]{3,2,1,0:T(8,128)(2,1)S(1)} %all-to-all-done.pulled_ref, bf16[192,256]{1,0:T(8,128)(2,1)S(1)} %get-tuple-element.36.refs_0_, ...), custom_call_target="tpu_custom_call" | custom-call | flops 1024 | bytes 1024 | tf_op jit(solution)/shard_map/local_rows/pallas_call | solution.py:624
  103.0 0.0 copy-start
  103.0 0.2 collective-permute-start.20
  103.2 4.6 %collective-permute-done.21 = bf16[96,4096]{1,0:T(8,128)(2,1)S(1)} collective-permute-done((bf16[96,4096]{1,0:T(8,128)(2,1)S(1)}, bf16[96,4096]{1,0:T(8,128)(2,1)S(1)}, u32[]{:S(2)}, u32[]{:S(2)}) %collective-permute-start.21) | collective-permute-done | bytes 786464 | tf_op jit(solution)/shard_map/ppermute | solution.py:804
  107.8 0.1 broadcast_select_fusion
  107.9 0.1 collective-permute-start.22
  108.0 2.3 %collective-permute-done.22.far_ref = bf16[96,4096]{1,0:T(8,128)(2,1)S(1)} collective-permute-done((bf16[96,4096]{1,0:T(8,128)(2,1)S(1)}, bf16[96,4096]{1,0:T(8,128)(2,1)S(1)}, u32[]{:S(2)}, u32[]{:S(2)}) %collective-permute-start.22) | collective-permute-done | bytes 786464 | tf_op jit(solution)/shard_map/ppermute | solution.py:801
  110.2 2.5 %finish.1 = bf16[96,8192]{1,0:T(8,128)(2,1)} custom-call(s32[4]{0:T(128)S(1)} %pad_add_fusion.place_ref, bf16[96,8192]{1,0:T(8,128)(2,1)S(1)} %copy-done, bf16[96,8192]{1,0:T(8,128)(2,1)S(1)} %get-tuple-element.51.own_ref, bf16[96,8192]{1,0:T(8,128)(2,1)S(1)} %collective-permute-done.20.peer_ref, bf16[96,4096]{1,0:T(8,128)(2,1)S(1)} %get-tuple-element.55.near_ref, ...), custom_call_target="tpu_custom_call" | custom-call | flops 1024 | bytes 1024 | tf_op jit(solution)/shard_map/finish/pallas_call | solution.py:685
  (28 shorter events, 0.1 us)
Async XLA Ops:
  0.6 17.9 %copy-start.7 = (s32[1,16,2]{1,2,0:T(2,128)S(1)}, s32[1,16,2]{1,2,0:T(2,128)}, u32[]{:S(2)}) copy-start(s32[1,16,2]{1,2,0:T(2,128)} %param.17) | copy-start | bytes 388
  4.4 11.5 %copy-start.9 = (bf16[96,4096]{1,0:T(8,128)(2,1)}, bf16[96,4096]{1,0:T(8,128)(2,1)S(1)}, u32[]{:S(2)}) copy-start(bf16[96,4096]{1,0:T(8,128)(2,1)S(1)} %get-tuple-element.29.far_own) | copy-start | bytes 2359300
  4.4 9.9 %collective-permute-start = (bf16[96,4096]{1,0:T(8,128)(2,1)S(1)}, bf16[96,4096]{1,0:T(8,128)(2,1)S(1)}, u32[]{:S(2)}, u32[]{:S(2)}) collective-permute-start(bf16[96,4096]{1,0:T(8,128)(2,1)S(1)} %get-tuple-element.29.far_own), channel_id=1, source_target_pairs={{0,1},{1,0},{2,3},{3,2},{4,5},{5,4},{6,7},{7,6},{8,9},{9,8},{10,11... | collective-permute-start | bytes 2359304 | tf_op jit(solution)/shard_map/ppermute | solution.py:801
  4.9 8.0 %collective-permute-start.6 = (bf16[4,64,256]{2,1,0:T(8,128)(2,1)S(1)}, bf16[4,64,256]{2,1,0:T(8,128)(2,1)S(1)}, u32[]{:S(2)}, u32[]{:S(2)}) collective-permute-start(bf16[4,64,256]{2,1,0:T(8,128)(2,1)S(1)} %get-tuple-element.32), channel_id=1, source_target_pairs={{0,2},{1,3},{2,0},{3,1},{4,6},{5,7},{6,4},{7,5},{8,10},{9,11},{10,... | collective-permute-start | bytes 393224 | tf_op jit(solution)/shard_map/ppermute | solution.py:818
  7.5 6.6 %collective-permute-start.7 = (bf16[4,64,256]{2,1,0:T(8,128)(2,1)S(1)}, bf16[4,64,256]{2,1,0:T(8,128)(2,1)S(1)}, u32[]{:S(2)}, u32[]{:S(2)}) collective-permute-start(bf16[4,64,256]{2,1,0:T(8,128)(2,1)S(1)} %get-tuple-element.33), channel_id=1, source_target_pairs={{0,3},{1,2},{2,1},{3,0},{4,7},{5,6},{6,5},{7,4},{8,11},{9,10},{10,... | collective-permute-start | bytes 393224 | tf_op jit(solution)/shard_map/ppermute | solution.py:818
  7.6 8.3 %collective-permute-start.2 = (s32[1,2,16]{2,1,0:T(2,128)}, s32[1,2,16]{2,1,0:T(2,128)S(1)}, u32[]{:S(2)}, u32[]{:S(2)}) collective-permute-start(s32[1,2,16]{2,1,0:T(2,128)} %bitcast.11), channel_id=1, source_target_pairs={{0,12},{4,0},{8,4},{12,8},{1,13},{5,1},{9,5},{13,9},{2,14},{6,2},{... | collective-permute-start | bytes 392 | tf_op jit(solution)/shard_map/ppermute | solution.py:814
  11.4 6.2 %collective-permute-start.3 = (s32[1,2,16]{2,1,0:T(2,128)}, s32[1,2,16]{2,1,0:T(2,128)}, u32[]{:S(2)}, u32[]{:S(2)}) collective-permute-start(s32[1,2,16]{2,1,0:T(2,128)} %bitcast.12), channel_id=1, source_target_pairs={{0,8},{4,12},{8,0},{12,4},{1,9},{5,13},{9,1},{13,5},{2,10},{6,14},... | collective-permute-start | bytes 392 | tf_op jit(solution)/shard_map/ppermute | solution.py:814
  12.9 5.6 %collective-permute-start.4 = (s32[1,2,16]{2,1,0:T(2,128)}, s32[1,2,16]{2,1,0:T(2,128)S(1)}, u32[]{:S(2)}, u32[]{:S(2)}) collective-permute-start(s32[1,2,16]{2,1,0:T(2,128)} %bitcast.13), channel_id=1, source_target_pairs={{0,4},{4,8},{8,12},{12,0},{1,5},{5,9},{9,13},{13,1},{2,6},{6,10},{... | collective-permute-start | bytes 392 | tf_op jit(solution)/shard_map/ppermute | solution.py:814
  14.2 4.3 %collective-permute-start.5 = (bf16[4,64,256]{2,1,0:T(8,128)(2,1)}, bf16[4,64,256]{2,1,0:T(8,128)(2,1)S(1)}, u32[]{:S(2)}, u32[]{:S(2)}) collective-permute-start(bf16[4,64,256]{2,1,0:T(8,128)(2,1)} %get-tuple-element.31), channel_id=1, source_target_pairs={{0,1},{1,0},{2,3},{3,2},{4,5},{5,4},{6,7},{7,6},{8,9},{9,8},{10,11... | collective-permute-start | bytes 393224 | tf_op jit(solution)/shard_map/ppermute | solution.py:818
  14.3 6.0 %copy-start.3 = (bf16[96,4096]{1,0:T(8,128)(2,1)}, bf16[96,4096]{1,0:T(8,128)(2,1)S(1)}, u32[]{:S(2)}) copy-start(bf16[96,4096]{1,0:T(8,128)(2,1)S(1)} %collective-permute-done.near_peer) | copy-start | bytes 2359300
  14.3 10.5 %collective-permute-start.1 = (bf16[96,4096]{1,0:T(8,128)(2,1)}, bf16[96,4096]{1,0:T(8,128)(2,1)}, u32[]{:S(2)}, u32[]{:S(2)}) collective-permute-start(bf16[96,4096]{1,0:T(8,128)(2,1)} %get-tuple-element.28.near_own), channel_id=1, source_target_pairs={{0,1},{1,0},{2,3},{3,2},{4,5},{5,4},{6,7},{7,6},{8,9},{9,8},{10,11... | collective-permute-start | bytes 2359304 | tf_op jit(solution)/shard_map/ppermute | solution.py:801
  15.9 20.4 %collective-permute-start.8 = (bf16[96,4096]{1,0:T(8,128)(2,1)S(1)}, bf16[96,4096]{1,0:T(8,128)(2,1)S(1)}, u32[]{:S(2)}, u32[]{:S(2)}) collective-permute-start(bf16[96,4096]{1,0:T(8,128)(2,1)S(1)} %get-tuple-element.57.refs_8_), channel_id=1, source_target_pairs={{0,2},{2,0},{1,3},{3,1},{4,6},{6,4},{5,7},{7,5},{8,10},{10,8},{9,1... | collective-permute-start | bytes 2359304 | tf_op jit(solution)/shard_map/ppermute | solution.py:804
  17.6 41.0 %collective-permute-start.13 = (bf16[96,4096]{1,0:T(8,128)(2,1)S(1)}, bf16[96,4096]{1,0:T(8,128)(2,1)}, u32[]{:S(2)}, u32[]{:S(2)}) collective-permute-start(bf16[96,4096]{1,0:T(8,128)(2,1)S(1)} %get-tuple-element.56.refs_9_), channel_id=1, source_target_pairs={{0,2},{2,0},{1,3},{3,1},{4,6},{6,4},{5,7},{7,5},{8,10},{10,8},{9,1... | collective-permute-start | bytes 2359304 | tf_op jit(solution)/shard_map/ppermute | solution.py:804
  20.3 30.1 %all-to-all-start = ((bf16[4,8,64,256]{3,2,1,0:T(8,128)(2,1)}), bf16[4,8,64,256]{3,2,1,0:T(8,128)(2,1)S(1)}, u32[]{:S(2)}, u32[]{:S(2)}) async-start(bf16[4,8,64,256]{3,2,1,0:T(8,128)(2,1)} %pick_pages.1.refs_0_), calls=%async_computation | async-start | bytes 2097152 | tf_op jit(solution)/shard_map/all_to_all | solution.py:830
  24.8 1.1 %copy-start.4 = (bf16[96,4096]{1,0:T(8,128)(2,1)S(1)}, bf16[96,4096]{1,0:T(8,128)(2,1)}, u32[]{:S(2)}) copy-start(bf16[96,4096]{1,0:T(8,128)(2,1)} %copy-done.3) | copy-start | bytes 2359300
  25.9 1.1 %copy-start.10 = (bf16[96,4096]{1,0:T(8,128)(2,1)S(1)}, bf16[96,4096]{1,0:T(8,128)(2,1)}, u32[]{:S(2)}) copy-start(bf16[96,4096]{1,0:T(8,128)(2,1)} %copy-done.9) | copy-start | bytes 2359300
  36.4 2.4 %copy-start.5 = (bf16[192,1024]{1,0:T(8,128)(2,1)}, bf16[192,1024]{1,0:T(8,128)(2,1)S(1)}, u32[]{:S(2)}) copy-start(bf16[192,1024]{1,0:T(8,128)(2,1)S(1)} %get-tuple-element.35.q_ref) | copy-start | bytes 1179652
  36.4 1.5 %collective-permute-start.10 = (bf16[96,1024]{1,0:T(8,128)(2,1)S(1)}, bf16[96,1024]{1,0:T(8,128)(2,1)S(1)}, u32[]{:S(2)}, u32[]{:S(2)}) collective-permute-start(bf16[96,1024]{1,0:T(8,128)(2,1)S(1)} %get-tuple-element.60), channel_id=1, source_target_pairs={{0,1},{1,0},{2,3},{3,2},{4,5},{5,4},{6,7},{7,6},{8,9},{9,8},{10,11... | collective-permute-start | bytes 589832 | tf_op jit(solution)/shard_map/ppermute | solution.py:801
  36.5 1.7 %collective-permute-start.11 = (bf16[96,1024]{1,0:T(8,128)(2,1)S(1)}, bf16[96,1024]{1,0:T(8,128)(2,1)S(1)}, u32[]{:S(2)}, u32[]{:S(2)}) collective-permute-start(bf16[96,1024]{1,0:T(8,128)(2,1)S(1)} %get-tuple-element.59), channel_id=1, source_target_pairs={{0,1},{1,0},{2,3},{3,2},{4,5},{5,4},{6,7},{7,6},{8,9},{9,8},{10,11... | collective-permute-start | bytes 589832 | tf_op jit(solution)/shard_map/ppermute | solution.py:801
  37.0 1.5 %collective-permute-start.12 = (bf16[96,1024]{1,0:T(8,128)(2,1)S(1)}, bf16[96,1024]{1,0:T(8,128)(2,1)S(1)}, u32[]{:S(2)}, u32[]{:S(2)}) collective-permute-start(bf16[96,1024]{1,0:T(8,128)(2,1)S(1)} %get-tuple-element.58), channel_id=1, source_target_pairs={{0,1},{1,0},{2,3},{3,2},{4,5},{5,4},{6,7},{7,6},{8,9},{9,8},{10,11... | collective-permute-start | bytes 589832 | tf_op jit(solution)/shard_map/ppermute | solution.py:801
  37.1 1.7 %collective-permute-start.9 = (bf16[96,1024]{1,0:T(8,128)(2,1)S(1)}, bf16[96,1024]{1,0:T(8,128)(2,1)S(1)}, u32[]{:S(2)}, u32[]{:S(2)}) collective-permute-start(bf16[96,1024]{1,0:T(8,128)(2,1)S(1)} %get-tuple-element.61), channel_id=1, source_target_pairs={{0,1},{1,0},{2,3},{3,2},{4,5},{5,4},{6,7},{7,6},{8,9},{9,8},{10,11... | collective-permute-start | bytes 589832 | tf_op jit(solution)/shard_map/ppermute | solution.py:801
  58.6 2.4 %collective-permute-start.14 = (bf16[96,4096]{1,0:T(8,128)(2,1)S(1)}, bf16[96,4096]{1,0:T(8,128)(2,1)S(1)}, u32[]{:S(2)}, u32[]{:S(2)}) collective-permute-start(bf16[96,4096]{1,0:T(8,128)(2,1)S(1)} %get-tuple-element.44), channel_id=1, source_target_pairs={{0,1},{1,0},{2,3},{3,2},{4,5},{5,4},{6,7},{7,6},{8,9},{9,8},{10,11... | collective-permute-start | bytes 2359304 | tf_op jit(solution)/shard_map/ppermute | solution.py:801
  61.2 2.6 %collective-permute-start.15 = (bf16[96,4096]{1,0:T(8,128)(2,1)}, bf16[96,4096]{1,0:T(8,128)(2,1)S(1)}, u32[]{:S(2)}, u32[]{:S(2)}) collective-permute-start(bf16[96,4096]{1,0:T(8,128)(2,1)} %collective-permute-done.13.near_ref), channel_id=1, source_target_pairs={{0,1},{1,0},{2,3},{3,2},{4,5},{5,4},{6,7},{7,6},{8,9},{9,8},{10,11... | collective-permute-start | bytes 2359304 | tf_op jit(solution)/shard_map/ppermute | solution.py:801
  61.4 19.8 %collective-permute-start.16 = (bf16[96,4096]{1,0:T(8,128)(2,1)S(1)}, bf16[96,4096]{1,0:T(8,128)(2,1)S(1)}, u32[]{:S(2)}, u32[]{:S(2)}) collective-permute-start(bf16[96,4096]{1,0:T(8,128)(2,1)S(1)} %add_pair.2), channel_id=1, source_target_pairs={{0,2},{2,0},{1,3},{3,1},{4,6},{6,4},{5,7},{7,5},{8,10},{10,8},{9,1... | collective-permute-start | bytes 2359304 | tf_op jit(solution)/shard_map/ppermute | solution.py:804
  72.6 18.2 %copy-start.1 = (bf16[4,4,64,256]{3,2,1,0:T(8,128)(2,1)S(1)}, bf16[4,4,64,256]{3,2,1,0:T(8,128)(2,1)}, u32[]{:S(2)}) copy-start(bf16[4,4,64,256]{3,2,1,0:T(8,128)(2,1)} %pool_ref.1) | copy-start | bytes 1572868
  72.6 18.2 %copy-start.8 = (s32[1,6]{1,0:T(1,128)S(1)}, s32[1,6]{1,0:T(1,128)}, u32[]{:S(2)}) copy-start(s32[1,6]{1,0:T(1,128)} %slot_ref.1) | copy-start | bytes 76
  79.7 12.6 %copy-start.6 = (bf16[192,1024]{1,0:T(8,128)(2,1)S(1)}, bf16[192,1024]{1,0:T(8,128)(2,1)}, u32[]{:S(2)}) copy-start(bf16[192,1024]{1,0:T(8,128)(2,1)} %copy-done.5) | copy-start | bytes 1179652
  81.2 2.3 %collective-permute-start.17 = (bf16[96,4096]{1,0:T(8,128)(2,1)S(1)}, bf16[96,4096]{1,0:T(8,128)(2,1)S(1)}, u32[]{:S(2)}, u32[]{:S(2)}) collective-permute-start(bf16[96,4096]{1,0:T(8,128)(2,1)S(1)} %get-tuple-element.50), channel_id=1, source_target_pairs={{0,1},{1,0},{2,3},{3,2},{4,5},{5,4},{6,7},{7,6},{8,9},{9,8},{10,11... | collective-permute-start | bytes 2359304 | tf_op jit(solution)/shard_map/ppermute | solution.py:801
  81.2 7.4 %collective-permute-start.18 = (bf16[384,256]{1,0:T(8,128)(2,1)S(1)}, bf16[384,256]{1,0:T(8,128)(2,1)S(1)}, u32[]{:S(2)}, u32[]{:S(2)}) collective-permute-start(bf16[384,256]{1,0:T(8,128)(2,1)S(1)} %constant_dynamic-update-slice_fusion.own_ref), channel_id=1, source_target_pairs={{0,2},{2,0},{1,3},{3,1},{4,6},{6,4},{5,7},{7,5},{8,10},{10,8},{9,1... | collective-permute-start | bytes 589832 | tf_op jit(solution)/shard_map/ppermute | solution.py:804
  88.6 19.2 %collective-permute-start.21 = (bf16[96,4096]{1,0:T(8,128)(2,1)S(1)}, bf16[96,4096]{1,0:T(8,128)(2,1)S(1)}, u32[]{:S(2)}, u32[]{:S(2)}) collective-permute-start(bf16[96,4096]{1,0:T(8,128)(2,1)S(1)} %add_pair.3.refs_4_), channel_id=1, source_target_pairs={{0,2},{2,0},{1,3},{3,1},{4,6},{6,4},{5,7},{7,5},{8,10},{10,8},{9,1... | collective-permute-start | bytes 2359304 | tf_op jit(solution)/shard_map/ppermute | solution.py:804
  89.0 1.8 %collective-permute-start.19 = (bf16[2,384,256]{2,1,0:T(8,128)(2,1)S(1)}, bf16[2,384,256]{2,1,0:T(8,128)(2,1)S(1)}, u32[]{:S(2)}, u32[]{:S(2)}) collective-permute-start(bf16[2,384,256]{2,1,0:T(8,128)(2,1)S(1)} %pad_maximum_fusion), channel_id=1, source_target_pairs={{0,1},{1,0},{2,3},{3,2},{4,5},{5,4},{6,7},{7,6},{8,9},{9,8},{10,11... | collective-permute-start | bytes 1179656 | tf_op jit(solution)/shard_map/ppermute | solution.py:801
  92.3 1.0 copy-start.2
  103.0 7.3 %copy-start = (bf16[96,8192]{1,0:T(8,128)(2,1)S(1)}, bf16[96,8192]{1,0:T(8,128)(2,1)}, u32[]{:S(2)}) copy-start(bf16[96,8192]{1,0:T(8,128)(2,1)} %x_ref.1) | copy-start | bytes 4718596
  103.0 7.3 %collective-permute-start.20 = (bf16[96,8192]{1,0:T(8,128)(2,1)S(1)}, bf16[96,8192]{1,0:T(8,128)(2,1)S(1)}, u32[]{:S(2)}, u32[]{:S(2)}) collective-permute-start(bf16[96,8192]{1,0:T(8,128)(2,1)S(1)} %get-tuple-element.52), channel_id=1, source_target_pairs={{0,1},{1,0},{2,3},{3,2},{4,5},{5,4},{6,7},{7,6},{8,9},{9,8},{10,11... | collective-permute-start | bytes 4718600 | tf_op jit(solution)/shard_map/ppermute | solution.py:801
  107.9 2.4 %collective-permute-start.22 = (bf16[96,4096]{1,0:T(8,128)(2,1)S(1)}, bf16[96,4096]{1,0:T(8,128)(2,1)S(1)}, u32[]{:S(2)}, u32[]{:S(2)}) collective-permute-start(bf16[96,4096]{1,0:T(8,128)(2,1)S(1)} %get-tuple-element.54), channel_id=1, source_target_pairs={{0,1},{1,0},{2,3},{3,2},{4,5},{5,4},{6,7},{7,6},{8,9},{9,8},{10,11... | collective-permute-start | bytes 2359304 | tf_op jit(solution)/shard_map/ppermute | solution.py:801

commit v7 on v6

--- a/solution.py
+++ b/solution.py
@@ -24,6 +24,7 @@
 SMEM = pl.BlockSpec(memory_space=pltpu.SMEM)
 VMEM = pl.BlockSpec(memory_space=pltpu.VMEM)
 SMALL = pl.CostEstimate(flops=1024, bytes_accessed=1024, transcendentals=0)
+MEDIUM = pl.CostEstimate(flops=1024, bytes_accessed=4000000, transcendentals=0)
 LARGE = pl.CostEstimate(flops=20000000000, bytes_accessed=200000000, transcendentals=0)
 
 
@@ -534,7 +535,9 @@
 
     def kernel(place_ref, q_ref, pulled_ref, *refs):
         fresh_refs = refs[:known]
-        wo, there_ref, stay_ref, wo_buf, sems = refs[known : known + 5]
+        wo = refs[known]
+        there_refs, refs_after = refs[known + 1 : known + 1 + out_steps], refs[known + 1 + out_steps :]
+        stay_ref, wo_buf, sems = refs_after[:3]
         core, side = place_ref[1], place_ref[2]
 
         def copy(j):
@@ -548,28 +551,29 @@
         if pad:
             pairs.append((jnp.zeros((pad, 2 * HEAD_DIM), BF16), jnp.int32(1 << 20)))
         mixed = attend_block(
-            place_ref, q_ref[...], base(side), pairs, pulled_ref, refs[known + 5 :]
+            place_ref, q_ref[...], base(side), pairs, pulled_ref, refs_after[3:]
         )
         for j in range(2 * out_steps):
             copy(j).wait()
-            out_ref = there_ref if j < out_steps else stay_ref
-            at = (j % out_steps) * wide
-            out_ref[:, at : at + wide] = jnp.dot(
-                mixed, wo_buf[j], preferred_element_type=F32
-            ).astype(BF16)
+            part = jnp.dot(mixed, wo_buf[j], preferred_element_type=F32).astype(BF16)
+            if j < out_steps:
+                there_refs[j][...] = part
+            else:
+                at = (j - out_steps) * wide
+                stay_ref[:, at : at + wide] = part
 
     return pl.pallas_call(
         kernel,
         in_specs=[SMEM] + [VMEM] * (2 + known) + [HBM],
-        out_specs=[VMEM] * 2,
-        out_shape=[shape((rows, half)), shape((rows, half))],
+        out_specs=[VMEM] * (out_steps + 1),
+        out_shape=[shape((rows, wide))] * out_steps + [shape((rows, half))],
         scratch_shapes=[
             pltpu.VMEM((2 * out_steps, depth, wide), BF16),
             pltpu.SemaphoreType.DMA((2 * out_steps,)),
         ]
         + attention_scratch(rows, heads, fresh_rows, pulled.shape[0] * pulled.shape[1]),
         compiler_params=params(30),
-        cost_estimate=SMALL,
+        cost_estimate=MEDIUM,
         name="attend_out",
     )(place, query, pulled, *fresh, w_out)
 
@@ -638,29 +642,28 @@
     )(place, query, pulled, *fresh, w_out, *after)
 
 
-def add_pair(left, right):
+def add_pair(left, pieces):
     rows, width = left.shape
-    step = 16
-
-    def kernel(left_ref, right_ref, out_ref):
-        def block(i, carry):
-            at = pl.ds(pl.multiple_of(i * step, step), step)
-            out_ref[at, :] = (left_ref[at, :].astype(F32) + right_ref[at, :].astype(F32)).astype(
+    count = len(pieces)
+    wide = width // count
+
+    def kernel(left_ref, *refs):
+        out_ref = refs[count]
+        for i in range(count):
+            cols = slice(i * wide, (i + 1) * wide)
+            out_ref[:, cols] = (left_ref[:, cols].astype(F32) + refs[i][...].astype(F32)).astype(
                 BF16
             )
-            return carry
-
-        lax.fori_loop(0, rows // step, block, 0)
 
     return pl.pallas_call(
         kernel,
-        in_specs=[VMEM, VMEM],
+        in_specs=[VMEM] * (1 + count),
         out_specs=VMEM,
         out_shape=shape((rows, width)),
         compiler_params=params(8),
         cost_estimate=SMALL,
         name="add_pair",
-    )(left, right)
+    )(left, *pieces)
 
 
 def finish(place, tokens, own, peer, near, far):
@@ -722,57 +725,54 @@
     )(place, *wanted, *held, *after)
 
 
-def write_pool(place, slots, kv_pool, own, core_new, y_new):
+def write_pool(place, slots, kv_pool, early, late):
     pages, heads = kv_pool.shape[:2]
     new_count = slots.shape[1]
-    side_pages = new_count // 2
-
-    def kernel(place_ref, slot_ref, pool_ref, own_ref, core_ref, y_ref, out_ref, sems):
+    early_rows, late_rows = early[0].shape[0], late[0].shape[0]
+    side_rows = (early_rows + late_rows) // 2
+    total_rows = early_rows + late_rows
+
+    def kernel(place_ref, slot_ref, pool_ref, *refs):
+        early_refs, late_refs, (out_ref, rows_ref) = refs[:3], refs[3:6], refs[6:]
         me, side = place_ref[0], place_ref[2]
-        sources = (own_ref, core_ref.at[0], y_ref, core_ref.at[1])
+
+        def source(group, i):
+            own, y, core = group
+            return (own, core.at[0], y, core.at[1])[i]
+
+        for i in range(heads):
+            rows_ref[i, :early_rows] = source(early_refs, i)[...]
+            rows_ref[i, early_rows:] = source(late_refs, i)[...]
         for p in range(pages):
             found = jnp.int32(-1)
             for j in range(new_count):
                 found = jnp.where(slot_ref[0, j] == me * pages + p, j, found)
-            far = (found >= side_pages).astype(jnp.int32)
-            inner = jnp.maximum(found - far * side_pages, 0)
-
-            @pl.when(found >= 0)
-            def _():
-                for i in range(heads):
-                    origin = side if i < 2 else 1 - side
-                    start = (jnp.bitwise_xor(far, origin) * side_pages + inner) * PAGE
-                    pltpu.make_async_copy(
-                        sources[i].at[pl.ds(pl.multiple_of(start, PAGE), PAGE)],
-                        out_ref.at[p, jnp.bitwise_xor(me, i)],
-                        sems.at[p * heads + i],
-                    ).start()
-
-            @pl.when(found < 0)
-            def _():
-                for i in range(heads):
-                    at = jnp.bitwise_xor(me, i)
-                    pltpu.make_async_copy(
-                        pool_ref.at[p, at], out_ref.at[p, at], sems.at[p * heads + i]
-                    ).start()
-
-        for p in range(pages):
+            first = jnp.maximum(found, 0) * PAGE
+            far = (first >= side_rows).astype(jnp.int32)
+            inner = first - far * side_rows
             for i in range(heads):
+                origin = side if i < 2 else 1 - side
+                start = jnp.bitwise_xor(far, origin) * side_rows + inner
                 at = jnp.bitwise_xor(me, i)
-                pltpu.make_async_copy(
-                    pool_ref.at[p, at], out_ref.at[p, at], sems.at[p * heads + i]
-                ).wait()
+
+                @pl.when(found >= 0)
+                def _():
+                    out_ref[p, at] = rows_ref[i, pl.ds(pl.multiple_of(start, PAGE), PAGE), :]
+
+                @pl.when(found < 0)
+                def _():
+                    out_ref[p, at] = pool_ref[p, at]
 
     return pl.pallas_call(
         kernel,
-        in_specs=[SMEM, SMEM] + [ANY] * 4,
-        out_specs=ANY,
+        in_specs=[SMEM, SMEM] + [VMEM] * 7,
+        out_specs=VMEM,
         out_shape=shape(kv_pool.shape),
-        scratch_shapes=[pltpu.SemaphoreType.DMA((pages * heads,))],
-        compiler_params=params(8),
+        scratch_shapes=[pltpu.VMEM((heads, total_rows, kv_pool.shape[3]), BF16)],
+        compiler_params=params(12),
         cost_estimate=SMALL,
         name="write_pool",
-    )(place, slots, kv_pool, own, core_new, y_new)
+    )(place, slots, kv_pool, *early, *late)
 
 
 def chip_pair_body(
@@ -847,37 +847,33 @@
     wide = first.shape[1] // 4
     pieces = [over_core(first[:, i * wide : (i + 1) * wide]) for i in range(4)]
     q_first, kv_first = project_held(first, pieces, wq, wkv)
-    there, stay = attend_out(
-        scalars, q_first, [kv_local, kv_first],
-        [local_base, first_base], first_base, pulled, w_out,
-    )
-    there = tie(there, second)
-    first_mix = add_pair(stay, over_core(there))
+    early_own = jnp.concatenate([kv_local, kv_first], axis=0)
+    early_y = over_y(early_own)
+    *there, stay = attend_out(
+        scalars, q_first, [kv_local, kv_first], [local_base, first_base], first_base, pulled, w_out
+    )
+    first_mix = add_pair(stay, [over_core(tie(part, early_y)) for part in there])
     first_sum = over_y(first_mix)
 
     second = tie(second, first_mix)
     q_second, kv_second = project_far(place, second, over_core(second), w_query, w_keyvalue, [])
     fresh = [kv_local, kv_first, kv_second]
     bases = [local_base, first_base, second_base]
-    there, stay = attend_out(
-        scalars, q_second, fresh, bases, second_base, pulled, w_out
-    )
-    there = tie(there, first_sum)
-    second_mix = add_pair(stay, over_core(there))
-
-
-    new_own = jnp.concatenate(fresh, axis=0)
-    y_new = over_y(new_own)
-    core_new = over_core(jnp.stack([new_own, y_new]))
-    second_sum = over_y(tie(second_mix, y_new))
-
-    pool_out = write_pool(place, new_slot, kv_pool, new_own, core_new, y_new)
+    *there, stay = attend_out(scalars, q_second, fresh, bases, second_base, pulled, w_out)
+    second_mix = add_pair(stay, [over_core(part) for part in there])
+    late_y = over_y(kv_second)
+    second_sum = over_y(tie(second_mix, late_y, first_sum))
 
     own_part, peer_part = local_rows(
-        scalars, q_local, fresh, bases, local_base, pulled, w_out,
-        [second_mix, pool_out],
+        scalars, q_local, fresh, bases, local_base, pulled, w_out, [second_mix]
     )
     peer_part = over_core(peer_part)
+
+    early = over_core(jnp.stack([early_own, early_y]))
+    late = over_core(jnp.stack([kv_second, late_y]))
+    pool_out = write_pool(
+        place, new_slot, kv_pool, [early_own, early_y, early], [kv_second, late_y, late]
+    )
 
     near = jnp.where(is_first, first_sum, second_sum)
     far = over_core(jnp.where(is_first, second_sum, first_sum))

time: 113 us -> 110 us (0.973)
  waiting for transfers between devices: 31 us -> 21.9 us
  starting transfers between devices: 17.9 us -> 25.7 us
    ppermute x12 -> x19, waiting for transfers between devices: 11.4 us -> 5.83 us  [over_core(): return lax.ppermute(x, 'tensor', [(0, 1), (1, 0), (2, 3), (3, 2)])]
    ppermute x5 -> x6, starting transfers between devices: 3.19 us -> 8.32 us  [over_y(): return lax.ppermute(x, 'tensor', [(0, 2), (2, 0), (1, 3), (3, 1)])]
    ppermute x12 -> x19, starting transfers between devices: 2.6 us -> 5.23 us  [over_core(): return lax.ppermute(x, 'tensor', [(0, 1), (1, 0), (2, 3), (3, 2)])]
    ppermute x5 -> x6, waiting for transfers between devices: 11 us -> 9.07 us  [over_y(): return lax.ppermute(x, 'tensor', [(0, 2), (2, 0), (1, 3), (3, 1)])]
    all_to_all x1, waiting for transfers between devices: 7.94 us -> 6.25 us  [chip_pair_body(): lax.all_to_all(picked, 'replica', split_axis=0, concat_axis=0, tiled=True)]
    pallas_call x2, Pallas kernels: 15.3 us -> 14.1 us  [attend_out(): pl.pallas_call(kernel, in_specs=[SMEM] + [VMEM] * (2 + known) + [HBM], ou...]
    unnamed x24 -> x21, local copies, waits for them, and re-layouts: 3.36 us -> 2.32 us
  transfers between devices with their start and end apart: 24 -> 32, of which waited for: 15 -> 17; matrix products, arithmetic and copies ran while one was open for 3% -> 3% of each run, Pallas kernels for 44% -> 45%
where the time goes in v7:
time: 110 us
  Pallas kernels  56 us (51%)
  starting transfers between devices  25.7 us (23%)
  waiting for transfers between devices  21.9 us (20%)
  local copies, waits for them, and re-layouts  3.87 us (4%)
  other arithmetic  1.46 us (1%)
    pallas_call x2, Pallas kernels, attend_out(): pl.pallas_call(kernel, in_specs=[SMEM] + [VMEM] * (2 + known) + [HBM], ou...  14.1 us
    pallas_call x1, Pallas kernels, local_rows(): pl.pallas_call(kernel, in_specs=[SMEM] + [VMEM] * (2 + known) + [HBM] + [...  10.2 us
    pallas_call x1, Pallas kernels, project_local(): pl.pallas_call(kernel, in_specs=[SMEM] + [VMEM] * 4 + [HBM] * 2 + [ANY] *...  9.27 us
    ppermute x6, waiting for transfers between devices, over_y(): return lax.ppermute(x, 'tensor', [(0, 2), (2, 0), (1, 3), (3, 1)])  9.07 us
    pallas_call x1, Pallas kernels, project_far(): pl.pallas_call(kernel, in_specs=[SMEM] + [VMEM] * 2 + [HBM] * 2 + [ANY] *...  8.84 us
    ppermute x6, starting transfers between devices, over_y(): return lax.ppermute(x, 'tensor', [(0, 2), (2, 0), (1, 3), (3, 1)])  8.32 us
    all_to_all x1, waiting for transfers between devices, chip_pair_body(): lax.all_to_all(picked, 'replica', split_axis=0, concat_axis=0, tiled=True)  6.25 us
    ppermute x19, waiting for transfers between devices, over_core(): return lax.ppermute(x, 'tensor', [(0, 1), (1, 0), (2, 3), (3, 2)])  5.83 us
  transfers between devices with their start and end apart: 32, of which 17 were waited for; matrix products, arithmetic and copies ran while one was open for 3% of the time, Pallas kernels for 45%

profile of v7, /device:TPU:0, one launch (start us, length us, event | category | flops | bytes accessed | tf_op | source)
XLA Modules:
  0.0 109.8 jit_solution(11583646570798629003)
XLA Ops:
  0.7 0.1 pad_add_fusion.place_ref
  0.7 3.7 %prepare.1 = (bf16[96,4096]{1,0:T(8,128)(2,1)}, bf16[96,4096]{1,0:T(8,128)(2,1)S(1)}, bf16[4,64,256]{2,1,0:T(8,128)(2,1)S(1)}, bf16[4,64,256]{2,1,0:T(8,128)(2,1...) custom-call(s32[4]{0:T(128)S(1)} %pad_add_fusion.place_ref, bf16[96,8192]{1,0:T(8,128)(2,1)} %x_ref.1, ...), custom_call_target="tpu_custom_call" | custom-call | flops 1024 | bytes 1024 | tf_op jit(solution)/shard_map/prepare/pallas_call | solution.py:233
  4.4 0.5 collective-permute-start
  4.9 2.6 %collective-permute-start.6 = (bf16[4,64,256]{2,1,0:T(8,128)(2,1)S(1)}, bf16[4,64,256]{2,1,0:T(8,128)(2,1)S(1)}, u32[]{:S(2)}, u32[]{:S(2)}) collective-permute-start(bf16[4,64,256]{2,1,0:T(8,128)(2,1)S(1)} %get-tuple-element.40), channel_id=1, source_target_pairs={{0,2},{1,3},{2,0},{3,1},{4,6},{5,7},{6,4},{7,5},{8,10},{9,11},{10,... | collective-permute-start | bytes 393224 | tf_op jit(solution)/shard_map/ppermute | solution.py:818
  7.6 3.8 %collective-permute-start.2 = (s32[1,2,16]{2,1,0:T(2,128)}, s32[1,2,16]{2,1,0:T(2,128)S(1)}, u32[]{:S(2)}, u32[]{:S(2)}) collective-permute-start(s32[1,2,16]{2,1,0:T(2,128)} %bitcast.15), channel_id=1, source_target_pairs={{0,12},{4,0},{8,4},{12,8},{1,13},{5,1},{9,5},{13,9},{2,14},{6,2},{... | collective-permute-start | bytes 392 | tf_op jit(solution)/shard_map/ppermute | solution.py:814
  11.4 0.8 reshape.7
  12.2 0.7 concatenate.7.refs_1_.place_ref
  12.9 1.0 collective-permute-start.4
  13.9 0.2 collective-permute-done.7.refs_7_
  14.2 0.1 collective-permute-start.5
  14.3 0.4 collective-permute-start.1
  14.7 1.2 %broadcast_select_fusion.2 = (bf16[96,4096]{1,0:T(8,128)(2,1)S(1)}, bf16[96,4096]{1,0:T(8,128)(2,1)S(1)}) fusion(bf16[96,4096]{1,0:T(8,128)(2,1)S(1)} %collective-permute-done.near_peer, bf16[96,4096]{1,0:T(8,128)(2,1)} %get-tuple-element.36.near_own, pred[]{:T(512)S(6)} %eq.5), kind=kLoop, calls=%fused_computation.2 | loop fusion | flops 786432 | bytes 3145729 | tf_op jit(solution)/shard_map/jit(_where)/select_n | solution.py:825
  15.9 1.7 %collective-permute-start.8 = (bf16[96,4096]{1,0:T(8,128)(2,1)S(1)}, bf16[96,4096]{1,0:T(8,128)(2,1)S(1)}, u32[]{:S(2)}, u32[]{:S(2)}) collective-permute-start(bf16[96,4096]{1,0:T(8,128)(2,1)S(1)} %get-tuple-element.73.refs_8_), channel_id=1, source_target_pairs={{0,2},{2,0},{1,3},{3,1},{4,6},{6,4},{5,7},{7,5},{8,10},{10,8},{9,1... | collective-permute-start | bytes 2359304 | tf_op jit(solution)/shard_map/ppermute | solution.py:804
  17.6 0.4 collective-permute-start.13
  18.0 0.5 collective-permute-done.4.refs_3_
  18.5 1.8 %pick_pages.1.refs_0_ = bf16[4,8,64,256]{3,2,1,0:T(8,128)(2,1)} custom-call(s32[4]{0:T(128)S(1)} %pad_add_fusion.place_ref, s32[1,2,16]{2,1,0:T(2,128)S(1)} %bitcast.18, s32[1,2,16]{2,1,0:T(2,128)S(1)} %collective-permute-done.2.refs_1_, s32[1,2,16]{2,1,0:T(2,128)} %collective-permute-done.3.refs_2_, s32[1,2,16]{2,1,0:T(2,128)S(1)} %collective-permute-done.4.refs_3_, ...), custom_call_target="tpu_custom_call" | custom-call | flops 1024 | bytes 1024 | tf_op jit(solution)/shard_map/pick_pages/pallas_call | solution.py:717
  20.3 4.5 %all-to-all-start = ((bf16[4,8,64,256]{3,2,1,0:T(8,128)(2,1)}), bf16[4,8,64,256]{3,2,1,0:T(8,128)(2,1)S(1)}, u32[]{:S(2)}, u32[]{:S(2)}) async-start(bf16[4,8,64,256]{3,2,1,0:T(8,128)(2,1)} %pick_pages.1.refs_0_), calls=%async_computation | async-start | bytes 2097152 | tf_op jit(solution)/shard_map/all_to_all | solution.py:830
  24.8 1.1 %copy-done.3 = bf16[96,4096]{1,0:T(8,128)(2,1)S(1)} copy-done((bf16[96,4096]{1,0:T(8,128)(2,1)S(1)}, bf16[96,4096]{1,0:T(8,128)(2,1)}, u32[]{:S(2)}) %copy-start.3) | copy-done | bytes 786456
  26.0 1.1 %copy-done.9 = bf16[96,4096]{1,0:T(8,128)(2,1)S(1)} copy-done((bf16[96,4096]{1,0:T(8,128)(2,1)S(1)}, bf16[96,4096]{1,0:T(8,128)(2,1)}, u32[]{:S(2)}) %copy-start.9) | copy-done | bytes 786456
  27.1 9.3 %project_local.1 = (bf16[192,1024]{1,0:T(8,128)(2,1)S(1)}, bf16[192,256]{1,0:T(8,128)(2,1)S(1)}, bf16[8,1024,1024]{2,1,0:T(8,128)(2,1)S(1)}, bf16[8,1024,256]{2,1,0:T(8,128)(2,1)S(1)}) custom-call(s32[4]{0:T(128)S(1)} %pad_add_fusion.place_ref, bf16[96,4096]{1,0:T(8,128)(2,1)} %get-tuple-element.36.near_own, bf16[96,4096]{1,0:T(8,128)(2,1)S(1)} %copy-done.3, ...), custom_call_target="tpu_custom_call" | custom-call | flops 20000000000 | bytes 200000000 | tf_op jit(solution)/shard_map/project_local/pallas_call | solution.py:287
  36.4 0.1 collective-permute-start.10
  36.5 0.5 collective-permute-start.11
  37.0 0.1 collective-permute-start.12
  37.1 0.4 collective-permute-start.9
  37.5 0.4 collective-permute-done.10.refs_1_
  38.0 0.3 collective-permute-done.11.refs_2_
  38.2 0.3 collective-permute-done.12.refs_3_
  38.5 0.3 collective-permute-done.9.refs_0_
  38.8 3.6 %project_held.1 = (bf16[96,1024]{1,0:T(8,128)(2,1)S(1)}, bf16[96,256]{1,0:T(8,128)(2,1)S(1)}) custom-call(bf16[96,4096]{1,0:T(8,128)(2,1)S(1)} %collective-permute-done.8.near_ref, bf16[96,1024]{1,0:T(8,128)(2,1)S(1)} %collective-permute-done.9.refs_0_, bf16[96,1024]{1,0:T(8,128)(2,1)S(1)} %collective-permute-done.10.refs_1_, ...), custom_call_target="tpu_custom_call" | custom-call | flops 1024 | bytes 1024 | tf_op jit(solution)/shard_map/project_held/pallas_call | solution.py:472
  42.5 1.7 %collective-permute-start.14 = (bf16[288,256]{1,0:T(8,128)(2,1)S(1)}, bf16[288,256]{1,0:T(8,128)(2,1)S(1)}, u32[]{:S(2)}, u32[]{:S(2)}) collective-permute-start(bf16[288,256]{1,0:T(8,128)(2,1)S(1)} %constant_dynamic-update-slice_fusion.refs_0_), channel_id=1, source_target_pairs={{0,2},{2,0},{1,3},{3,1},{4,6},{6,4},{5,7},{7,5},{8,10},{10,8},{9,1... | collective-permute-start | bytes 442376 | tf_op jit(solution)/shard_map/ppermute | solution.py:804
  44.1 6.3 %all-to-all-done.pulled_ref = bf16[4,8,64,256]{3,2,1,0:T(8,128)(2,1)S(1)} async-done(((bf16[4,8,64,256]{3,2,1,0:T(8,128)(2,1)}), bf16[4,8,64,256]{3,2,1,0:T(8,128)(2,1)S(1)}, u32[]{:S(2)}, u32[]{:S(2)}) %all-to-all-start) | async-done | bytes 1048608 | tf_op jit(solution)/shard_map/all_to_all | solution.py:830
  50.4 7.0 %attend_out.2 = (bf16[96,1024]{1,0:T(8,128)(2,1)S(1)}, bf16[96,1024]{1,0:T(8,128)(2,1)S(1)}, bf16[96,1024]{1,0:T(8,128)(2,1)S(1)}, bf16[96,1024]{1,0:T(8,128)(2,1)S(1)}, bf16[96,4096]{1,0:T(8,128)(2,1)S(1)}) custom-call(s32[40]{0:T(128)S(1)} %concatenate.7.refs_1_.place_ref, bf16[96,1024]{1,0:T(8,128)(2,1)S(1)} %get-tuple-element.49.q_ref, ...), custom_call_target="tpu_custom_call" | custom-call | flops 1024 | bytes 4000000 | tf_op jit(solution)/shard_map/attend_out/pallas_call | solution.py:565
  57.5 0.5 collective-permute-start.17
  58.0 0.1 collective-permute-start.16
  58.1 0.4 collective-permute-start.15
  58.5 0.4 collective-permute-done.18.refs_3_
  58.9 0.3 collective-permute-done.17.refs_2_
  59.2 0.3 collective-permute-done.16.refs_1_
  59.5 0.3 collective-permute-done.15.refs_0_
  59.8 0.2 add_pair.2
  60.0 0.3 collective-permute-start.19
  60.3 1.5 %collective-permute-start.25 = (bf16[96,4096]{1,0:T(8,128)(2,1)S(1)}, bf16[96,4096]{1,0:T(8,128)(2,1)S(1)}, u32[]{:S(2)}, u32[]{:S(2)}) collective-permute-start(bf16[96,4096]{1,0:T(8,128)(2,1)S(1)} %add_pair.2), channel_id=1, source_target_pairs={{0,2},{2,0},{1,3},{3,1},{4,6},{6,4},{5,7},{7,5},{8,10},{10,8},{9,1... | collective-permute-start | bytes 2359304 | tf_op jit(solution)/shard_map/ppermute | solution.py:804
  61.8 0.7 collective-permute-done.19.far_ref
  62.5 8.8 %project_far.1 = (bf16[96,1024]{1,0:T(8,128)(2,1)S(1)}, bf16[96,256]{1,0:T(8,128)(2,1)S(1)}) custom-call(s32[4]{0:T(128)S(1)} %pad_add_fusion.place_ref, bf16[96,4096]{1,0:T(8,128)(2,1)} %collective-permute-done.13.near_ref, bf16[96,4096]{1,0:T(8,128)(2,1)S(1)} %collective-permute-done.19.far_ref, bf16[8192,1024]{1,0:T(8,128)(2,1)} %wq.3, bf16[8192,256]{1,0:T(8,128)(2,1)} %wkv.3), custom_call_target="tpu_custom_call" | custom-call | flops 1024 | bytes 1024 | tf_op jit(solution)/shard_map/project_far/pallas_call | solution.py:508
  71.4 7.1 %attend_out.3 = (bf16[96,1024]{1,0:T(8,128)(2,1)S(1)}, bf16[96,1024]{1,0:T(8,128)(2,1)S(1)}, bf16[96,1024]{1,0:T(8,128)(2,1)S(1)}, bf16[96,1024]{1,0:T(8,128)(2,1)S(1)}, bf16[96,4096]{1,0:T(8,128)(2,1)S(1)}) custom-call(s32[40]{0:T(128)S(1)} %concatenate.7.refs_1_.place_ref, bf16[96,1024]{1,0:T(8,128)(2,1)S(1)} %get-tuple-element.61.q_ref, ...), custom_call_target="tpu_custom_call" | custom-call | flops 1024 | bytes 4000000 | tf_op jit(solution)/shard_map/attend_out/pallas_call | solution.py:565
  78.5 0.3 collective-permute-start.20
  78.8 0.3 collective-permute-start.21
  79.1 0.2 collective-permute-start.22
  79.3 0.3 collective-permute-start.23
  79.6 0.4 collective-permute-done.20.refs_0_
  80.0 1.5 %collective-permute-start.26 = (bf16[96,256]{1,0:T(8,128)(2,1)S(1)}, bf16[96,256]{1,0:T(8,128)(2,1)S(1)}, u32[]{:S(2)}, u32[]{:S(2)}) collective-permute-start(bf16[96,256]{1,0:T(8,128)(2,1)S(1)} %get-tuple-element.60.refs_2_.refs_3_), channel_id=1, source_target_pairs={{0,2},{2,0},{1,3},{3,1},{4,6},{6,4},{5,7},{7,5},{8,10},{10,8},{9,1... | collective-permute-start | bytes 147464 | tf_op jit(solution)/shard_map/ppermute | solution.py:804
  81.5 0.2 add_pair.3.refs_4_
  81.8 2.3 %collective-permute-done.26.refs_4_ = bf16[96,256]{1,0:T(8,128)(2,1)S(1)} collective-permute-done((bf16[96,256]{1,0:T(8,128)(2,1)S(1)}, bf16[96,256]{1,0:T(8,128)(2,1)S(1)}, u32[]{:S(2)}, u32[]{:S(2)}) %collective-permute-start.26) | collective-permute-done | bytes 49184 | tf_op jit(solution)/shard_map/ppermute | solution.py:804
  84.1 1.5 %collective-permute-start.27 = (bf16[96,4096]{1,0:T(8,128)(2,1)S(1)}, bf16[96,4096]{1,0:T(8,128)(2,1)S(1)}, u32[]{:S(2)}, u32[]{:S(2)}) collective-permute-start(bf16[96,4096]{1,0:T(8,128)(2,1)S(1)} %add_pair.3.refs_4_), channel_id=1, source_target_pairs={{0,2},{2,0},{1,3},{3,1},{4,6},{6,4},{5,7},{7,5},{8,10},{10,8},{9,1... | collective-permute-start | bytes 2359304 | tf_op jit(solution)/shard_map/ppermute | solution.py:804
  85.6 10.2 %local_rows.1 = (bf16[96,8192]{1,0:T(8,128)(2,1)S(1)}, bf16[96,8192]{1,0:T(8,128)(2,1)S(1)}) custom-call(s32[40]{0:T(128)S(1)} %concatenate.7.refs_1_.place_ref, bf16[192,1024]{1,0:T(8,128)(2,1)S(1)} %copy-done.5, bf16[4,8,64,256]{3,2,1,0:T(8,128)(2,1)S(1)} %all-to-all-done.pulled_ref, bf16[192,256]{1,0:T(8,128)(2,1)S(1)} %get-tuple-element.44.refs_0_, ...), custom_call_target="tpu_custom_call" | custom-call | flops 1024 | bytes 1024 | tf_op jit(solution)/shard_map/local_rows/pallas_call | solution.py:628
  95.8 0.1 collective-permute-start.24
  95.9 6.7 %collective-permute-done.27 = bf16[96,4096]{1,0:T(8,128)(2,1)S(1)} collective-permute-done((bf16[96,4096]{1,0:T(8,128)(2,1)S(1)}, bf16[96,4096]{1,0:T(8,128)(2,1)S(1)}, u32[]{:S(2)}, u32[]{:S(2)}) %collective-permute-start.27) | collective-permute-done | bytes 786464 | tf_op jit(solution)/shard_map/ppermute | solution.py:804
  102.6 0.1 broadcast_select_fusion
  102.8 0.6 collective-permute-start.29
  103.4 0.1 collective-permute-start.30
  103.5 2.0 %collective-permute-done.29.refs_2_ = bf16[2,288,256]{2,1,0:T(8,128)(2,1)S(1)} collective-permute-done((bf16[2,288,256]{2,1,0:T(8,128)(2,1)S(1)}, bf16[2,288,256]{2,1,0:T(8,128)(2,1)S(1)}, u32[]{:S(2)}, u32[]{:S(2)}) %collective-permute-start.29) | collective-permute-done | bytes 294944 | tf_op jit(solution)/shard_map/ppermute | solution.py:801
  105.5 0.1 collective-permute-done.30.refs_5_
  105.7 1.6 %write_pool.1 = bf16[4,4,64,256]{3,2,1,0:T(8,128)(2,1)} custom-call(s32[4]{0:T(128)S(1)} %pad_add_fusion.place_ref, s32[1,6]{1,0:T(1,128)S(1)} %copy-done.7, bf16[4,4,64,256]{3,2,1,0:T(8,128)(2,1)S(1)} %copy-done.1, bf16[288,256]{1,0:T(8,128)(2,1)S(1)} %constant_dynamic-update-slice_fusion.refs_0_, bf16[288,256]{1,0:T(8,128)(2,1)S(1)} %collective-permute-done.14.refs_1_, ...), custom_call_target="tpu_custom_call" | custom-call | flops 1024 | bytes 1024 | tf_op jit(solution)/shard_map/write_pool/pallas_call | solution.py:766
  107.2 2.5 %finish.1 = bf16[96,8192]{1,0:T(8,128)(2,1)} custom-call(s32[4]{0:T(128)S(1)} %pad_add_fusion.place_ref, bf16[96,8192]{1,0:T(8,128)(2,1)S(1)} %copy-done, bf16[96,8192]{1,0:T(8,128)(2,1)S(1)} %get-tuple-element.67.own_ref, bf16[96,8192]{1,0:T(8,128)(2,1)S(1)} %collective-permute-done.24.peer_ref, bf16[96,4096]{1,0:T(8,128)(2,1)S(1)} %get-tuple-element.71.near_ref, ...), custom_call_target="tpu_custom_call" | custom-call | flops 1024 | bytes 1024 | tf_op jit(solution)/shard_map/finish/pallas_call | solution.py:688
  (42 shorter events, 0.4 us)
Async XLA Ops:
  0.6 17.9 %copy-start.6 = (s32[1,16,2]{1,2,0:T(2,128)S(1)}, s32[1,16,2]{1,2,0:T(2,128)}, u32[]{:S(2)}) copy-start(s32[1,16,2]{1,2,0:T(2,128)} %param.17) | copy-start | bytes 388
  4.4 11.5 %copy-start.8 = (bf16[96,4096]{1,0:T(8,128)(2,1)}, bf16[96,4096]{1,0:T(8,128)(2,1)S(1)}, u32[]{:S(2)}) copy-start(bf16[96,4096]{1,0:T(8,128)(2,1)S(1)} %get-tuple-element.37.far_own) | copy-start | bytes 2359300
  4.4 9.9 %collective-permute-start = (bf16[96,4096]{1,0:T(8,128)(2,1)S(1)}, bf16[96,4096]{1,0:T(8,128)(2,1)S(1)}, u32[]{:S(2)}, u32[]{:S(2)}) collective-permute-start(bf16[96,4096]{1,0:T(8,128)(2,1)S(1)} %get-tuple-element.37.far_own), channel_id=1, source_target_pairs={{0,1},{1,0},{2,3},{3,2},{4,5},{5,4},{6,7},{7,6},{8,9},{9,8},{10,11... | collective-permute-start | bytes 2359304 | tf_op jit(solution)/shard_map/ppermute | solution.py:801
  4.9 8.0 %collective-permute-start.6 = (bf16[4,64,256]{2,1,0:T(8,128)(2,1)S(1)}, bf16[4,64,256]{2,1,0:T(8,128)(2,1)S(1)}, u32[]{:S(2)}, u32[]{:S(2)}) collective-permute-start(bf16[4,64,256]{2,1,0:T(8,128)(2,1)S(1)} %get-tuple-element.40), channel_id=1, source_target_pairs={{0,2},{1,3},{2,0},{3,1},{4,6},{5,7},{6,4},{7,5},{8,10},{9,11},{10,... | collective-permute-start | bytes 393224 | tf_op jit(solution)/shard_map/ppermute | solution.py:818
  7.5 6.6 %collective-permute-start.7 = (bf16[4,64,256]{2,1,0:T(8,128)(2,1)S(1)}, bf16[4,64,256]{2,1,0:T(8,128)(2,1)S(1)}, u32[]{:S(2)}, u32[]{:S(2)}) collective-permute-start(bf16[4,64,256]{2,1,0:T(8,128)(2,1)S(1)} %get-tuple-element.41), channel_id=1, source_target_pairs={{0,3},{1,2},{2,1},{3,0},{4,7},{5,6},{6,5},{7,4},{8,11},{9,10},{10,... | collective-permute-start | bytes 393224 | tf_op jit(solution)/shard_map/ppermute | solution.py:818
  7.6 8.3 %collective-permute-start.2 = (s32[1,2,16]{2,1,0:T(2,128)}, s32[1,2,16]{2,1,0:T(2,128)S(1)}, u32[]{:S(2)}, u32[]{:S(2)}) collective-permute-start(s32[1,2,16]{2,1,0:T(2,128)} %bitcast.15), channel_id=1, source_target_pairs={{0,12},{4,0},{8,4},{12,8},{1,13},{5,1},{9,5},{13,9},{2,14},{6,2},{... | collective-permute-start | bytes 392 | tf_op jit(solution)/shard_map/ppermute | solution.py:814
  11.4 6.2 %collective-permute-start.3 = (s32[1,2,16]{2,1,0:T(2,128)}, s32[1,2,16]{2,1,0:T(2,128)}, u32[]{:S(2)}, u32[]{:S(2)}) collective-permute-start(s32[1,2,16]{2,1,0:T(2,128)} %bitcast.16), channel_id=1, source_target_pairs={{0,8},{4,12},{8,0},{12,4},{1,9},{5,13},{9,1},{13,5},{2,10},{6,14},... | collective-permute-start | bytes 392 | tf_op jit(solution)/shard_map/ppermute | solution.py:814
  12.9 5.6 %collective-permute-start.4 = (s32[1,2,16]{2,1,0:T(2,128)}, s32[1,2,16]{2,1,0:T(2,128)S(1)}, u32[]{:S(2)}, u32[]{:S(2)}) collective-permute-start(s32[1,2,16]{2,1,0:T(2,128)} %bitcast.17), channel_id=1, source_target_pairs={{0,4},{4,8},{8,12},{12,0},{1,5},{5,9},{9,13},{13,1},{2,6},{6,10},{... | collective-permute-start | bytes 392 | tf_op jit(solution)/shard_map/ppermute | solution.py:814
  14.2 4.3 %collective-permute-start.5 = (bf16[4,64,256]{2,1,0:T(8,128)(2,1)}, bf16[4,64,256]{2,1,0:T(8,128)(2,1)S(1)}, u32[]{:S(2)}, u32[]{:S(2)}) collective-permute-start(bf16[4,64,256]{2,1,0:T(8,128)(2,1)} %get-tuple-element.39), channel_id=1, source_target_pairs={{0,1},{1,0},{2,3},{3,2},{4,5},{5,4},{6,7},{7,6},{8,9},{9,8},{10,11... | collective-permute-start | bytes 393224 | tf_op jit(solution)/shard_map/ppermute | solution.py:818
  14.3 6.0 %copy-start.2 = (bf16[96,4096]{1,0:T(8,128)(2,1)}, bf16[96,4096]{1,0:T(8,128)(2,1)S(1)}, u32[]{:S(2)}) copy-start(bf16[96,4096]{1,0:T(8,128)(2,1)S(1)} %collective-permute-done.near_peer) | copy-start | bytes 2359300
  14.3 10.5 %collective-permute-start.1 = (bf16[96,4096]{1,0:T(8,128)(2,1)}, bf16[96,4096]{1,0:T(8,128)(2,1)}, u32[]{:S(2)}, u32[]{:S(2)}) collective-permute-start(bf16[96,4096]{1,0:T(8,128)(2,1)} %get-tuple-element.36.near_own), channel_id=1, source_target_pairs={{0,1},{1,0},{2,3},{3,2},{4,5},{5,4},{6,7},{7,6},{8,9},{9,8},{10,11... | collective-permute-start | bytes 2359304 | tf_op jit(solution)/shard_map/ppermute | solution.py:801
  15.9 20.4 %collective-permute-start.8 = (bf16[96,4096]{1,0:T(8,128)(2,1)S(1)}, bf16[96,4096]{1,0:T(8,128)(2,1)S(1)}, u32[]{:S(2)}, u32[]{:S(2)}) collective-permute-start(bf16[96,4096]{1,0:T(8,128)(2,1)S(1)} %get-tuple-element.73.refs_8_), channel_id=1, source_target_pairs={{0,2},{2,0},{1,3},{3,1},{4,6},{6,4},{5,7},{7,5},{8,10},{10,8},{9,1... | collective-permute-start | bytes 2359304 | tf_op jit(solution)/shard_map/ppermute | solution.py:804
  17.6 42.4 %collective-permute-start.13 = (bf16[96,4096]{1,0:T(8,128)(2,1)S(1)}, bf16[96,4096]{1,0:T(8,128)(2,1)}, u32[]{:S(2)}, u32[]{:S(2)}) collective-permute-start(bf16[96,4096]{1,0:T(8,128)(2,1)S(1)} %get-tuple-element.72.refs_9_), channel_id=1, source_target_pairs={{0,2},{2,0},{1,3},{3,1},{4,6},{6,4},{5,7},{7,5},{8,10},{10,8},{9,1... | collective-permute-start | bytes 2359304 | tf_op jit(solution)/shard_map/ppermute | solution.py:804
  20.3 30.1 %all-to-all-start = ((bf16[4,8,64,256]{3,2,1,0:T(8,128)(2,1)}), bf16[4,8,64,256]{3,2,1,0:T(8,128)(2,1)S(1)}, u32[]{:S(2)}, u32[]{:S(2)}) async-start(bf16[4,8,64,256]{3,2,1,0:T(8,128)(2,1)} %pick_pages.1.refs_0_), calls=%async_computation | async-start | bytes 2097152 | tf_op jit(solution)/shard_map/all_to_all | solution.py:830
  24.8 1.1 %copy-start.3 = (bf16[96,4096]{1,0:T(8,128)(2,1)S(1)}, bf16[96,4096]{1,0:T(8,128)(2,1)}, u32[]{:S(2)}) copy-start(bf16[96,4096]{1,0:T(8,128)(2,1)} %copy-done.2) | copy-start | bytes 2359300
  25.9 1.1 %copy-start.9 = (bf16[96,4096]{1,0:T(8,128)(2,1)S(1)}, bf16[96,4096]{1,0:T(8,128)(2,1)}, u32[]{:S(2)}) copy-start(bf16[96,4096]{1,0:T(8,128)(2,1)} %copy-done.8) | copy-start | bytes 2359300
  36.4 6.1 %copy-start.4 = (bf16[192,1024]{1,0:T(8,128)(2,1)}, bf16[192,1024]{1,0:T(8,128)(2,1)S(1)}, u32[]{:S(2)}) copy-start(bf16[192,1024]{1,0:T(8,128)(2,1)S(1)} %get-tuple-element.43.q_ref) | copy-start | bytes 1179652
  36.4 1.5 %collective-permute-start.10 = (bf16[96,1024]{1,0:T(8,128)(2,1)S(1)}, bf16[96,1024]{1,0:T(8,128)(2,1)S(1)}, u32[]{:S(2)}, u32[]{:S(2)}) collective-permute-start(bf16[96,1024]{1,0:T(8,128)(2,1)S(1)} %get-tuple-element.76), channel_id=1, source_target_pairs={{0,1},{1,0},{2,3},{3,2},{4,5},{5,4},{6,7},{7,6},{8,9},{9,8},{10,11... | collective-permute-start | bytes 589832 | tf_op jit(solution)/shard_map/ppermute | solution.py:801
  36.5 1.7 %collective-permute-start.11 = (bf16[96,1024]{1,0:T(8,128)(2,1)S(1)}, bf16[96,1024]{1,0:T(8,128)(2,1)S(1)}, u32[]{:S(2)}, u32[]{:S(2)}) collective-permute-start(bf16[96,1024]{1,0:T(8,128)(2,1)S(1)} %get-tuple-element.75), channel_id=1, source_target_pairs={{0,1},{1,0},{2,3},{3,2},{4,5},{5,4},{6,7},{7,6},{8,9},{9,8},{10,11... | collective-permute-start | bytes 589832 | tf_op jit(solution)/shard_map/ppermute | solution.py:801
  37.0 1.5 %collective-permute-start.12 = (bf16[96,1024]{1,0:T(8,128)(2,1)S(1)}, bf16[96,1024]{1,0:T(8,128)(2,1)S(1)}, u32[]{:S(2)}, u32[]{:S(2)}) collective-permute-start(bf16[96,1024]{1,0:T(8,128)(2,1)S(1)} %get-tuple-element.74), channel_id=1, source_target_pairs={{0,1},{1,0},{2,3},{3,2},{4,5},{5,4},{6,7},{7,6},{8,9},{9,8},{10,11... | collective-permute-start | bytes 589832 | tf_op jit(solution)/shard_map/ppermute | solution.py:801
  37.1 1.7 %collective-permute-start.9 = (bf16[96,1024]{1,0:T(8,128)(2,1)S(1)}, bf16[96,1024]{1,0:T(8,128)(2,1)S(1)}, u32[]{:S(2)}, u32[]{:S(2)}) collective-permute-start(bf16[96,1024]{1,0:T(8,128)(2,1)S(1)} %get-tuple-element.77), channel_id=1, source_target_pairs={{0,1},{1,0},{2,3},{3,2},{4,5},{5,4},{6,7},{7,6},{8,9},{9,8},{10,11... | collective-permute-start | bytes 589832 | tf_op jit(solution)/shard_map/ppermute | solution.py:801
  42.5 15.0 %collective-permute-start.14 = (bf16[288,256]{1,0:T(8,128)(2,1)S(1)}, bf16[288,256]{1,0:T(8,128)(2,1)S(1)}, u32[]{:S(2)}, u32[]{:S(2)}) collective-permute-start(bf16[288,256]{1,0:T(8,128)(2,1)S(1)} %constant_dynamic-update-slice_fusion.refs_0_), channel_id=1, source_target_pairs={{0,2},{2,0},{1,3},{3,1},{4,6},{6,4},{5,7},{7,5},{8,10},{10,8},{9,1... | collective-permute-start | bytes 442376 | tf_op jit(solution)/shard_map/ppermute | solution.py:804
  57.4 1.5 %collective-permute-start.18 = (bf16[96,1024]{1,0:T(8,128)(2,1)S(1)}, bf16[96,1024]{1,0:T(8,128)(2,1)S(1)}, u32[]{:S(2)}, u32[]{:S(2)}) collective-permute-start(bf16[96,1024]{1,0:T(8,128)(2,1)S(1)} %get-tuple-element.58), channel_id=1, source_target_pairs={{0,1},{1,0},{2,3},{3,2},{4,5},{5,4},{6,7},{7,6},{8,9},{9,8},{10,11... | collective-permute-start | bytes 589832 | tf_op jit(solution)/shard_map/ppermute | solution.py:801
  57.5 1.7 %collective-permute-start.17 = (bf16[96,1024]{1,0:T(8,128)(2,1)S(1)}, bf16[96,1024]{1,0:T(8,128)(2,1)S(1)}, u32[]{:S(2)}, u32[]{:S(2)}) collective-permute-start(bf16[96,1024]{1,0:T(8,128)(2,1)S(1)} %get-tuple-element.56), channel_id=1, source_target_pairs={{0,1},{1,0},{2,3},{3,2},{4,5},{5,4},{6,7},{7,6},{8,9},{9,8},{10,11... | collective-permute-start | bytes 589832 | tf_op jit(solution)/shard_map/ppermute | solution.py:801
  58.0 1.5 %collective-permute-start.16 = (bf16[96,1024]{1,0:T(8,128)(2,1)S(1)}, bf16[96,1024]{1,0:T(8,128)(2,1)S(1)}, u32[]{:S(2)}, u32[]{:S(2)}) collective-permute-start(bf16[96,1024]{1,0:T(8,128)(2,1)S(1)} %get-tuple-element.54), channel_id=1, source_target_pairs={{0,1},{1,0},{2,3},{3,2},{4,5},{5,4},{6,7},{7,6},{8,9},{9,8},{10,11... | collective-permute-start | bytes 589832 | tf_op jit(solution)/shard_map/ppermute | solution.py:801
  58.1 1.7 %collective-permute-start.15 = (bf16[96,1024]{1,0:T(8,128)(2,1)S(1)}, bf16[96,1024]{1,0:T(8,128)(2,1)S(1)}, u32[]{:S(2)}, u32[]{:S(2)}) collective-permute-start(bf16[96,1024]{1,0:T(8,128)(2,1)S(1)} %get-tuple-element.52), channel_id=1, source_target_pairs={{0,1},{1,0},{2,3},{3,2},{4,5},{5,4},{6,7},{7,6},{8,9},{9,8},{10,11... | collective-permute-start | bytes 589832 | tf_op jit(solution)/shard_map/ppermute | solution.py:801
  60.0 2.6 %collective-permute-start.19 = (bf16[96,4096]{1,0:T(8,128)(2,1)}, bf16[96,4096]{1,0:T(8,128)(2,1)S(1)}, u32[]{:S(2)}, u32[]{:S(2)}) collective-permute-start(bf16[96,4096]{1,0:T(8,128)(2,1)} %collective-permute-done.13.near_ref), channel_id=1, source_target_pairs={{0,1},{1,0},{2,3},{3,2},{4,5},{5,4},{6,7},{7,6},{8,9},{9,8},{10,11... | collective-permute-start | bytes 2359304 | tf_op jit(solution)/shard_map/ppermute | solution.py:801
  60.3 21.5 %collective-permute-start.25 = (bf16[96,4096]{1,0:T(8,128)(2,1)S(1)}, bf16[96,4096]{1,0:T(8,128)(2,1)S(1)}, u32[]{:S(2)}, u32[]{:S(2)}) collective-permute-start(bf16[96,4096]{1,0:T(8,128)(2,1)S(1)} %add_pair.2), channel_id=1, source_target_pairs={{0,2},{2,0},{1,3},{3,1},{4,6},{6,4},{5,7},{7,5},{8,10},{10,8},{9,1... | collective-permute-start | bytes 2359304 | tf_op jit(solution)/shard_map/ppermute | solution.py:804
  71.4 14.2 %copy-start.5 = (bf16[192,1024]{1,0:T(8,128)(2,1)S(1)}, bf16[192,1024]{1,0:T(8,128)(2,1)}, u32[]{:S(2)}) copy-start(bf16[192,1024]{1,0:T(8,128)(2,1)} %copy-done.4) | copy-start | bytes 1179652
  78.5 1.5 %collective-permute-start.20 = (bf16[96,1024]{1,0:T(8,128)(2,1)S(1)}, bf16[96,1024]{1,0:T(8,128)(2,1)S(1)}, u32[]{:S(2)}, u32[]{:S(2)}) collective-permute-start(bf16[96,1024]{1,0:T(8,128)(2,1)S(1)} %get-tuple-element.63), channel_id=1, source_target_pairs={{0,1},{1,0},{2,3},{3,2},{4,5},{5,4},{6,7},{7,6},{8,9},{9,8},{10,11... | collective-permute-start | bytes 589832 | tf_op jit(solution)/shard_map/ppermute | solution.py:801
  78.8 2.7 %collective-permute-start.21 = (bf16[96,1024]{1,0:T(8,128)(2,1)S(1)}, bf16[96,1024]{1,0:T(8,128)(2,1)S(1)}, u32[]{:S(2)}, u32[]{:S(2)}) collective-permute-start(bf16[96,1024]{1,0:T(8,128)(2,1)S(1)} %get-tuple-element.64), channel_id=1, source_target_pairs={{0,1},{1,0},{2,3},{3,2},{4,5},{5,4},{6,7},{7,6},{8,9},{9,8},{10,11... | collective-permute-start | bytes 589832 | tf_op jit(solution)/shard_map/ppermute | solution.py:801
  79.1 2.5 %collective-permute-start.22 = (bf16[96,1024]{1,0:T(8,128)(2,1)S(1)}, bf16[96,1024]{1,0:T(8,128)(2,1)S(1)}, u32[]{:S(2)}, u32[]{:S(2)}) collective-permute-start(bf16[96,1024]{1,0:T(8,128)(2,1)S(1)} %get-tuple-element.65), channel_id=1, source_target_pairs={{0,1},{1,0},{2,3},{3,2},{4,5},{5,4},{6,7},{7,6},{8,9},{9,8},{10,11... | collective-permute-start | bytes 589832 | tf_op jit(solution)/shard_map/ppermute | solution.py:801
  79.3 2.2 %collective-permute-start.23 = (bf16[96,1024]{1,0:T(8,128)(2,1)S(1)}, bf16[96,1024]{1,0:T(8,128)(2,1)S(1)}, u32[]{:S(2)}, u32[]{:S(2)}) collective-permute-start(bf16[96,1024]{1,0:T(8,128)(2,1)S(1)} %get-tuple-element.66), channel_id=1, source_target_pairs={{0,1},{1,0},{2,3},{3,2},{4,5},{5,4},{6,7},{7,6},{8,9},{9,8},{10,11... | collective-permute-start | bytes 589832 | tf_op jit(solution)/shard_map/ppermute | solution.py:801
  80.0 4.1 %collective-permute-start.26 = (bf16[96,256]{1,0:T(8,128)(2,1)S(1)}, bf16[96,256]{1,0:T(8,128)(2,1)S(1)}, u32[]{:S(2)}, u32[]{:S(2)}) collective-permute-start(bf16[96,256]{1,0:T(8,128)(2,1)S(1)} %get-tuple-element.60.refs_2_.refs_3_), channel_id=1, source_target_pairs={{0,2},{2,0},{1,3},{3,1},{4,6},{6,4},{5,7},{7,5},{8,10},{10,8},{9,1... | collective-permute-start | bytes 147464 | tf_op jit(solution)/shard_map/ppermute | solution.py:804
  81.7 23.9 %copy-start.7 = (s32[1,6]{1,0:T(1,128)S(1)}, s32[1,6]{1,0:T(1,128)}, u32[]{:S(2)}) copy-start(s32[1,6]{1,0:T(1,128)} %slot_ref.1) | copy-start | bytes 76
  84.1 18.5 %collective-permute-start.27 = (bf16[96,4096]{1,0:T(8,128)(2,1)S(1)}, bf16[96,4096]{1,0:T(8,128)(2,1)S(1)}, u32[]{:S(2)}, u32[]{:S(2)}) collective-permute-start(bf16[96,4096]{1,0:T(8,128)(2,1)S(1)} %add_pair.3.refs_4_), channel_id=1, source_target_pairs={{0,2},{2,0},{1,3},{3,1},{4,6},{6,4},{5,7},{7,5},{8,10},{10,8},{9,1... | collective-permute-start | bytes 2359304 | tf_op jit(solution)/shard_map/ppermute | solution.py:804
  95.8 9.8 %copy-start.1 = (bf16[4,4,64,256]{3,2,1,0:T(8,128)(2,1)S(1)}, bf16[4,4,64,256]{3,2,1,0:T(8,128)(2,1)}, u32[]{:S(2)}) copy-start(bf16[4,4,64,256]{3,2,1,0:T(8,128)(2,1)} %pool_ref.1) | copy-start | bytes 1572868
  95.8 11.4 %copy-start = (bf16[96,8192]{1,0:T(8,128)(2,1)S(1)}, bf16[96,8192]{1,0:T(8,128)(2,1)}, u32[]{:S(2)}) copy-start(bf16[96,8192]{1,0:T(8,128)(2,1)} %x_ref.1) | copy-start | bytes 4718596
  95.8 11.4 %collective-permute-start.24 = (bf16[96,8192]{1,0:T(8,128)(2,1)S(1)}, bf16[96,8192]{1,0:T(8,128)(2,1)S(1)}, u32[]{:S(2)}, u32[]{:S(2)}) collective-permute-start(bf16[96,8192]{1,0:T(8,128)(2,1)S(1)} %get-tuple-element.68), channel_id=1, source_target_pairs={{0,1},{1,0},{2,3},{3,2},{4,5},{5,4},{6,7},{7,6},{8,9},{9,8},{10,11... | collective-permute-start | bytes 4718600 | tf_op jit(solution)/shard_map/ppermute | solution.py:801
  102.7 4.5 %collective-permute-start.28 = (bf16[96,4096]{1,0:T(8,128)(2,1)S(1)}, bf16[96,4096]{1,0:T(8,128)(2,1)S(1)}, u32[]{:S(2)}, u32[]{:S(2)}) collective-permute-start(bf16[96,4096]{1,0:T(8,128)(2,1)S(1)} %get-tuple-element.70), channel_id=1, source_target_pairs={{0,1},{1,0},{2,3},{3,2},{4,5},{5,4},{6,7},{7,6},{8,9},{9,8},{10,11... | collective-permute-start | bytes 2359304 | tf_op jit(solution)/shard_map/ppermute | solution.py:801
  102.8 2.7 %collective-permute-start.29 = (bf16[2,288,256]{2,1,0:T(8,128)(2,1)S(1)}, bf16[2,288,256]{2,1,0:T(8,128)(2,1)S(1)}, u32[]{:S(2)}, u32[]{:S(2)}) collective-permute-start(bf16[2,288,256]{2,1,0:T(8,128)(2,1)S(1)} %pad_maximum_fusion), channel_id=1, source_target_pairs={{0,1},{1,0},{2,3},{3,2},{4,5},{5,4},{6,7},{7,6},{8,9},{9,8},{10,11... | collective-permute-start | bytes 884744 | tf_op jit(solution)/shard_map/ppermute | solution.py:801
  103.4 2.2 %collective-permute-start.30 = (bf16[2,96,256]{2,1,0:T(8,128)(2,1)S(1)}, bf16[2,96,256]{2,1,0:T(8,128)(2,1)S(1)}, u32[]{:S(2)}, u32[]{:S(2)}) collective-permute-start(bf16[2,96,256]{2,1,0:T(8,128)(2,1)S(1)} %pad_maximum_fusion.1), channel_id=1, source_target_pairs={{0,1},{1,0},{2,3},{3,2},{4,5},{5,4},{6,7},{7,6},{8,9},{9,8},{10,11... | collective-permute-start | bytes 294920 | tf_op jit(solution)/shard_map/ppermute | solution.py:801

commit v8 on v7

--- a/solution.py
+++ b/solution.py
@@ -447,7 +447,7 @@
     )
 
 
-def project_held(near, far, w_query, w_keyvalue):
+def project_held(near, far, w_query, w_keyvalue, after):
     rows, half = near.shape
     pieces = len(far)
     steps, depth, q_width = w_query.shape
@@ -455,7 +455,8 @@
 
     def kernel(near_ref, *refs):
         far_refs = refs[:pieces]
-        wq, wkv, q_ref, kv_ref = refs[pieces:]
+        wq, wkv = refs[pieces : pieces + 2]
+        q_ref, kv_ref = refs[pieces + 2 + len(after) :]
         for w, out in ((wq, q_ref), (wkv, kv_ref)):
             total = None
             for j in range(steps):
@@ -471,13 +472,13 @@
 
     return pl.pallas_call(
         kernel,
-        in_specs=[VMEM] * (3 + pieces),
+        in_specs=[VMEM] * (3 + pieces) + [ANY] * len(after),
         out_specs=[VMEM] * 2,
         out_shape=[shape((rows, q_width)), shape((rows, kv_width))],
         compiler_params=params(6),
         cost_estimate=SMALL,
         name="project_held",
-    )(near, *far, w_query, w_keyvalue)
+    )(near, *far, w_query, w_keyvalue, *after)
 
 
 def project_far(place, near, far, w_query, w_keyvalue, after):
@@ -846,7 +847,7 @@
     first = tie(first, q_local)
     wide = first.shape[1] // 4
     pieces = [over_core(first[:, i * wide : (i + 1) * wide]) for i in range(4)]
-    q_first, kv_first = project_held(first, pieces, wq, wkv)
+    q_first, kv_first = project_held(first, pieces, wq, wkv, [])
     early_own = jnp.concatenate([kv_local, kv_first], axis=0)
     early_y = over_y(early_own)
     *there, stay = attend_out(
@@ -860,9 +861,9 @@
     fresh = [kv_local, kv_first, kv_second]
     bases = [local_base, first_base, second_base]
     *there, stay = attend_out(scalars, q_second, fresh, bases, second_base, pulled, w_out)
-    second_mix = add_pair(stay, [over_core(part) for part in there])
     late_y = over_y(kv_second)
-    second_sum = over_y(tie(second_mix, late_y, first_sum))
+    second_mix = add_pair(stay, [over_core(tie(part, late_y)) for part in there])
+    second_sum = over_y(tie(second_mix, first_sum))
 
     own_part, peer_part = local_rows(
         scalars, q_local, fresh, bases, local_base, pulled, w_out, [second_mix]
@@ -875,6 +876,7 @@
         place, new_slot, kv_pool, [early_own, early_y, early], [kv_second, late_y, late]
     )
 
+    second_sum = tie(second_sum, pool_out)
     near = jnp.where(is_first, first_sum, second_sum)
     far = over_core(jnp.where(is_first, second_sum, first_sum))
     layer_out = finish(place, tokens, own_part, peer_part, near, far)

time: 110 us -> 109 us (level)
  waiting for transfers between devices: 21.9 us -> 19.5 us
  Pallas kernels: 56 us -> 57.3 us
    ppermute x6, waiting for transfers between devices: 9.07 us -> 4.61 us  [over_y(): return lax.ppermute(x, 'tensor', [(0, 2), (2, 0), (1, 3), (3, 1)])]
    ppermute x19, waiting for transfers between devices: 5.83 us -> 7.93 us  [over_core(): return lax.ppermute(x, 'tensor', [(0, 1), (1, 0), (2, 3), (3, 2)])]
  transfers between devices with their start and end apart: 32 -> 32, of which waited for: 17 -> 21; matrix products, arithmetic and copies ran while one was open for 3% -> 3% of each run, Pallas kernels for 45% -> 47%
where the time goes in v8:
time: 109 us
  Pallas kernels  57.3 us (53%)
  starting transfers between devices  25.9 us (24%)
  waiting for transfers between devices  19.5 us (18%)
  local copies, waits for them, and re-layouts  3.87 us (4%)
  other arithmetic  1.46 us (1%)
    pallas_call x2, Pallas kernels, attend_out(): pl.pallas_call(kernel, in_specs=[SMEM] + [VMEM] * (2 + known) + [HBM], ou...  14.6 us
    pallas_call x1, Pallas kernels, local_rows(): pl.pallas_call(kernel, in_specs=[SMEM] + [VMEM] * (2 + known) + [HBM] + [...  10.8 us
    pallas_call x1, Pallas kernels, project_local(): pl.pallas_call(kernel, in_specs=[SMEM] + [VMEM] * 4 + [HBM] * 2 + [ANY] *...  9.27 us
    pallas_call x1, Pallas kernels, project_far(): pl.pallas_call(kernel, in_specs=[SMEM] + [VMEM] * 2 + [HBM] * 2 + [ANY] *...  8.84 us
    ppermute x6, starting transfers between devices, over_y(): return lax.ppermute(x, 'tensor', [(0, 2), (2, 0), (1, 3), (3, 1)])  8.47 us
    ppermute x19, waiting for transfers between devices, over_core(): return lax.ppermute(x, 'tensor', [(0, 1), (1, 0), (2, 3), (3, 2)])  7.93 us
    all_to_all x1, waiting for transfers between devices, chip_pair_body(): lax.all_to_all(picked, 'replica', split_axis=0, concat_axis=0, tiled=True)  6.25 us
    ppermute x19, starting transfers between devices, over_core(): return lax.ppermute(x, 'tensor', [(0, 1), (1, 0), (2, 3), (3, 2)])  5.27 us
  transfers between devices with their start and end apart: 32, of which 21 were waited for; matrix products, arithmetic and copies ran while one was open for 3% of the time, Pallas kernels for 47%

profile of v8, /device:TPU:0, one launch (start us, length us, event | category | flops | bytes accessed | tf_op | source)
XLA Modules:
  0.0 108.8 jit_solution(14247990412011205508)
XLA Ops:
  0.7 0.1 pad_add_fusion.place_ref
  0.7 3.7 %prepare.1 = (bf16[96,4096]{1,0:T(8,128)(2,1)}, bf16[96,4096]{1,0:T(8,128)(2,1)S(1)}, bf16[4,64,256]{2,1,0:T(8,128)(2,1)S(1)}, bf16[4,64,256]{2,1,0:T(8,128)(2,1...) custom-call(s32[4]{0:T(128)S(1)} %pad_add_fusion.place_ref, bf16[96,8192]{1,0:T(8,128)(2,1)} %x_ref.1, ...), custom_call_target="tpu_custom_call" | custom-call | flops 1024 | bytes 1024 | tf_op jit(solution)/shard_map/prepare/pallas_call | solution.py:233
  4.4 0.5 collective-permute-start
  4.9 2.6 %collective-permute-start.6 = (bf16[4,64,256]{2,1,0:T(8,128)(2,1)S(1)}, bf16[4,64,256]{2,1,0:T(8,128)(2,1)S(1)}, u32[]{:S(2)}, u32[]{:S(2)}) collective-permute-start(bf16[4,64,256]{2,1,0:T(8,128)(2,1)S(1)} %get-tuple-element.45), channel_id=1, source_target_pairs={{0,2},{1,3},{2,0},{3,1},{4,6},{5,7},{6,4},{7,5},{8,10},{9,11},{10,... | collective-permute-start | bytes 393224 | tf_op jit(solution)/shard_map/ppermute | solution.py:819
  7.6 3.8 %collective-permute-start.2 = (s32[1,2,16]{2,1,0:T(2,128)}, s32[1,2,16]{2,1,0:T(2,128)S(1)}, u32[]{:S(2)}, u32[]{:S(2)}) collective-permute-start(s32[1,2,16]{2,1,0:T(2,128)} %bitcast.15), channel_id=1, source_target_pairs={{0,12},{4,0},{8,4},{12,8},{1,13},{5,1},{9,5},{13,9},{2,14},{6,2},{... | collective-permute-start | bytes 392 | tf_op jit(solution)/shard_map/ppermute | solution.py:815
  11.4 0.8 reshape.7
  12.2 0.7 concatenate.7.refs_1_.place_ref
  12.9 1.0 collective-permute-start.4
  13.9 0.2 collective-permute-done.7.refs_7_
  14.2 0.1 collective-permute-start.5
  14.3 0.4 collective-permute-start.1
  14.7 1.2 %broadcast_select_fusion.2 = (bf16[96,4096]{1,0:T(8,128)(2,1)S(1)}, bf16[96,4096]{1,0:T(8,128)(2,1)S(1)}) fusion(bf16[96,4096]{1,0:T(8,128)(2,1)S(1)} %collective-permute-done.near_peer, bf16[96,4096]{1,0:T(8,128)(2,1)} %get-tuple-element.41.near_own, pred[]{:T(512)S(6)} %eq.5), kind=kLoop, calls=%fused_computation.2 | loop fusion | flops 786432 | bytes 3145729 | tf_op jit(solution)/shard_map/jit(_where)/select_n | solution.py:826
  15.9 1.7 %collective-permute-start.8 = (bf16[96,4096]{1,0:T(8,128)(2,1)S(1)}, bf16[96,4096]{1,0:T(8,128)(2,1)S(1)}, u32[]{:S(2)}, u32[]{:S(2)}) collective-permute-start(bf16[96,4096]{1,0:T(8,128)(2,1)S(1)} %get-tuple-element.83.refs_8_), channel_id=1, source_target_pairs={{0,2},{2,0},{1,3},{3,1},{4,6},{6,4},{5,7},{7,5},{8,10},{10,8},{9,1... | collective-permute-start | bytes 2359304 | tf_op jit(solution)/shard_map/ppermute | solution.py:805
  17.6 0.4 collective-permute-start.13
  18.0 0.5 collective-permute-done.4.refs_3_
  18.5 1.8 %pick_pages.1.refs_0_ = bf16[4,8,64,256]{3,2,1,0:T(8,128)(2,1)} custom-call(s32[4]{0:T(128)S(1)} %pad_add_fusion.place_ref, s32[1,2,16]{2,1,0:T(2,128)S(1)} %bitcast.18, s32[1,2,16]{2,1,0:T(2,128)S(1)} %collective-permute-done.2.refs_1_, s32[1,2,16]{2,1,0:T(2,128)} %collective-permute-done.3.refs_2_, s32[1,2,16]{2,1,0:T(2,128)S(1)} %collective-permute-done.4.refs_3_, ...), custom_call_target="tpu_custom_call" | custom-call | flops 1024 | bytes 1024 | tf_op jit(solution)/shard_map/pick_pages/pallas_call | solution.py:718
  20.3 4.5 %all-to-all-start = ((bf16[4,8,64,256]{3,2,1,0:T(8,128)(2,1)}), bf16[4,8,64,256]{3,2,1,0:T(8,128)(2,1)S(1)}, u32[]{:S(2)}, u32[]{:S(2)}) async-start(bf16[4,8,64,256]{3,2,1,0:T(8,128)(2,1)} %pick_pages.1.refs_0_), calls=%async_computation | async-start | bytes 2097152 | tf_op jit(solution)/shard_map/all_to_all | solution.py:831
  24.8 1.1 %copy-done.3 = bf16[96,4096]{1,0:T(8,128)(2,1)S(1)} copy-done((bf16[96,4096]{1,0:T(8,128)(2,1)S(1)}, bf16[96,4096]{1,0:T(8,128)(2,1)}, u32[]{:S(2)}) %copy-start.3) | copy-done | bytes 786456
  26.0 1.1 %copy-done.9 = bf16[96,4096]{1,0:T(8,128)(2,1)S(1)} copy-done((bf16[96,4096]{1,0:T(8,128)(2,1)S(1)}, bf16[96,4096]{1,0:T(8,128)(2,1)}, u32[]{:S(2)}) %copy-start.9) | copy-done | bytes 786456
  27.1 9.3 %project_local.1 = (bf16[192,1024]{1,0:T(8,128)(2,1)S(1)}, bf16[192,256]{1,0:T(8,128)(2,1)S(1)}, bf16[8,1024,1024]{2,1,0:T(8,128)(2,1)S(1)}, bf16[8,1024,256]{2,1,0:T(8,128)(2,1)S(1)}) custom-call(s32[4]{0:T(128)S(1)} %pad_add_fusion.place_ref, bf16[96,4096]{1,0:T(8,128)(2,1)} %get-tuple-element.41.near_own, bf16[96,4096]{1,0:T(8,128)(2,1)S(1)} %copy-done.3, ...), custom_call_target="tpu_custom_call" | custom-call | flops 20000000000 | bytes 200000000 | tf_op jit(solution)/shard_map/project_local/pallas_call | solution.py:287
  36.5 0.5 collective-permute-start.11
  37.0 0.1 collective-permute-start.12
  37.1 0.4 collective-permute-start.9
  37.5 0.4 collective-permute-done.10.refs_1_
  38.0 0.3 collective-permute-done.11.refs_2_
  38.2 0.3 collective-permute-done.12.refs_3_
  38.5 0.3 collective-permute-done.9.refs_0_
  38.8 3.6 %project_held.1 = (bf16[96,1024]{1,0:T(8,128)(2,1)S(1)}, bf16[96,256]{1,0:T(8,128)(2,1)S(1)}) custom-call(bf16[96,4096]{1,0:T(8,128)(2,1)S(1)} %collective-permute-done.8.near_ref, bf16[96,1024]{1,0:T(8,128)(2,1)S(1)} %collective-permute-done.9.refs_0_, bf16[96,1024]{1,0:T(8,128)(2,1)S(1)} %collective-permute-done.10.refs_1_, ...), custom_call_target="tpu_custom_call" | custom-call | flops 1024 | bytes 1024 | tf_op jit(solution)/shard_map/project_held/pallas_call | solution.py:473
  42.5 1.7 %collective-permute-start.14 = (bf16[288,256]{1,0:T(8,128)(2,1)S(1)}, bf16[288,256]{1,0:T(8,128)(2,1)S(1)}, u32[]{:S(2)}, u32[]{:S(2)}) collective-permute-start(bf16[288,256]{1,0:T(8,128)(2,1)S(1)} %constant_dynamic-update-slice_fusion.refs_0_), channel_id=1, source_target_pairs={{0,2},{2,0},{1,3},{3,1},{4,6},{6,4},{5,7},{7,5},{8,10},{10,8},{9,1... | collective-permute-start | bytes 442376 | tf_op jit(solution)/shard_map/ppermute | solution.py:805
  44.1 6.3 %all-to-all-done.pulled_ref = bf16[4,8,64,256]{3,2,1,0:T(8,128)(2,1)S(1)} async-done(((bf16[4,8,64,256]{3,2,1,0:T(8,128)(2,1)}), bf16[4,8,64,256]{3,2,1,0:T(8,128)(2,1)S(1)}, u32[]{:S(2)}, u32[]{:S(2)}) %all-to-all-start) | async-done | bytes 1048608 | tf_op jit(solution)/shard_map/all_to_all | solution.py:831
  50.4 7.6 %attend_out.2 = (bf16[96,1024]{1,0:T(8,128)(2,1)S(1)}, bf16[96,1024]{1,0:T(8,128)(2,1)S(1)}, bf16[96,1024]{1,0:T(8,128)(2,1)S(1)}, bf16[96,1024]{1,0:T(8,128)(2,1)S(1)}, bf16[96,4096]{1,0:T(8,128)(2,1)S(1)}) custom-call(s32[40]{0:T(128)S(1)} %concatenate.7.refs_1_.place_ref, bf16[96,1024]{1,0:T(8,128)(2,1)S(1)} %get-tuple-element.54.q_ref, ...), custom_call_target="tpu_custom_call" | custom-call | flops 1024 | bytes 4000000 | tf_op jit(solution)/shard_map/attend_out/pallas_call | solution.py:566
  58.1 0.5 collective-permute-start.17
  58.6 0.1 collective-permute-start.16
  58.7 0.4 collective-permute-start.15
  59.1 0.4 collective-permute-done.18.refs_3_
  59.5 0.3 collective-permute-done.17.refs_2_
  59.8 0.3 collective-permute-done.16.refs_1_
  60.1 0.3 collective-permute-done.15.refs_0_
  60.4 0.2 add_pair.2
  60.6 0.3 collective-permute-start.19
  60.9 1.5 %collective-permute-start.26 = (bf16[96,4096]{1,0:T(8,128)(2,1)S(1)}, bf16[96,4096]{1,0:T(8,128)(2,1)S(1)}, u32[]{:S(2)}, u32[]{:S(2)}) collective-permute-start(bf16[96,4096]{1,0:T(8,128)(2,1)S(1)} %add_pair.2), channel_id=1, source_target_pairs={{0,2},{2,0},{1,3},{3,1},{4,6},{6,4},{5,7},{7,5},{8,10},{10,8},{9,1... | collective-permute-start | bytes 2359304 | tf_op jit(solution)/shard_map/ppermute | solution.py:805
  62.4 0.7 collective-permute-done.19.far_ref
  63.1 8.8 %project_far.1 = (bf16[96,1024]{1,0:T(8,128)(2,1)S(1)}, bf16[96,256]{1,0:T(8,128)(2,1)S(1)}) custom-call(s32[4]{0:T(128)S(1)} %pad_add_fusion.place_ref, bf16[96,4096]{1,0:T(8,128)(2,1)} %collective-permute-done.13.near_ref, bf16[96,4096]{1,0:T(8,128)(2,1)S(1)} %collective-permute-done.19.far_ref, bf16[8192,1024]{1,0:T(8,128)(2,1)} %wq.3, bf16[8192,256]{1,0:T(8,128)(2,1)} %wkv.3), custom_call_target="tpu_custom_call" | custom-call | flops 1024 | bytes 1024 | tf_op jit(solution)/shard_map/project_far/pallas_call | solution.py:509
  72.0 1.6 %collective-permute-start.20 = (bf16[96,256]{1,0:T(8,128)(2,1)S(1)}, bf16[96,256]{1,0:T(8,128)(2,1)S(1)}, u32[]{:S(2)}, u32[]{:S(2)}) collective-permute-start(bf16[96,256]{1,0:T(8,128)(2,1)S(1)} %get-tuple-element.65.refs_2_.refs_3_), channel_id=1, source_target_pairs={{0,2},{2,0},{1,3},{3,1},{4,6},{6,4},{5,7},{7,5},{8,10},{10,8},{9,1... | collective-permute-start | bytes 147464 | tf_op jit(solution)/shard_map/ppermute | solution.py:805
  73.6 7.0 %attend_out.3 = (bf16[96,1024]{1,0:T(8,128)(2,1)S(1)}, bf16[96,1024]{1,0:T(8,128)(2,1)S(1)}, bf16[96,1024]{1,0:T(8,128)(2,1)S(1)}, bf16[96,1024]{1,0:T(8,128)(2,1)S(1)}, bf16[96,4096]{1,0:T(8,128)(2,1)S(1)}) custom-call(s32[40]{0:T(128)S(1)} %concatenate.7.refs_1_.place_ref, bf16[96,1024]{1,0:T(8,128)(2,1)S(1)} %get-tuple-element.66.q_ref, ...), custom_call_target="tpu_custom_call" | custom-call | flops 1024 | bytes 4000000 | tf_op jit(solution)/shard_map/attend_out/pallas_call | solution.py:566
  80.6 1.1 collective-permute-done.20.refs_4_
  81.6 0.5 collective-permute-start.23
  82.2 0.5 collective-permute-start.21
  82.7 0.4 collective-permute-done.24.refs_3_
  83.1 0.3 collective-permute-done.23.refs_2_
  83.4 0.3 collective-permute-done.22.refs_1_
  83.6 0.3 collective-permute-done.21.refs_0_
  83.9 0.2 add_pair.3.refs_4_
  84.1 1.6 %collective-permute-start.27 = (bf16[96,4096]{1,0:T(8,128)(2,1)S(1)}, bf16[96,4096]{1,0:T(8,128)(2,1)S(1)}, u32[]{:S(2)}, u32[]{:S(2)}) collective-permute-start(bf16[96,4096]{1,0:T(8,128)(2,1)S(1)} %add_pair.3.refs_4_), channel_id=1, source_target_pairs={{0,2},{2,0},{1,3},{3,1},{4,6},{6,4},{5,7},{7,5},{8,10},{10,8},{9,1... | collective-permute-start | bytes 2359304 | tf_op jit(solution)/shard_map/ppermute | solution.py:805
  85.8 0.6 collective-permute-start.29
  86.4 1.0 collective-permute-done.28.refs_2_
  87.4 0.1 collective-permute-done.29.refs_5_
  87.5 1.8 %write_pool.1 = bf16[4,4,64,256]{3,2,1,0:T(8,128)(2,1)} custom-call(s32[4]{0:T(128)S(1)} %pad_add_fusion.place_ref, s32[1,6]{1,0:T(1,128)S(1)} %copy-done.7, bf16[4,4,64,256]{3,2,1,0:T(8,128)(2,1)S(1)} %copy-done.1, bf16[288,256]{1,0:T(8,128)(2,1)S(1)} %constant_dynamic-update-slice_fusion.refs_0_, bf16[288,256]{1,0:T(8,128)(2,1)S(1)} %collective-permute-done.14.refs_1_, ...), custom_call_target="tpu_custom_call" | custom-call | flops 1024 | bytes 1024 | tf_op jit(solution)/shard_map/write_pool/pallas_call | solution.py:767
  89.3 10.8 %local_rows.1 = (bf16[96,8192]{1,0:T(8,128)(2,1)S(1)}, bf16[96,8192]{1,0:T(8,128)(2,1)S(1)}) custom-call(s32[40]{0:T(128)S(1)} %concatenate.7.refs_1_.place_ref, bf16[192,1024]{1,0:T(8,128)(2,1)S(1)} %copy-done.5, bf16[4,8,64,256]{3,2,1,0:T(8,128)(2,1)S(1)} %all-to-all-done.pulled_ref, bf16[192,256]{1,0:T(8,128)(2,1)S(1)} %get-tuple-element.49.refs_0_, ...), custom_call_target="tpu_custom_call" | custom-call | flops 1024 | bytes 1024 | tf_op jit(solution)/shard_map/local_rows/pallas_call | solution.py:629
  100.1 0.2 collective-permute-start.25
  100.3 3.5 %collective-permute-done.27 = bf16[96,4096]{1,0:T(8,128)(2,1)S(1)} collective-permute-done((bf16[96,4096]{1,0:T(8,128)(2,1)S(1)}, bf16[96,4096]{1,0:T(8,128)(2,1)S(1)}, u32[]{:S(2)}, u32[]{:S(2)}) %collective-permute-start.27) | collective-permute-done | bytes 786464 | tf_op jit(solution)/shard_map/ppermute | solution.py:805
  103.9 0.1 broadcast_select_fusion
  104.0 2.3 %collective-permute-done.30.far_ref = bf16[96,4096]{1,0:T(8,128)(2,1)S(1)} collective-permute-done((bf16[96,4096]{1,0:T(8,128)(2,1)S(1)}, bf16[96,4096]{1,0:T(8,128)(2,1)S(1)}, u32[]{:S(2)}, u32[]{:S(2)}) %collective-permute-start.30) | collective-permute-done | bytes 786464 | tf_op jit(solution)/shard_map/ppermute | solution.py:802
  106.3 2.5 %finish.1 = bf16[96,8192]{1,0:T(8,128)(2,1)} custom-call(s32[4]{0:T(128)S(1)} %pad_add_fusion.place_ref, bf16[96,8192]{1,0:T(8,128)(2,1)S(1)} %copy-done, bf16[96,8192]{1,0:T(8,128)(2,1)S(1)} %get-tuple-element.76.own_ref, bf16[96,8192]{1,0:T(8,128)(2,1)S(1)} %collective-permute-done.25.peer_ref, bf16[96,4096]{1,0:T(8,128)(2,1)S(1)} %get-tuple-element.81.near_ref, ...), custom_call_target="tpu_custom_call" | custom-call | flops 1024 | bytes 1024 | tf_op jit(solution)/shard_map/finish/pallas_call | solution.py:689
  (42 shorter events, 0.5 us)
Async XLA Ops:
  0.6 17.9 %copy-start.6 = (s32[1,16,2]{1,2,0:T(2,128)S(1)}, s32[1,16,2]{1,2,0:T(2,128)}, u32[]{:S(2)}) copy-start(s32[1,16,2]{1,2,0:T(2,128)} %param.17) | copy-start | bytes 388
  4.4 11.5 %copy-start.8 = (bf16[96,4096]{1,0:T(8,128)(2,1)}, bf16[96,4096]{1,0:T(8,128)(2,1)S(1)}, u32[]{:S(2)}) copy-start(bf16[96,4096]{1,0:T(8,128)(2,1)S(1)} %get-tuple-element.42.far_own) | copy-start | bytes 2359300
  4.4 9.9 %collective-permute-start = (bf16[96,4096]{1,0:T(8,128)(2,1)S(1)}, bf16[96,4096]{1,0:T(8,128)(2,1)S(1)}, u32[]{:S(2)}, u32[]{:S(2)}) collective-permute-start(bf16[96,4096]{1,0:T(8,128)(2,1)S(1)} %get-tuple-element.42.far_own), channel_id=1, source_target_pairs={{0,1},{1,0},{2,3},{3,2},{4,5},{5,4},{6,7},{7,6},{8,9},{9,8},{10,11... | collective-permute-start | bytes 2359304 | tf_op jit(solution)/shard_map/ppermute | solution.py:802
  4.9 8.0 %collective-permute-start.6 = (bf16[4,64,256]{2,1,0:T(8,128)(2,1)S(1)}, bf16[4,64,256]{2,1,0:T(8,128)(2,1)S(1)}, u32[]{:S(2)}, u32[]{:S(2)}) collective-permute-start(bf16[4,64,256]{2,1,0:T(8,128)(2,1)S(1)} %get-tuple-element.45), channel_id=1, source_target_pairs={{0,2},{1,3},{2,0},{3,1},{4,6},{5,7},{6,4},{7,5},{8,10},{9,11},{10,... | collective-permute-start | bytes 393224 | tf_op jit(solution)/shard_map/ppermute | solution.py:819
  7.5 6.6 %collective-permute-start.7 = (bf16[4,64,256]{2,1,0:T(8,128)(2,1)S(1)}, bf16[4,64,256]{2,1,0:T(8,128)(2,1)S(1)}, u32[]{:S(2)}, u32[]{:S(2)}) collective-permute-start(bf16[4,64,256]{2,1,0:T(8,128)(2,1)S(1)} %get-tuple-element.46), channel_id=1, source_target_pairs={{0,3},{1,2},{2,1},{3,0},{4,7},{5,6},{6,5},{7,4},{8,11},{9,10},{10,... | collective-permute-start | bytes 393224 | tf_op jit(solution)/shard_map/ppermute | solution.py:819
  7.6 8.3 %collective-permute-start.2 = (s32[1,2,16]{2,1,0:T(2,128)}, s32[1,2,16]{2,1,0:T(2,128)S(1)}, u32[]{:S(2)}, u32[]{:S(2)}) collective-permute-start(s32[1,2,16]{2,1,0:T(2,128)} %bitcast.15), channel_id=1, source_target_pairs={{0,12},{4,0},{8,4},{12,8},{1,13},{5,1},{9,5},{13,9},{2,14},{6,2},{... | collective-permute-start | bytes 392 | tf_op jit(solution)/shard_map/ppermute | solution.py:815
  11.4 6.2 %collective-permute-start.3 = (s32[1,2,16]{2,1,0:T(2,128)}, s32[1,2,16]{2,1,0:T(2,128)}, u32[]{:S(2)}, u32[]{:S(2)}) collective-permute-start(s32[1,2,16]{2,1,0:T(2,128)} %bitcast.16), channel_id=1, source_target_pairs={{0,8},{4,12},{8,0},{12,4},{1,9},{5,13},{9,1},{13,5},{2,10},{6,14},... | collective-permute-start | bytes 392 | tf_op jit(solution)/shard_map/ppermute | solution.py:815
  12.9 5.6 %collective-permute-start.4 = (s32[1,2,16]{2,1,0:T(2,128)}, s32[1,2,16]{2,1,0:T(2,128)S(1)}, u32[]{:S(2)}, u32[]{:S(2)}) collective-permute-start(s32[1,2,16]{2,1,0:T(2,128)} %bitcast.17), channel_id=1, source_target_pairs={{0,4},{4,8},{8,12},{12,0},{1,5},{5,9},{9,13},{13,1},{2,6},{6,10},{... | collective-permute-start | bytes 392 | tf_op jit(solution)/shard_map/ppermute | solution.py:815
  14.2 4.3 %collective-permute-start.5 = (bf16[4,64,256]{2,1,0:T(8,128)(2,1)}, bf16[4,64,256]{2,1,0:T(8,128)(2,1)S(1)}, u32[]{:S(2)}, u32[]{:S(2)}) collective-permute-start(bf16[4,64,256]{2,1,0:T(8,128)(2,1)} %get-tuple-element.44), channel_id=1, source_target_pairs={{0,1},{1,0},{2,3},{3,2},{4,5},{5,4},{6,7},{7,6},{8,9},{9,8},{10,11... | collective-permute-start | bytes 393224 | tf_op jit(solution)/shard_map/ppermute | solution.py:819
  14.3 6.0 %copy-start.2 = (bf16[96,4096]{1,0:T(8,128)(2,1)}, bf16[96,4096]{1,0:T(8,128)(2,1)S(1)}, u32[]{:S(2)}) copy-start(bf16[96,4096]{1,0:T(8,128)(2,1)S(1)} %collective-permute-done.near_peer) | copy-start | bytes 2359300
  14.3 10.5 %collective-permute-start.1 = (bf16[96,4096]{1,0:T(8,128)(2,1)}, bf16[96,4096]{1,0:T(8,128)(2,1)}, u32[]{:S(2)}, u32[]{:S(2)}) collective-permute-start(bf16[96,4096]{1,0:T(8,128)(2,1)} %get-tuple-element.41.near_own), channel_id=1, source_target_pairs={{0,1},{1,0},{2,3},{3,2},{4,5},{5,4},{6,7},{7,6},{8,9},{9,8},{10,11... | collective-permute-start | bytes 2359304 | tf_op jit(solution)/shard_map/ppermute | solution.py:802
  15.9 20.4 %collective-permute-start.8 = (bf16[96,4096]{1,0:T(8,128)(2,1)S(1)}, bf16[96,4096]{1,0:T(8,128)(2,1)S(1)}, u32[]{:S(2)}, u32[]{:S(2)}) collective-permute-start(bf16[96,4096]{1,0:T(8,128)(2,1)S(1)} %get-tuple-element.83.refs_8_), channel_id=1, source_target_pairs={{0,2},{2,0},{1,3},{3,1},{4,6},{6,4},{5,7},{7,5},{8,10},{10,8},{9,1... | collective-permute-start | bytes 2359304 | tf_op jit(solution)/shard_map/ppermute | solution.py:805
  17.6 42.9 %collective-permute-start.13 = (bf16[96,4096]{1,0:T(8,128)(2,1)S(1)}, bf16[96,4096]{1,0:T(8,128)(2,1)}, u32[]{:S(2)}, u32[]{:S(2)}) collective-permute-start(bf16[96,4096]{1,0:T(8,128)(2,1)S(1)} %get-tuple-element.82.refs_9_), channel_id=1, source_target_pairs={{0,2},{2,0},{1,3},{3,1},{4,6},{6,4},{5,7},{7,5},{8,10},{10,8},{9,1... | collective-permute-start | bytes 2359304 | tf_op jit(solution)/shard_map/ppermute | solution.py:805
  20.3 30.1 %all-to-all-start = ((bf16[4,8,64,256]{3,2,1,0:T(8,128)(2,1)}), bf16[4,8,64,256]{3,2,1,0:T(8,128)(2,1)S(1)}, u32[]{:S(2)}, u32[]{:S(2)}) async-start(bf16[4,8,64,256]{3,2,1,0:T(8,128)(2,1)} %pick_pages.1.refs_0_), calls=%async_computation | async-start | bytes 2097152 | tf_op jit(solution)/shard_map/all_to_all | solution.py:831
  24.8 1.1 %copy-start.3 = (bf16[96,4096]{1,0:T(8,128)(2,1)S(1)}, bf16[96,4096]{1,0:T(8,128)(2,1)}, u32[]{:S(2)}) copy-start(bf16[96,4096]{1,0:T(8,128)(2,1)} %copy-done.2) | copy-start | bytes 2359300
  25.9 1.1 %copy-start.9 = (bf16[96,4096]{1,0:T(8,128)(2,1)S(1)}, bf16[96,4096]{1,0:T(8,128)(2,1)}, u32[]{:S(2)}) copy-start(bf16[96,4096]{1,0:T(8,128)(2,1)} %copy-done.8) | copy-start | bytes 2359300
  36.4 6.1 %copy-start.4 = (bf16[192,1024]{1,0:T(8,128)(2,1)}, bf16[192,1024]{1,0:T(8,128)(2,1)S(1)}, u32[]{:S(2)}) copy-start(bf16[192,1024]{1,0:T(8,128)(2,1)S(1)} %get-tuple-element.48.q_ref) | copy-start | bytes 1179652
  36.4 1.5 %collective-permute-start.10 = (bf16[96,1024]{1,0:T(8,128)(2,1)S(1)}, bf16[96,1024]{1,0:T(8,128)(2,1)S(1)}, u32[]{:S(2)}, u32[]{:S(2)}) collective-permute-start(bf16[96,1024]{1,0:T(8,128)(2,1)S(1)} %get-tuple-element.86), channel_id=1, source_target_pairs={{0,1},{1,0},{2,3},{3,2},{4,5},{5,4},{6,7},{7,6},{8,9},{9,8},{10,11... | collective-permute-start | bytes 589832 | tf_op jit(solution)/shard_map/ppermute | solution.py:802
  36.5 1.7 %collective-permute-start.11 = (bf16[96,1024]{1,0:T(8,128)(2,1)S(1)}, bf16[96,1024]{1,0:T(8,128)(2,1)S(1)}, u32[]{:S(2)}, u32[]{:S(2)}) collective-permute-start(bf16[96,1024]{1,0:T(8,128)(2,1)S(1)} %get-tuple-element.85), channel_id=1, source_target_pairs={{0,1},{1,0},{2,3},{3,2},{4,5},{5,4},{6,7},{7,6},{8,9},{9,8},{10,11... | collective-permute-start | bytes 589832 | tf_op jit(solution)/shard_map/ppermute | solution.py:802
  37.0 1.5 %collective-permute-start.12 = (bf16[96,1024]{1,0:T(8,128)(2,1)S(1)}, bf16[96,1024]{1,0:T(8,128)(2,1)S(1)}, u32[]{:S(2)}, u32[]{:S(2)}) collective-permute-start(bf16[96,1024]{1,0:T(8,128)(2,1)S(1)} %get-tuple-element.84), channel_id=1, source_target_pairs={{0,1},{1,0},{2,3},{3,2},{4,5},{5,4},{6,7},{7,6},{8,9},{9,8},{10,11... | collective-permute-start | bytes 589832 | tf_op jit(solution)/shard_map/ppermute | solution.py:802
  37.1 1.7 %collective-permute-start.9 = (bf16[96,1024]{1,0:T(8,128)(2,1)S(1)}, bf16[96,1024]{1,0:T(8,128)(2,1)S(1)}, u32[]{:S(2)}, u32[]{:S(2)}) collective-permute-start(bf16[96,1024]{1,0:T(8,128)(2,1)S(1)} %get-tuple-element.87), channel_id=1, source_target_pairs={{0,1},{1,0},{2,3},{3,2},{4,5},{5,4},{6,7},{7,6},{8,9},{9,8},{10,11... | collective-permute-start | bytes 589832 | tf_op jit(solution)/shard_map/ppermute | solution.py:802
  42.5 15.6 %collective-permute-start.14 = (bf16[288,256]{1,0:T(8,128)(2,1)S(1)}, bf16[288,256]{1,0:T(8,128)(2,1)S(1)}, u32[]{:S(2)}, u32[]{:S(2)}) collective-permute-start(bf16[288,256]{1,0:T(8,128)(2,1)S(1)} %constant_dynamic-update-slice_fusion.refs_0_), channel_id=1, source_target_pairs={{0,2},{2,0},{1,3},{3,1},{4,6},{6,4},{5,7},{7,5},{8,10},{10,8},{9,1... | collective-permute-start | bytes 442376 | tf_op jit(solution)/shard_map/ppermute | solution.py:805
  58.0 1.5 %collective-permute-start.18 = (bf16[96,1024]{1,0:T(8,128)(2,1)S(1)}, bf16[96,1024]{1,0:T(8,128)(2,1)S(1)}, u32[]{:S(2)}, u32[]{:S(2)}) collective-permute-start(bf16[96,1024]{1,0:T(8,128)(2,1)S(1)} %get-tuple-element.63), channel_id=1, source_target_pairs={{0,1},{1,0},{2,3},{3,2},{4,5},{5,4},{6,7},{7,6},{8,9},{9,8},{10,11... | collective-permute-start | bytes 589832 | tf_op jit(solution)/shard_map/ppermute | solution.py:802
  58.1 1.7 %collective-permute-start.17 = (bf16[96,1024]{1,0:T(8,128)(2,1)S(1)}, bf16[96,1024]{1,0:T(8,128)(2,1)S(1)}, u32[]{:S(2)}, u32[]{:S(2)}) collective-permute-start(bf16[96,1024]{1,0:T(8,128)(2,1)S(1)} %get-tuple-element.61), channel_id=1, source_target_pairs={{0,1},{1,0},{2,3},{3,2},{4,5},{5,4},{6,7},{7,6},{8,9},{9,8},{10,11... | collective-permute-start | bytes 589832 | tf_op jit(solution)/shard_map/ppermute | solution.py:802
  58.6 1.5 %collective-permute-start.16 = (bf16[96,1024]{1,0:T(8,128)(2,1)S(1)}, bf16[96,1024]{1,0:T(8,128)(2,1)S(1)}, u32[]{:S(2)}, u32[]{:S(2)}) collective-permute-start(bf16[96,1024]{1,0:T(8,128)(2,1)S(1)} %get-tuple-element.59), channel_id=1, source_target_pairs={{0,1},{1,0},{2,3},{3,2},{4,5},{5,4},{6,7},{7,6},{8,9},{9,8},{10,11... | collective-permute-start | bytes 589832 | tf_op jit(solution)/shard_map/ppermute | solution.py:802
  58.7 1.7 %collective-permute-start.15 = (bf16[96,1024]{1,0:T(8,128)(2,1)S(1)}, bf16[96,1024]{1,0:T(8,128)(2,1)S(1)}, u32[]{:S(2)}, u32[]{:S(2)}) collective-permute-start(bf16[96,1024]{1,0:T(8,128)(2,1)S(1)} %get-tuple-element.57), channel_id=1, source_target_pairs={{0,1},{1,0},{2,3},{3,2},{4,5},{5,4},{6,7},{7,6},{8,9},{9,8},{10,11... | collective-permute-start | bytes 589832 | tf_op jit(solution)/shard_map/ppermute | solution.py:802
  60.6 2.6 %collective-permute-start.19 = (bf16[96,4096]{1,0:T(8,128)(2,1)}, bf16[96,4096]{1,0:T(8,128)(2,1)S(1)}, u32[]{:S(2)}, u32[]{:S(2)}) collective-permute-start(bf16[96,4096]{1,0:T(8,128)(2,1)} %collective-permute-done.13.near_ref), channel_id=1, source_target_pairs={{0,1},{1,0},{2,3},{3,2},{4,5},{5,4},{6,7},{7,6},{8,9},{9,8},{10,11... | collective-permute-start | bytes 2359304 | tf_op jit(solution)/shard_map/ppermute | solution.py:802
  60.9 23.3 %collective-permute-start.26 = (bf16[96,4096]{1,0:T(8,128)(2,1)S(1)}, bf16[96,4096]{1,0:T(8,128)(2,1)S(1)}, u32[]{:S(2)}, u32[]{:S(2)}) collective-permute-start(bf16[96,4096]{1,0:T(8,128)(2,1)S(1)} %add_pair.2), channel_id=1, source_target_pairs={{0,2},{2,0},{1,3},{3,1},{4,6},{6,4},{5,7},{7,5},{8,10},{10,8},{9,1... | collective-permute-start | bytes 2359304 | tf_op jit(solution)/shard_map/ppermute | solution.py:805
  72.0 9.7 %collective-permute-start.20 = (bf16[96,256]{1,0:T(8,128)(2,1)S(1)}, bf16[96,256]{1,0:T(8,128)(2,1)S(1)}, u32[]{:S(2)}, u32[]{:S(2)}) collective-permute-start(bf16[96,256]{1,0:T(8,128)(2,1)S(1)} %get-tuple-element.65.refs_2_.refs_3_), channel_id=1, source_target_pairs={{0,2},{2,0},{1,3},{3,1},{4,6},{6,4},{5,7},{7,5},{8,10},{10,8},{9,1... | collective-permute-start | bytes 147464 | tf_op jit(solution)/shard_map/ppermute | solution.py:805
  73.6 14.0 %copy-start.1 = (bf16[4,4,64,256]{3,2,1,0:T(8,128)(2,1)S(1)}, bf16[4,4,64,256]{3,2,1,0:T(8,128)(2,1)}, u32[]{:S(2)}) copy-start(bf16[4,4,64,256]{3,2,1,0:T(8,128)(2,1)} %pool_ref.1) | copy-start | bytes 1572868
  73.6 14.0 %copy-start.7 = (s32[1,6]{1,0:T(1,128)S(1)}, s32[1,6]{1,0:T(1,128)}, u32[]{:S(2)}) copy-start(s32[1,6]{1,0:T(1,128)} %slot_ref.1) | copy-start | bytes 76
  80.6 8.8 %copy-start.5 = (bf16[192,1024]{1,0:T(8,128)(2,1)S(1)}, bf16[192,1024]{1,0:T(8,128)(2,1)}, u32[]{:S(2)}) copy-start(bf16[192,1024]{1,0:T(8,128)(2,1)} %copy-done.4) | copy-start | bytes 1179652
  81.6 1.4 %collective-permute-start.24 = (bf16[96,1024]{1,0:T(8,128)(2,1)S(1)}, bf16[96,1024]{1,0:T(8,128)(2,1)S(1)}, u32[]{:S(2)}, u32[]{:S(2)}) collective-permute-start(bf16[96,1024]{1,0:T(8,128)(2,1)S(1)} %get-tuple-element.75), channel_id=1, source_target_pairs={{0,1},{1,0},{2,3},{3,2},{4,5},{5,4},{6,7},{7,6},{8,9},{9,8},{10,11... | collective-permute-start | bytes 589832 | tf_op jit(solution)/shard_map/ppermute | solution.py:802
  81.6 1.7 %collective-permute-start.23 = (bf16[96,1024]{1,0:T(8,128)(2,1)S(1)}, bf16[96,1024]{1,0:T(8,128)(2,1)S(1)}, u32[]{:S(2)}, u32[]{:S(2)}) collective-permute-start(bf16[96,1024]{1,0:T(8,128)(2,1)S(1)} %get-tuple-element.73), channel_id=1, source_target_pairs={{0,1},{1,0},{2,3},{3,2},{4,5},{5,4},{6,7},{7,6},{8,9},{9,8},{10,11... | collective-permute-start | bytes 589832 | tf_op jit(solution)/shard_map/ppermute | solution.py:802
  82.1 1.5 %collective-permute-start.22 = (bf16[96,1024]{1,0:T(8,128)(2,1)S(1)}, bf16[96,1024]{1,0:T(8,128)(2,1)S(1)}, u32[]{:S(2)}, u32[]{:S(2)}) collective-permute-start(bf16[96,1024]{1,0:T(8,128)(2,1)S(1)} %get-tuple-element.71), channel_id=1, source_target_pairs={{0,1},{1,0},{2,3},{3,2},{4,5},{5,4},{6,7},{7,6},{8,9},{9,8},{10,11... | collective-permute-start | bytes 589832 | tf_op jit(solution)/shard_map/ppermute | solution.py:802
  82.2 1.8 %collective-permute-start.21 = (bf16[96,1024]{1,0:T(8,128)(2,1)S(1)}, bf16[96,1024]{1,0:T(8,128)(2,1)S(1)}, u32[]{:S(2)}, u32[]{:S(2)}) collective-permute-start(bf16[96,1024]{1,0:T(8,128)(2,1)S(1)} %get-tuple-element.69), channel_id=1, source_target_pairs={{0,1},{1,0},{2,3},{3,2},{4,5},{5,4},{6,7},{7,6},{8,9},{9,8},{10,11... | collective-permute-start | bytes 589832 | tf_op jit(solution)/shard_map/ppermute | solution.py:802
  84.1 19.7 %collective-permute-start.27 = (bf16[96,4096]{1,0:T(8,128)(2,1)S(1)}, bf16[96,4096]{1,0:T(8,128)(2,1)S(1)}, u32[]{:S(2)}, u32[]{:S(2)}) collective-permute-start(bf16[96,4096]{1,0:T(8,128)(2,1)S(1)} %add_pair.3.refs_4_), channel_id=1, source_target_pairs={{0,2},{2,0},{1,3},{3,1},{4,6},{6,4},{5,7},{7,5},{8,10},{10,8},{9,1... | collective-permute-start | bytes 2359304 | tf_op jit(solution)/shard_map/ppermute | solution.py:805
  85.7 1.6 %collective-permute-start.28 = (bf16[2,288,256]{2,1,0:T(8,128)(2,1)S(1)}, bf16[2,288,256]{2,1,0:T(8,128)(2,1)S(1)}, u32[]{:S(2)}, u32[]{:S(2)}) collective-permute-start(bf16[2,288,256]{2,1,0:T(8,128)(2,1)S(1)} %pad_maximum_fusion), channel_id=1, source_target_pairs={{0,1},{1,0},{2,3},{3,2},{4,5},{5,4},{6,7},{7,6},{8,9},{9,8},{10,11... | collective-permute-start | bytes 884744 | tf_op jit(solution)/shard_map/ppermute | solution.py:802
  85.8 1.7 %collective-permute-start.29 = (bf16[2,96,256]{2,1,0:T(8,128)(2,1)S(1)}, bf16[2,96,256]{2,1,0:T(8,128)(2,1)S(1)}, u32[]{:S(2)}, u32[]{:S(2)}) collective-permute-start(bf16[2,96,256]{2,1,0:T(8,128)(2,1)S(1)} %pad_maximum_fusion.1), channel_id=1, source_target_pairs={{0,1},{1,0},{2,3},{3,2},{4,5},{5,4},{6,7},{7,6},{8,9},{9,8},{10,11... | collective-permute-start | bytes 294920 | tf_op jit(solution)/shard_map/ppermute | solution.py:802
  100.1 6.2 %copy-start = (bf16[96,8192]{1,0:T(8,128)(2,1)S(1)}, bf16[96,8192]{1,0:T(8,128)(2,1)}, u32[]{:S(2)}) copy-start(bf16[96,8192]{1,0:T(8,128)(2,1)} %x_ref.1) | copy-start | bytes 4718596
  100.1 6.2 %collective-permute-start.25 = (bf16[96,8192]{1,0:T(8,128)(2,1)S(1)}, bf16[96,8192]{1,0:T(8,128)(2,1)S(1)}, u32[]{:S(2)}, u32[]{:S(2)}) collective-permute-start(bf16[96,8192]{1,0:T(8,128)(2,1)S(1)} %get-tuple-element.77), channel_id=1, source_target_pairs={{0,1},{1,0},{2,3},{3,2},{4,5},{5,4},{6,7},{7,6},{8,9},{9,8},{10,11... | collective-permute-start | bytes 4718600 | tf_op jit(solution)/shard_map/ppermute | solution.py:802
  104.0 2.4 %collective-permute-start.30 = (bf16[96,4096]{1,0:T(8,128)(2,1)S(1)}, bf16[96,4096]{1,0:T(8,128)(2,1)S(1)}, u32[]{:S(2)}, u32[]{:S(2)}) collective-permute-start(bf16[96,4096]{1,0:T(8,128)(2,1)S(1)} %get-tuple-element.80), channel_id=1, source_target_pairs={{0,1},{1,0},{2,3},{3,2},{4,5},{5,4},{6,7},{7,6},{8,9},{9,8},{10,11... | collective-permute-start | bytes 2359304 | tf_op jit(solution)/shard_map/ppermute | solution.py:802

commit v9 on v8

--- a/solution.py
+++ b/solution.py
@@ -488,17 +488,25 @@
     depth = 2 * half // steps
 
     def kernel(place_ref, near_ref, far_ref, wq, wkv, *refs):
-        q_ref, kv_ref, wq_buf, wkv_buf, sems = refs[len(after) :]
+        q_ref, kv_ref, wq_buf, wkv_buf, x_buf, sems = refs[len(after) :]
+        rows_in = [
+            pltpu.make_async_copy(ref, x_buf.at[i], sems.at[2 * steps + i])
+            for i, ref in enumerate((near_ref, far_ref))
+        ]
         stream = weight_stream(place_ref[1], half, steps, (wq, wkv), (wq_buf, wkv_buf), sems)
         for j in range(steps):
             for copy in stream(j):
                 copy.start()
+            if j < 2:
+                rows_in[j].start()
         q_sum = kv_sum = None
         for j in range(steps):
             for copy in stream(j):
                 copy.wait()
-            x_ref = near_ref if j < steps // 2 else far_ref
-            x = x_ref[:, (j % (steps // 2)) * depth : (j % (steps // 2) + 1) * depth]
+            group, inner = divmod(j, steps // 2)
+            if inner == 0:
+                rows_in[group].wait()
+            x = x_buf[group, :, inner * depth : (inner + 1) * depth]
             q_part = jnp.dot(x, wq_buf[j], preferred_element_type=F32)
             kv_part = jnp.dot(x, wkv_buf[j], preferred_element_type=F32)
             q_sum = q_part if j == 0 else q_sum + q_part
@@ -508,13 +516,14 @@
 
     return pl.pallas_call(
         kernel,
-        in_specs=[SMEM] + [VMEM] * 2 + [HBM] * 2 + [ANY] * len(after),
+        in_specs=[SMEM] + [ANY] * 2 + [HBM] * 2 + [ANY] * len(after),
         out_specs=[VMEM] * 2,
         out_shape=[shape((rows, q_width)), shape((rows, kv_width))],
         scratch_shapes=[
             pltpu.VMEM((steps, depth, q_width), BF16),
             pltpu.VMEM((steps, depth, kv_width), BF16),
-            pltpu.SemaphoreType.DMA((2 * steps,)),
+            pltpu.VMEM((2, rows, half), BF16),
+            pltpu.SemaphoreType.DMA((2 * steps + 2,)),
         ],
         compiler_params=params(32),
         cost_estimate=SMALL,
@@ -795,9 +804,6 @@
     rows = tokens.shape[0]
     rep = lax.axis_index("replica")
     place = jnp.stack([me, core, side, rep]).astype(jnp.int32)
-    requests = jnp.swapaxes(page_request, 1, 2).reshape(-1)
-    scalars = jnp.concatenate([place, suffix_pages[0], requests])
-
     def over_core(x):
         return lax.ppermute(x, "tensor", [(0, 1), (1, 0), (2, 3), (3, 2)])
 
@@ -828,6 +834,9 @@
     second = over_y(second_half)
 
     picked = pick_pages(place, wanted, held, [first_half, second_half])
+    sizes, requests = lax.optimization_barrier((suffix_pages, page_request, picked))[:2]
+    requests = jnp.swapaxes(requests, 1, 2).reshape(-1)
+    scalars = jnp.concatenate([place, sizes[0], requests])
     pulled = lax.all_to_all(picked, "replica", split_axis=0, concat_axis=0, tiled=True)
 
     q_local, kv_local, wq, wkv = project_local(

time: 109 us -> 109 us (level)
  Pallas kernels: 57.3 us -> 55.6 us
  starting transfers between devices: 25.9 us -> 27.2 us
    all_to_all x1, waiting for transfers between devices: 6.25 us -> 4.84 us  [chip_pair_body(): lax.all_to_all(picked, 'replica', split_axis=0, concat_axis=0, tiled=True)]
  transfers between devices with their start and end apart: 32 -> 32, of which waited for: 21 -> 21; matrix products, arithmetic and copies ran while one was open for 3% -> 3% of each run, Pallas kernels for 47% -> 46%
where the time goes in v9:
time: 109 us; the launch traced here: 108 us
  Pallas kernels  55.6 us (51%)
  starting transfers between devices  27.2 us (25%)
  waiting for transfers between devices  19.1 us (18%)
  local copies, waits for them, and re-layouts  3.87 us (4%)
  other arithmetic  1.46 us (1%)
    pallas_call x2, Pallas kernels, attend_out(): pl.pallas_call(kernel, in_specs=[SMEM] + [VMEM] * (2 + known) + [HBM], ou...  14 us
    pallas_call x1, Pallas kernels, local_rows(): pl.pallas_call(kernel, in_specs=[SMEM] + [VMEM] * (2 + known) + [HBM] + [...  10.2 us
    pallas_call x1, Pallas kernels, project_local(): pl.pallas_call(kernel, in_specs=[SMEM] + [VMEM] * 4 + [HBM] * 2 + [ANY] *...  9.27 us
    pallas_call x1, Pallas kernels, project_far(): pl.pallas_call(kernel, in_specs=[SMEM] + [ANY] * 2 + [HBM] * 2 + [ANY] *...  8.48 us
    ppermute x6, starting transfers between devices, over_y(): return lax.ppermute(x, 'tensor', [(0, 2), (2, 0), (1, 3), (3, 1)])  8.36 us
    ppermute x19, waiting for transfers between devices, over_core(): return lax.ppermute(x, 'tensor', [(0, 1), (1, 0), (2, 3), (3, 2)])  7.94 us
    ppermute x3, starting transfers between devices, chip_pair_body(): wanted.append(lax.ppermute(wanted[0], 'replica', back))  5.82 us
    ppermute x6, waiting for transfers between devices, over_y(): return lax.ppermute(x, 'tensor', [(0, 2), (2, 0), (1, 3), (3, 1)])  5.56 us
  transfers between devices with their start and end apart: 32, of which 21 were waited for; matrix products, arithmetic and copies ran while one was open for 3% of the time, Pallas kernels for 46%

profile of v9, /device:TPU:0, one launch (start us, length us, event | category | flops | bytes accessed | tf_op | source)
XLA Modules:
  0.0 108.1 jit_solution(13626098001331333451)
XLA Ops:
  0.7 0.1 pad_add_fusion.place_ref
  0.7 3.7 %prepare.1 = (bf16[96,4096]{1,0:T(8,128)(2,1)}, bf16[96,4096]{1,0:T(8,128)(2,1)S(1)}, bf16[4,64,256]{2,1,0:T(8,128)(2,1)S(1)}, bf16[4,64,256]{2,1,0:T(8,128)(2,1...) custom-call(s32[4]{0:T(128)S(1)} %pad_add_fusion.place_ref, bf16[96,8192]{1,0:T(8,128)(2,1)} %x_ref.1, ...), custom_call_target="tpu_custom_call" | custom-call | flops 1024 | bytes 1024 | tf_op jit(solution)/shard_map/prepare/pallas_call | solution.py:233
  4.4 0.5 collective-permute-start.6
  4.9 2.6 %collective-permute-start.4 = (bf16[4,64,256]{2,1,0:T(8,128)(2,1)S(1)}, bf16[4,64,256]{2,1,0:T(8,128)(2,1)S(1)}, u32[]{:S(2)}, u32[]{:S(2)}) collective-permute-start(bf16[4,64,256]{2,1,0:T(8,128)(2,1)S(1)} %get-tuple-element.45), channel_id=1, source_target_pairs={{0,2},{1,3},{2,0},{3,1},{4,6},{5,7},{6,4},{7,5},{8,10},{9,11},{10,... | collective-permute-start | bytes 393224 | tf_op jit(solution)/shard_map/ppermute | solution.py:825
  7.6 3.8 %collective-permute-start = (s32[1,2,16]{2,1,0:T(2,128)}, s32[1,2,16]{2,1,0:T(2,128)S(1)}, u32[]{:S(2)}, u32[]{:S(2)}) collective-permute-start(s32[1,2,16]{2,1,0:T(2,128)} %bitcast.15), channel_id=1, source_target_pairs={{0,12},{4,0},{8,4},{12,8},{1,13},{5,1},{9,5},{13,9},{2,14},{6,2},{... | collective-permute-start | bytes 392 | tf_op jit(solution)/shard_map/ppermute | solution.py:821
  11.4 0.5 collective-permute-done.4.refs_6_
  11.9 2.0 %collective-permute-start.2 = (s32[1,2,16]{2,1,0:T(2,128)}, s32[1,2,16]{2,1,0:T(2,128)S(1)}, u32[]{:S(2)}, u32[]{:S(2)}) collective-permute-start(s32[1,2,16]{2,1,0:T(2,128)} %bitcast.17), channel_id=1, source_target_pairs={{0,4},{4,8},{8,12},{12,0},{1,5},{5,9},{9,13},{13,1},{2,6},{6,10},{... | collective-permute-start | bytes 392 | tf_op jit(solution)/shard_map/ppermute | solution.py:821
  13.9 0.3 collective-permute-done.5.refs_7_
  14.2 0.1 collective-permute-start.3
  14.3 0.4 collective-permute-start.7
  14.7 1.2 %broadcast_select_fusion.2 = (bf16[96,4096]{1,0:T(8,128)(2,1)S(1)}, bf16[96,4096]{1,0:T(8,128)(2,1)S(1)}) fusion(bf16[96,4096]{1,0:T(8,128)(2,1)S(1)} %collective-permute-done.6.near_peer, bf16[96,4096]{1,0:T(8,128)(2,1)} %get-tuple-element.47.near_own, pred[]{:T(512)S(6)} %eq.5), kind=kLoop, calls=%fused_computation.2 | loop fusion | flops 786432 | bytes 3145729 | tf_op jit(solution)/shard_map/jit(_where)/select_n | solution.py:832
  15.9 1.7 %collective-permute-start.8 = (bf16[96,4096]{1,0:T(8,128)(2,1)S(1)}, bf16[96,4096]{1,0:T(8,128)(2,1)S(1)}, u32[]{:S(2)}, u32[]{:S(2)}) collective-permute-start(bf16[96,4096]{1,0:T(8,128)(2,1)S(1)} %get-tuple-element.87.refs_8_), channel_id=1, source_target_pairs={{0,2},{2,0},{1,3},{3,1},{4,6},{6,4},{5,7},{7,5},{8,10},{10,8},{9,1... | collective-permute-start | bytes 2359304 | tf_op jit(solution)/shard_map/ppermute | solution.py:811
  17.6 0.4 collective-permute-start.13
  18.0 1.7 %pick_pages.1.refs_0_ = bf16[4,8,64,256]{3,2,1,0:T(8,128)(2,1)} custom-call(s32[4]{0:T(128)S(1)} %pad_add_fusion.place_ref, s32[1,2,16]{2,1,0:T(2,128)S(1)} %bitcast.18, s32[1,2,16]{2,1,0:T(2,128)S(1)} %collective-permute-done.refs_1_, s32[1,2,16]{2,1,0:T(2,128)S(1)} %collective-permute-done.1.refs_2_, s32[1,2,16]{2,1,0:T(2,128)S(1)} %collective-permute-done.2.refs_3_, ...), custom_call_target="tpu_custom_call" | custom-call | flops 1024 | bytes 1024 | tf_op jit(solution)/shard_map/pick_pages/pallas_call | solution.py:727
  19.7 5.0 %all-to-all-start = ((bf16[4,8,64,256]{3,2,1,0:T(8,128)(2,1)}), bf16[4,8,64,256]{3,2,1,0:T(8,128)(2,1)S(1)}, u32[]{:S(2)}, u32[]{:S(2)}) async-start(bf16[4,8,64,256]{3,2,1,0:T(8,128)(2,1)} %pick_pages.1.refs_0_), calls=%async_computation | async-start | bytes 2097152 | tf_op jit(solution)/shard_map/all_to_all | solution.py:840
  24.7 0.8 reshape.7
  25.4 0.7 concatenate.7.refs_1_.place_ref
  26.2 1.1 %copy-done.3 = bf16[96,4096]{1,0:T(8,128)(2,1)S(1)} copy-done((bf16[96,4096]{1,0:T(8,128)(2,1)S(1)}, bf16[96,4096]{1,0:T(8,128)(2,1)}, u32[]{:S(2)}) %copy-start.3) | copy-done | bytes 786456
  27.3 1.1 %copy-done.9 = bf16[96,4096]{1,0:T(8,128)(2,1)S(1)} copy-done((bf16[96,4096]{1,0:T(8,128)(2,1)S(1)}, bf16[96,4096]{1,0:T(8,128)(2,1)}, u32[]{:S(2)}) %copy-start.9) | copy-done | bytes 786456
  28.4 9.3 %project_local.1 = (bf16[192,1024]{1,0:T(8,128)(2,1)S(1)}, bf16[192,256]{1,0:T(8,128)(2,1)S(1)}, bf16[8,1024,1024]{2,1,0:T(8,128)(2,1)S(1)}, bf16[8,1024,256]{2,1,0:T(8,128)(2,1)S(1)}) custom-call(s32[4]{0:T(128)S(1)} %pad_add_fusion.place_ref, bf16[96,4096]{1,0:T(8,128)(2,1)} %get-tuple-element.47.near_own, bf16[96,4096]{1,0:T(8,128)(2,1)S(1)} %copy-done.3, ...), custom_call_target="tpu_custom_call" | custom-call | flops 20000000000 | bytes 200000000 | tf_op jit(solution)/shard_map/project_local/pallas_call | solution.py:287
  37.9 0.5 collective-permute-start.11
  38.4 0.1 collective-permute-start.12
  38.5 0.4 collective-permute-start.9
  38.9 0.4 collective-permute-done.10.refs_1_
  39.3 0.3 collective-permute-done.11.refs_2_
  39.6 0.3 collective-permute-done.12.refs_3_
  39.9 0.3 collective-permute-done.9.refs_0_
  40.2 3.6 %project_held.1 = (bf16[96,1024]{1,0:T(8,128)(2,1)S(1)}, bf16[96,256]{1,0:T(8,128)(2,1)S(1)}) custom-call(bf16[96,4096]{1,0:T(8,128)(2,1)S(1)} %collective-permute-done.8.near_ref, bf16[96,1024]{1,0:T(8,128)(2,1)S(1)} %collective-permute-done.9.refs_0_, bf16[96,1024]{1,0:T(8,128)(2,1)S(1)} %collective-permute-done.10.refs_1_, ...), custom_call_target="tpu_custom_call" | custom-call | flops 1024 | bytes 1024 | tf_op jit(solution)/shard_map/project_held/pallas_call | solution.py:473
  43.8 1.6 %collective-permute-start.14 = (bf16[288,256]{1,0:T(8,128)(2,1)S(1)}, bf16[288,256]{1,0:T(8,128)(2,1)S(1)}, u32[]{:S(2)}, u32[]{:S(2)}) collective-permute-start(bf16[288,256]{1,0:T(8,128)(2,1)S(1)} %constant_dynamic-update-slice_fusion.refs_0_), channel_id=1, source_target_pairs={{0,2},{2,0},{1,3},{3,1},{4,6},{6,4},{5,7},{7,5},{8,10},{10,8},{9,1... | collective-permute-start | bytes 442376 | tf_op jit(solution)/shard_map/ppermute | solution.py:811
  45.4 4.8 %all-to-all-done.pulled_ref = bf16[4,8,64,256]{3,2,1,0:T(8,128)(2,1)S(1)} async-done(((bf16[4,8,64,256]{3,2,1,0:T(8,128)(2,1)}), bf16[4,8,64,256]{3,2,1,0:T(8,128)(2,1)S(1)}, u32[]{:S(2)}, u32[]{:S(2)}) %all-to-all-start) | async-done | bytes 1048608 | tf_op jit(solution)/shard_map/all_to_all | solution.py:840
  50.2 7.0 %attend_out.2 = (bf16[96,1024]{1,0:T(8,128)(2,1)S(1)}, bf16[96,1024]{1,0:T(8,128)(2,1)S(1)}, bf16[96,1024]{1,0:T(8,128)(2,1)S(1)}, bf16[96,1024]{1,0:T(8,128)(2,1)S(1)}, bf16[96,4096]{1,0:T(8,128)(2,1)S(1)}) custom-call(s32[40]{0:T(128)S(1)} %concatenate.7.refs_1_.place_ref, bf16[96,1024]{1,0:T(8,128)(2,1)S(1)} %get-tuple-element.58.q_ref, ...), custom_call_target="tpu_custom_call" | custom-call | flops 1024 | bytes 4000000 | tf_op jit(solution)/shard_map/attend_out/pallas_call | solution.py:575
  57.4 0.5 collective-permute-start.17
  57.9 0.1 collective-permute-start.16
  57.9 0.4 collective-permute-start.15
  58.4 0.4 collective-permute-done.18.refs_3_
  58.8 0.3 collective-permute-done.17.refs_2_
  59.1 0.3 collective-permute-done.16.refs_1_
  59.4 0.3 collective-permute-done.15.refs_0_
  59.6 0.2 add_pair.2
  59.8 0.3 collective-permute-start.19
  60.1 1.5 %collective-permute-start.26 = (bf16[96,4096]{1,0:T(8,128)(2,1)S(1)}, bf16[96,4096]{1,0:T(8,128)(2,1)S(1)}, u32[]{:S(2)}, u32[]{:S(2)}) collective-permute-start(bf16[96,4096]{1,0:T(8,128)(2,1)S(1)} %add_pair.2), channel_id=1, source_target_pairs={{0,2},{2,0},{1,3},{3,1},{4,6},{6,4},{5,7},{7,5},{8,10},{10,8},{9,1... | collective-permute-start | bytes 2359304 | tf_op jit(solution)/shard_map/ppermute | solution.py:811
  61.7 0.7 collective-permute-done.19.far_ref
  62.4 8.5 %project_far.1 = (bf16[96,1024]{1,0:T(8,128)(2,1)S(1)}, bf16[96,256]{1,0:T(8,128)(2,1)S(1)}) custom-call(s32[4]{0:T(128)S(1)} %pad_add_fusion.place_ref, bf16[96,4096]{1,0:T(8,128)(2,1)} %collective-permute-done.13.near_ref, bf16[96,4096]{1,0:T(8,128)(2,1)S(1)} %collective-permute-done.19.far_ref, bf16[8192,1024]{1,0:T(8,128)(2,1)} %wq.3, bf16[8192,256]{1,0:T(8,128)(2,1)} %wkv.3), custom_call_target="tpu_custom_call" | custom-call | flops 1024 | bytes 1024 | tf_op jit(solution)/shard_map/project_far/pallas_call | solution.py:517
  70.9 1.6 %collective-permute-start.20 = (bf16[96,256]{1,0:T(8,128)(2,1)S(1)}, bf16[96,256]{1,0:T(8,128)(2,1)S(1)}, u32[]{:S(2)}, u32[]{:S(2)}) collective-permute-start(bf16[96,256]{1,0:T(8,128)(2,1)S(1)} %get-tuple-element.69.refs_2_.refs_3_), channel_id=1, source_target_pairs={{0,2},{2,0},{1,3},{3,1},{4,6},{6,4},{5,7},{7,5},{8,10},{10,8},{9,1... | collective-permute-start | bytes 147464 | tf_op jit(solution)/shard_map/ppermute | solution.py:811
  72.5 7.0 %attend_out.3 = (bf16[96,1024]{1,0:T(8,128)(2,1)S(1)}, bf16[96,1024]{1,0:T(8,128)(2,1)S(1)}, bf16[96,1024]{1,0:T(8,128)(2,1)S(1)}, bf16[96,1024]{1,0:T(8,128)(2,1)S(1)}, bf16[96,4096]{1,0:T(8,128)(2,1)S(1)}) custom-call(s32[40]{0:T(128)S(1)} %concatenate.7.refs_1_.place_ref, bf16[96,1024]{1,0:T(8,128)(2,1)S(1)} %get-tuple-element.70.q_ref, ...), custom_call_target="tpu_custom_call" | custom-call | flops 1024 | bytes 4000000 | tf_op jit(solution)/shard_map/attend_out/pallas_call | solution.py:575
  79.5 1.4 %collective-permute-done.20.refs_4_ = bf16[96,256]{1,0:T(8,128)(2,1)S(1)} collective-permute-done((bf16[96,256]{1,0:T(8,128)(2,1)S(1)}, bf16[96,256]{1,0:T(8,128)(2,1)S(1)}, u32[]{:S(2)}, u32[]{:S(2)}) %collective-permute-start.20) | collective-permute-done | bytes 49184 | tf_op jit(solution)/shard_map/ppermute | solution.py:811
  80.9 0.5 collective-permute-start.23
  81.4 0.5 collective-permute-start.21
  81.9 0.4 collective-permute-done.24.refs_3_
  82.4 0.3 collective-permute-done.23.refs_2_
  82.6 0.3 collective-permute-done.22.refs_1_
  82.9 0.3 collective-permute-done.21.refs_0_
  83.2 0.2 add_pair.3.refs_4_
  83.4 1.6 %collective-permute-start.27 = (bf16[96,4096]{1,0:T(8,128)(2,1)S(1)}, bf16[96,4096]{1,0:T(8,128)(2,1)S(1)}, u32[]{:S(2)}, u32[]{:S(2)}) collective-permute-start(bf16[96,4096]{1,0:T(8,128)(2,1)S(1)} %add_pair.3.refs_4_), channel_id=1, source_target_pairs={{0,2},{2,0},{1,3},{3,1},{4,6},{6,4},{5,7},{7,5},{8,10},{10,8},{9,1... | collective-permute-start | bytes 2359304 | tf_op jit(solution)/shard_map/ppermute | solution.py:811
  85.1 0.6 collective-permute-start.29
  85.7 1.0 collective-permute-done.28.refs_2_
  86.7 0.1 collective-permute-done.29.refs_5_
  86.8 1.8 %write_pool.1 = bf16[4,4,64,256]{3,2,1,0:T(8,128)(2,1)} custom-call(s32[4]{0:T(128)S(1)} %pad_add_fusion.place_ref, s32[1,6]{1,0:T(1,128)S(1)} %copy-done.7, bf16[4,4,64,256]{3,2,1,0:T(8,128)(2,1)S(1)} %copy-done.1, bf16[288,256]{1,0:T(8,128)(2,1)S(1)} %constant_dynamic-update-slice_fusion.refs_0_, bf16[288,256]{1,0:T(8,128)(2,1)S(1)} %collective-permute-done.14.refs_1_, ...), custom_call_target="tpu_custom_call" | custom-call | flops 1024 | bytes 1024 | tf_op jit(solution)/shard_map/write_pool/pallas_call | solution.py:776
  88.6 10.2 %local_rows.1 = (bf16[96,8192]{1,0:T(8,128)(2,1)S(1)}, bf16[96,8192]{1,0:T(8,128)(2,1)S(1)}) custom-call(s32[40]{0:T(128)S(1)} %concatenate.7.refs_1_.place_ref, bf16[192,1024]{1,0:T(8,128)(2,1)S(1)} %copy-done.5, bf16[4,8,64,256]{3,2,1,0:T(8,128)(2,1)S(1)} %all-to-all-done.pulled_ref, bf16[192,256]{1,0:T(8,128)(2,1)S(1)} %get-tuple-element.53.refs_0_, ...), custom_call_target="tpu_custom_call" | custom-call | flops 1024 | bytes 1024 | tf_op jit(solution)/shard_map/local_rows/pallas_call | solution.py:638
  98.8 0.2 collective-permute-start.25
  99.0 4.1 %collective-permute-done.27 = bf16[96,4096]{1,0:T(8,128)(2,1)S(1)} collective-permute-done((bf16[96,4096]{1,0:T(8,128)(2,1)S(1)}, bf16[96,4096]{1,0:T(8,128)(2,1)S(1)}, u32[]{:S(2)}, u32[]{:S(2)}) %collective-permute-start.27) | collective-permute-done | bytes 786464 | tf_op jit(solution)/shard_map/ppermute | solution.py:811
  103.1 0.1 broadcast_select_fusion
  103.3 2.3 %collective-permute-done.30.far_ref = bf16[96,4096]{1,0:T(8,128)(2,1)S(1)} collective-permute-done((bf16[96,4096]{1,0:T(8,128)(2,1)S(1)}, bf16[96,4096]{1,0:T(8,128)(2,1)S(1)}, u32[]{:S(2)}, u32[]{:S(2)}) %collective-permute-start.30) | collective-permute-done | bytes 786464 | tf_op jit(solution)/shard_map/ppermute | solution.py:808
  105.6 2.5 %finish.1 = bf16[96,8192]{1,0:T(8,128)(2,1)} custom-call(s32[4]{0:T(128)S(1)} %pad_add_fusion.place_ref, bf16[96,8192]{1,0:T(8,128)(2,1)S(1)} %copy-done, bf16[96,8192]{1,0:T(8,128)(2,1)S(1)} %get-tuple-element.80.own_ref, bf16[96,8192]{1,0:T(8,128)(2,1)S(1)} %collective-permute-done.25.peer_ref, bf16[96,4096]{1,0:T(8,128)(2,1)S(1)} %get-tuple-element.85.near_ref, ...), custom_call_target="tpu_custom_call" | custom-call | flops 1024 | bytes 1024 | tf_op jit(solution)/shard_map/finish/pallas_call | solution.py:698
  (42 shorter events, 0.5 us)
Async XLA Ops:
  0.6 17.4 %copy-start.6 = (s32[1,16,2]{1,2,0:T(2,128)S(1)}, s32[1,16,2]{1,2,0:T(2,128)}, u32[]{:S(2)}) copy-start(s32[1,16,2]{1,2,0:T(2,128)} %param.17) | copy-start | bytes 388
  4.4 11.5 %copy-start.8 = (bf16[96,4096]{1,0:T(8,128)(2,1)}, bf16[96,4096]{1,0:T(8,128)(2,1)S(1)}, u32[]{:S(2)}) copy-start(bf16[96,4096]{1,0:T(8,128)(2,1)S(1)} %get-tuple-element.48.far_own) | copy-start | bytes 2359300
  4.4 9.9 %collective-permute-start.6 = (bf16[96,4096]{1,0:T(8,128)(2,1)S(1)}, bf16[96,4096]{1,0:T(8,128)(2,1)S(1)}, u32[]{:S(2)}, u32[]{:S(2)}) collective-permute-start(bf16[96,4096]{1,0:T(8,128)(2,1)S(1)} %get-tuple-element.48.far_own), channel_id=1, source_target_pairs={{0,1},{1,0},{2,3},{3,2},{4,5},{5,4},{6,7},{7,6},{8,9},{9,8},{10,11... | collective-permute-start | bytes 2359304 | tf_op jit(solution)/shard_map/ppermute | solution.py:808
  4.9 6.9 %collective-permute-start.4 = (bf16[4,64,256]{2,1,0:T(8,128)(2,1)S(1)}, bf16[4,64,256]{2,1,0:T(8,128)(2,1)S(1)}, u32[]{:S(2)}, u32[]{:S(2)}) collective-permute-start(bf16[4,64,256]{2,1,0:T(8,128)(2,1)S(1)} %get-tuple-element.45), channel_id=1, source_target_pairs={{0,2},{1,3},{2,0},{3,1},{4,6},{5,7},{6,4},{7,5},{8,10},{9,11},{10,... | collective-permute-start | bytes 393224 | tf_op jit(solution)/shard_map/ppermute | solution.py:825
  7.5 6.6 %collective-permute-start.5 = (bf16[4,64,256]{2,1,0:T(8,128)(2,1)S(1)}, bf16[4,64,256]{2,1,0:T(8,128)(2,1)S(1)}, u32[]{:S(2)}, u32[]{:S(2)}) collective-permute-start(bf16[4,64,256]{2,1,0:T(8,128)(2,1)S(1)} %get-tuple-element.46), channel_id=1, source_target_pairs={{0,3},{1,2},{2,1},{3,0},{4,7},{5,6},{6,5},{7,4},{8,11},{9,10},{10,... | collective-permute-start | bytes 393224 | tf_op jit(solution)/shard_map/ppermute | solution.py:825
  7.6 8.3 %collective-permute-start = (s32[1,2,16]{2,1,0:T(2,128)}, s32[1,2,16]{2,1,0:T(2,128)S(1)}, u32[]{:S(2)}, u32[]{:S(2)}) collective-permute-start(s32[1,2,16]{2,1,0:T(2,128)} %bitcast.15), channel_id=1, source_target_pairs={{0,12},{4,0},{8,4},{12,8},{1,13},{5,1},{9,5},{13,9},{2,14},{6,2},{... | collective-permute-start | bytes 392 | tf_op jit(solution)/shard_map/ppermute | solution.py:821
  11.4 6.2 %collective-permute-start.1 = (s32[1,2,16]{2,1,0:T(2,128)}, s32[1,2,16]{2,1,0:T(2,128)S(1)}, u32[]{:S(2)}, u32[]{:S(2)}) collective-permute-start(s32[1,2,16]{2,1,0:T(2,128)} %bitcast.16), channel_id=1, source_target_pairs={{0,8},{4,12},{8,0},{12,4},{1,9},{5,13},{9,1},{13,5},{2,10},{6,14},... | collective-permute-start | bytes 392 | tf_op jit(solution)/shard_map/ppermute | solution.py:821
  11.9 6.2 %collective-permute-start.2 = (s32[1,2,16]{2,1,0:T(2,128)}, s32[1,2,16]{2,1,0:T(2,128)S(1)}, u32[]{:S(2)}, u32[]{:S(2)}) collective-permute-start(s32[1,2,16]{2,1,0:T(2,128)} %bitcast.17), channel_id=1, source_target_pairs={{0,4},{4,8},{8,12},{12,0},{1,5},{5,9},{9,13},{13,1},{2,6},{6,10},{... | collective-permute-start | bytes 392 | tf_op jit(solution)/shard_map/ppermute | solution.py:821
  14.2 3.9 %collective-permute-start.3 = (bf16[4,64,256]{2,1,0:T(8,128)(2,1)}, bf16[4,64,256]{2,1,0:T(8,128)(2,1)S(1)}, u32[]{:S(2)}, u32[]{:S(2)}) collective-permute-start(bf16[4,64,256]{2,1,0:T(8,128)(2,1)} %get-tuple-element.44), channel_id=1, source_target_pairs={{0,1},{1,0},{2,3},{3,2},{4,5},{5,4},{6,7},{7,6},{8,9},{9,8},{10,11... | collective-permute-start | bytes 393224 | tf_op jit(solution)/shard_map/ppermute | solution.py:825
  14.3 5.4 %copy-start.2 = (bf16[96,4096]{1,0:T(8,128)(2,1)}, bf16[96,4096]{1,0:T(8,128)(2,1)S(1)}, u32[]{:S(2)}) copy-start(bf16[96,4096]{1,0:T(8,128)(2,1)S(1)} %collective-permute-done.6.near_peer) | copy-start | bytes 2359300
  14.3 11.9 %collective-permute-start.7 = (bf16[96,4096]{1,0:T(8,128)(2,1)}, bf16[96,4096]{1,0:T(8,128)(2,1)}, u32[]{:S(2)}, u32[]{:S(2)}) collective-permute-start(bf16[96,4096]{1,0:T(8,128)(2,1)} %get-tuple-element.47.near_own), channel_id=1, source_target_pairs={{0,1},{1,0},{2,3},{3,2},{4,5},{5,4},{6,7},{7,6},{8,9},{9,8},{10,11... | collective-permute-start | bytes 2359304 | tf_op jit(solution)/shard_map/ppermute | solution.py:808
  15.9 21.8 %collective-permute-start.8 = (bf16[96,4096]{1,0:T(8,128)(2,1)S(1)}, bf16[96,4096]{1,0:T(8,128)(2,1)S(1)}, u32[]{:S(2)}, u32[]{:S(2)}) collective-permute-start(bf16[96,4096]{1,0:T(8,128)(2,1)S(1)} %get-tuple-element.87.refs_8_), channel_id=1, source_target_pairs={{0,2},{2,0},{1,3},{3,1},{4,6},{6,4},{5,7},{7,5},{8,10},{10,8},{9,1... | collective-permute-start | bytes 2359304 | tf_op jit(solution)/shard_map/ppermute | solution.py:811
  17.6 42.2 %collective-permute-start.13 = (bf16[96,4096]{1,0:T(8,128)(2,1)S(1)}, bf16[96,4096]{1,0:T(8,128)(2,1)}, u32[]{:S(2)}, u32[]{:S(2)}) collective-permute-start(bf16[96,4096]{1,0:T(8,128)(2,1)S(1)} %get-tuple-element.86.refs_9_), channel_id=1, source_target_pairs={{0,2},{2,0},{1,3},{3,1},{4,6},{6,4},{5,7},{7,5},{8,10},{10,8},{9,1... | collective-permute-start | bytes 2359304 | tf_op jit(solution)/shard_map/ppermute | solution.py:811
  19.7 30.5 %all-to-all-start = ((bf16[4,8,64,256]{3,2,1,0:T(8,128)(2,1)}), bf16[4,8,64,256]{3,2,1,0:T(8,128)(2,1)S(1)}, u32[]{:S(2)}, u32[]{:S(2)}) async-start(bf16[4,8,64,256]{3,2,1,0:T(8,128)(2,1)} %pick_pages.1.refs_0_), calls=%async_computation | async-start | bytes 2097152 | tf_op jit(solution)/shard_map/all_to_all | solution.py:840
  26.2 1.1 %copy-start.3 = (bf16[96,4096]{1,0:T(8,128)(2,1)S(1)}, bf16[96,4096]{1,0:T(8,128)(2,1)}, u32[]{:S(2)}) copy-start(bf16[96,4096]{1,0:T(8,128)(2,1)} %copy-done.2) | copy-start | bytes 2359300
  27.3 1.1 %copy-start.9 = (bf16[96,4096]{1,0:T(8,128)(2,1)S(1)}, bf16[96,4096]{1,0:T(8,128)(2,1)}, u32[]{:S(2)}) copy-start(bf16[96,4096]{1,0:T(8,128)(2,1)} %copy-done.8) | copy-start | bytes 2359300
  37.7 6.1 %copy-start.4 = (bf16[192,1024]{1,0:T(8,128)(2,1)}, bf16[192,1024]{1,0:T(8,128)(2,1)S(1)}, u32[]{:S(2)}) copy-start(bf16[192,1024]{1,0:T(8,128)(2,1)S(1)} %get-tuple-element.52.q_ref) | copy-start | bytes 1179652
  37.8 1.5 %collective-permute-start.10 = (bf16[96,1024]{1,0:T(8,128)(2,1)S(1)}, bf16[96,1024]{1,0:T(8,128)(2,1)S(1)}, u32[]{:S(2)}, u32[]{:S(2)}) collective-permute-start(bf16[96,1024]{1,0:T(8,128)(2,1)S(1)} %get-tuple-element.90), channel_id=1, source_target_pairs={{0,1},{1,0},{2,3},{3,2},{4,5},{5,4},{6,7},{7,6},{8,9},{9,8},{10,11... | collective-permute-start | bytes 589832 | tf_op jit(solution)/shard_map/ppermute | solution.py:808
  37.9 1.7 %collective-permute-start.11 = (bf16[96,1024]{1,0:T(8,128)(2,1)S(1)}, bf16[96,1024]{1,0:T(8,128)(2,1)S(1)}, u32[]{:S(2)}, u32[]{:S(2)}) collective-permute-start(bf16[96,1024]{1,0:T(8,128)(2,1)S(1)} %get-tuple-element.89), channel_id=1, source_target_pairs={{0,1},{1,0},{2,3},{3,2},{4,5},{5,4},{6,7},{7,6},{8,9},{9,8},{10,11... | collective-permute-start | bytes 589832 | tf_op jit(solution)/shard_map/ppermute | solution.py:808
  38.4 1.5 %collective-permute-start.12 = (bf16[96,1024]{1,0:T(8,128)(2,1)S(1)}, bf16[96,1024]{1,0:T(8,128)(2,1)S(1)}, u32[]{:S(2)}, u32[]{:S(2)}) collective-permute-start(bf16[96,1024]{1,0:T(8,128)(2,1)S(1)} %get-tuple-element.88), channel_id=1, source_target_pairs={{0,1},{1,0},{2,3},{3,2},{4,5},{5,4},{6,7},{7,6},{8,9},{9,8},{10,11... | collective-permute-start | bytes 589832 | tf_op jit(solution)/shard_map/ppermute | solution.py:808
  38.5 1.7 %collective-permute-start.9 = (bf16[96,1024]{1,0:T(8,128)(2,1)S(1)}, bf16[96,1024]{1,0:T(8,128)(2,1)S(1)}, u32[]{:S(2)}, u32[]{:S(2)}) collective-permute-start(bf16[96,1024]{1,0:T(8,128)(2,1)S(1)} %get-tuple-element.91), channel_id=1, source_target_pairs={{0,1},{1,0},{2,3},{3,2},{4,5},{5,4},{6,7},{7,6},{8,9},{9,8},{10,11... | collective-permute-start | bytes 589832 | tf_op jit(solution)/shard_map/ppermute | solution.py:808
  43.8 13.5 %collective-permute-start.14 = (bf16[288,256]{1,0:T(8,128)(2,1)S(1)}, bf16[288,256]{1,0:T(8,128)(2,1)S(1)}, u32[]{:S(2)}, u32[]{:S(2)}) collective-permute-start(bf16[288,256]{1,0:T(8,128)(2,1)S(1)} %constant_dynamic-update-slice_fusion.refs_0_), channel_id=1, source_target_pairs={{0,2},{2,0},{1,3},{3,1},{4,6},{6,4},{5,7},{7,5},{8,10},{10,8},{9,1... | collective-permute-start | bytes 442376 | tf_op jit(solution)/shard_map/ppermute | solution.py:811
  57.3 1.5 %collective-permute-start.18 = (bf16[96,1024]{1,0:T(8,128)(2,1)S(1)}, bf16[96,1024]{1,0:T(8,128)(2,1)S(1)}, u32[]{:S(2)}, u32[]{:S(2)}) collective-permute-start(bf16[96,1024]{1,0:T(8,128)(2,1)S(1)} %get-tuple-element.67), channel_id=1, source_target_pairs={{0,1},{1,0},{2,3},{3,2},{4,5},{5,4},{6,7},{7,6},{8,9},{9,8},{10,11... | collective-permute-start | bytes 589832 | tf_op jit(solution)/shard_map/ppermute | solution.py:808
  57.4 1.7 %collective-permute-start.17 = (bf16[96,1024]{1,0:T(8,128)(2,1)S(1)}, bf16[96,1024]{1,0:T(8,128)(2,1)S(1)}, u32[]{:S(2)}, u32[]{:S(2)}) collective-permute-start(bf16[96,1024]{1,0:T(8,128)(2,1)S(1)} %get-tuple-element.65), channel_id=1, source_target_pairs={{0,1},{1,0},{2,3},{3,2},{4,5},{5,4},{6,7},{7,6},{8,9},{9,8},{10,11... | collective-permute-start | bytes 589832 | tf_op jit(solution)/shard_map/ppermute | solution.py:808
  57.9 1.5 %collective-permute-start.16 = (bf16[96,1024]{1,0:T(8,128)(2,1)S(1)}, bf16[96,1024]{1,0:T(8,128)(2,1)S(1)}, u32[]{:S(2)}, u32[]{:S(2)}) collective-permute-start(bf16[96,1024]{1,0:T(8,128)(2,1)S(1)} %get-tuple-element.63), channel_id=1, source_target_pairs={{0,1},{1,0},{2,3},{3,2},{4,5},{5,4},{6,7},{7,6},{8,9},{9,8},{10,11... | collective-permute-start | bytes 589832 | tf_op jit(solution)/shard_map/ppermute | solution.py:808
  57.9 1.7 %collective-permute-start.15 = (bf16[96,1024]{1,0:T(8,128)(2,1)S(1)}, bf16[96,1024]{1,0:T(8,128)(2,1)S(1)}, u32[]{:S(2)}, u32[]{:S(2)}) collective-permute-start(bf16[96,1024]{1,0:T(8,128)(2,1)S(1)} %get-tuple-element.61), channel_id=1, source_target_pairs={{0,1},{1,0},{2,3},{3,2},{4,5},{5,4},{6,7},{7,6},{8,9},{9,8},{10,11... | collective-permute-start | bytes 589832 | tf_op jit(solution)/shard_map/ppermute | solution.py:808
  59.8 2.6 %collective-permute-start.19 = (bf16[96,4096]{1,0:T(8,128)(2,1)}, bf16[96,4096]{1,0:T(8,128)(2,1)S(1)}, u32[]{:S(2)}, u32[]{:S(2)}) collective-permute-start(bf16[96,4096]{1,0:T(8,128)(2,1)} %collective-permute-done.13.near_ref), channel_id=1, source_target_pairs={{0,1},{1,0},{2,3},{3,2},{4,5},{5,4},{6,7},{7,6},{8,9},{9,8},{10,11... | collective-permute-start | bytes 2359304 | tf_op jit(solution)/shard_map/ppermute | solution.py:808
  60.1 23.3 %collective-permute-start.26 = (bf16[96,4096]{1,0:T(8,128)(2,1)S(1)}, bf16[96,4096]{1,0:T(8,128)(2,1)S(1)}, u32[]{:S(2)}, u32[]{:S(2)}) collective-permute-start(bf16[96,4096]{1,0:T(8,128)(2,1)S(1)} %add_pair.2), channel_id=1, source_target_pairs={{0,2},{2,0},{1,3},{3,1},{4,6},{6,4},{5,7},{7,5},{8,10},{10,8},{9,1... | collective-permute-start | bytes 2359304 | tf_op jit(solution)/shard_map/ppermute | solution.py:811
  70.9 10.0 %collective-permute-start.20 = (bf16[96,256]{1,0:T(8,128)(2,1)S(1)}, bf16[96,256]{1,0:T(8,128)(2,1)S(1)}, u32[]{:S(2)}, u32[]{:S(2)}) collective-permute-start(bf16[96,256]{1,0:T(8,128)(2,1)S(1)} %get-tuple-element.69.refs_2_.refs_3_), channel_id=1, source_target_pairs={{0,2},{2,0},{1,3},{3,1},{4,6},{6,4},{5,7},{7,5},{8,10},{10,8},{9,1... | collective-permute-start | bytes 147464 | tf_op jit(solution)/shard_map/ppermute | solution.py:811
  72.5 14.3 %copy-start.1 = (bf16[4,4,64,256]{3,2,1,0:T(8,128)(2,1)S(1)}, bf16[4,4,64,256]{3,2,1,0:T(8,128)(2,1)}, u32[]{:S(2)}) copy-start(bf16[4,4,64,256]{3,2,1,0:T(8,128)(2,1)} %pool_ref.1) | copy-start | bytes 1572868
  72.5 14.3 %copy-start.7 = (s32[1,6]{1,0:T(1,128)S(1)}, s32[1,6]{1,0:T(1,128)}, u32[]{:S(2)}) copy-start(s32[1,6]{1,0:T(1,128)} %slot_ref.1) | copy-start | bytes 76
  79.5 9.1 %copy-start.5 = (bf16[192,1024]{1,0:T(8,128)(2,1)S(1)}, bf16[192,1024]{1,0:T(8,128)(2,1)}, u32[]{:S(2)}) copy-start(bf16[192,1024]{1,0:T(8,128)(2,1)} %copy-done.4) | copy-start | bytes 1179652
  80.9 1.4 %collective-permute-start.24 = (bf16[96,1024]{1,0:T(8,128)(2,1)S(1)}, bf16[96,1024]{1,0:T(8,128)(2,1)S(1)}, u32[]{:S(2)}, u32[]{:S(2)}) collective-permute-start(bf16[96,1024]{1,0:T(8,128)(2,1)S(1)} %get-tuple-element.79), channel_id=1, source_target_pairs={{0,1},{1,0},{2,3},{3,2},{4,5},{5,4},{6,7},{7,6},{8,9},{9,8},{10,11... | collective-permute-start | bytes 589832 | tf_op jit(solution)/shard_map/ppermute | solution.py:808
  80.9 1.7 %collective-permute-start.23 = (bf16[96,1024]{1,0:T(8,128)(2,1)S(1)}, bf16[96,1024]{1,0:T(8,128)(2,1)S(1)}, u32[]{:S(2)}, u32[]{:S(2)}) collective-permute-start(bf16[96,1024]{1,0:T(8,128)(2,1)S(1)} %get-tuple-element.77), channel_id=1, source_target_pairs={{0,1},{1,0},{2,3},{3,2},{4,5},{5,4},{6,7},{7,6},{8,9},{9,8},{10,11... | collective-permute-start | bytes 589832 | tf_op jit(solution)/shard_map/ppermute | solution.py:808
  81.4 1.5 %collective-permute-start.22 = (bf16[96,1024]{1,0:T(8,128)(2,1)S(1)}, bf16[96,1024]{1,0:T(8,128)(2,1)S(1)}, u32[]{:S(2)}, u32[]{:S(2)}) collective-permute-start(bf16[96,1024]{1,0:T(8,128)(2,1)S(1)} %get-tuple-element.75), channel_id=1, source_target_pairs={{0,1},{1,0},{2,3},{3,2},{4,5},{5,4},{6,7},{7,6},{8,9},{9,8},{10,11... | collective-permute-start | bytes 589832 | tf_op jit(solution)/shard_map/ppermute | solution.py:808
  81.4 1.8 %collective-permute-start.21 = (bf16[96,1024]{1,0:T(8,128)(2,1)S(1)}, bf16[96,1024]{1,0:T(8,128)(2,1)S(1)}, u32[]{:S(2)}, u32[]{:S(2)}) collective-permute-start(bf16[96,1024]{1,0:T(8,128)(2,1)S(1)} %get-tuple-element.73), channel_id=1, source_target_pairs={{0,1},{1,0},{2,3},{3,2},{4,5},{5,4},{6,7},{7,6},{8,9},{9,8},{10,11... | collective-permute-start | bytes 589832 | tf_op jit(solution)/shard_map/ppermute | solution.py:808
  83.4 19.7 %collective-permute-start.27 = (bf16[96,4096]{1,0:T(8,128)(2,1)S(1)}, bf16[96,4096]{1,0:T(8,128)(2,1)S(1)}, u32[]{:S(2)}, u32[]{:S(2)}) collective-permute-start(bf16[96,4096]{1,0:T(8,128)(2,1)S(1)} %add_pair.3.refs_4_), channel_id=1, source_target_pairs={{0,2},{2,0},{1,3},{3,1},{4,6},{6,4},{5,7},{7,5},{8,10},{10,8},{9,1... | collective-permute-start | bytes 2359304 | tf_op jit(solution)/shard_map/ppermute | solution.py:811
  85.0 1.6 %collective-permute-start.28 = (bf16[2,288,256]{2,1,0:T(8,128)(2,1)S(1)}, bf16[2,288,256]{2,1,0:T(8,128)(2,1)S(1)}, u32[]{:S(2)}, u32[]{:S(2)}) collective-permute-start(bf16[2,288,256]{2,1,0:T(8,128)(2,1)S(1)} %pad_maximum_fusion), channel_id=1, source_target_pairs={{0,1},{1,0},{2,3},{3,2},{4,5},{5,4},{6,7},{7,6},{8,9},{9,8},{10,11... | collective-permute-start | bytes 884744 | tf_op jit(solution)/shard_map/ppermute | solution.py:808
  85.1 1.7 %collective-permute-start.29 = (bf16[2,96,256]{2,1,0:T(8,128)(2,1)S(1)}, bf16[2,96,256]{2,1,0:T(8,128)(2,1)S(1)}, u32[]{:S(2)}, u32[]{:S(2)}) collective-permute-start(bf16[2,96,256]{2,1,0:T(8,128)(2,1)S(1)} %pad_maximum_fusion.1), channel_id=1, source_target_pairs={{0,1},{1,0},{2,3},{3,2},{4,5},{5,4},{6,7},{7,6},{8,9},{9,8},{10,11... | collective-permute-start | bytes 294920 | tf_op jit(solution)/shard_map/ppermute | solution.py:808
  98.8 6.8 %copy-start = (bf16[96,8192]{1,0:T(8,128)(2,1)S(1)}, bf16[96,8192]{1,0:T(8,128)(2,1)}, u32[]{:S(2)}) copy-start(bf16[96,8192]{1,0:T(8,128)(2,1)} %x_ref.1) | copy-start | bytes 4718596
  98.8 6.8 %collective-permute-start.25 = (bf16[96,8192]{1,0:T(8,128)(2,1)S(1)}, bf16[96,8192]{1,0:T(8,128)(2,1)S(1)}, u32[]{:S(2)}, u32[]{:S(2)}) collective-permute-start(bf16[96,8192]{1,0:T(8,128)(2,1)S(1)} %get-tuple-element.81), channel_id=1, source_target_pairs={{0,1},{1,0},{2,3},{3,2},{4,5},{5,4},{6,7},{7,6},{8,9},{9,8},{10,11... | collective-permute-start | bytes 4718600 | tf_op jit(solution)/shard_map/ppermute | solution.py:808
  103.2 2.4 %collective-permute-start.30 = (bf16[96,4096]{1,0:T(8,128)(2,1)S(1)}, bf16[96,4096]{1,0:T(8,128)(2,1)S(1)}, u32[]{:S(2)}, u32[]{:S(2)}) collective-permute-start(bf16[96,4096]{1,0:T(8,128)(2,1)S(1)} %get-tuple-element.84), channel_id=1, source_target_pairs={{0,1},{1,0},{2,3},{3,2},{4,5},{5,4},{6,7},{7,6},{8,9},{9,8},{10,11... | collective-permute-start | bytes 2359304 | tf_op jit(solution)/shard_map/ppermute | solution.py:808

commit v10 on v9

--- a/solution.py
+++ b/solution.py
@@ -676,34 +676,79 @@
     )(left, *pieces)
 
 
-def finish(place, tokens, own, peer, near, far):
+def finish_near(place, tokens, own, peer, near):
     rows, width = tokens.shape
     half = width // 2
     step = 16
 
-    def kernel(place_ref, x_ref, own_ref, peer_ref, near_ref, far_ref, out_ref):
+    def kernel(place_ref, x_ref, own_ref, peer_ref, near_ref, done_ref, local_ref):
         core = place_ref[1]
+        near_cols = pl.ds(pl.multiple_of(core * half, half), half)
+        far_cols = pl.ds(pl.multiple_of((1 - core) * half, half), half)
 
         def block(i, carry):
             at = pl.ds(pl.multiple_of(i * step, step), step)
-            for start, part in ((core, near_ref), (1 - core, far_ref)):
-                cols = pl.ds(pl.multiple_of(start * half, half), half)
-                local = own_ref[at, cols].astype(F32) + peer_ref[at, cols].astype(F32)
-                total = local + part[at, :].astype(F32)
-                out_ref[at, cols] = (x_ref[at, cols].astype(F32) + total).astype(BF16)
+            local = own_ref[at, near_cols].astype(F32) + peer_ref[at, near_cols].astype(F32)
+            total = local + near_ref[at, :].astype(F32)
+            done_ref[at, :] = (x_ref[at, near_cols].astype(F32) + total).astype(BF16)
+            local_ref[at, :] = own_ref[at, far_cols].astype(F32) + peer_ref[at, far_cols].astype(F32)
             return carry
 
         lax.fori_loop(0, rows // step, block, 0)
 
     return pl.pallas_call(
         kernel,
-        in_specs=[SMEM] + [VMEM] * 5,
-        out_specs=VMEM,
+        in_specs=[SMEM] + [VMEM] * 4,
+        out_specs=[VMEM] * 2,
+        out_shape=[shape((rows, half)), shape((rows, half), F32)],
+        compiler_params=params(16),
+        cost_estimate=SMALL,
+        name="finish_near",
+    )(place, tokens, own, peer, near)
+
+
+def finish(place, tokens, done, local, far):
+    rows, width = tokens.shape
+    half = width // 2
+    step = 32
+    blocks = rows // step
+
+    def kernel(place_ref, x_ref, done_ref, local_ref, far_ref, out_ref, buf, sems):
+        core = place_ref[1]
+        near_cols = pl.ds(pl.multiple_of(core * half, half), half)
+        far_cols = pl.ds(pl.multiple_of((1 - core) * half, half), half)
+
+        def near_copy():
+            return pltpu.make_async_copy(done_ref, out_ref.at[:, near_cols], sems.at[blocks])
+
+        def far_copy(b):
+            at = pl.ds(b * step, step)
+            return pltpu.make_async_copy(buf.at[at], out_ref.at[at, far_cols], sems.at[b])
+
+        near_copy().start()
+        for b in range(blocks):
+            for i in range(0, step, 16):
+                at = slice(b * step + i, b * step + i + 16)
+                total = local_ref[at, :] + far_ref[at, :].astype(F32)
+                buf[at, :] = (x_ref[at, far_cols].astype(F32) + total).astype(BF16)
+            far_copy(b).start()
+        near_copy().wait()
+        for b in range(blocks):
+            far_copy(b).wait()
+
+    return pl.pallas_call(
+        kernel,
+        in_specs=[SMEM] + [VMEM] * 4,
+        out_specs=ANY,
         out_shape=shape((rows, width)),
+        scratch_shapes=[
+            pltpu.VMEM((rows, half), BF16),
+            pltpu.SemaphoreType.DMA((blocks + 1,)),
+        ],
         compiler_params=params(16),
         cost_estimate=SMALL,
         name="finish",
-    )(place, tokens, own, peer, near, far)
+    )(place, tokens, done, local, far)
 
 
 def pick_pages(place, wanted, held, after):
@@ -888,7 +933,8 @@
     second_sum = tie(second_sum, pool_out)
     near = jnp.where(is_first, first_sum, second_sum)
     far = over_core(jnp.where(is_first, second_sum, first_sum))
-    layer_out = finish(place, tokens, own_part, peer_part, near, far)
+    done, local = finish_near(place, tokens, own_part, peer_part, near)
+    layer_out = finish(place, tokens, done, local, far)
     return (layer_out, pool_out)
 
 

time: 109 us -> 109 us (level)
  local copies, waits for them, and re-layouts: 3.87 us -> 2.55 us
    all_to_all x1, waiting for transfers between devices: 4.84 us -> 6.16 us  [chip_pair_body(): lax.all_to_all(picked, 'replica', split_axis=0, concat_axis=0, tiled=True)]
    ppermute x19, waiting for transfers between devices: 7.94 us -> 6.8 us  [over_core(): return lax.ppermute(x, 'tensor', [(0, 1), (1, 0), (2, 3), (3, 2)])]
    pallas_call x1 -> x2, Pallas kernels: 2.52 us -> 2.83 us  [the longest x1 1.71 us: finish(): pl.pallas_call(kernel, in_specs=[SMEM] + [VMEM] * 4, out_specs=ANY, out_s...]
    unnamed x21 -> x25, local copies, waits for them, and re-layouts: 2.31 us -> 2.32 us
  transfers between devices with their start and end apart: 32 -> 32, of which waited for: 21 -> 21; matrix products, arithmetic and copies ran while one was open for 3% -> 1% of each run, Pallas kernels for 46% -> 47%
where the time goes in v10:
time: 109 us; the launch traced here: 108 us
  Pallas kernels  56.5 us (52%)
  starting transfers between devices  27.4 us (25%)
  waiting for transfers between devices  19.3 us (18%)
  local copies, waits for them, and re-layouts  2.55 us (2%)
  other arithmetic  1.46 us (1%)
  between operations  1.11 us (1%)
    pallas_call x2, Pallas kernels, attend_out(): pl.pallas_call(kernel, in_specs=[SMEM] + [VMEM] * (2 + known) + [HBM], ou...  14.6 us
    pallas_call x1, Pallas kernels, local_rows(): pl.pallas_call(kernel, in_specs=[SMEM] + [VMEM] * (2 + known) + [HBM] + [...  10.2 us
    pallas_call x1, Pallas kernels, project_local(): pl.pallas_call(kernel, in_specs=[SMEM] + [VMEM] * 4 + [HBM] * 2 + [ANY] *...  9.27 us
    pallas_call x1, Pallas kernels, project_far(): pl.pallas_call(kernel, in_specs=[SMEM] + [ANY] * 2 + [HBM] * 2 + [ANY] *...  8.48 us
    ppermute x6, starting transfers between devices, over_y(): return lax.ppermute(x, 'tensor', [(0, 2), (2, 0), (1, 3), (3, 1)])  8.34 us
    ppermute x19, waiting for transfers between devices, over_core(): return lax.ppermute(x, 'tensor', [(0, 1), (1, 0), (2, 3), (3, 2)])  6.8 us
    all_to_all x1, waiting for transfers between devices, chip_pair_body(): lax.all_to_all(picked, 'replica', split_axis=0, concat_axis=0, tiled=True)  6.16 us
    ppermute x3, starting transfers between devices, chip_pair_body(): wanted.append(lax.ppermute(wanted[0], 'replica', back))  5.82 us
  transfers between devices with their start and end apart: 32, of which 21 were waited for; matrix products, arithmetic and copies ran while one was open for 1% of the time, Pallas kernels for 47%

profile of v10, /device:TPU:0, one launch (start us, length us, event | category | flops | bytes accessed | tf_op | source)
XLA Modules:
  0.0 108.2 jit_solution(8481252143123528130)
XLA Ops:
  0.7 3.7 %prepare.1 = (bf16[96,4096]{1,0:T(8,128)(2,1)}, bf16[96,4096]{1,0:T(8,128)(2,1)S(1)}, bf16[4,64,256]{2,1,0:T(8,128)(2,1)S(1)}, bf16[4,64,256]{2,1,0:T(8,128)(2,1...) custom-call(s32[4]{0:T(128)S(1)} %pad_add_fusion.place_ref, bf16[96,8192]{1,0:T(8,128)(2,1)} %x_ref.3, ...), custom_call_target="tpu_custom_call" | custom-call | flops 1024 | bytes 1024 | tf_op jit(solution)/shard_map/prepare/pallas_call | solution.py:233
  4.4 0.5 collective-permute-start.6
  4.9 2.6 %collective-permute-start.4 = (bf16[4,64,256]{2,1,0:T(8,128)(2,1)S(1)}, bf16[4,64,256]{2,1,0:T(8,128)(2,1)S(1)}, u32[]{:S(2)}, u32[]{:S(2)}) collective-permute-start(bf16[4,64,256]{2,1,0:T(8,128)(2,1)S(1)} %get-tuple-element.47), channel_id=1, source_target_pairs={{0,2},{1,3},{2,0},{3,1},{4,6},{5,7},{6,4},{7,5},{8,10},{9,11},{10,... | collective-permute-start | bytes 393224 | tf_op jit(solution)/shard_map/ppermute | solution.py:870
  7.6 3.8 %collective-permute-start = (s32[1,2,16]{2,1,0:T(2,128)S(1)}, s32[1,2,16]{2,1,0:T(2,128)S(1)}, u32[]{:S(2)}, u32[]{:S(2)}) collective-permute-start(s32[1,2,16]{2,1,0:T(2,128)S(1)} %bitcast.15), channel_id=1, source_target_pairs={{0,12},{4,0},{8,4},{12,8},{1,13},{5,1},{9,5},{13,9},{2,14},{6,2},{... | collective-permute-start | bytes 392 | tf_op jit(solution)/shard_map/ppermute | solution.py:866
  11.4 0.5 collective-permute-done.4.refs_6_
  11.9 2.0 %collective-permute-start.2 = (s32[1,2,16]{2,1,0:T(2,128)S(1)}, s32[1,2,16]{2,1,0:T(2,128)S(1)}, u32[]{:S(2)}, u32[]{:S(2)}) collective-permute-start(s32[1,2,16]{2,1,0:T(2,128)S(1)} %bitcast.17), channel_id=1, source_target_pairs={{0,4},{4,8},{8,12},{12,0},{1,5},{5,9},{9,13},{13,1},{2,6},{6,10},{... | collective-permute-start | bytes 392 | tf_op jit(solution)/shard_map/ppermute | solution.py:866
  13.9 0.3 collective-permute-done.5.refs_7_
  14.2 0.1 collective-permute-start.3
  14.3 0.4 collective-permute-start.7
  14.7 1.2 %broadcast_select_fusion.2 = (bf16[96,4096]{1,0:T(8,128)(2,1)S(1)}, bf16[96,4096]{1,0:T(8,128)(2,1)S(1)}) fusion(bf16[96,4096]{1,0:T(8,128)(2,1)S(1)} %collective-permute-done.6.near_peer, bf16[96,4096]{1,0:T(8,128)(2,1)} %get-tuple-element.49.near_own, pred[]{:T(512)S(6)} %eq.5), kind=kLoop, calls=%fused_computation.2 | loop fusion | flops 786432 | bytes 3145729 | tf_op jit(solution)/shard_map/jit(_where)/select_n | solution.py:877
  15.9 1.7 %collective-permute-start.8 = (bf16[96,4096]{1,0:T(8,128)(2,1)S(1)}, bf16[96,4096]{1,0:T(8,128)(2,1)S(1)}, u32[]{:S(2)}, u32[]{:S(2)}) collective-permute-start(bf16[96,4096]{1,0:T(8,128)(2,1)S(1)} %get-tuple-element.91.refs_8_), channel_id=1, source_target_pairs={{0,2},{2,0},{1,3},{3,1},{4,6},{6,4},{5,7},{7,5},{8,10},{10,8},{9,1... | collective-permute-start | bytes 2359304 | tf_op jit(solution)/shard_map/ppermute | solution.py:856
  17.6 0.4 collective-permute-start.13
  18.0 1.7 %pick_pages.1.refs_0_ = bf16[4,8,64,256]{3,2,1,0:T(8,128)(2,1)} custom-call(s32[4]{0:T(128)S(1)} %pad_add_fusion.place_ref, s32[1,2,16]{2,1,0:T(2,128)S(1)} %bitcast.18, s32[1,2,16]{2,1,0:T(2,128)S(1)} %collective-permute-done.refs_1_, s32[1,2,16]{2,1,0:T(2,128)S(1)} %collective-permute-done.1.refs_2_, s32[1,2,16]{2,1,0:T(2,128)S(1)} %collective-permute-done.2.refs_3_, ...), custom_call_target="tpu_custom_call" | custom-call | flops 1024 | bytes 1024 | tf_op jit(solution)/shard_map/pick_pages/pallas_call | solution.py:772
  19.7 5.1 %all-to-all-start = ((bf16[4,8,64,256]{3,2,1,0:T(8,128)(2,1)}), bf16[4,8,64,256]{3,2,1,0:T(8,128)(2,1)S(1)}, u32[]{:S(2)}, u32[]{:S(2)}) async-start(bf16[4,8,64,256]{3,2,1,0:T(8,128)(2,1)} %pick_pages.1.refs_0_), calls=%async_computation | async-start | bytes 2097152 | tf_op jit(solution)/shard_map/all_to_all | solution.py:885
  24.8 0.1 reshape.7
  24.9 0.1 concatenate.7.refs_1_.place_ref
  25.0 1.1 %copy-done.3 = bf16[96,4096]{1,0:T(8,128)(2,1)S(1)} copy-done((bf16[96,4096]{1,0:T(8,128)(2,1)S(1)}, bf16[96,4096]{1,0:T(8,128)(2,1)}, u32[]{:S(2)}) %copy-start.3) | copy-done | bytes 786456
  26.1 1.1 %copy-done.9 = bf16[96,4096]{1,0:T(8,128)(2,1)S(1)} copy-done((bf16[96,4096]{1,0:T(8,128)(2,1)S(1)}, bf16[96,4096]{1,0:T(8,128)(2,1)}, u32[]{:S(2)}) %copy-start.9) | copy-done | bytes 786456
  27.2 9.3 %project_local.1 = (bf16[192,1024]{1,0:T(8,128)(2,1)S(1)}, bf16[192,256]{1,0:T(8,128)(2,1)S(1)}, bf16[8,1024,1024]{2,1,0:T(8,128)(2,1)S(1)}, bf16[8,1024,256]{2,1,0:T(8,128)(2,1)S(1)}) custom-call(s32[4]{0:T(128)S(1)} %pad_add_fusion.place_ref, bf16[96,4096]{1,0:T(8,128)(2,1)} %get-tuple-element.49.near_own, bf16[96,4096]{1,0:T(8,128)(2,1)S(1)} %copy-done.3, ...), custom_call_target="tpu_custom_call" | custom-call | flops 20000000000 | bytes 200000000 | tf_op jit(solution)/shard_map/project_local/pallas_call | solution.py:287
  36.7 0.5 collective-permute-start.11
  37.2 0.1 collective-permute-start.12
  37.3 0.4 collective-permute-start.9
  37.7 0.4 collective-permute-done.10.refs_1_
  38.1 0.3 collective-permute-done.11.refs_2_
  38.4 0.3 collective-permute-done.12.refs_3_
  38.7 0.3 collective-permute-done.9.refs_0_
  39.0 3.6 %project_held.1 = (bf16[96,1024]{1,0:T(8,128)(2,1)S(1)}, bf16[96,256]{1,0:T(8,128)(2,1)S(1)}) custom-call(bf16[96,4096]{1,0:T(8,128)(2,1)S(1)} %collective-permute-done.8.near_ref, bf16[96,1024]{1,0:T(8,128)(2,1)S(1)} %collective-permute-done.9.refs_0_, bf16[96,1024]{1,0:T(8,128)(2,1)S(1)} %collective-permute-done.10.refs_1_, ...), custom_call_target="tpu_custom_call" | custom-call | flops 1024 | bytes 1024 | tf_op jit(solution)/shard_map/project_held/pallas_call | solution.py:473
  42.6 1.6 %collective-permute-start.14 = (bf16[288,256]{1,0:T(8,128)(2,1)S(1)}, bf16[288,256]{1,0:T(8,128)(2,1)S(1)}, u32[]{:S(2)}, u32[]{:S(2)}) collective-permute-start(bf16[288,256]{1,0:T(8,128)(2,1)S(1)} %constant_dynamic-update-slice_fusion.refs_0_), channel_id=1, source_target_pairs={{0,2},{2,0},{1,3},{3,1},{4,6},{6,4},{5,7},{7,5},{8,10},{10,8},{9,1... | collective-permute-start | bytes 442376 | tf_op jit(solution)/shard_map/ppermute | solution.py:856
  44.2 6.2 %all-to-all-done.pulled_ref = bf16[4,8,64,256]{3,2,1,0:T(8,128)(2,1)S(1)} async-done(((bf16[4,8,64,256]{3,2,1,0:T(8,128)(2,1)}), bf16[4,8,64,256]{3,2,1,0:T(8,128)(2,1)S(1)}, u32[]{:S(2)}, u32[]{:S(2)}) %all-to-all-start) | async-done | bytes 1048608 | tf_op jit(solution)/shard_map/all_to_all | solution.py:885
  50.4 7.6 %attend_out.2 = (bf16[96,1024]{1,0:T(8,128)(2,1)S(1)}, bf16[96,1024]{1,0:T(8,128)(2,1)S(1)}, bf16[96,1024]{1,0:T(8,128)(2,1)S(1)}, bf16[96,1024]{1,0:T(8,128)(2,1)S(1)}, bf16[96,4096]{1,0:T(8,128)(2,1)S(1)}) custom-call(s32[40]{0:T(128)S(1)} %concatenate.7.refs_1_.place_ref, bf16[96,1024]{1,0:T(8,128)(2,1)S(1)} %get-tuple-element.60.q_ref, ...), custom_call_target="tpu_custom_call" | custom-call | flops 1024 | bytes 4000000 | tf_op jit(solution)/shard_map/attend_out/pallas_call | solution.py:575
  58.1 0.5 collective-permute-start.17
  58.6 0.1 collective-permute-start.16
  58.7 0.4 collective-permute-start.15
  59.1 0.4 collective-permute-done.18.refs_3_
  59.5 0.3 collective-permute-done.17.refs_2_
  59.8 0.3 collective-permute-done.16.refs_1_
  60.1 0.3 collective-permute-done.15.refs_0_
  60.4 0.2 add_pair.2
  60.6 0.3 collective-permute-start.19
  60.8 1.5 %collective-permute-start.26 = (bf16[96,4096]{1,0:T(8,128)(2,1)S(1)}, bf16[96,4096]{1,0:T(8,128)(2,1)S(1)}, u32[]{:S(2)}, u32[]{:S(2)}) collective-permute-start(bf16[96,4096]{1,0:T(8,128)(2,1)S(1)} %add_pair.2), channel_id=1, source_target_pairs={{0,2},{2,0},{1,3},{3,1},{4,6},{6,4},{5,7},{7,5},{8,10},{10,8},{9,1... | collective-permute-start | bytes 2359304 | tf_op jit(solution)/shard_map/ppermute | solution.py:856
  62.4 0.8 collective-permute-done.19.far_ref
  63.1 8.5 %project_far.1 = (bf16[96,1024]{1,0:T(8,128)(2,1)S(1)}, bf16[96,256]{1,0:T(8,128)(2,1)S(1)}) custom-call(s32[4]{0:T(128)S(1)} %pad_add_fusion.place_ref, bf16[96,4096]{1,0:T(8,128)(2,1)} %collective-permute-done.13.near_ref, bf16[96,4096]{1,0:T(8,128)(2,1)S(1)} %collective-permute-done.19.far_ref, bf16[8192,1024]{1,0:T(8,128)(2,1)} %wq.3, bf16[8192,256]{1,0:T(8,128)(2,1)} %wkv.3), custom_call_target="tpu_custom_call" | custom-call | flops 1024 | bytes 1024 | tf_op jit(solution)/shard_map/project_far/pallas_call | solution.py:517
  71.6 1.6 %collective-permute-start.20 = (bf16[96,256]{1,0:T(8,128)(2,1)S(1)}, bf16[96,256]{1,0:T(8,128)(2,1)S(1)}, u32[]{:S(2)}, u32[]{:S(2)}) collective-permute-start(bf16[96,256]{1,0:T(8,128)(2,1)S(1)} %get-tuple-element.71.refs_2_.refs_3_), channel_id=1, source_target_pairs={{0,2},{2,0},{1,3},{3,1},{4,6},{6,4},{5,7},{7,5},{8,10},{10,8},{9,1... | collective-permute-start | bytes 147464 | tf_op jit(solution)/shard_map/ppermute | solution.py:856
  73.2 7.0 %attend_out.3 = (bf16[96,1024]{1,0:T(8,128)(2,1)S(1)}, bf16[96,1024]{1,0:T(8,128)(2,1)S(1)}, bf16[96,1024]{1,0:T(8,128)(2,1)S(1)}, bf16[96,1024]{1,0:T(8,128)(2,1)S(1)}, bf16[96,4096]{1,0:T(8,128)(2,1)S(1)}) custom-call(s32[40]{0:T(128)S(1)} %concatenate.7.refs_1_.place_ref, bf16[96,1024]{1,0:T(8,128)(2,1)S(1)} %get-tuple-element.72.q_ref, ...), custom_call_target="tpu_custom_call" | custom-call | flops 1024 | bytes 4000000 | tf_op jit(solution)/shard_map/attend_out/pallas_call | solution.py:575
  80.2 1.4 %collective-permute-done.20.refs_4_ = bf16[96,256]{1,0:T(8,128)(2,1)S(1)} collective-permute-done((bf16[96,256]{1,0:T(8,128)(2,1)S(1)}, bf16[96,256]{1,0:T(8,128)(2,1)S(1)}, u32[]{:S(2)}, u32[]{:S(2)}) %collective-permute-start.20) | collective-permute-done | bytes 49184 | tf_op jit(solution)/shard_map/ppermute | solution.py:856
  81.6 0.5 collective-permute-start.23
  82.1 0.5 collective-permute-start.21
  82.7 0.4 collective-permute-done.24.refs_3_
  83.1 0.3 collective-permute-done.23.refs_2_
  83.4 0.3 collective-permute-done.22.refs_1_
  83.6 0.3 collective-permute-done.21.refs_0_
  83.9 0.2 add_pair.3.refs_4_
  84.1 1.6 %collective-permute-start.27 = (bf16[96,4096]{1,0:T(8,128)(2,1)S(1)}, bf16[96,4096]{1,0:T(8,128)(2,1)S(1)}, u32[]{:S(2)}, u32[]{:S(2)}) collective-permute-start(bf16[96,4096]{1,0:T(8,128)(2,1)S(1)} %add_pair.3.refs_4_), channel_id=1, source_target_pairs={{0,2},{2,0},{1,3},{3,1},{4,6},{6,4},{5,7},{7,5},{8,10},{10,8},{9,1... | collective-permute-start | bytes 2359304 | tf_op jit(solution)/shard_map/ppermute | solution.py:856
  85.8 0.6 collective-permute-start.29
  86.4 1.0 collective-permute-done.28.refs_2_
  87.4 0.1 collective-permute-done.29.refs_5_
  87.5 1.8 %write_pool.1 = bf16[4,4,64,256]{3,2,1,0:T(8,128)(2,1)} custom-call(s32[4]{0:T(128)S(1)} %pad_add_fusion.place_ref, s32[1,6]{1,0:T(1,128)S(1)} %copy-done.7, bf16[4,4,64,256]{3,2,1,0:T(8,128)(2,1)S(1)} %copy-done.1, bf16[288,256]{1,0:T(8,128)(2,1)S(1)} %constant_dynamic-update-slice_fusion.refs_0_, bf16[288,256]{1,0:T(8,128)(2,1)S(1)} %collective-permute-done.14.refs_1_, ...), custom_call_target="tpu_custom_call" | custom-call | flops 1024 | bytes 1024 | tf_op jit(solution)/shard_map/write_pool/pallas_call | solution.py:821
  89.3 10.2 %local_rows.1 = (bf16[96,8192]{1,0:T(8,128)(2,1)S(1)}, bf16[96,8192]{1,0:T(8,128)(2,1)S(1)}) custom-call(s32[40]{0:T(128)S(1)} %concatenate.7.refs_1_.place_ref, bf16[192,1024]{1,0:T(8,128)(2,1)S(1)} %copy-done.5, bf16[4,8,64,256]{3,2,1,0:T(8,128)(2,1)S(1)} %all-to-all-done.pulled_ref, bf16[192,256]{1,0:T(8,128)(2,1)S(1)} %get-tuple-element.55.refs_0_, ...), custom_call_target="tpu_custom_call" | custom-call | flops 1024 | bytes 1024 | tf_op jit(solution)/shard_map/local_rows/pallas_call | solution.py:638
  99.5 0.3 collective-permute-start.25
  99.8 4.1 %collective-permute-done.27 = bf16[96,4096]{1,0:T(8,128)(2,1)S(1)} collective-permute-done((bf16[96,4096]{1,0:T(8,128)(2,1)S(1)}, bf16[96,4096]{1,0:T(8,128)(2,1)S(1)}, u32[]{:S(2)}, u32[]{:S(2)}) %collective-permute-start.27) | collective-permute-done | bytes 786464 | tf_op jit(solution)/shard_map/ppermute | solution.py:856
  103.9 0.1 broadcast_select_fusion
  104.1 1.1 %finish_near.1 = (bf16[96,4096]{1,0:T(8,128)(2,1)S(1)}, f32[96,4096]{1,0:T(8,128)S(1)}) custom-call(s32[4]{0:T(128)S(1)} %pad_add_fusion.place_ref, bf16[96,8192]{1,0:T(8,128)(2,1)S(1)} %copy-done, bf16[96,8192]{1,0:T(8,128)(2,1)S(1)} %get-tuple-element.82.own_ref, bf16[96,8192]{1,0:T(8,128)(2,1)S(1)} %collective-permute-done.25.peer_ref, ...), custom_call_target="tpu_custom_call" | custom-call | flops 1024 | bytes 1024 | tf_op jit(solution)/shard_map/finish_near/pallas_call | solution.py:699
  105.2 1.1 %collective-permute-done.30.far_ref = bf16[96,4096]{1,0:T(8,128)(2,1)S(1)} collective-permute-done((bf16[96,4096]{1,0:T(8,128)(2,1)S(1)}, bf16[96,4096]{1,0:T(8,128)(2,1)S(1)}, u32[]{:S(2)}, u32[]{:S(2)}) %collective-permute-start.30) | collective-permute-done | bytes 786464 | tf_op jit(solution)/shard_map/ppermute | solution.py:853
  106.3 1.7 %finish.1 = bf16[96,8192]{1,0:T(8,128)(2,1)} custom-call(s32[4]{0:T(128)S(1)} %pad_add_fusion.place_ref, bf16[96,8192]{1,0:T(8,128)(2,1)S(1)} %copy-done, bf16[96,4096]{1,0:T(8,128)(2,1)S(1)} %get-tuple-element.86.done_ref, f32[96,4096]{1,0:T(8,128)S(1)} %get-tuple-element.87.local_ref, bf16[96,4096]{1,0:T(8,128)(2,1)S(1)} %collective-permute-done.30.far_ref), custom_call_target="tpu_custom_call" | custom-call | flops 1024 | bytes 1024 | tf_op jit(solution)/shard_map/finish/pallas_call | solution.py:739
  (47 shorter events, 0.6 us)
Async XLA Ops:
  0.6 7.0 %copy-start.6 = (s32[1,16,2]{1,2,0:T(2,128)S(1)}, s32[1,16,2]{1,2,0:T(2,128)}, u32[]{:S(2)}) copy-start(s32[1,16,2]{1,2,0:T(2,128)} %param.17) | copy-start | bytes 388
  4.4 11.5 %copy-start.8 = (bf16[96,4096]{1,0:T(8,128)(2,1)}, bf16[96,4096]{1,0:T(8,128)(2,1)S(1)}, u32[]{:S(2)}) copy-start(bf16[96,4096]{1,0:T(8,128)(2,1)S(1)} %get-tuple-element.50.far_own) | copy-start | bytes 2359300
  4.4 9.9 %collective-permute-start.6 = (bf16[96,4096]{1,0:T(8,128)(2,1)S(1)}, bf16[96,4096]{1,0:T(8,128)(2,1)S(1)}, u32[]{:S(2)}, u32[]{:S(2)}) collective-permute-start(bf16[96,4096]{1,0:T(8,128)(2,1)S(1)} %get-tuple-element.50.far_own), channel_id=1, source_target_pairs={{0,1},{1,0},{2,3},{3,2},{4,5},{5,4},{6,7},{7,6},{8,9},{9,8},{10,11... | collective-permute-start | bytes 2359304 | tf_op jit(solution)/shard_map/ppermute | solution.py:853
  4.9 6.9 %collective-permute-start.4 = (bf16[4,64,256]{2,1,0:T(8,128)(2,1)S(1)}, bf16[4,64,256]{2,1,0:T(8,128)(2,1)S(1)}, u32[]{:S(2)}, u32[]{:S(2)}) collective-permute-start(bf16[4,64,256]{2,1,0:T(8,128)(2,1)S(1)} %get-tuple-element.47), channel_id=1, source_target_pairs={{0,2},{1,3},{2,0},{3,1},{4,6},{5,7},{6,4},{7,5},{8,10},{9,11},{10,... | collective-permute-start | bytes 393224 | tf_op jit(solution)/shard_map/ppermute | solution.py:870
  7.5 6.6 %collective-permute-start.5 = (bf16[4,64,256]{2,1,0:T(8,128)(2,1)S(1)}, bf16[4,64,256]{2,1,0:T(8,128)(2,1)S(1)}, u32[]{:S(2)}, u32[]{:S(2)}) collective-permute-start(bf16[4,64,256]{2,1,0:T(8,128)(2,1)S(1)} %get-tuple-element.48), channel_id=1, source_target_pairs={{0,3},{1,2},{2,1},{3,0},{4,7},{5,6},{6,5},{7,4},{8,11},{9,10},{10,... | collective-permute-start | bytes 393224 | tf_op jit(solution)/shard_map/ppermute | solution.py:870
  7.6 8.3 %collective-permute-start = (s32[1,2,16]{2,1,0:T(2,128)S(1)}, s32[1,2,16]{2,1,0:T(2,128)S(1)}, u32[]{:S(2)}, u32[]{:S(2)}) collective-permute-start(s32[1,2,16]{2,1,0:T(2,128)S(1)} %bitcast.15), channel_id=1, source_target_pairs={{0,12},{4,0},{8,4},{12,8},{1,13},{5,1},{9,5},{13,9},{2,14},{6,2},{... | collective-permute-start | bytes 392 | tf_op jit(solution)/shard_map/ppermute | solution.py:866
  11.4 6.2 %collective-permute-start.1 = (s32[1,2,16]{2,1,0:T(2,128)S(1)}, s32[1,2,16]{2,1,0:T(2,128)S(1)}, u32[]{:S(2)}, u32[]{:S(2)}) collective-permute-start(s32[1,2,16]{2,1,0:T(2,128)S(1)} %bitcast.16), channel_id=1, source_target_pairs={{0,8},{4,12},{8,0},{12,4},{1,9},{5,13},{9,1},{13,5},{2,10},{6,14},... | collective-permute-start | bytes 392 | tf_op jit(solution)/shard_map/ppermute | solution.py:866
  11.9 6.2 %collective-permute-start.2 = (s32[1,2,16]{2,1,0:T(2,128)S(1)}, s32[1,2,16]{2,1,0:T(2,128)S(1)}, u32[]{:S(2)}, u32[]{:S(2)}) collective-permute-start(s32[1,2,16]{2,1,0:T(2,128)S(1)} %bitcast.17), channel_id=1, source_target_pairs={{0,4},{4,8},{8,12},{12,0},{1,5},{5,9},{9,13},{13,1},{2,6},{6,10},{... | collective-permute-start | bytes 392 | tf_op jit(solution)/shard_map/ppermute | solution.py:866
  14.2 3.9 %collective-permute-start.3 = (bf16[4,64,256]{2,1,0:T(8,128)(2,1)}, bf16[4,64,256]{2,1,0:T(8,128)(2,1)S(1)}, u32[]{:S(2)}, u32[]{:S(2)}) collective-permute-start(bf16[4,64,256]{2,1,0:T(8,128)(2,1)} %get-tuple-element.46), channel_id=1, source_target_pairs={{0,1},{1,0},{2,3},{3,2},{4,5},{5,4},{6,7},{7,6},{8,9},{9,8},{10,11... | collective-permute-start | bytes 393224 | tf_op jit(solution)/shard_map/ppermute | solution.py:870
  14.3 1.7 %copy-start.2 = (bf16[96,4096]{1,0:T(8,128)(2,1)}, bf16[96,4096]{1,0:T(8,128)(2,1)S(1)}, u32[]{:S(2)}) copy-start(bf16[96,4096]{1,0:T(8,128)(2,1)S(1)} %collective-permute-done.6.near_peer) | copy-start | bytes 2359300
  14.3 10.7 %collective-permute-start.7 = (bf16[96,4096]{1,0:T(8,128)(2,1)}, bf16[96,4096]{1,0:T(8,128)(2,1)}, u32[]{:S(2)}, u32[]{:S(2)}) collective-permute-start(bf16[96,4096]{1,0:T(8,128)(2,1)} %get-tuple-element.49.near_own), channel_id=1, source_target_pairs={{0,1},{1,0},{2,3},{3,2},{4,5},{5,4},{6,7},{7,6},{8,9},{9,8},{10,11... | collective-permute-start | bytes 2359304 | tf_op jit(solution)/shard_map/ppermute | solution.py:853
  15.9 20.6 %collective-permute-start.8 = (bf16[96,4096]{1,0:T(8,128)(2,1)S(1)}, bf16[96,4096]{1,0:T(8,128)(2,1)S(1)}, u32[]{:S(2)}, u32[]{:S(2)}) collective-permute-start(bf16[96,4096]{1,0:T(8,128)(2,1)S(1)} %get-tuple-element.91.refs_8_), channel_id=1, source_target_pairs={{0,2},{2,0},{1,3},{3,1},{4,6},{6,4},{5,7},{7,5},{8,10},{10,8},{9,1... | collective-permute-start | bytes 2359304 | tf_op jit(solution)/shard_map/ppermute | solution.py:856
  17.6 42.9 %collective-permute-start.13 = (bf16[96,4096]{1,0:T(8,128)(2,1)S(1)}, bf16[96,4096]{1,0:T(8,128)(2,1)}, u32[]{:S(2)}, u32[]{:S(2)}) collective-permute-start(bf16[96,4096]{1,0:T(8,128)(2,1)S(1)} %get-tuple-element.90.refs_9_), channel_id=1, source_target_pairs={{0,2},{2,0},{1,3},{3,1},{4,6},{6,4},{5,7},{7,5},{8,10},{10,8},{9,1... | collective-permute-start | bytes 2359304 | tf_op jit(solution)/shard_map/ppermute | solution.py:856
  19.7 5.1 %copy-start.11 = (s32[1,16,2]{1,2,0:T(2,128)S(1)}, s32[1,16,2]{1,2,0:T(2,128)}, u32[]{:S(2)}) copy-start(s32[1,16,2]{1,2,0:T(2,128)} %param.18) | copy-start | bytes 388
  19.7 5.2 %copy-start.10 = (s32[1,4]{1,0:T(1,128)S(1)}, s32[1,4]{1,0:T(1,128)}, u32[]{:S(2)}) copy-start(s32[1,4]{1,0:T(1,128)} %param.16) | copy-start | bytes 52
  19.7 30.7 %all-to-all-start = ((bf16[4,8,64,256]{3,2,1,0:T(8,128)(2,1)}), bf16[4,8,64,256]{3,2,1,0:T(8,128)(2,1)S(1)}, u32[]{:S(2)}, u32[]{:S(2)}) async-start(bf16[4,8,64,256]{3,2,1,0:T(8,128)(2,1)} %pick_pages.1.refs_0_), calls=%async_computation | async-start | bytes 2097152 | tf_op jit(solution)/shard_map/all_to_all | solution.py:885
  25.0 1.1 %copy-start.3 = (bf16[96,4096]{1,0:T(8,128)(2,1)S(1)}, bf16[96,4096]{1,0:T(8,128)(2,1)}, u32[]{:S(2)}) copy-start(bf16[96,4096]{1,0:T(8,128)(2,1)} %copy-done.2) | copy-start | bytes 2359300
  26.1 1.1 %copy-start.9 = (bf16[96,4096]{1,0:T(8,128)(2,1)S(1)}, bf16[96,4096]{1,0:T(8,128)(2,1)}, u32[]{:S(2)}) copy-start(bf16[96,4096]{1,0:T(8,128)(2,1)} %copy-done.8) | copy-start | bytes 2359300
  36.5 6.1 %copy-start.4 = (bf16[192,1024]{1,0:T(8,128)(2,1)}, bf16[192,1024]{1,0:T(8,128)(2,1)S(1)}, u32[]{:S(2)}) copy-start(bf16[192,1024]{1,0:T(8,128)(2,1)S(1)} %get-tuple-element.54.q_ref) | copy-start | bytes 1179652
  36.6 1.5 %collective-permute-start.10 = (bf16[96,1024]{1,0:T(8,128)(2,1)S(1)}, bf16[96,1024]{1,0:T(8,128)(2,1)S(1)}, u32[]{:S(2)}, u32[]{:S(2)}) collective-permute-start(bf16[96,1024]{1,0:T(8,128)(2,1)S(1)} %get-tuple-element.94), channel_id=1, source_target_pairs={{0,1},{1,0},{2,3},{3,2},{4,5},{5,4},{6,7},{7,6},{8,9},{9,8},{10,11... | collective-permute-start | bytes 589832 | tf_op jit(solution)/shard_map/ppermute | solution.py:853
  36.7 1.7 %collective-permute-start.11 = (bf16[96,1024]{1,0:T(8,128)(2,1)S(1)}, bf16[96,1024]{1,0:T(8,128)(2,1)S(1)}, u32[]{:S(2)}, u32[]{:S(2)}) collective-permute-start(bf16[96,1024]{1,0:T(8,128)(2,1)S(1)} %get-tuple-element.93), channel_id=1, source_target_pairs={{0,1},{1,0},{2,3},{3,2},{4,5},{5,4},{6,7},{7,6},{8,9},{9,8},{10,11... | collective-permute-start | bytes 589832 | tf_op jit(solution)/shard_map/ppermute | solution.py:853
  37.2 1.5 %collective-permute-start.12 = (bf16[96,1024]{1,0:T(8,128)(2,1)S(1)}, bf16[96,1024]{1,0:T(8,128)(2,1)S(1)}, u32[]{:S(2)}, u32[]{:S(2)}) collective-permute-start(bf16[96,1024]{1,0:T(8,128)(2,1)S(1)} %get-tuple-element.92), channel_id=1, source_target_pairs={{0,1},{1,0},{2,3},{3,2},{4,5},{5,4},{6,7},{7,6},{8,9},{9,8},{10,11... | collective-permute-start | bytes 589832 | tf_op jit(solution)/shard_map/ppermute | solution.py:853
  37.3 1.7 %collective-permute-start.9 = (bf16[96,1024]{1,0:T(8,128)(2,1)S(1)}, bf16[96,1024]{1,0:T(8,128)(2,1)S(1)}, u32[]{:S(2)}, u32[]{:S(2)}) collective-permute-start(bf16[96,1024]{1,0:T(8,128)(2,1)S(1)} %get-tuple-element.95), channel_id=1, source_target_pairs={{0,1},{1,0},{2,3},{3,2},{4,5},{5,4},{6,7},{7,6},{8,9},{9,8},{10,11... | collective-permute-start | bytes 589832 | tf_op jit(solution)/shard_map/ppermute | solution.py:853
  42.6 15.4 %collective-permute-start.14 = (bf16[288,256]{1,0:T(8,128)(2,1)S(1)}, bf16[288,256]{1,0:T(8,128)(2,1)S(1)}, u32[]{:S(2)}, u32[]{:S(2)}) collective-permute-start(bf16[288,256]{1,0:T(8,128)(2,1)S(1)} %constant_dynamic-update-slice_fusion.refs_0_), channel_id=1, source_target_pairs={{0,2},{2,0},{1,3},{3,1},{4,6},{6,4},{5,7},{7,5},{8,10},{10,8},{9,1... | collective-permute-start | bytes 442376 | tf_op jit(solution)/shard_map/ppermute | solution.py:856
  58.0 1.5 %collective-permute-start.18 = (bf16[96,1024]{1,0:T(8,128)(2,1)S(1)}, bf16[96,1024]{1,0:T(8,128)(2,1)S(1)}, u32[]{:S(2)}, u32[]{:S(2)}) collective-permute-start(bf16[96,1024]{1,0:T(8,128)(2,1)S(1)} %get-tuple-element.69), channel_id=1, source_target_pairs={{0,1},{1,0},{2,3},{3,2},{4,5},{5,4},{6,7},{7,6},{8,9},{9,8},{10,11... | collective-permute-start | bytes 589832 | tf_op jit(solution)/shard_map/ppermute | solution.py:853
  58.1 1.7 %collective-permute-start.17 = (bf16[96,1024]{1,0:T(8,128)(2,1)S(1)}, bf16[96,1024]{1,0:T(8,128)(2,1)S(1)}, u32[]{:S(2)}, u32[]{:S(2)}) collective-permute-start(bf16[96,1024]{1,0:T(8,128)(2,1)S(1)} %get-tuple-element.67), channel_id=1, source_target_pairs={{0,1},{1,0},{2,3},{3,2},{4,5},{5,4},{6,7},{7,6},{8,9},{9,8},{10,11... | collective-permute-start | bytes 589832 | tf_op jit(solution)/shard_map/ppermute | solution.py:853
  58.6 1.5 %collective-permute-start.16 = (bf16[96,1024]{1,0:T(8,128)(2,1)S(1)}, bf16[96,1024]{1,0:T(8,128)(2,1)S(1)}, u32[]{:S(2)}, u32[]{:S(2)}) collective-permute-start(bf16[96,1024]{1,0:T(8,128)(2,1)S(1)} %get-tuple-element.65), channel_id=1, source_target_pairs={{0,1},{1,0},{2,3},{3,2},{4,5},{5,4},{6,7},{7,6},{8,9},{9,8},{10,11... | collective-permute-start | bytes 589832 | tf_op jit(solution)/shard_map/ppermute | solution.py:853
  58.7 1.7 %collective-permute-start.15 = (bf16[96,1024]{1,0:T(8,128)(2,1)S(1)}, bf16[96,1024]{1,0:T(8,128)(2,1)S(1)}, u32[]{:S(2)}, u32[]{:S(2)}) collective-permute-start(bf16[96,1024]{1,0:T(8,128)(2,1)S(1)} %get-tuple-element.63), channel_id=1, source_target_pairs={{0,1},{1,0},{2,3},{3,2},{4,5},{5,4},{6,7},{7,6},{8,9},{9,8},{10,11... | collective-permute-start | bytes 589832 | tf_op jit(solution)/shard_map/ppermute | solution.py:853
  60.6 2.6 %collective-permute-start.19 = (bf16[96,4096]{1,0:T(8,128)(2,1)}, bf16[96,4096]{1,0:T(8,128)(2,1)S(1)}, u32[]{:S(2)}, u32[]{:S(2)}) collective-permute-start(bf16[96,4096]{1,0:T(8,128)(2,1)} %collective-permute-done.13.near_ref), channel_id=1, source_target_pairs={{0,1},{1,0},{2,3},{3,2},{4,5},{5,4},{6,7},{7,6},{8,9},{9,8},{10,11... | collective-permute-start | bytes 2359304 | tf_op jit(solution)/shard_map/ppermute | solution.py:853
  60.8 23.3 %collective-permute-start.26 = (bf16[96,4096]{1,0:T(8,128)(2,1)S(1)}, bf16[96,4096]{1,0:T(8,128)(2,1)S(1)}, u32[]{:S(2)}, u32[]{:S(2)}) collective-permute-start(bf16[96,4096]{1,0:T(8,128)(2,1)S(1)} %add_pair.2), channel_id=1, source_target_pairs={{0,2},{2,0},{1,3},{3,1},{4,6},{6,4},{5,7},{7,5},{8,10},{10,8},{9,1... | collective-permute-start | bytes 2359304 | tf_op jit(solution)/shard_map/ppermute | solution.py:856
  71.6 10.0 %collective-permute-start.20 = (bf16[96,256]{1,0:T(8,128)(2,1)S(1)}, bf16[96,256]{1,0:T(8,128)(2,1)S(1)}, u32[]{:S(2)}, u32[]{:S(2)}) collective-permute-start(bf16[96,256]{1,0:T(8,128)(2,1)S(1)} %get-tuple-element.71.refs_2_.refs_3_), channel_id=1, source_target_pairs={{0,2},{2,0},{1,3},{3,1},{4,6},{6,4},{5,7},{7,5},{8,10},{10,8},{9,1... | collective-permute-start | bytes 147464 | tf_op jit(solution)/shard_map/ppermute | solution.py:856
  81.6 1.4 %collective-permute-start.24 = (bf16[96,1024]{1,0:T(8,128)(2,1)S(1)}, bf16[96,1024]{1,0:T(8,128)(2,1)S(1)}, u32[]{:S(2)}, u32[]{:S(2)}) collective-permute-start(bf16[96,1024]{1,0:T(8,128)(2,1)S(1)} %get-tuple-element.81), channel_id=1, source_target_pairs={{0,1},{1,0},{2,3},{3,2},{4,5},{5,4},{6,7},{7,6},{8,9},{9,8},{10,11... | collective-permute-start | bytes 589832 | tf_op jit(solution)/shard_map/ppermute | solution.py:853
  81.6 1.7 %collective-permute-start.23 = (bf16[96,1024]{1,0:T(8,128)(2,1)S(1)}, bf16[96,1024]{1,0:T(8,128)(2,1)S(1)}, u32[]{:S(2)}, u32[]{:S(2)}) collective-permute-start(bf16[96,1024]{1,0:T(8,128)(2,1)S(1)} %get-tuple-element.79), channel_id=1, source_target_pairs={{0,1},{1,0},{2,3},{3,2},{4,5},{5,4},{6,7},{7,6},{8,9},{9,8},{10,11... | collective-permute-start | bytes 589832 | tf_op jit(solution)/shard_map/ppermute | solution.py:853
  82.1 1.5 %collective-permute-start.22 = (bf16[96,1024]{1,0:T(8,128)(2,1)S(1)}, bf16[96,1024]{1,0:T(8,128)(2,1)S(1)}, u32[]{:S(2)}, u32[]{:S(2)}) collective-permute-start(bf16[96,1024]{1,0:T(8,128)(2,1)S(1)} %get-tuple-element.77), channel_id=1, source_target_pairs={{0,1},{1,0},{2,3},{3,2},{4,5},{5,4},{6,7},{7,6},{8,9},{9,8},{10,11... | collective-permute-start | bytes 589832 | tf_op jit(solution)/shard_map/ppermute | solution.py:853
  82.1 1.8 %collective-permute-start.21 = (bf16[96,1024]{1,0:T(8,128)(2,1)S(1)}, bf16[96,1024]{1,0:T(8,128)(2,1)S(1)}, u32[]{:S(2)}, u32[]{:S(2)}) collective-permute-start(bf16[96,1024]{1,0:T(8,128)(2,1)S(1)} %get-tuple-element.75), channel_id=1, source_target_pairs={{0,1},{1,0},{2,3},{3,2},{4,5},{5,4},{6,7},{7,6},{8,9},{9,8},{10,11... | collective-permute-start | bytes 589832 | tf_op jit(solution)/shard_map/ppermute | solution.py:853
  83.9 3.6 %copy-start.1 = (bf16[4,4,64,256]{3,2,1,0:T(8,128)(2,1)S(1)}, bf16[4,4,64,256]{3,2,1,0:T(8,128)(2,1)}, u32[]{:S(2)}) copy-start(bf16[4,4,64,256]{3,2,1,0:T(8,128)(2,1)} %pool_ref.1) | copy-start | bytes 1572868
  83.9 3.6 %copy-start.7 = (s32[1,6]{1,0:T(1,128)S(1)}, s32[1,6]{1,0:T(1,128)}, u32[]{:S(2)}) copy-start(s32[1,6]{1,0:T(1,128)} %slot_ref.1) | copy-start | bytes 76
  84.1 5.2 %copy-start.5 = (bf16[192,1024]{1,0:T(8,128)(2,1)S(1)}, bf16[192,1024]{1,0:T(8,128)(2,1)}, u32[]{:S(2)}) copy-start(bf16[192,1024]{1,0:T(8,128)(2,1)} %copy-done.4) | copy-start | bytes 1179652
  84.1 19.7 %collective-permute-start.27 = (bf16[96,4096]{1,0:T(8,128)(2,1)S(1)}, bf16[96,4096]{1,0:T(8,128)(2,1)S(1)}, u32[]{:S(2)}, u32[]{:S(2)}) collective-permute-start(bf16[96,4096]{1,0:T(8,128)(2,1)S(1)} %add_pair.3.refs_4_), channel_id=1, source_target_pairs={{0,2},{2,0},{1,3},{3,1},{4,6},{6,4},{5,7},{7,5},{8,10},{10,8},{9,1... | collective-permute-start | bytes 2359304 | tf_op jit(solution)/shard_map/ppermute | solution.py:856
  85.7 1.6 %collective-permute-start.28 = (bf16[2,288,256]{2,1,0:T(8,128)(2,1)S(1)}, bf16[2,288,256]{2,1,0:T(8,128)(2,1)S(1)}, u32[]{:S(2)}, u32[]{:S(2)}) collective-permute-start(bf16[2,288,256]{2,1,0:T(8,128)(2,1)S(1)} %pad_maximum_fusion), channel_id=1, source_target_pairs={{0,1},{1,0},{2,3},{3,2},{4,5},{5,4},{6,7},{7,6},{8,9},{9,8},{10,11... | collective-permute-start | bytes 884744 | tf_op jit(solution)/shard_map/ppermute | solution.py:853
  85.8 1.7 %collective-permute-start.29 = (bf16[2,96,256]{2,1,0:T(8,128)(2,1)S(1)}, bf16[2,96,256]{2,1,0:T(8,128)(2,1)S(1)}, u32[]{:S(2)}, u32[]{:S(2)}) collective-permute-start(bf16[2,96,256]{2,1,0:T(8,128)(2,1)S(1)} %pad_maximum_fusion.1), channel_id=1, source_target_pairs={{0,1},{1,0},{2,3},{3,2},{4,5},{5,4},{6,7},{7,6},{8,9},{9,8},{10,11... | collective-permute-start | bytes 294920 | tf_op jit(solution)/shard_map/ppermute | solution.py:853
  99.5 4.6 %copy-start = (bf16[96,8192]{1,0:T(8,128)(2,1)S(1)}, bf16[96,8192]{1,0:T(8,128)(2,1)}, u32[]{:S(2)}) copy-start(bf16[96,8192]{1,0:T(8,128)(2,1)} %x_ref.3) | copy-start | bytes 4718596
  99.5 4.5 %collective-permute-start.25 = (bf16[96,8192]{1,0:T(8,128)(2,1)S(1)}, bf16[96,8192]{1,0:T(8,128)(2,1)S(1)}, u32[]{:S(2)}, u32[]{:S(2)}) collective-permute-start(bf16[96,8192]{1,0:T(8,128)(2,1)S(1)} %get-tuple-element.83), channel_id=1, source_target_pairs={{0,1},{1,0},{2,3},{3,2},{4,5},{5,4},{6,7},{7,6},{8,9},{9,8},{10,11... | collective-permute-start | bytes 4718600 | tf_op jit(solution)/shard_map/ppermute | solution.py:853
  104.0 2.4 %collective-permute-start.30 = (bf16[96,4096]{1,0:T(8,128)(2,1)S(1)}, bf16[96,4096]{1,0:T(8,128)(2,1)S(1)}, u32[]{:S(2)}, u32[]{:S(2)}) collective-permute-start(bf16[96,4096]{1,0:T(8,128)(2,1)S(1)} %get-tuple-element.88), channel_id=1, source_target_pairs={{0,1},{1,0},{2,3},{3,2},{4,5},{5,4},{6,7},{7,6},{8,9},{9,8},{10,11... | collective-permute-start | bytes 2359304 | tf_op jit(solution)/shard_map/ppermute | solution.py:853

commit v11 on v10

--- a/solution.py
+++ b/solution.py
@@ -916,7 +916,8 @@
     bases = [local_base, first_base, second_base]
     *there, stay = attend_out(scalars, q_second, fresh, bases, second_base, pulled, w_out)
     late_y = over_y(kv_second)
-    second_mix = add_pair(stay, [over_core(tie(part, late_y)) for part in there])
+    there[-1] = tie(there[-1], late_y)
+    second_mix = add_pair(stay, [over_core(part) for part in there])
     second_sum = over_y(tie(second_mix, first_sum))
 
     own_part, peer_part = local_rows(

time: 109 us -> 108 us (level)
  waiting for transfers between devices: 19.3 us -> 15.8 us
  starting transfers between devices: 27.4 us -> 29.1 us
  Pallas kernels: 56.5 us -> 57.6 us
    ppermute x6, waiting for transfers between devices: 5.54 us -> 2.64 us  [over_y(): return lax.ppermute(x, 'tensor', [(0, 2), (2, 0), (1, 3), (3, 1)])]
    ppermute x6, starting transfers between devices: 8.34 us -> 10.5 us  [over_y(): return lax.ppermute(x, 'tensor', [(0, 2), (2, 0), (1, 3), (3, 1)])]
    pallas_call x1, Pallas kernels: 10.2 us -> 12 us  [local_rows(): pl.pallas_call(kernel, in_specs=[SMEM] + [VMEM] * (2 + known) + [HBM] + [...]
  transfers between devices with their start and end apart: 32 -> 32, of which waited for: 21 -> 21; matrix products, arithmetic and copies ran while one was open for 1% -> 2% of each run, Pallas kernels for 47% -> 49%
where the time goes in v11:
time: 108 us
  Pallas kernels  57.6 us (53%)
  starting transfers between devices  29.1 us (27%)
  waiting for transfers between devices  15.8 us (15%)
  local copies, waits for them, and re-layouts  2.55 us (2%)
  other arithmetic  1.46 us (1%)
  between operations  1.1 us (1%)
    pallas_call x2, Pallas kernels, attend_out(): pl.pallas_call(kernel, in_specs=[SMEM] + [VMEM] * (2 + known) + [HBM], ou...  14 us
    pallas_call x1, Pallas kernels, local_rows(): pl.pallas_call(kernel, in_specs=[SMEM] + [VMEM] * (2 + known) + [HBM] + [...  12 us
    ppermute x6, starting transfers between devices, over_y(): return lax.ppermute(x, 'tensor', [(0, 2), (2, 0), (1, 3), (3, 1)])  10.5 us
    pallas_call x1, Pallas kernels, project_local(): pl.pallas_call(kernel, in_specs=[SMEM] + [VMEM] * 4 + [HBM] * 2 + [ANY] *...  9.27 us
    pallas_call x1, Pallas kernels, project_far(): pl.pallas_call(kernel, in_specs=[SMEM] + [ANY] * 2 + [HBM] * 2 + [ANY] *...  8.48 us
    ppermute x19, waiting for transfers between devices, over_core(): return lax.ppermute(x, 'tensor', [(0, 1), (1, 0), (2, 3), (3, 2)])  6.24 us
    all_to_all x1, waiting for transfers between devices, chip_pair_body(): lax.all_to_all(picked, 'replica', split_axis=0, concat_axis=0, tiled=True)  6.16 us
    ppermute x3, starting transfers between devices, chip_pair_body(): wanted.append(lax.ppermute(wanted[0], 'replica', back))  5.82 us
  transfers between devices with their start and end apart: 32, of which 21 were waited for; matrix products, arithmetic and copies ran while one was open for 2% of the time, Pallas kernels for 49%

profile of v11, /device:TPU:0, one launch (start us, length us, event | category | flops | bytes accessed | tf_op | source)
XLA Modules:
  0.0 107.7 jit_solution(536584454035676557)
XLA Ops:
  0.7 3.7 %prepare.1 = (bf16[96,4096]{1,0:T(8,128)(2,1)}, bf16[96,4096]{1,0:T(8,128)(2,1)S(1)}, bf16[4,64,256]{2,1,0:T(8,128)(2,1)S(1)}, bf16[4,64,256]{2,1,0:T(8,128)(2,1...) custom-call(s32[4]{0:T(128)S(1)} %pad_add_fusion.place_ref, bf16[96,8192]{1,0:T(8,128)(2,1)} %x_ref.3, ...), custom_call_target="tpu_custom_call" | custom-call | flops 1024 | bytes 1024 | tf_op jit(solution)/shard_map/prepare/pallas_call | solution.py:233
  4.4 0.5 collective-permute-start.6
  4.9 2.6 %collective-permute-start.4 = (bf16[4,64,256]{2,1,0:T(8,128)(2,1)S(1)}, bf16[4,64,256]{2,1,0:T(8,128)(2,1)S(1)}, u32[]{:S(2)}, u32[]{:S(2)}) collective-permute-start(bf16[4,64,256]{2,1,0:T(8,128)(2,1)S(1)} %get-tuple-element.44), channel_id=1, source_target_pairs={{0,2},{1,3},{2,0},{3,1},{4,6},{5,7},{6,4},{7,5},{8,10},{9,11},{10,... | collective-permute-start | bytes 393224 | tf_op jit(solution)/shard_map/ppermute | solution.py:870
  7.6 3.8 %collective-permute-start = (s32[1,2,16]{2,1,0:T(2,128)S(1)}, s32[1,2,16]{2,1,0:T(2,128)S(1)}, u32[]{:S(2)}, u32[]{:S(2)}) collective-permute-start(s32[1,2,16]{2,1,0:T(2,128)S(1)} %bitcast.15), channel_id=1, source_target_pairs={{0,12},{4,0},{8,4},{12,8},{1,13},{5,1},{9,5},{13,9},{2,14},{6,2},{... | collective-permute-start | bytes 392 | tf_op jit(solution)/shard_map/ppermute | solution.py:866
  11.4 0.5 collective-permute-done.4.refs_6_
  11.9 2.0 %collective-permute-start.2 = (s32[1,2,16]{2,1,0:T(2,128)S(1)}, s32[1,2,16]{2,1,0:T(2,128)S(1)}, u32[]{:S(2)}, u32[]{:S(2)}) collective-permute-start(s32[1,2,16]{2,1,0:T(2,128)S(1)} %bitcast.17), channel_id=1, source_target_pairs={{0,4},{4,8},{8,12},{12,0},{1,5},{5,9},{9,13},{13,1},{2,6},{6,10},{... | collective-permute-start | bytes 392 | tf_op jit(solution)/shard_map/ppermute | solution.py:866
  13.9 0.3 collective-permute-done.5.refs_7_
  14.2 0.1 collective-permute-start.3
  14.3 0.4 collective-permute-start.7
  14.7 1.2 %broadcast_select_fusion.2 = (bf16[96,4096]{1,0:T(8,128)(2,1)S(1)}, bf16[96,4096]{1,0:T(8,128)(2,1)S(1)}) fusion(bf16[96,4096]{1,0:T(8,128)(2,1)S(1)} %collective-permute-done.6.near_peer, bf16[96,4096]{1,0:T(8,128)(2,1)} %get-tuple-element.46.near_own, pred[]{:T(512)S(6)} %eq.5), kind=kLoop, calls=%fused_computation.2 | loop fusion | flops 786432 | bytes 3145729 | tf_op jit(solution)/shard_map/jit(_where)/select_n | solution.py:877
  15.9 1.7 %collective-permute-start.8 = (bf16[96,4096]{1,0:T(8,128)(2,1)S(1)}, bf16[96,4096]{1,0:T(8,128)(2,1)S(1)}, u32[]{:S(2)}, u32[]{:S(2)}) collective-permute-start(bf16[96,4096]{1,0:T(8,128)(2,1)S(1)} %get-tuple-element.85.refs_8_), channel_id=1, source_target_pairs={{0,2},{2,0},{1,3},{3,1},{4,6},{6,4},{5,7},{7,5},{8,10},{10,8},{9,1... | collective-permute-start | bytes 2359304 | tf_op jit(solution)/shard_map/ppermute | solution.py:856
  17.6 0.4 collective-permute-start.13
  18.0 1.7 %pick_pages.1.refs_0_ = bf16[4,8,64,256]{3,2,1,0:T(8,128)(2,1)} custom-call(s32[4]{0:T(128)S(1)} %pad_add_fusion.place_ref, s32[1,2,16]{2,1,0:T(2,128)S(1)} %bitcast.18, s32[1,2,16]{2,1,0:T(2,128)S(1)} %collective-permute-done.refs_1_, s32[1,2,16]{2,1,0:T(2,128)S(1)} %collective-permute-done.1.refs_2_, s32[1,2,16]{2,1,0:T(2,128)S(1)} %collective-permute-done.2.refs_3_, ...), custom_call_target="tpu_custom_call" | custom-call | flops 1024 | bytes 1024 | tf_op jit(solution)/shard_map/pick_pages/pallas_call | solution.py:772
  19.7 5.1 %all-to-all-start = ((bf16[4,8,64,256]{3,2,1,0:T(8,128)(2,1)}), bf16[4,8,64,256]{3,2,1,0:T(8,128)(2,1)S(1)}, u32[]{:S(2)}, u32[]{:S(2)}) async-start(bf16[4,8,64,256]{3,2,1,0:T(8,128)(2,1)} %pick_pages.1.refs_0_), calls=%async_computation | async-start | bytes 2097152 | tf_op jit(solution)/shard_map/all_to_all | solution.py:885
  24.8 0.1 reshape.7
  24.9 0.1 concatenate.7.refs_1_.place_ref
  25.0 1.1 %copy-done.3 = bf16[96,4096]{1,0:T(8,128)(2,1)S(1)} copy-done((bf16[96,4096]{1,0:T(8,128)(2,1)S(1)}, bf16[96,4096]{1,0:T(8,128)(2,1)}, u32[]{:S(2)}) %copy-start.3) | copy-done | bytes 786456
  26.1 1.1 %copy-done.9 = bf16[96,4096]{1,0:T(8,128)(2,1)S(1)} copy-done((bf16[96,4096]{1,0:T(8,128)(2,1)S(1)}, bf16[96,4096]{1,0:T(8,128)(2,1)}, u32[]{:S(2)}) %copy-start.9) | copy-done | bytes 786456
  27.2 9.3 %project_local.1 = (bf16[192,1024]{1,0:T(8,128)(2,1)S(1)}, bf16[192,256]{1,0:T(8,128)(2,1)S(1)}, bf16[8,1024,1024]{2,1,0:T(8,128)(2,1)S(1)}, bf16[8,1024,256]{2,1,0:T(8,128)(2,1)S(1)}) custom-call(s32[4]{0:T(128)S(1)} %pad_add_fusion.place_ref, bf16[96,4096]{1,0:T(8,128)(2,1)} %get-tuple-element.46.near_own, bf16[96,4096]{1,0:T(8,128)(2,1)S(1)} %copy-done.3, ...), custom_call_target="tpu_custom_call" | custom-call | flops 20000000000 | bytes 200000000 | tf_op jit(solution)/shard_map/project_local/pallas_call | solution.py:287
  36.7 0.5 collective-permute-start.11
  37.2 0.1 collective-permute-start.12
  37.3 0.4 collective-permute-start.9
  37.7 0.4 collective-permute-done.10.refs_1_
  38.1 0.3 collective-permute-done.11.refs_2_
  38.4 0.3 collective-permute-done.12.refs_3_
  38.7 0.3 collective-permute-done.9.refs_0_
  39.0 3.6 %project_held.1 = (bf16[96,1024]{1,0:T(8,128)(2,1)S(1)}, bf16[96,256]{1,0:T(8,128)(2,1)S(1)}) custom-call(bf16[96,4096]{1,0:T(8,128)(2,1)S(1)} %collective-permute-done.8.near_ref, bf16[96,1024]{1,0:T(8,128)(2,1)S(1)} %collective-permute-done.9.refs_0_, bf16[96,1024]{1,0:T(8,128)(2,1)S(1)} %collective-permute-done.10.refs_1_, ...), custom_call_target="tpu_custom_call" | custom-call | flops 1024 | bytes 1024 | tf_op jit(solution)/shard_map/project_held/pallas_call | solution.py:473
  42.6 1.6 %collective-permute-start.14 = (bf16[288,256]{1,0:T(8,128)(2,1)S(1)}, bf16[288,256]{1,0:T(8,128)(2,1)S(1)}, u32[]{:S(2)}, u32[]{:S(2)}) collective-permute-start(bf16[288,256]{1,0:T(8,128)(2,1)S(1)} %constant_dynamic-update-slice_fusion.refs_0_), channel_id=1, source_target_pairs={{0,2},{2,0},{1,3},{3,1},{4,6},{6,4},{5,7},{7,5},{8,10},{10,8},{9,1... | collective-permute-start | bytes 442376 | tf_op jit(solution)/shard_map/ppermute | solution.py:856
  44.2 6.2 %all-to-all-done.pulled_ref = bf16[4,8,64,256]{3,2,1,0:T(8,128)(2,1)S(1)} async-done(((bf16[4,8,64,256]{3,2,1,0:T(8,128)(2,1)}), bf16[4,8,64,256]{3,2,1,0:T(8,128)(2,1)S(1)}, u32[]{:S(2)}, u32[]{:S(2)}) %all-to-all-start) | async-done | bytes 1048608 | tf_op jit(solution)/shard_map/all_to_all | solution.py:885
  50.4 7.0 %attend_out.2 = (bf16[96,1024]{1,0:T(8,128)(2,1)S(1)}, bf16[96,1024]{1,0:T(8,128)(2,1)S(1)}, bf16[96,1024]{1,0:T(8,128)(2,1)S(1)}, bf16[96,1024]{1,0:T(8,128)(2,1)S(1)}, bf16[96,4096]{1,0:T(8,128)(2,1)S(1)}) custom-call(s32[40]{0:T(128)S(1)} %concatenate.7.refs_1_.place_ref, bf16[96,1024]{1,0:T(8,128)(2,1)S(1)} %get-tuple-element.57.q_ref, ...), custom_call_target="tpu_custom_call" | custom-call | flops 1024 | bytes 4000000 | tf_op jit(solution)/shard_map/attend_out/pallas_call | solution.py:575
  57.5 0.5 collective-permute-start.17
  58.0 0.1 collective-permute-start.16
  58.0 0.4 collective-permute-start.15
  58.5 0.4 collective-permute-done.18.refs_3_
  58.9 0.3 collective-permute-done.17.refs_2_
  59.2 0.3 collective-permute-done.16.refs_1_
  59.5 0.3 collective-permute-done.15.refs_0_
  59.7 0.2 add_pair.2
  59.9 0.3 collective-permute-start.19
  60.2 2.7 %collective-permute-start.26 = (bf16[96,4096]{1,0:T(8,128)(2,1)S(1)}, bf16[96,4096]{1,0:T(8,128)(2,1)S(1)}, u32[]{:S(2)}, u32[]{:S(2)}) collective-permute-start(bf16[96,4096]{1,0:T(8,128)(2,1)S(1)} %add_pair.2), channel_id=1, source_target_pairs={{0,2},{2,0},{1,3},{3,1},{4,6},{6,4},{5,7},{7,5},{8,10},{10,8},{9,1... | collective-permute-start | bytes 2359304 | tf_op jit(solution)/shard_map/ppermute | solution.py:856
  63.0 8.5 %project_far.1 = (bf16[96,1024]{1,0:T(8,128)(2,1)S(1)}, bf16[96,256]{1,0:T(8,128)(2,1)S(1)}) custom-call(s32[4]{0:T(128)S(1)} %pad_add_fusion.place_ref, bf16[96,4096]{1,0:T(8,128)(2,1)} %collective-permute-done.13.near_ref, bf16[96,4096]{1,0:T(8,128)(2,1)S(1)} %collective-permute-done.19.far_ref, bf16[8192,1024]{1,0:T(8,128)(2,1)} %wq.3, bf16[8192,256]{1,0:T(8,128)(2,1)} %wkv.3), custom_call_target="tpu_custom_call" | custom-call | flops 1024 | bytes 1024 | tf_op jit(solution)/shard_map/project_far/pallas_call | solution.py:517
  71.4 2.3 %collective-permute-start.23 = (bf16[96,256]{1,0:T(8,128)(2,1)S(1)}, bf16[96,256]{1,0:T(8,128)(2,1)S(1)}, u32[]{:S(2)}, u32[]{:S(2)}) collective-permute-start(bf16[96,256]{1,0:T(8,128)(2,1)S(1)} %get-tuple-element.68.refs_2_.refs_3_), channel_id=1, source_target_pairs={{0,2},{2,0},{1,3},{3,1},{4,6},{6,4},{5,7},{7,5},{8,10},{10,8},{9,1... | collective-permute-start | bytes 147464 | tf_op jit(solution)/shard_map/ppermute | solution.py:856
  73.8 7.0 %attend_out.3 = (bf16[96,1024]{1,0:T(8,128)(2,1)S(1)}, bf16[96,1024]{1,0:T(8,128)(2,1)S(1)}, bf16[96,1024]{1,0:T(8,128)(2,1)S(1)}, bf16[96,1024]{1,0:T(8,128)(2,1)S(1)}, bf16[96,4096]{1,0:T(8,128)(2,1)S(1)}) custom-call(s32[40]{0:T(128)S(1)} %concatenate.7.refs_1_.place_ref, bf16[96,1024]{1,0:T(8,128)(2,1)S(1)} %get-tuple-element.69.q_ref, ...), custom_call_target="tpu_custom_call" | custom-call | flops 1024 | bytes 4000000 | tf_op jit(solution)/shard_map/attend_out/pallas_call | solution.py:575
  80.9 0.5 collective-permute-start.21
  81.4 0.1 collective-permute-start.22
  81.4 0.6 collective-permute-done.23.refs_4_
  82.0 0.3 collective-permute-done.20.refs_0_
  82.3 0.3 collective-permute-done.21.refs_1_
  82.6 0.3 collective-permute-done.22.refs_2_
  82.9 0.6 collective-permute-done.24.refs_3_
  83.4 0.2 add_pair.3.refs_4_
  83.6 1.8 %collective-permute-start.27 = (bf16[96,4096]{1,0:T(8,128)(2,1)S(1)}, bf16[96,4096]{1,0:T(8,128)(2,1)S(1)}, u32[]{:S(2)}, u32[]{:S(2)}) collective-permute-start(bf16[96,4096]{1,0:T(8,128)(2,1)S(1)} %add_pair.3.refs_4_), channel_id=1, source_target_pairs={{0,2},{2,0},{1,3},{3,1},{4,6},{6,4},{5,7},{7,5},{8,10},{10,8},{9,1... | collective-permute-start | bytes 2359304 | tf_op jit(solution)/shard_map/ppermute | solution.py:856
  85.6 0.6 collective-permute-start.29
  86.1 1.0 collective-permute-done.28.refs_2_
  87.1 0.1 collective-permute-done.29.refs_5_
  87.3 1.8 %write_pool.1 = bf16[4,4,64,256]{3,2,1,0:T(8,128)(2,1)} custom-call(s32[4]{0:T(128)S(1)} %pad_add_fusion.place_ref, s32[1,6]{1,0:T(1,128)S(1)} %copy-done.7, bf16[4,4,64,256]{3,2,1,0:T(8,128)(2,1)S(1)} %copy-done.1, bf16[288,256]{1,0:T(8,128)(2,1)S(1)} %constant_dynamic-update-slice_fusion.refs_0_, bf16[288,256]{1,0:T(8,128)(2,1)S(1)} %collective-permute-done.14.refs_1_, ...), custom_call_target="tpu_custom_call" | custom-call | flops 1024 | bytes 1024 | tf_op jit(solution)/shard_map/write_pool/pallas_call | solution.py:821
  89.1 12.0 %local_rows.1 = (bf16[96,8192]{1,0:T(8,128)(2,1)S(1)}, bf16[96,8192]{1,0:T(8,128)(2,1)S(1)}) custom-call(s32[40]{0:T(128)S(1)} %concatenate.7.refs_1_.place_ref, bf16[192,1024]{1,0:T(8,128)(2,1)S(1)} %copy-done.5, bf16[4,8,64,256]{3,2,1,0:T(8,128)(2,1)S(1)} %all-to-all-done.pulled_ref, bf16[192,256]{1,0:T(8,128)(2,1)S(1)} %get-tuple-element.52.refs_0_, ...), custom_call_target="tpu_custom_call" | custom-call | flops 1024 | bytes 1024 | tf_op jit(solution)/shard_map/local_rows/pallas_call | solution.py:638
  101.0 0.2 collective-permute-start.25
  101.2 2.1 %collective-permute-done.27 = bf16[96,4096]{1,0:T(8,128)(2,1)S(1)} collective-permute-done((bf16[96,4096]{1,0:T(8,128)(2,1)S(1)}, bf16[96,4096]{1,0:T(8,128)(2,1)S(1)}, u32[]{:S(2)}, u32[]{:S(2)}) %collective-permute-start.27) | collective-permute-done | bytes 786464 | tf_op jit(solution)/shard_map/ppermute | solution.py:856
  103.3 0.1 broadcast_select_fusion
  103.5 1.0 collective-permute-done.25.peer_ref
  104.5 1.1 %finish_near.1 = (bf16[96,4096]{1,0:T(8,128)(2,1)S(1)}, f32[96,4096]{1,0:T(8,128)S(1)}) custom-call(s32[4]{0:T(128)S(1)} %pad_add_fusion.place_ref, bf16[96,8192]{1,0:T(8,128)(2,1)S(1)} %copy-done, bf16[96,8192]{1,0:T(8,128)(2,1)S(1)} %get-tuple-element.76.own_ref, bf16[96,8192]{1,0:T(8,128)(2,1)S(1)} %collective-permute-done.25.peer_ref, ...), custom_call_target="tpu_custom_call" | custom-call | flops 1024 | bytes 1024 | tf_op jit(solution)/shard_map/finish_near/pallas_call | solution.py:699
  105.6 0.1 collective-permute-done.30.far_ref
  105.8 1.7 %finish.1 = bf16[96,8192]{1,0:T(8,128)(2,1)} custom-call(s32[4]{0:T(128)S(1)} %pad_add_fusion.place_ref, bf16[96,8192]{1,0:T(8,128)(2,1)S(1)} %copy-done, bf16[96,4096]{1,0:T(8,128)(2,1)S(1)} %get-tuple-element.80.done_ref, f32[96,4096]{1,0:T(8,128)S(1)} %get-tuple-element.81.local_ref, bf16[96,4096]{1,0:T(8,128)(2,1)S(1)} %collective-permute-done.30.far_ref), custom_call_target="tpu_custom_call" | custom-call | flops 1024 | bytes 1024 | tf_op jit(solution)/shard_map/finish/pallas_call | solution.py:739
  (47 shorter events, 0.7 us)
Async XLA Ops:
  0.6 7.0 %copy-start.6 = (s32[1,16,2]{1,2,0:T(2,128)S(1)}, s32[1,16,2]{1,2,0:T(2,128)}, u32[]{:S(2)}) copy-start(s32[1,16,2]{1,2,0:T(2,128)} %param.17) | copy-start | bytes 388
  4.4 11.5 %copy-start.8 = (bf16[96,4096]{1,0:T(8,128)(2,1)}, bf16[96,4096]{1,0:T(8,128)(2,1)S(1)}, u32[]{:S(2)}) copy-start(bf16[96,4096]{1,0:T(8,128)(2,1)S(1)} %get-tuple-element.47.far_own) | copy-start | bytes 2359300
  4.4 9.9 %collective-permute-start.6 = (bf16[96,4096]{1,0:T(8,128)(2,1)S(1)}, bf16[96,4096]{1,0:T(8,128)(2,1)S(1)}, u32[]{:S(2)}, u32[]{:S(2)}) collective-permute-start(bf16[96,4096]{1,0:T(8,128)(2,1)S(1)} %get-tuple-element.47.far_own), channel_id=1, source_target_pairs={{0,1},{1,0},{2,3},{3,2},{4,5},{5,4},{6,7},{7,6},{8,9},{9,8},{10,11... | collective-permute-start | bytes 2359304 | tf_op jit(solution)/shard_map/ppermute | solution.py:853
  4.9 6.9 %collective-permute-start.4 = (bf16[4,64,256]{2,1,0:T(8,128)(2,1)S(1)}, bf16[4,64,256]{2,1,0:T(8,128)(2,1)S(1)}, u32[]{:S(2)}, u32[]{:S(2)}) collective-permute-start(bf16[4,64,256]{2,1,0:T(8,128)(2,1)S(1)} %get-tuple-element.44), channel_id=1, source_target_pairs={{0,2},{1,3},{2,0},{3,1},{4,6},{5,7},{6,4},{7,5},{8,10},{9,11},{10,... | collective-permute-start | bytes 393224 | tf_op jit(solution)/shard_map/ppermute | solution.py:870
  7.5 6.6 %collective-permute-start.5 = (bf16[4,64,256]{2,1,0:T(8,128)(2,1)S(1)}, bf16[4,64,256]{2,1,0:T(8,128)(2,1)S(1)}, u32[]{:S(2)}, u32[]{:S(2)}) collective-permute-start(bf16[4,64,256]{2,1,0:T(8,128)(2,1)S(1)} %get-tuple-element.45), channel_id=1, source_target_pairs={{0,3},{1,2},{2,1},{3,0},{4,7},{5,6},{6,5},{7,4},{8,11},{9,10},{10,... | collective-permute-start | bytes 393224 | tf_op jit(solution)/shard_map/ppermute | solution.py:870
  7.6 8.3 %collective-permute-start = (s32[1,2,16]{2,1,0:T(2,128)S(1)}, s32[1,2,16]{2,1,0:T(2,128)S(1)}, u32[]{:S(2)}, u32[]{:S(2)}) collective-permute-start(s32[1,2,16]{2,1,0:T(2,128)S(1)} %bitcast.15), channel_id=1, source_target_pairs={{0,12},{4,0},{8,4},{12,8},{1,13},{5,1},{9,5},{13,9},{2,14},{6,2},{... | collective-permute-start | bytes 392 | tf_op jit(solution)/shard_map/ppermute | solution.py:866
  11.4 6.2 %collective-permute-start.1 = (s32[1,2,16]{2,1,0:T(2,128)S(1)}, s32[1,2,16]{2,1,0:T(2,128)S(1)}, u32[]{:S(2)}, u32[]{:S(2)}) collective-permute-start(s32[1,2,16]{2,1,0:T(2,128)S(1)} %bitcast.16), channel_id=1, source_target_pairs={{0,8},{4,12},{8,0},{12,4},{1,9},{5,13},{9,1},{13,5},{2,10},{6,14},... | collective-permute-start | bytes 392 | tf_op jit(solution)/shard_map/ppermute | solution.py:866
  11.9 6.2 %collective-permute-start.2 = (s32[1,2,16]{2,1,0:T(2,128)S(1)}, s32[1,2,16]{2,1,0:T(2,128)S(1)}, u32[]{:S(2)}, u32[]{:S(2)}) collective-permute-start(s32[1,2,16]{2,1,0:T(2,128)S(1)} %bitcast.17), channel_id=1, source_target_pairs={{0,4},{4,8},{8,12},{12,0},{1,5},{5,9},{9,13},{13,1},{2,6},{6,10},{... | collective-permute-start | bytes 392 | tf_op jit(solution)/shard_map/ppermute | solution.py:866
  14.2 3.9 %collective-permute-start.3 = (bf16[4,64,256]{2,1,0:T(8,128)(2,1)}, bf16[4,64,256]{2,1,0:T(8,128)(2,1)S(1)}, u32[]{:S(2)}, u32[]{:S(2)}) collective-permute-start(bf16[4,64,256]{2,1,0:T(8,128)(2,1)} %get-tuple-element.43), channel_id=1, source_target_pairs={{0,1},{1,0},{2,3},{3,2},{4,5},{5,4},{6,7},{7,6},{8,9},{9,8},{10,11... | collective-permute-start | bytes 393224 | tf_op jit(solution)/shard_map/ppermute | solution.py:870
  14.3 1.7 %copy-start.2 = (bf16[96,4096]{1,0:T(8,128)(2,1)}, bf16[96,4096]{1,0:T(8,128)(2,1)S(1)}, u32[]{:S(2)}) copy-start(bf16[96,4096]{1,0:T(8,128)(2,1)S(1)} %collective-permute-done.6.near_peer) | copy-start | bytes 2359300
  14.3 10.7 %collective-permute-start.7 = (bf16[96,4096]{1,0:T(8,128)(2,1)}, bf16[96,4096]{1,0:T(8,128)(2,1)}, u32[]{:S(2)}, u32[]{:S(2)}) collective-permute-start(bf16[96,4096]{1,0:T(8,128)(2,1)} %get-tuple-element.46.near_own), channel_id=1, source_target_pairs={{0,1},{1,0},{2,3},{3,2},{4,5},{5,4},{6,7},{7,6},{8,9},{9,8},{10,11... | collective-permute-start | bytes 2359304 | tf_op jit(solution)/shard_map/ppermute | solution.py:853
  15.9 20.6 %collective-permute-start.8 = (bf16[96,4096]{1,0:T(8,128)(2,1)S(1)}, bf16[96,4096]{1,0:T(8,128)(2,1)S(1)}, u32[]{:S(2)}, u32[]{:S(2)}) collective-permute-start(bf16[96,4096]{1,0:T(8,128)(2,1)S(1)} %get-tuple-element.85.refs_8_), channel_id=1, source_target_pairs={{0,2},{2,0},{1,3},{3,1},{4,6},{6,4},{5,7},{7,5},{8,10},{10,8},{9,1... | collective-permute-start | bytes 2359304 | tf_op jit(solution)/shard_map/ppermute | solution.py:856
  17.6 42.3 %collective-permute-start.13 = (bf16[96,4096]{1,0:T(8,128)(2,1)S(1)}, bf16[96,4096]{1,0:T(8,128)(2,1)}, u32[]{:S(2)}, u32[]{:S(2)}) collective-permute-start(bf16[96,4096]{1,0:T(8,128)(2,1)S(1)} %get-tuple-element.84.refs_9_), channel_id=1, source_target_pairs={{0,2},{2,0},{1,3},{3,1},{4,6},{6,4},{5,7},{7,5},{8,10},{10,8},{9,1... | collective-permute-start | bytes 2359304 | tf_op jit(solution)/shard_map/ppermute | solution.py:856
  19.7 5.1 %copy-start.11 = (s32[1,16,2]{1,2,0:T(2,128)S(1)}, s32[1,16,2]{1,2,0:T(2,128)}, u32[]{:S(2)}) copy-start(s32[1,16,2]{1,2,0:T(2,128)} %param.18) | copy-start | bytes 388
  19.7 5.2 %copy-start.10 = (s32[1,4]{1,0:T(1,128)S(1)}, s32[1,4]{1,0:T(1,128)}, u32[]{:S(2)}) copy-start(s32[1,4]{1,0:T(1,128)} %param.16) | copy-start | bytes 52
  19.7 30.7 %all-to-all-start = ((bf16[4,8,64,256]{3,2,1,0:T(8,128)(2,1)}), bf16[4,8,64,256]{3,2,1,0:T(8,128)(2,1)S(1)}, u32[]{:S(2)}, u32[]{:S(2)}) async-start(bf16[4,8,64,256]{3,2,1,0:T(8,128)(2,1)} %pick_pages.1.refs_0_), calls=%async_computation | async-start | bytes 2097152 | tf_op jit(solution)/shard_map/all_to_all | solution.py:885
  25.0 1.1 %copy-start.3 = (bf16[96,4096]{1,0:T(8,128)(2,1)S(1)}, bf16[96,4096]{1,0:T(8,128)(2,1)}, u32[]{:S(2)}) copy-start(bf16[96,4096]{1,0:T(8,128)(2,1)} %copy-done.2) | copy-start | bytes 2359300
  26.1 1.1 %copy-start.9 = (bf16[96,4096]{1,0:T(8,128)(2,1)S(1)}, bf16[96,4096]{1,0:T(8,128)(2,1)}, u32[]{:S(2)}) copy-start(bf16[96,4096]{1,0:T(8,128)(2,1)} %copy-done.8) | copy-start | bytes 2359300
  36.5 6.1 %copy-start.4 = (bf16[192,1024]{1,0:T(8,128)(2,1)}, bf16[192,1024]{1,0:T(8,128)(2,1)S(1)}, u32[]{:S(2)}) copy-start(bf16[192,1024]{1,0:T(8,128)(2,1)S(1)} %get-tuple-element.51.q_ref) | copy-start | bytes 1179652
  36.6 1.5 %collective-permute-start.10 = (bf16[96,1024]{1,0:T(8,128)(2,1)S(1)}, bf16[96,1024]{1,0:T(8,128)(2,1)S(1)}, u32[]{:S(2)}, u32[]{:S(2)}) collective-permute-start(bf16[96,1024]{1,0:T(8,128)(2,1)S(1)} %get-tuple-element.88), channel_id=1, source_target_pairs={{0,1},{1,0},{2,3},{3,2},{4,5},{5,4},{6,7},{7,6},{8,9},{9,8},{10,11... | collective-permute-start | bytes 589832 | tf_op jit(solution)/shard_map/ppermute | solution.py:853
  36.7 1.7 %collective-permute-start.11 = (bf16[96,1024]{1,0:T(8,128)(2,1)S(1)}, bf16[96,1024]{1,0:T(8,128)(2,1)S(1)}, u32[]{:S(2)}, u32[]{:S(2)}) collective-permute-start(bf16[96,1024]{1,0:T(8,128)(2,1)S(1)} %get-tuple-element.87), channel_id=1, source_target_pairs={{0,1},{1,0},{2,3},{3,2},{4,5},{5,4},{6,7},{7,6},{8,9},{9,8},{10,11... | collective-permute-start | bytes 589832 | tf_op jit(solution)/shard_map/ppermute | solution.py:853
  37.2 1.5 %collective-permute-start.12 = (bf16[96,1024]{1,0:T(8,128)(2,1)S(1)}, bf16[96,1024]{1,0:T(8,128)(2,1)S(1)}, u32[]{:S(2)}, u32[]{:S(2)}) collective-permute-start(bf16[96,1024]{1,0:T(8,128)(2,1)S(1)} %get-tuple-element.86), channel_id=1, source_target_pairs={{0,1},{1,0},{2,3},{3,2},{4,5},{5,4},{6,7},{7,6},{8,9},{9,8},{10,11... | collective-permute-start | bytes 589832 | tf_op jit(solution)/shard_map/ppermute | solution.py:853
  37.3 1.7 %collective-permute-start.9 = (bf16[96,1024]{1,0:T(8,128)(2,1)S(1)}, bf16[96,1024]{1,0:T(8,128)(2,1)S(1)}, u32[]{:S(2)}, u32[]{:S(2)}) collective-permute-start(bf16[96,1024]{1,0:T(8,128)(2,1)S(1)} %get-tuple-element.89), channel_id=1, source_target_pairs={{0,1},{1,0},{2,3},{3,2},{4,5},{5,4},{6,7},{7,6},{8,9},{9,8},{10,11... | collective-permute-start | bytes 589832 | tf_op jit(solution)/shard_map/ppermute | solution.py:853
  42.6 14.8 %collective-permute-start.14 = (bf16[288,256]{1,0:T(8,128)(2,1)S(1)}, bf16[288,256]{1,0:T(8,128)(2,1)S(1)}, u32[]{:S(2)}, u32[]{:S(2)}) collective-permute-start(bf16[288,256]{1,0:T(8,128)(2,1)S(1)} %constant_dynamic-update-slice_fusion.refs_0_), channel_id=1, source_target_pairs={{0,2},{2,0},{1,3},{3,1},{4,6},{6,4},{5,7},{7,5},{8,10},{10,8},{9,1... | collective-permute-start | bytes 442376 | tf_op jit(solution)/shard_map/ppermute | solution.py:856
  57.4 1.5 %collective-permute-start.18 = (bf16[96,1024]{1,0:T(8,128)(2,1)S(1)}, bf16[96,1024]{1,0:T(8,128)(2,1)S(1)}, u32[]{:S(2)}, u32[]{:S(2)}) collective-permute-start(bf16[96,1024]{1,0:T(8,128)(2,1)S(1)} %get-tuple-element.66), channel_id=1, source_target_pairs={{0,1},{1,0},{2,3},{3,2},{4,5},{5,4},{6,7},{7,6},{8,9},{9,8},{10,11... | collective-permute-start | bytes 589832 | tf_op jit(solution)/shard_map/ppermute | solution.py:853
  57.5 1.7 %collective-permute-start.17 = (bf16[96,1024]{1,0:T(8,128)(2,1)S(1)}, bf16[96,1024]{1,0:T(8,128)(2,1)S(1)}, u32[]{:S(2)}, u32[]{:S(2)}) collective-permute-start(bf16[96,1024]{1,0:T(8,128)(2,1)S(1)} %get-tuple-element.64), channel_id=1, source_target_pairs={{0,1},{1,0},{2,3},{3,2},{4,5},{5,4},{6,7},{7,6},{8,9},{9,8},{10,11... | collective-permute-start | bytes 589832 | tf_op jit(solution)/shard_map/ppermute | solution.py:853
  58.0 1.5 %collective-permute-start.16 = (bf16[96,1024]{1,0:T(8,128)(2,1)S(1)}, bf16[96,1024]{1,0:T(8,128)(2,1)S(1)}, u32[]{:S(2)}, u32[]{:S(2)}) collective-permute-start(bf16[96,1024]{1,0:T(8,128)(2,1)S(1)} %get-tuple-element.62), channel_id=1, source_target_pairs={{0,1},{1,0},{2,3},{3,2},{4,5},{5,4},{6,7},{7,6},{8,9},{9,8},{10,11... | collective-permute-start | bytes 589832 | tf_op jit(solution)/shard_map/ppermute | solution.py:853
  58.0 1.7 %collective-permute-start.15 = (bf16[96,1024]{1,0:T(8,128)(2,1)S(1)}, bf16[96,1024]{1,0:T(8,128)(2,1)S(1)}, u32[]{:S(2)}, u32[]{:S(2)}) collective-permute-start(bf16[96,1024]{1,0:T(8,128)(2,1)S(1)} %get-tuple-element.60), channel_id=1, source_target_pairs={{0,1},{1,0},{2,3},{3,2},{4,5},{5,4},{6,7},{7,6},{8,9},{9,8},{10,11... | collective-permute-start | bytes 589832 | tf_op jit(solution)/shard_map/ppermute | solution.py:853
  59.9 3.0 %collective-permute-start.19 = (bf16[96,4096]{1,0:T(8,128)(2,1)}, bf16[96,4096]{1,0:T(8,128)(2,1)S(1)}, u32[]{:S(2)}, u32[]{:S(2)}) collective-permute-start(bf16[96,4096]{1,0:T(8,128)(2,1)} %collective-permute-done.13.near_ref), channel_id=1, source_target_pairs={{0,1},{1,0},{2,3},{3,2},{4,5},{5,4},{6,7},{7,6},{8,9},{9,8},{10,11... | collective-permute-start | bytes 2359304 | tf_op jit(solution)/shard_map/ppermute | solution.py:853
  60.2 23.4 %collective-permute-start.26 = (bf16[96,4096]{1,0:T(8,128)(2,1)S(1)}, bf16[96,4096]{1,0:T(8,128)(2,1)S(1)}, u32[]{:S(2)}, u32[]{:S(2)}) collective-permute-start(bf16[96,4096]{1,0:T(8,128)(2,1)S(1)} %add_pair.2), channel_id=1, source_target_pairs={{0,2},{2,0},{1,3},{3,1},{4,6},{6,4},{5,7},{7,5},{8,10},{10,8},{9,1... | collective-permute-start | bytes 2359304 | tf_op jit(solution)/shard_map/ppermute | solution.py:856
  71.4 10.5 %collective-permute-start.23 = (bf16[96,256]{1,0:T(8,128)(2,1)S(1)}, bf16[96,256]{1,0:T(8,128)(2,1)S(1)}, u32[]{:S(2)}, u32[]{:S(2)}) collective-permute-start(bf16[96,256]{1,0:T(8,128)(2,1)S(1)} %get-tuple-element.68.refs_2_.refs_3_), channel_id=1, source_target_pairs={{0,2},{2,0},{1,3},{3,1},{4,6},{6,4},{5,7},{7,5},{8,10},{10,8},{9,1... | collective-permute-start | bytes 147464 | tf_op jit(solution)/shard_map/ppermute | solution.py:856
  80.8 1.5 %collective-permute-start.20 = (bf16[96,1024]{1,0:T(8,128)(2,1)S(1)}, bf16[96,1024]{1,0:T(8,128)(2,1)S(1)}, u32[]{:S(2)}, u32[]{:S(2)}) collective-permute-start(bf16[96,1024]{1,0:T(8,128)(2,1)S(1)} %get-tuple-element.71), channel_id=1, source_target_pairs={{0,1},{1,0},{2,3},{3,2},{4,5},{5,4},{6,7},{7,6},{8,9},{9,8},{10,11... | collective-permute-start | bytes 589832 | tf_op jit(solution)/shard_map/ppermute | solution.py:853
  80.9 1.7 %collective-permute-start.21 = (bf16[96,1024]{1,0:T(8,128)(2,1)S(1)}, bf16[96,1024]{1,0:T(8,128)(2,1)S(1)}, u32[]{:S(2)}, u32[]{:S(2)}) collective-permute-start(bf16[96,1024]{1,0:T(8,128)(2,1)S(1)} %get-tuple-element.72), channel_id=1, source_target_pairs={{0,1},{1,0},{2,3},{3,2},{4,5},{5,4},{6,7},{7,6},{8,9},{9,8},{10,11... | collective-permute-start | bytes 589832 | tf_op jit(solution)/shard_map/ppermute | solution.py:853
  81.4 1.5 %collective-permute-start.22 = (bf16[96,1024]{1,0:T(8,128)(2,1)S(1)}, bf16[96,1024]{1,0:T(8,128)(2,1)S(1)}, u32[]{:S(2)}, u32[]{:S(2)}) collective-permute-start(bf16[96,1024]{1,0:T(8,128)(2,1)S(1)} %get-tuple-element.73), channel_id=1, source_target_pairs={{0,1},{1,0},{2,3},{3,2},{4,5},{5,4},{6,7},{7,6},{8,9},{9,8},{10,11... | collective-permute-start | bytes 589832 | tf_op jit(solution)/shard_map/ppermute | solution.py:853
  82.0 1.4 %collective-permute-start.24 = (bf16[96,1024]{1,0:T(8,128)(2,1)S(1)}, bf16[96,1024]{1,0:T(8,128)(2,1)S(1)}, u32[]{:S(2)}, u32[]{:S(2)}) collective-permute-start(bf16[96,1024]{1,0:T(8,128)(2,1)S(1)} %get-tuple-element.75), channel_id=1, source_target_pairs={{0,1},{1,0},{2,3},{3,2},{4,5},{5,4},{6,7},{7,6},{8,9},{9,8},{10,11... | collective-permute-start | bytes 589832 | tf_op jit(solution)/shard_map/ppermute | solution.py:853
  83.4 3.8 %copy-start.1 = (bf16[4,4,64,256]{3,2,1,0:T(8,128)(2,1)S(1)}, bf16[4,4,64,256]{3,2,1,0:T(8,128)(2,1)}, u32[]{:S(2)}) copy-start(bf16[4,4,64,256]{3,2,1,0:T(8,128)(2,1)} %pool_ref.1) | copy-start | bytes 1572868
  83.4 3.8 %copy-start.7 = (s32[1,6]{1,0:T(1,128)S(1)}, s32[1,6]{1,0:T(1,128)}, u32[]{:S(2)}) copy-start(s32[1,6]{1,0:T(1,128)} %slot_ref.1) | copy-start | bytes 76
  83.6 5.4 %copy-start.5 = (bf16[192,1024]{1,0:T(8,128)(2,1)S(1)}, bf16[192,1024]{1,0:T(8,128)(2,1)}, u32[]{:S(2)}) copy-start(bf16[192,1024]{1,0:T(8,128)(2,1)} %copy-done.4) | copy-start | bytes 1179652
  83.6 19.7 %collective-permute-start.27 = (bf16[96,4096]{1,0:T(8,128)(2,1)S(1)}, bf16[96,4096]{1,0:T(8,128)(2,1)S(1)}, u32[]{:S(2)}, u32[]{:S(2)}) collective-permute-start(bf16[96,4096]{1,0:T(8,128)(2,1)S(1)} %add_pair.3.refs_4_), channel_id=1, source_target_pairs={{0,2},{2,0},{1,3},{3,1},{4,6},{6,4},{5,7},{7,5},{8,10},{10,8},{9,1... | collective-permute-start | bytes 2359304 | tf_op jit(solution)/shard_map/ppermute | solution.py:856
  85.5 1.6 %collective-permute-start.28 = (bf16[2,288,256]{2,1,0:T(8,128)(2,1)S(1)}, bf16[2,288,256]{2,1,0:T(8,128)(2,1)S(1)}, u32[]{:S(2)}, u32[]{:S(2)}) collective-permute-start(bf16[2,288,256]{2,1,0:T(8,128)(2,1)S(1)} %pad_maximum_fusion), channel_id=1, source_target_pairs={{0,1},{1,0},{2,3},{3,2},{4,5},{5,4},{6,7},{7,6},{8,9},{9,8},{10,11... | collective-permute-start | bytes 884744 | tf_op jit(solution)/shard_map/ppermute | solution.py:853
  85.6 1.7 %collective-permute-start.29 = (bf16[2,96,256]{2,1,0:T(8,128)(2,1)S(1)}, bf16[2,96,256]{2,1,0:T(8,128)(2,1)S(1)}, u32[]{:S(2)}, u32[]{:S(2)}) collective-permute-start(bf16[2,96,256]{2,1,0:T(8,128)(2,1)S(1)} %pad_maximum_fusion.1), channel_id=1, source_target_pairs={{0,1},{1,0},{2,3},{3,2},{4,5},{5,4},{6,7},{7,6},{8,9},{9,8},{10,11... | collective-permute-start | bytes 294920 | tf_op jit(solution)/shard_map/ppermute | solution.py:853
  101.0 3.5 %copy-start = (bf16[96,8192]{1,0:T(8,128)(2,1)S(1)}, bf16[96,8192]{1,0:T(8,128)(2,1)}, u32[]{:S(2)}) copy-start(bf16[96,8192]{1,0:T(8,128)(2,1)} %x_ref.3) | copy-start | bytes 4718596
  101.0 3.5 %collective-permute-start.25 = (bf16[96,8192]{1,0:T(8,128)(2,1)S(1)}, bf16[96,8192]{1,0:T(8,128)(2,1)S(1)}, u32[]{:S(2)}, u32[]{:S(2)}) collective-permute-start(bf16[96,8192]{1,0:T(8,128)(2,1)S(1)} %get-tuple-element.77), channel_id=1, source_target_pairs={{0,1},{1,0},{2,3},{3,2},{4,5},{5,4},{6,7},{7,6},{8,9},{9,8},{10,11... | collective-permute-start | bytes 4718600 | tf_op jit(solution)/shard_map/ppermute | solution.py:853
  103.4 2.4 %collective-permute-start.30 = (bf16[96,4096]{1,0:T(8,128)(2,1)S(1)}, bf16[96,4096]{1,0:T(8,128)(2,1)S(1)}, u32[]{:S(2)}, u32[]{:S(2)}) collective-permute-start(bf16[96,4096]{1,0:T(8,128)(2,1)S(1)} %get-tuple-element.82), channel_id=1, source_target_pairs={{0,1},{1,0},{2,3},{3,2},{4,5},{5,4},{6,7},{7,6},{8,9},{9,8},{10,11... | collective-permute-start | bytes 2359304 | tf_op jit(solution)/shard_map/ppermute | solution.py:853

commit v12 on v11

--- a/solution.py
+++ b/solution.py
@@ -320,7 +320,7 @@
     return copies
 
 
-PAGES_STEP = 4
+PAGES_STEP = 8
 REQUESTS = 4
 SIZES_AT = 4
 REQUESTS_AT = 8

time: 108 us -> 107 us (level)
  waiting for transfers between devices: 15.8 us -> 19.3 us
  Pallas kernels: 57.6 us -> 55.3 us
  starting transfers between devices: 29.1 us -> 27 us
    ppermute x6, waiting for transfers between devices: 2.64 us -> 5.41 us  [over_y(): return lax.ppermute(x, 'tensor', [(0, 2), (2, 0), (1, 3), (3, 1)])]
    pallas_call x1, Pallas kernels: 12 us -> 9.59 us  [local_rows(): pl.pallas_call(kernel, in_specs=[SMEM] + [VMEM] * (2 + known) + [HBM] + [...]
    ppermute x6, starting transfers between devices: 10.5 us -> 8.36 us  [over_y(): return lax.ppermute(x, 'tensor', [(0, 2), (2, 0), (1, 3), (3, 1)])]
  transfers between devices with their start and end apart: 32 -> 32, of which waited for: 21 -> 21; matrix products, arithmetic and copies ran while one was open for 2% -> 2% of each run, Pallas kernels for 49% -> 47%
where the time goes in v12:
time: 107 us
  Pallas kernels  55.3 us (52%)
  starting transfers between devices  27 us (25%)
  waiting for transfers between devices  19.3 us (18%)
  local copies, waits for them, and re-layouts  2.55 us (2%)
  other arithmetic  1.46 us (1%)
  between operations  1.12 us (1%)
    pallas_call x2, Pallas kernels, attend_out(): pl.pallas_call(kernel, in_specs=[SMEM] + [VMEM] * (2 + known) + [HBM], ou...  14 us
    pallas_call x1, Pallas kernels, local_rows(): pl.pallas_call(kernel, in_specs=[SMEM] + [VMEM] * (2 + known) + [HBM] + [...  9.59 us
    pallas_call x1, Pallas kernels, project_local(): pl.pallas_call(kernel, in_specs=[SMEM] + [VMEM] * 4 + [HBM] * 2 + [ANY] *...  9.27 us
    pallas_call x1, Pallas kernels, project_far(): pl.pallas_call(kernel, in_specs=[SMEM] + [ANY] * 2 + [HBM] * 2 + [ANY] *...  8.48 us
    ppermute x6, starting transfers between devices, over_y(): return lax.ppermute(x, 'tensor', [(0, 2), (2, 0), (1, 3), (3, 1)])  8.36 us
    ppermute x19, waiting for transfers between devices, over_core(): return lax.ppermute(x, 'tensor', [(0, 1), (1, 0), (2, 3), (3, 2)])  6.97 us
    all_to_all x1, waiting for transfers between devices, chip_pair_body(): lax.all_to_all(picked, 'replica', split_axis=0, concat_axis=0, tiled=True)  6.16 us
    ppermute x3, starting transfers between devices, chip_pair_body(): wanted.append(lax.ppermute(wanted[0], 'replica', back))  5.82 us
  transfers between devices with their start and end apart: 32, of which 21 were waited for; matrix products, arithmetic and copies ran while one was open for 2% of the time, Pallas kernels for 47%

profile of v12, /device:TPU:0, one launch (start us, length us, event | category | flops | bytes accessed | tf_op | source)
XLA Modules:
  0.0 106.7 jit_solution(12676678843615123307)
XLA Ops:
  0.7 0.1 pad_add_fusion.place_ref
  0.7 3.7 %prepare.1 = (bf16[96,4096]{1,0:T(8,128)(2,1)}, bf16[96,4096]{1,0:T(8,128)(2,1)S(1)}, bf16[4,64,256]{2,1,0:T(8,128)(2,1)S(1)}, bf16[4,64,256]{2,1,0:T(8,128)(2,1...) custom-call(s32[4]{0:T(128)S(1)} %pad_add_fusion.place_ref, bf16[96,8192]{1,0:T(8,128)(2,1)} %x_ref.3, ...), custom_call_target="tpu_custom_call" | custom-call | flops 1024 | bytes 1024 | tf_op jit(solution)/shard_map/prepare/pallas_call | solution.py:233
  4.4 0.5 collective-permute-start.6
  4.9 2.6 %collective-permute-start.4 = (bf16[4,64,256]{2,1,0:T(8,128)(2,1)S(1)}, bf16[4,64,256]{2,1,0:T(8,128)(2,1)S(1)}, u32[]{:S(2)}, u32[]{:S(2)}) collective-permute-start(bf16[4,64,256]{2,1,0:T(8,128)(2,1)S(1)} %get-tuple-element.44), channel_id=1, source_target_pairs={{0,2},{1,3},{2,0},{3,1},{4,6},{5,7},{6,4},{7,5},{8,10},{9,11},{10,... | collective-permute-start | bytes 393224 | tf_op jit(solution)/shard_map/ppermute | solution.py:870
  7.6 3.8 %collective-permute-start = (s32[1,2,16]{2,1,0:T(2,128)S(1)}, s32[1,2,16]{2,1,0:T(2,128)S(1)}, u32[]{:S(2)}, u32[]{:S(2)}) collective-permute-start(s32[1,2,16]{2,1,0:T(2,128)S(1)} %bitcast.15), channel_id=1, source_target_pairs={{0,12},{4,0},{8,4},{12,8},{1,13},{5,1},{9,5},{13,9},{2,14},{6,2},{... | collective-permute-start | bytes 392 | tf_op jit(solution)/shard_map/ppermute | solution.py:866
  11.4 0.5 collective-permute-done.4.refs_6_
  11.9 2.0 %collective-permute-start.2 = (s32[1,2,16]{2,1,0:T(2,128)S(1)}, s32[1,2,16]{2,1,0:T(2,128)S(1)}, u32[]{:S(2)}, u32[]{:S(2)}) collective-permute-start(s32[1,2,16]{2,1,0:T(2,128)S(1)} %bitcast.17), channel_id=1, source_target_pairs={{0,4},{4,8},{8,12},{12,0},{1,5},{5,9},{9,13},{13,1},{2,6},{6,10},{... | collective-permute-start | bytes 392 | tf_op jit(solution)/shard_map/ppermute | solution.py:866
  13.9 0.3 collective-permute-done.5.refs_7_
  14.2 0.1 collective-permute-start.3
  14.3 0.4 collective-permute-start.7
  14.7 1.2 %broadcast_select_fusion.2 = (bf16[96,4096]{1,0:T(8,128)(2,1)S(1)}, bf16[96,4096]{1,0:T(8,128)(2,1)S(1)}) fusion(bf16[96,4096]{1,0:T(8,128)(2,1)S(1)} %collective-permute-done.6.near_peer, bf16[96,4096]{1,0:T(8,128)(2,1)} %get-tuple-element.46.near_own, pred[]{:T(512)S(6)} %eq.5), kind=kLoop, calls=%fused_computation.2 | loop fusion | flops 786432 | bytes 3145729 | tf_op jit(solution)/shard_map/jit(_where)/select_n | solution.py:877
  15.9 1.7 %collective-permute-start.8 = (bf16[96,4096]{1,0:T(8,128)(2,1)S(1)}, bf16[96,4096]{1,0:T(8,128)(2,1)S(1)}, u32[]{:S(2)}, u32[]{:S(2)}) collective-permute-start(bf16[96,4096]{1,0:T(8,128)(2,1)S(1)} %get-tuple-element.85.refs_8_), channel_id=1, source_target_pairs={{0,2},{2,0},{1,3},{3,1},{4,6},{6,4},{5,7},{7,5},{8,10},{10,8},{9,1... | collective-permute-start | bytes 2359304 | tf_op jit(solution)/shard_map/ppermute | solution.py:856
  17.6 0.4 collective-permute-start.13
  18.0 1.7 %pick_pages.1.refs_0_ = bf16[4,8,64,256]{3,2,1,0:T(8,128)(2,1)} custom-call(s32[4]{0:T(128)S(1)} %pad_add_fusion.place_ref, s32[1,2,16]{2,1,0:T(2,128)S(1)} %bitcast.18, s32[1,2,16]{2,1,0:T(2,128)S(1)} %collective-permute-done.refs_1_, s32[1,2,16]{2,1,0:T(2,128)S(1)} %collective-permute-done.1.refs_2_, s32[1,2,16]{2,1,0:T(2,128)S(1)} %collective-permute-done.2.refs_3_, ...), custom_call_target="tpu_custom_call" | custom-call | flops 1024 | bytes 1024 | tf_op jit(solution)/shard_map/pick_pages/pallas_call | solution.py:772
  19.7 5.1 %all-to-all-start = ((bf16[4,8,64,256]{3,2,1,0:T(8,128)(2,1)}), bf16[4,8,64,256]{3,2,1,0:T(8,128)(2,1)S(1)}, u32[]{:S(2)}, u32[]{:S(2)}) async-start(bf16[4,8,64,256]{3,2,1,0:T(8,128)(2,1)} %pick_pages.1.refs_0_), calls=%async_computation | async-start | bytes 2097152 | tf_op jit(solution)/shard_map/all_to_all | solution.py:885
  24.8 0.1 reshape.7
  24.9 0.1 concatenate.7.refs_1_.place_ref
  25.0 1.1 %copy-done.3 = bf16[96,4096]{1,0:T(8,128)(2,1)S(1)} copy-done((bf16[96,4096]{1,0:T(8,128)(2,1)S(1)}, bf16[96,4096]{1,0:T(8,128)(2,1)}, u32[]{:S(2)}) %copy-start.3) | copy-done | bytes 786456
  26.1 1.1 %copy-done.9 = bf16[96,4096]{1,0:T(8,128)(2,1)S(1)} copy-done((bf16[96,4096]{1,0:T(8,128)(2,1)S(1)}, bf16[96,4096]{1,0:T(8,128)(2,1)}, u32[]{:S(2)}) %copy-start.9) | copy-done | bytes 786456
  27.2 9.3 %project_local.1 = (bf16[192,1024]{1,0:T(8,128)(2,1)S(1)}, bf16[192,256]{1,0:T(8,128)(2,1)S(1)}, bf16[8,1024,1024]{2,1,0:T(8,128)(2,1)S(1)}, bf16[8,1024,256]{2,1,0:T(8,128)(2,1)S(1)}) custom-call(s32[4]{0:T(128)S(1)} %pad_add_fusion.place_ref, bf16[96,4096]{1,0:T(8,128)(2,1)} %get-tuple-element.46.near_own, bf16[96,4096]{1,0:T(8,128)(2,1)S(1)} %copy-done.3, ...), custom_call_target="tpu_custom_call" | custom-call | flops 20000000000 | bytes 200000000 | tf_op jit(solution)/shard_map/project_local/pallas_call | solution.py:287
  36.7 0.5 collective-permute-start.11
  37.2 0.1 collective-permute-start.12
  37.3 0.4 collective-permute-start.9
  37.7 0.4 collective-permute-done.10.refs_1_
  38.1 0.3 collective-permute-done.11.refs_2_
  38.4 0.3 collective-permute-done.12.refs_3_
  38.7 0.3 collective-permute-done.9.refs_0_
  39.0 3.6 %project_held.1 = (bf16[96,1024]{1,0:T(8,128)(2,1)S(1)}, bf16[96,256]{1,0:T(8,128)(2,1)S(1)}) custom-call(bf16[96,4096]{1,0:T(8,128)(2,1)S(1)} %collective-permute-done.8.near_ref, bf16[96,1024]{1,0:T(8,128)(2,1)S(1)} %collective-permute-done.9.refs_0_, bf16[96,1024]{1,0:T(8,128)(2,1)S(1)} %collective-permute-done.10.refs_1_, ...), custom_call_target="tpu_custom_call" | custom-call | flops 1024 | bytes 1024 | tf_op jit(solution)/shard_map/project_held/pallas_call | solution.py:473
  42.6 1.6 %collective-permute-start.14 = (bf16[288,256]{1,0:T(8,128)(2,1)S(1)}, bf16[288,256]{1,0:T(8,128)(2,1)S(1)}, u32[]{:S(2)}, u32[]{:S(2)}) collective-permute-start(bf16[288,256]{1,0:T(8,128)(2,1)S(1)} %constant_dynamic-update-slice_fusion.refs_0_), channel_id=1, source_target_pairs={{0,2},{2,0},{1,3},{3,1},{4,6},{6,4},{5,7},{7,5},{8,10},{10,8},{9,1... | collective-permute-start | bytes 442376 | tf_op jit(solution)/shard_map/ppermute | solution.py:856
  44.2 6.2 %all-to-all-done.pulled_ref = bf16[4,8,64,256]{3,2,1,0:T(8,128)(2,1)S(1)} async-done(((bf16[4,8,64,256]{3,2,1,0:T(8,128)(2,1)}), bf16[4,8,64,256]{3,2,1,0:T(8,128)(2,1)S(1)}, u32[]{:S(2)}, u32[]{:S(2)}) %all-to-all-start) | async-done | bytes 1048608 | tf_op jit(solution)/shard_map/all_to_all | solution.py:885
  50.4 7.0 %attend_out.2 = (bf16[96,1024]{1,0:T(8,128)(2,1)S(1)}, bf16[96,1024]{1,0:T(8,128)(2,1)S(1)}, bf16[96,1024]{1,0:T(8,128)(2,1)S(1)}, bf16[96,1024]{1,0:T(8,128)(2,1)S(1)}, bf16[96,4096]{1,0:T(8,128)(2,1)S(1)}) custom-call(s32[40]{0:T(128)S(1)} %concatenate.7.refs_1_.place_ref, bf16[96,1024]{1,0:T(8,128)(2,1)S(1)} %get-tuple-element.57.q_ref, ...), custom_call_target="tpu_custom_call" | custom-call | flops 1024 | bytes 4000000 | tf_op jit(solution)/shard_map/attend_out/pallas_call | solution.py:575
  57.5 0.5 collective-permute-start.17
  58.0 0.1 collective-permute-start.16
  58.0 0.4 collective-permute-start.15
  58.5 0.4 collective-permute-done.18.refs_3_
  58.9 0.3 collective-permute-done.17.refs_2_
  59.2 0.3 collective-permute-done.16.refs_1_
  59.5 0.3 collective-permute-done.15.refs_0_
  59.7 0.2 add_pair.2
  59.9 0.3 collective-permute-start.19
  60.2 1.5 %collective-permute-start.26 = (bf16[96,4096]{1,0:T(8,128)(2,1)S(1)}, bf16[96,4096]{1,0:T(8,128)(2,1)S(1)}, u32[]{:S(2)}, u32[]{:S(2)}) collective-permute-start(bf16[96,4096]{1,0:T(8,128)(2,1)S(1)} %add_pair.2), channel_id=1, source_target_pairs={{0,2},{2,0},{1,3},{3,1},{4,6},{6,4},{5,7},{7,5},{8,10},{10,8},{9,1... | collective-permute-start | bytes 2359304 | tf_op jit(solution)/shard_map/ppermute | solution.py:856
  61.7 0.7 collective-permute-done.19.far_ref
  62.5 8.5 %project_far.1 = (bf16[96,1024]{1,0:T(8,128)(2,1)S(1)}, bf16[96,256]{1,0:T(8,128)(2,1)S(1)}) custom-call(s32[4]{0:T(128)S(1)} %pad_add_fusion.place_ref, bf16[96,4096]{1,0:T(8,128)(2,1)} %collective-permute-done.13.near_ref, bf16[96,4096]{1,0:T(8,128)(2,1)S(1)} %collective-permute-done.19.far_ref, bf16[8192,1024]{1,0:T(8,128)(2,1)} %wq.3, bf16[8192,256]{1,0:T(8,128)(2,1)} %wkv.3), custom_call_target="tpu_custom_call" | custom-call | flops 1024 | bytes 1024 | tf_op jit(solution)/shard_map/project_far/pallas_call | solution.py:517
  71.0 1.6 %collective-permute-start.23 = (bf16[96,256]{1,0:T(8,128)(2,1)S(1)}, bf16[96,256]{1,0:T(8,128)(2,1)S(1)}, u32[]{:S(2)}, u32[]{:S(2)}) collective-permute-start(bf16[96,256]{1,0:T(8,128)(2,1)S(1)} %get-tuple-element.68.refs_2_.refs_3_), channel_id=1, source_target_pairs={{0,2},{2,0},{1,3},{3,1},{4,6},{6,4},{5,7},{7,5},{8,10},{10,8},{9,1... | collective-permute-start | bytes 147464 | tf_op jit(solution)/shard_map/ppermute | solution.py:856
  72.6 7.0 %attend_out.3 = (bf16[96,1024]{1,0:T(8,128)(2,1)S(1)}, bf16[96,1024]{1,0:T(8,128)(2,1)S(1)}, bf16[96,1024]{1,0:T(8,128)(2,1)S(1)}, bf16[96,1024]{1,0:T(8,128)(2,1)S(1)}, bf16[96,4096]{1,0:T(8,128)(2,1)S(1)}) custom-call(s32[40]{0:T(128)S(1)} %concatenate.7.refs_1_.place_ref, bf16[96,1024]{1,0:T(8,128)(2,1)S(1)} %get-tuple-element.69.q_ref, ...), custom_call_target="tpu_custom_call" | custom-call | flops 1024 | bytes 4000000 | tf_op jit(solution)/shard_map/attend_out/pallas_call | solution.py:575
  79.7 0.5 collective-permute-start.21
  80.1 0.1 collective-permute-start.22
  80.2 0.8 collective-permute-done.23.refs_4_
  81.1 0.3 collective-permute-done.21.refs_1_
  81.4 0.3 collective-permute-done.22.refs_2_
  81.6 0.8 collective-permute-done.24.refs_3_
  82.5 0.2 add_pair.3.refs_4_
  82.7 1.6 %collective-permute-start.27 = (bf16[96,4096]{1,0:T(8,128)(2,1)S(1)}, bf16[96,4096]{1,0:T(8,128)(2,1)S(1)}, u32[]{:S(2)}, u32[]{:S(2)}) collective-permute-start(bf16[96,4096]{1,0:T(8,128)(2,1)S(1)} %add_pair.3.refs_4_), channel_id=1, source_target_pairs={{0,2},{2,0},{1,3},{3,1},{4,6},{6,4},{5,7},{7,5},{8,10},{10,8},{9,1... | collective-permute-start | bytes 2359304 | tf_op jit(solution)/shard_map/ppermute | solution.py:856
  84.4 0.6 collective-permute-start.29
  84.9 1.0 collective-permute-done.28.refs_2_
  85.9 0.1 collective-permute-done.29.refs_5_
  86.1 1.8 %write_pool.1 = bf16[4,4,64,256]{3,2,1,0:T(8,128)(2,1)} custom-call(s32[4]{0:T(128)S(1)} %pad_add_fusion.place_ref, s32[1,6]{1,0:T(1,128)S(1)} %copy-done.7, bf16[4,4,64,256]{3,2,1,0:T(8,128)(2,1)S(1)} %copy-done.1, bf16[288,256]{1,0:T(8,128)(2,1)S(1)} %constant_dynamic-update-slice_fusion.refs_0_, bf16[288,256]{1,0:T(8,128)(2,1)S(1)} %collective-permute-done.14.refs_1_, ...), custom_call_target="tpu_custom_call" | custom-call | flops 1024 | bytes 1024 | tf_op jit(solution)/shard_map/write_pool/pallas_call | solution.py:821
  87.9 9.6 %local_rows.1 = (bf16[96,8192]{1,0:T(8,128)(2,1)S(1)}, bf16[96,8192]{1,0:T(8,128)(2,1)S(1)}) custom-call(s32[40]{0:T(128)S(1)} %concatenate.7.refs_1_.place_ref, bf16[192,1024]{1,0:T(8,128)(2,1)S(1)} %copy-done.5, bf16[4,8,64,256]{3,2,1,0:T(8,128)(2,1)S(1)} %all-to-all-done.pulled_ref, bf16[192,256]{1,0:T(8,128)(2,1)S(1)} %get-tuple-element.52.refs_0_, ...), custom_call_target="tpu_custom_call" | custom-call | flops 1024 | bytes 1024 | tf_op jit(solution)/shard_map/local_rows/pallas_call | solution.py:638
  97.5 0.2 collective-permute-start.25
  97.7 4.6 %collective-permute-done.27 = bf16[96,4096]{1,0:T(8,128)(2,1)S(1)} collective-permute-done((bf16[96,4096]{1,0:T(8,128)(2,1)S(1)}, bf16[96,4096]{1,0:T(8,128)(2,1)S(1)}, u32[]{:S(2)}, u32[]{:S(2)}) %collective-permute-start.27) | collective-permute-done | bytes 786464 | tf_op jit(solution)/shard_map/ppermute | solution.py:856
  102.3 0.1 broadcast_select_fusion
  102.5 1.1 %finish_near.1 = (bf16[96,4096]{1,0:T(8,128)(2,1)S(1)}, f32[96,4096]{1,0:T(8,128)S(1)}) custom-call(s32[4]{0:T(128)S(1)} %pad_add_fusion.place_ref, bf16[96,8192]{1,0:T(8,128)(2,1)S(1)} %copy-done, bf16[96,8192]{1,0:T(8,128)(2,1)S(1)} %get-tuple-element.76.own_ref, bf16[96,8192]{1,0:T(8,128)(2,1)S(1)} %collective-permute-done.25.peer_ref, ...), custom_call_target="tpu_custom_call" | custom-call | flops 1024 | bytes 1024 | tf_op jit(solution)/shard_map/finish_near/pallas_call | solution.py:699
  103.6 1.1 %collective-permute-done.30.far_ref = bf16[96,4096]{1,0:T(8,128)(2,1)S(1)} collective-permute-done((bf16[96,4096]{1,0:T(8,128)(2,1)S(1)}, bf16[96,4096]{1,0:T(8,128)(2,1)S(1)}, u32[]{:S(2)}, u32[]{:S(2)}) %collective-permute-start.30) | collective-permute-done | bytes 786464 | tf_op jit(solution)/shard_map/ppermute | solution.py:853
  104.8 1.7 %finish.1 = bf16[96,8192]{1,0:T(8,128)(2,1)} custom-call(s32[4]{0:T(128)S(1)} %pad_add_fusion.place_ref, bf16[96,8192]{1,0:T(8,128)(2,1)S(1)} %copy-done, bf16[96,4096]{1,0:T(8,128)(2,1)S(1)} %get-tuple-element.80.done_ref, f32[96,4096]{1,0:T(8,128)S(1)} %get-tuple-element.81.local_ref, bf16[96,4096]{1,0:T(8,128)(2,1)S(1)} %collective-permute-done.30.far_ref), custom_call_target="tpu_custom_call" | custom-call | flops 1024 | bytes 1024 | tf_op jit(solution)/shard_map/finish/pallas_call | solution.py:739
  (47 shorter events, 0.7 us)
Async XLA Ops:
  0.6 7.0 %copy-start.6 = (s32[1,16,2]{1,2,0:T(2,128)S(1)}, s32[1,16,2]{1,2,0:T(2,128)}, u32[]{:S(2)}) copy-start(s32[1,16,2]{1,2,0:T(2,128)} %param.17) | copy-start | bytes 388
  4.4 11.5 %copy-start.8 = (bf16[96,4096]{1,0:T(8,128)(2,1)}, bf16[96,4096]{1,0:T(8,128)(2,1)S(1)}, u32[]{:S(2)}) copy-start(bf16[96,4096]{1,0:T(8,128)(2,1)S(1)} %get-tuple-element.47.far_own) | copy-start | bytes 2359300
  4.4 9.9 %collective-permute-start.6 = (bf16[96,4096]{1,0:T(8,128)(2,1)S(1)}, bf16[96,4096]{1,0:T(8,128)(2,1)S(1)}, u32[]{:S(2)}, u32[]{:S(2)}) collective-permute-start(bf16[96,4096]{1,0:T(8,128)(2,1)S(1)} %get-tuple-element.47.far_own), channel_id=1, source_target_pairs={{0,1},{1,0},{2,3},{3,2},{4,5},{5,4},{6,7},{7,6},{8,9},{9,8},{10,11... | collective-permute-start | bytes 2359304 | tf_op jit(solution)/shard_map/ppermute | solution.py:853
  4.9 6.9 %collective-permute-start.4 = (bf16[4,64,256]{2,1,0:T(8,128)(2,1)S(1)}, bf16[4,64,256]{2,1,0:T(8,128)(2,1)S(1)}, u32[]{:S(2)}, u32[]{:S(2)}) collective-permute-start(bf16[4,64,256]{2,1,0:T(8,128)(2,1)S(1)} %get-tuple-element.44), channel_id=1, source_target_pairs={{0,2},{1,3},{2,0},{3,1},{4,6},{5,7},{6,4},{7,5},{8,10},{9,11},{10,... | collective-permute-start | bytes 393224 | tf_op jit(solution)/shard_map/ppermute | solution.py:870
  7.5 6.6 %collective-permute-start.5 = (bf16[4,64,256]{2,1,0:T(8,128)(2,1)S(1)}, bf16[4,64,256]{2,1,0:T(8,128)(2,1)S(1)}, u32[]{:S(2)}, u32[]{:S(2)}) collective-permute-start(bf16[4,64,256]{2,1,0:T(8,128)(2,1)S(1)} %get-tuple-element.45), channel_id=1, source_target_pairs={{0,3},{1,2},{2,1},{3,0},{4,7},{5,6},{6,5},{7,4},{8,11},{9,10},{10,... | collective-permute-start | bytes 393224 | tf_op jit(solution)/shard_map/ppermute | solution.py:870
  7.6 8.3 %collective-permute-start = (s32[1,2,16]{2,1,0:T(2,128)S(1)}, s32[1,2,16]{2,1,0:T(2,128)S(1)}, u32[]{:S(2)}, u32[]{:S(2)}) collective-permute-start(s32[1,2,16]{2,1,0:T(2,128)S(1)} %bitcast.15), channel_id=1, source_target_pairs={{0,12},{4,0},{8,4},{12,8},{1,13},{5,1},{9,5},{13,9},{2,14},{6,2},{... | collective-permute-start | bytes 392 | tf_op jit(solution)/shard_map/ppermute | solution.py:866
  11.4 6.2 %collective-permute-start.1 = (s32[1,2,16]{2,1,0:T(2,128)S(1)}, s32[1,2,16]{2,1,0:T(2,128)S(1)}, u32[]{:S(2)}, u32[]{:S(2)}) collective-permute-start(s32[1,2,16]{2,1,0:T(2,128)S(1)} %bitcast.16), channel_id=1, source_target_pairs={{0,8},{4,12},{8,0},{12,4},{1,9},{5,13},{9,1},{13,5},{2,10},{6,14},... | collective-permute-start | bytes 392 | tf_op jit(solution)/shard_map/ppermute | solution.py:866
  11.9 6.2 %collective-permute-start.2 = (s32[1,2,16]{2,1,0:T(2,128)S(1)}, s32[1,2,16]{2,1,0:T(2,128)S(1)}, u32[]{:S(2)}, u32[]{:S(2)}) collective-permute-start(s32[1,2,16]{2,1,0:T(2,128)S(1)} %bitcast.17), channel_id=1, source_target_pairs={{0,4},{4,8},{8,12},{12,0},{1,5},{5,9},{9,13},{13,1},{2,6},{6,10},{... | collective-permute-start | bytes 392 | tf_op jit(solution)/shard_map/ppermute | solution.py:866
  14.2 3.9 %collective-permute-start.3 = (bf16[4,64,256]{2,1,0:T(8,128)(2,1)}, bf16[4,64,256]{2,1,0:T(8,128)(2,1)S(1)}, u32[]{:S(2)}, u32[]{:S(2)}) collective-permute-start(bf16[4,64,256]{2,1,0:T(8,128)(2,1)} %get-tuple-element.43), channel_id=1, source_target_pairs={{0,1},{1,0},{2,3},{3,2},{4,5},{5,4},{6,7},{7,6},{8,9},{9,8},{10,11... | collective-permute-start | bytes 393224 | tf_op jit(solution)/shard_map/ppermute | solution.py:870
  14.3 1.7 %copy-start.2 = (bf16[96,4096]{1,0:T(8,128)(2,1)}, bf16[96,4096]{1,0:T(8,128)(2,1)S(1)}, u32[]{:S(2)}) copy-start(bf16[96,4096]{1,0:T(8,128)(2,1)S(1)} %collective-permute-done.6.near_peer) | copy-start | bytes 2359300
  14.3 10.7 %collective-permute-start.7 = (bf16[96,4096]{1,0:T(8,128)(2,1)}, bf16[96,4096]{1,0:T(8,128)(2,1)}, u32[]{:S(2)}, u32[]{:S(2)}) collective-permute-start(bf16[96,4096]{1,0:T(8,128)(2,1)} %get-tuple-element.46.near_own), channel_id=1, source_target_pairs={{0,1},{1,0},{2,3},{3,2},{4,5},{5,4},{6,7},{7,6},{8,9},{9,8},{10,11... | collective-permute-start | bytes 2359304 | tf_op jit(solution)/shard_map/ppermute | solution.py:853
  15.9 20.6 %collective-permute-start.8 = (bf16[96,4096]{1,0:T(8,128)(2,1)S(1)}, bf16[96,4096]{1,0:T(8,128)(2,1)S(1)}, u32[]{:S(2)}, u32[]{:S(2)}) collective-permute-start(bf16[96,4096]{1,0:T(8,128)(2,1)S(1)} %get-tuple-element.85.refs_8_), channel_id=1, source_target_pairs={{0,2},{2,0},{1,3},{3,1},{4,6},{6,4},{5,7},{7,5},{8,10},{10,8},{9,1... | collective-permute-start | bytes 2359304 | tf_op jit(solution)/shard_map/ppermute | solution.py:856
  17.6 42.3 %collective-permute-start.13 = (bf16[96,4096]{1,0:T(8,128)(2,1)S(1)}, bf16[96,4096]{1,0:T(8,128)(2,1)}, u32[]{:S(2)}, u32[]{:S(2)}) collective-permute-start(bf16[96,4096]{1,0:T(8,128)(2,1)S(1)} %get-tuple-element.84.refs_9_), channel_id=1, source_target_pairs={{0,2},{2,0},{1,3},{3,1},{4,6},{6,4},{5,7},{7,5},{8,10},{10,8},{9,1... | collective-permute-start | bytes 2359304 | tf_op jit(solution)/shard_map/ppermute | solution.py:856
  19.7 5.1 %copy-start.11 = (s32[1,16,2]{1,2,0:T(2,128)S(1)}, s32[1,16,2]{1,2,0:T(2,128)}, u32[]{:S(2)}) copy-start(s32[1,16,2]{1,2,0:T(2,128)} %param.18) | copy-start | bytes 388
  19.7 5.2 %copy-start.10 = (s32[1,4]{1,0:T(1,128)S(1)}, s32[1,4]{1,0:T(1,128)}, u32[]{:S(2)}) copy-start(s32[1,4]{1,0:T(1,128)} %param.16) | copy-start | bytes 52
  19.7 30.7 %all-to-all-start = ((bf16[4,8,64,256]{3,2,1,0:T(8,128)(2,1)}), bf16[4,8,64,256]{3,2,1,0:T(8,128)(2,1)S(1)}, u32[]{:S(2)}, u32[]{:S(2)}) async-start(bf16[4,8,64,256]{3,2,1,0:T(8,128)(2,1)} %pick_pages.1.refs_0_), calls=%async_computation | async-start | bytes 2097152 | tf_op jit(solution)/shard_map/all_to_all | solution.py:885
  25.0 1.1 %copy-start.3 = (bf16[96,4096]{1,0:T(8,128)(2,1)S(1)}, bf16[96,4096]{1,0:T(8,128)(2,1)}, u32[]{:S(2)}) copy-start(bf16[96,4096]{1,0:T(8,128)(2,1)} %copy-done.2) | copy-start | bytes 2359300
  26.1 1.1 %copy-start.9 = (bf16[96,4096]{1,0:T(8,128)(2,1)S(1)}, bf16[96,4096]{1,0:T(8,128)(2,1)}, u32[]{:S(2)}) copy-start(bf16[96,4096]{1,0:T(8,128)(2,1)} %copy-done.8) | copy-start | bytes 2359300
  36.5 6.1 %copy-start.4 = (bf16[192,1024]{1,0:T(8,128)(2,1)}, bf16[192,1024]{1,0:T(8,128)(2,1)S(1)}, u32[]{:S(2)}) copy-start(bf16[192,1024]{1,0:T(8,128)(2,1)S(1)} %get-tuple-element.51.q_ref) | copy-start | bytes 1179652
  36.6 1.5 %collective-permute-start.10 = (bf16[96,1024]{1,0:T(8,128)(2,1)S(1)}, bf16[96,1024]{1,0:T(8,128)(2,1)S(1)}, u32[]{:S(2)}, u32[]{:S(2)}) collective-permute-start(bf16[96,1024]{1,0:T(8,128)(2,1)S(1)} %get-tuple-element.88), channel_id=1, source_target_pairs={{0,1},{1,0},{2,3},{3,2},{4,5},{5,4},{6,7},{7,6},{8,9},{9,8},{10,11... | collective-permute-start | bytes 589832 | tf_op jit(solution)/shard_map/ppermute | solution.py:853
  36.7 1.7 %collective-permute-start.11 = (bf16[96,1024]{1,0:T(8,128)(2,1)S(1)}, bf16[96,1024]{1,0:T(8,128)(2,1)S(1)}, u32[]{:S(2)}, u32[]{:S(2)}) collective-permute-start(bf16[96,1024]{1,0:T(8,128)(2,1)S(1)} %get-tuple-element.87), channel_id=1, source_target_pairs={{0,1},{1,0},{2,3},{3,2},{4,5},{5,4},{6,7},{7,6},{8,9},{9,8},{10,11... | collective-permute-start | bytes 589832 | tf_op jit(solution)/shard_map/ppermute | solution.py:853
  37.2 1.5 %collective-permute-start.12 = (bf16[96,1024]{1,0:T(8,128)(2,1)S(1)}, bf16[96,1024]{1,0:T(8,128)(2,1)S(1)}, u32[]{:S(2)}, u32[]{:S(2)}) collective-permute-start(bf16[96,1024]{1,0:T(8,128)(2,1)S(1)} %get-tuple-element.86), channel_id=1, source_target_pairs={{0,1},{1,0},{2,3},{3,2},{4,5},{5,4},{6,7},{7,6},{8,9},{9,8},{10,11... | collective-permute-start | bytes 589832 | tf_op jit(solution)/shard_map/ppermute | solution.py:853
  37.3 1.7 %collective-permute-start.9 = (bf16[96,1024]{1,0:T(8,128)(2,1)S(1)}, bf16[96,1024]{1,0:T(8,128)(2,1)S(1)}, u32[]{:S(2)}, u32[]{:S(2)}) collective-permute-start(bf16[96,1024]{1,0:T(8,128)(2,1)S(1)} %get-tuple-element.89), channel_id=1, source_target_pairs={{0,1},{1,0},{2,3},{3,2},{4,5},{5,4},{6,7},{7,6},{8,9},{9,8},{10,11... | collective-permute-start | bytes 589832 | tf_op jit(solution)/shard_map/ppermute | solution.py:853
  42.6 14.8 %collective-permute-start.14 = (bf16[288,256]{1,0:T(8,128)(2,1)S(1)}, bf16[288,256]{1,0:T(8,128)(2,1)S(1)}, u32[]{:S(2)}, u32[]{:S(2)}) collective-permute-start(bf16[288,256]{1,0:T(8,128)(2,1)S(1)} %constant_dynamic-update-slice_fusion.refs_0_), channel_id=1, source_target_pairs={{0,2},{2,0},{1,3},{3,1},{4,6},{6,4},{5,7},{7,5},{8,10},{10,8},{9,1... | collective-permute-start | bytes 442376 | tf_op jit(solution)/shard_map/ppermute | solution.py:856
  57.4 1.5 %collective-permute-start.18 = (bf16[96,1024]{1,0:T(8,128)(2,1)S(1)}, bf16[96,1024]{1,0:T(8,128)(2,1)S(1)}, u32[]{:S(2)}, u32[]{:S(2)}) collective-permute-start(bf16[96,1024]{1,0:T(8,128)(2,1)S(1)} %get-tuple-element.66), channel_id=1, source_target_pairs={{0,1},{1,0},{2,3},{3,2},{4,5},{5,4},{6,7},{7,6},{8,9},{9,8},{10,11... | collective-permute-start | bytes 589832 | tf_op jit(solution)/shard_map/ppermute | solution.py:853
  57.5 1.7 %collective-permute-start.17 = (bf16[96,1024]{1,0:T(8,128)(2,1)S(1)}, bf16[96,1024]{1,0:T(8,128)(2,1)S(1)}, u32[]{:S(2)}, u32[]{:S(2)}) collective-permute-start(bf16[96,1024]{1,0:T(8,128)(2,1)S(1)} %get-tuple-element.64), channel_id=1, source_target_pairs={{0,1},{1,0},{2,3},{3,2},{4,5},{5,4},{6,7},{7,6},{8,9},{9,8},{10,11... | collective-permute-start | bytes 589832 | tf_op jit(solution)/shard_map/ppermute | solution.py:853
  58.0 1.5 %collective-permute-start.16 = (bf16[96,1024]{1,0:T(8,128)(2,1)S(1)}, bf16[96,1024]{1,0:T(8,128)(2,1)S(1)}, u32[]{:S(2)}, u32[]{:S(2)}) collective-permute-start(bf16[96,1024]{1,0:T(8,128)(2,1)S(1)} %get-tuple-element.62), channel_id=1, source_target_pairs={{0,1},{1,0},{2,3},{3,2},{4,5},{5,4},{6,7},{7,6},{8,9},{9,8},{10,11... | collective-permute-start | bytes 589832 | tf_op jit(solution)/shard_map/ppermute | solution.py:853
  58.0 1.7 %collective-permute-start.15 = (bf16[96,1024]{1,0:T(8,128)(2,1)S(1)}, bf16[96,1024]{1,0:T(8,128)(2,1)S(1)}, u32[]{:S(2)}, u32[]{:S(2)}) collective-permute-start(bf16[96,1024]{1,0:T(8,128)(2,1)S(1)} %get-tuple-element.60), channel_id=1, source_target_pairs={{0,1},{1,0},{2,3},{3,2},{4,5},{5,4},{6,7},{7,6},{8,9},{9,8},{10,11... | collective-permute-start | bytes 589832 | tf_op jit(solution)/shard_map/ppermute | solution.py:853
  59.9 2.6 %collective-permute-start.19 = (bf16[96,4096]{1,0:T(8,128)(2,1)}, bf16[96,4096]{1,0:T(8,128)(2,1)S(1)}, u32[]{:S(2)}, u32[]{:S(2)}) collective-permute-start(bf16[96,4096]{1,0:T(8,128)(2,1)} %collective-permute-done.13.near_ref), channel_id=1, source_target_pairs={{0,1},{1,0},{2,3},{3,2},{4,5},{5,4},{6,7},{7,6},{8,9},{9,8},{10,11... | collective-permute-start | bytes 2359304 | tf_op jit(solution)/shard_map/ppermute | solution.py:853
  60.2 22.4 %collective-permute-start.26 = (bf16[96,4096]{1,0:T(8,128)(2,1)S(1)}, bf16[96,4096]{1,0:T(8,128)(2,1)S(1)}, u32[]{:S(2)}, u32[]{:S(2)}) collective-permute-start(bf16[96,4096]{1,0:T(8,128)(2,1)S(1)} %add_pair.2), channel_id=1, source_target_pairs={{0,2},{2,0},{1,3},{3,1},{4,6},{6,4},{5,7},{7,5},{8,10},{10,8},{9,1... | collective-permute-start | bytes 2359304 | tf_op jit(solution)/shard_map/ppermute | solution.py:856
  71.0 10.0 %collective-permute-start.23 = (bf16[96,256]{1,0:T(8,128)(2,1)S(1)}, bf16[96,256]{1,0:T(8,128)(2,1)S(1)}, u32[]{:S(2)}, u32[]{:S(2)}) collective-permute-start(bf16[96,256]{1,0:T(8,128)(2,1)S(1)} %get-tuple-element.68.refs_2_.refs_3_), channel_id=1, source_target_pairs={{0,2},{2,0},{1,3},{3,1},{4,6},{6,4},{5,7},{7,5},{8,10},{10,8},{9,1... | collective-permute-start | bytes 147464 | tf_op jit(solution)/shard_map/ppermute | solution.py:856
  79.6 1.5 %collective-permute-start.20 = (bf16[96,1024]{1,0:T(8,128)(2,1)S(1)}, bf16[96,1024]{1,0:T(8,128)(2,1)S(1)}, u32[]{:S(2)}, u32[]{:S(2)}) collective-permute-start(bf16[96,1024]{1,0:T(8,128)(2,1)S(1)} %get-tuple-element.71), channel_id=1, source_target_pairs={{0,1},{1,0},{2,3},{3,2},{4,5},{5,4},{6,7},{7,6},{8,9},{9,8},{10,11... | collective-permute-start | bytes 589832 | tf_op jit(solution)/shard_map/ppermute | solution.py:853
  79.7 1.7 %collective-permute-start.21 = (bf16[96,1024]{1,0:T(8,128)(2,1)S(1)}, bf16[96,1024]{1,0:T(8,128)(2,1)S(1)}, u32[]{:S(2)}, u32[]{:S(2)}) collective-permute-start(bf16[96,1024]{1,0:T(8,128)(2,1)S(1)} %get-tuple-element.72), channel_id=1, source_target_pairs={{0,1},{1,0},{2,3},{3,2},{4,5},{5,4},{6,7},{7,6},{8,9},{9,8},{10,11... | collective-permute-start | bytes 589832 | tf_op jit(solution)/shard_map/ppermute | solution.py:853
  80.1 1.5 %collective-permute-start.22 = (bf16[96,1024]{1,0:T(8,128)(2,1)S(1)}, bf16[96,1024]{1,0:T(8,128)(2,1)S(1)}, u32[]{:S(2)}, u32[]{:S(2)}) collective-permute-start(bf16[96,1024]{1,0:T(8,128)(2,1)S(1)} %get-tuple-element.73), channel_id=1, source_target_pairs={{0,1},{1,0},{2,3},{3,2},{4,5},{5,4},{6,7},{7,6},{8,9},{9,8},{10,11... | collective-permute-start | bytes 589832 | tf_op jit(solution)/shard_map/ppermute | solution.py:853
  81.0 1.4 %collective-permute-start.24 = (bf16[96,1024]{1,0:T(8,128)(2,1)S(1)}, bf16[96,1024]{1,0:T(8,128)(2,1)S(1)}, u32[]{:S(2)}, u32[]{:S(2)}) collective-permute-start(bf16[96,1024]{1,0:T(8,128)(2,1)S(1)} %get-tuple-element.75), channel_id=1, source_target_pairs={{0,1},{1,0},{2,3},{3,2},{4,5},{5,4},{6,7},{7,6},{8,9},{9,8},{10,11... | collective-permute-start | bytes 589832 | tf_op jit(solution)/shard_map/ppermute | solution.py:853
  82.4 3.6 %copy-start.1 = (bf16[4,4,64,256]{3,2,1,0:T(8,128)(2,1)S(1)}, bf16[4,4,64,256]{3,2,1,0:T(8,128)(2,1)}, u32[]{:S(2)}) copy-start(bf16[4,4,64,256]{3,2,1,0:T(8,128)(2,1)} %pool_ref.1) | copy-start | bytes 1572868
  82.5 3.6 %copy-start.7 = (s32[1,6]{1,0:T(1,128)S(1)}, s32[1,6]{1,0:T(1,128)}, u32[]{:S(2)}) copy-start(s32[1,6]{1,0:T(1,128)} %slot_ref.1) | copy-start | bytes 76
  82.6 5.2 %copy-start.5 = (bf16[192,1024]{1,0:T(8,128)(2,1)S(1)}, bf16[192,1024]{1,0:T(8,128)(2,1)}, u32[]{:S(2)}) copy-start(bf16[192,1024]{1,0:T(8,128)(2,1)} %copy-done.4) | copy-start | bytes 1179652
  82.7 19.6 %collective-permute-start.27 = (bf16[96,4096]{1,0:T(8,128)(2,1)S(1)}, bf16[96,4096]{1,0:T(8,128)(2,1)S(1)}, u32[]{:S(2)}, u32[]{:S(2)}) collective-permute-start(bf16[96,4096]{1,0:T(8,128)(2,1)S(1)} %add_pair.3.refs_4_), channel_id=1, source_target_pairs={{0,2},{2,0},{1,3},{3,1},{4,6},{6,4},{5,7},{7,5},{8,10},{10,8},{9,1... | collective-permute-start | bytes 2359304 | tf_op jit(solution)/shard_map/ppermute | solution.py:856
  84.3 1.6 %collective-permute-start.28 = (bf16[2,288,256]{2,1,0:T(8,128)(2,1)S(1)}, bf16[2,288,256]{2,1,0:T(8,128)(2,1)S(1)}, u32[]{:S(2)}, u32[]{:S(2)}) collective-permute-start(bf16[2,288,256]{2,1,0:T(8,128)(2,1)S(1)} %pad_maximum_fusion), channel_id=1, source_target_pairs={{0,1},{1,0},{2,3},{3,2},{4,5},{5,4},{6,7},{7,6},{8,9},{9,8},{10,11... | collective-permute-start | bytes 884744 | tf_op jit(solution)/shard_map/ppermute | solution.py:853
  84.4 1.7 %collective-permute-start.29 = (bf16[2,96,256]{2,1,0:T(8,128)(2,1)S(1)}, bf16[2,96,256]{2,1,0:T(8,128)(2,1)S(1)}, u32[]{:S(2)}, u32[]{:S(2)}) collective-permute-start(bf16[2,96,256]{2,1,0:T(8,128)(2,1)S(1)} %pad_maximum_fusion.1), channel_id=1, source_target_pairs={{0,1},{1,0},{2,3},{3,2},{4,5},{5,4},{6,7},{7,6},{8,9},{9,8},{10,11... | collective-permute-start | bytes 294920 | tf_op jit(solution)/shard_map/ppermute | solution.py:853
  97.4 5.1 %copy-start = (bf16[96,8192]{1,0:T(8,128)(2,1)S(1)}, bf16[96,8192]{1,0:T(8,128)(2,1)}, u32[]{:S(2)}) copy-start(bf16[96,8192]{1,0:T(8,128)(2,1)} %x_ref.3) | copy-start | bytes 4718596
  97.5 5.0 %collective-permute-start.25 = (bf16[96,8192]{1,0:T(8,128)(2,1)S(1)}, bf16[96,8192]{1,0:T(8,128)(2,1)S(1)}, u32[]{:S(2)}, u32[]{:S(2)}) collective-permute-start(bf16[96,8192]{1,0:T(8,128)(2,1)S(1)} %get-tuple-element.77), channel_id=1, source_target_pairs={{0,1},{1,0},{2,3},{3,2},{4,5},{5,4},{6,7},{7,6},{8,9},{9,8},{10,11... | collective-permute-start | bytes 4718600 | tf_op jit(solution)/shard_map/ppermute | solution.py:853
  102.4 2.4 %collective-permute-start.30 = (bf16[96,4096]{1,0:T(8,128)(2,1)S(1)}, bf16[96,4096]{1,0:T(8,128)(2,1)S(1)}, u32[]{:S(2)}, u32[]{:S(2)}) collective-permute-start(bf16[96,4096]{1,0:T(8,128)(2,1)S(1)} %get-tuple-element.82), channel_id=1, source_target_pairs={{0,1},{1,0},{2,3},{3,2},{4,5},{5,4},{6,7},{7,6},{8,9},{9,8},{10,11... | collective-permute-start | bytes 2359304 | tf_op jit(solution)/shard_map/ppermute | solution.py:853
